TPU v7x, 32 devices: a whole 2x2x4 slice. The times are simulated.
32 devices in a mesh: groups: 2 (over y), slab: 4 (over z), tilt: 2 (over x), rep: 2 (over core).
Axes of the slice: x: 2, y: 2, z: 4, core: 2. Of those that a mesh axis runs over, the one named last changes fastest.
Arguments:
- object_slab: bfloat16 [4, 2, 4, 512, 512], P(('groups', 'tilt'), None, None, 'slab'), parts along dimension 0, may hold values from -4 to 4
- probe_field: bfloat16 [2, 128, 128], replicated, may hold values from -6 to 6
- phases: float32 [128], replicated, may hold values from -3.140625 to 3.140625
- cotangent: bfloat16 [4, 32, 2, 128, 128], P(('groups', 'tilt'), ('slab', 'rep')), parts along dimension 0, may hold values from -6 to 6
- positions: int32 [4, 32], P(('groups', 'tilt'), ('slab', 'rep')), parts along dimension 0, may hold values from 0 to 384
- pair_index: int32 [3, 4, 4, 4, 16], P(None, ('groups', 'tilt'), 'slab'), parts along dimension 1, may hold values from 0 to 127, as said below
- pair_counts: int32 [4, 4, 4], P(('groups', 'tilt'), 'slab'), parts along dimension 0, may hold values from 0 to 16, as said below
- row_interp: float32 [8, 16, 16], replicated, may hold values from -0.75 to 0.75
- col_interp: float32 [8, 128, 128], replicated, may hold values from -0.5 to 0.5
Outputs:
- volume_grad: float32 [512, 2, 16, 128], P(('groups', 'slab', 'tilt', 'rep')), parts along dimension 0
There are 2 independent parts, one for each index of `groups`. A program takes and returns all parts, laid end to end along the dimension named above; an argument that names none is the same for every part. Nothing has to cross between parts.
Inputs may be any that keep to these rules, and one draw needn't show every extreme that they name: `pair_index`: component 0 lies below 128, component 1 below 64, component 2 below 8. `pair_counts`: in each angle each source slab has exactly 16 live slots towards one destination slab at most one slab away, 12 to 16 towards every other slab at most three away, and none towards slabs more than three away.
All inputs are finite; a program needn't handle non-finite values.
Results may differ from a plain program's by a relative error of at most 0.015.
Values sent between devices are 32-bit elements; how exact they have to be, the bound alone decides.
No kernel may reach another device: no remote copies, remote signals or barrier semaphores. Data moves between devices by JAX's collectives and lax.ppermute only.
A program may use at most 64 MiB of HBM per device.

v0:
```python
import math

import jax
import jax.numpy as jnp
from jax import lax
from jax.sharding import PartitionSpec as P

VB_DEV = 64


def propagators(phases):
    length = phases.shape[0]
    frequency = jnp.arange(length, dtype=jnp.int32)
    products = frequency[:, None] * frequency[None, :] % length
    angle_table = products.astype(jnp.float32) * (2.0 * math.pi / length) + phases[:, None]
    kernel_re = jnp.mean(jnp.cos(angle_table), axis=0)
    kernel_im = jnp.mean(jnp.sin(angle_table), axis=0)
    offset = (frequency[:, None] - frequency[None, :]) % length
    selector = (offset.reshape(-1)[:, None] == frequency[None, :]).astype(jnp.float32)
    kernels = jnp.stack([kernel_re, kernel_im], axis=-1)
    circulant = jnp.dot(selector, kernels, precision=lax.Precision.HIGHEST).reshape(
        length, length, 2
    )
    real_part = circulant[:, :, 0].astype(jnp.bfloat16)
    imag_part = circulant[:, :, 1].astype(jnp.bfloat16)
    forward = jnp.stack([jnp.stack([real_part, -imag_part]), jnp.stack([imag_part, real_part])])
    adjoint = jnp.stack(
        [jnp.stack([real_part.T, imag_part.T]), jnp.stack([-imag_part.T, real_part.T])]
    )
    return (forward, adjoint)


def apply_left(matrix, source):
    return jnp.einsum("oimk,ikn->omn", matrix, source, preferred_element_type=jnp.float32)


def apply_right(source, matrix):
    return jnp.einsum("imk,iokn->omn", source, matrix, preferred_element_type=jnp.float32)


def complex_product(left_field, right_field):
    return jnp.stack(
        [
            left_field[0] * right_field[0] - left_field[1] * right_field[1],
            left_field[0] * right_field[1] + left_field[1] * right_field[0],
        ]
    )


def conj_product(left_field, right_field):
    return jnp.stack(
        [
            left_field[0] * right_field[0] + left_field[1] * right_field[1],
            left_field[0] * right_field[1] - left_field[1] * right_field[0],
        ]
    )


def window_gradient(window, incoming, probe_field, forward, adjoint):
    slices = window.shape[1]
    field_now = probe_field
    fields_kept = []
    for slice_index in range(slices):
        fields_kept.append(field_now)
        if slice_index + 1 < slices:
            passed = complex_product(
                window[:, slice_index].astype(jnp.float32), field_now.astype(jnp.float32)
            ).astype(jnp.bfloat16)
            partial_value = apply_left(forward, passed).astype(jnp.bfloat16)
            field_now = apply_right(partial_value, adjoint).astype(jnp.bfloat16)
    gradients = [None] * slices
    back_field = incoming
    for slice_index in reversed(range(slices)):
        back_wide = back_field.astype(jnp.float32)
        gradients[slice_index] = conj_product(
            fields_kept[slice_index].astype(jnp.float32), back_wide
        )
        if slice_index > 0:
            turned = conj_product(window[:, slice_index].astype(jnp.float32), back_wide).astype(
                jnp.bfloat16
            )
            partial_value = apply_left(adjoint, turned).astype(jnp.bfloat16)
            back_field = apply_right(partial_value, forward).astype(jnp.bfloat16)
    return jnp.stack(gradients, axis=1)


def band_gradient(object_band, cotangent, positions, probe_field, forward, adjoint):
    window_size = probe_field.shape[-1]

    def cut_window(column):
        return lax.dynamic_slice_in_dim(object_band, column, window_size, 3)

    windows = jax.vmap(cut_window)(positions)
    updates = jax.vmap(
        lambda window, incoming: window_gradient(window, incoming, probe_field, forward, adjoint)
    )(windows, cotangent)
    initial = jnp.zeros(object_band.shape, jnp.float32)

    def accumulate(counter, running):
        column = positions[counter]
        current = lax.dynamic_slice_in_dim(running, column, window_size, 3)
        return lax.dynamic_update_slice_in_dim(running, current + updates[counter], column, 3)

    return lax.fori_loop(0, positions.shape[0], accumulate, initial)


def band_blocks(band_grad, block_rows, block_cols):
    parts_count, slices, rows_total, cols_total = band_grad.shape
    shaped = band_grad.reshape(
        parts_count,
        slices,
        rows_total // block_rows,
        block_rows,
        cols_total // block_cols,
        block_cols,
    )
    shaped = shaped.transpose(1, 2, 4, 0, 3, 5)
    return shaped.reshape(-1, parts_count, block_rows, block_cols)


def interpolate(blocks, weights, row_interp, col_interp):
    tile_count = row_interp.shape[0]
    block_rows = row_interp.shape[-1]
    block_cols = col_interp.shape[-1]
    selector = (weights[:, None] == jnp.arange(tile_count, dtype=jnp.int32)[None, :]).astype(
        jnp.float32
    )
    row_sel = jnp.dot(
        selector, row_interp.reshape(tile_count, -1), precision=lax.Precision.HIGHEST
    ).reshape(-1, block_rows, block_rows)
    col_sel = jnp.dot(
        selector, col_interp.reshape(tile_count, -1), precision=lax.Precision.HIGHEST
    ).reshape(-1, block_cols, block_cols)
    inner_term = jnp.einsum("icqk,ikl->icql", blocks, col_sel, precision=lax.Precision.HIGHEST)
    return jnp.einsum("ipq,icql->icpl", row_sel, inner_term, precision=lax.Precision.HIGHEST)


def on_device(
    object_slab,
    probe_field,
    phases,
    cotangent,
    positions,
    pair_index,
    pair_counts,
    row_interp,
    col_interp,
):
    forward, adjoint = propagators(phases)
    band_grad = band_gradient(
        object_slab[0], cotangent[0], positions[0], probe_field, forward, adjoint
    )
    block_rows = row_interp.shape[-1]
    block_cols = col_interp.shape[-1]
    peers = lax.axis_size("slab")
    capacity = pair_index.shape[-1]
    counts = pair_counts[0, 0]
    chosen = pair_index[:, 0, 0]
    blocks = band_blocks(band_grad, block_rows, block_cols)
    slot_ids = jnp.arange(capacity, dtype=jnp.int32)
    is_valid = (slot_ids[None, :] < counts[:, None]).astype(jnp.int32)
    outgoing = jnp.take(blocks, chosen[0].reshape(-1), axis=0).reshape(
        peers, capacity, 2, block_rows, block_cols
    )
    details = jnp.stack([chosen[1], chosen[2], is_valid], axis=-1)
    arrived = lax.all_to_all(outgoing, "slab", split_axis=0, concat_axis=0, tiled=True)
    arrived_details = lax.all_to_all(details, "slab", split_axis=0, concat_axis=0, tiled=True)

    def per_source(packed):
        return interpolate(packed[0], packed[1][:, 1], row_interp, col_interp)

    mixed_blocks = lax.map(per_source, (arrived, arrived_details))
    mixed_blocks, got_details = (mixed_blocks, arrived_details)
    flat_blocks = mixed_blocks.reshape(-1, 2 * block_rows * block_cols)
    target = got_details[..., 0].reshape(-1)
    is_live = got_details[..., 2].reshape(-1)
    placing = (
        (target[None, :] == jnp.arange(VB_DEV, dtype=jnp.int32)[:, None]) & (is_live[None, :] > 0)
    ).astype(jnp.float32)
    volume_local = jnp.dot(placing, flat_blocks, precision=lax.Precision.HIGHEST)
    owned_rows = lax.psum_scatter(volume_local, ("tilt", "rep"), scatter_dimension=0, tiled=True)
    return owned_rows.reshape(-1, 2, block_rows, block_cols)


def solution(mesh):
    in_specs = (
        P(("groups", "tilt"), None, None, "slab", None),
        P(),
        P(),
        P(("groups", "tilt"), ("slab", "rep"), None, None, None),
        P(("groups", "tilt"), ("slab", "rep")),
        P(None, ("groups", "tilt"), "slab", None, None),
        P(("groups", "tilt"), "slab", None),
        P(),
        P(),
    )
    out_specs = P(("groups", "slab", "tilt", "rep"), None, None, None)
    return jax.shard_map(
        on_device, mesh=mesh, in_specs=in_specs, out_specs=out_specs, check_vma=False
    )
```

profile of v0, /device:TPU:0, one launch (start us, length us, event | category | flops | bytes accessed | tf_op | source)
XLA Modules:
  0.0 155.0 jit_solution(14279759990435542014)
XLA Ops:
  8.7 6.3 %all-to-all-start = ((s32[4,16,3]{1,2,0:T(4,128)}), s32[4,16,3]{1,2,0:T(4,128)S(1)}, u32[]{:S(2)}, u32[]{:S(2)}) async-start(s32[4,16,3]{1,2,0:T(4,128)} %copy.184), calls=%async_computation | async-start | bytes 16384 | tf_op jit(solution)/shard_map/all_to_all | solution.py:167
  16.1 5.8 %fusion.47 = bf16[1,2,128,128]{3,1,2,0:T(2,128)(2,1)S(1)} fusion(s32[16384]{0:T(1024)S(1)} %add_select_fusion.1, f32[128,1]{0,1:T(1,128)S(1)} %get-tuple-element.231, f32[128,1]{0,1:T(1,128)S(1)} %get-tuple-element.232), kind=kOutput, calls=%fused_computation.70 | convolution fusion | flops 52429056 | bytes 132096 | tf_op jit(solution)/shard_map/dot_general | solution.py:21
  24.9 1.5 gather_fusion
  26.4 1.6 %fusion.106 = (bf16[4,2,1,128,128]{3,2,1,4,0:T(2,128)(2,1)S(1)}, bf16[4,2,1,128,128]{3,2,1,4,0:T(2,128)(2,1)S(1)}, bf16[4,2,1,128,128]{3,2,1,4,0:T(2,128)(2,1)S(1)}, bf16[4,2,1,128,128]{3,2,1,4,0:T(2,128)(2,1)S(1)}) fusion(bf16[4,2,4,128,128]{3,2,1,4,0:T(4,128)(2,1)S(1)} %gather_fusion), kind=kLoop, calls=%fused_computation.195 | loop fusion | bytes 2097152 | tf_op jit(solution)/shard_map/vmap()/slice | solution.py:79
  32.1 1.3 fusion.32
  34.8 1.3 fusion.24
  37.8 1.5 fusion.28
  40.2 1.6 %fusion.36 = f32[4,2,128,128]{3,2,0,1:T(8,128)S(1)} fusion(bf16[1,2,128,128]{2,3,1,0:T(8,128)(2,1)} %copy-done.10, bf16[1,2,128,128]{2,3,1,0:T(8,128)(2,1)} %copy-done.8, bf16[1,4,128,128]{3,2,1,0:T(8,128)(2,1)} %get-tuple-element.216, bf16[1,4,128,128]{3,2,1,0:T(8,128)(2,1)} %get-tuple-element.217, bf16[1,2,128,128]{3,2,1,0:T(8,128)(2,1)} %get-tuple-element.227, ...), kind=kOutput, calls=%fused_computation.59 | convolution fusion | flops 135069696 | bytes 1048576 | tf_op jit(solution)/shard_map/vmap(imk,iokn->omn)/dot_general | solution.py:38
  42.7 1.5 fusion.40
  44.5 1.5 maximum_bitcast_fusion
  46.6 27.5 %while.24 = (s32[]{:T(128)}, f32[2,4,128,512]{3,2,1,0:T(8,128)S(1)}, s32[4]{0:T(128)S(1)}, f32[4,2,4,128,128]{4,3,0,1,2:T(8,128)}, s32[]{:T(128)}, /*index=5*/s32[]{:T(128)}, s32[]{:T(128)}) while((s32[]{:T(128)}, f32[2,4,128,512]{3,2,1,0:T(8,128)S(1)}, s32[4]{0:T(128)S(1)}, f32[4,2,4,128,128]{4,3,0,1,2:T(8,128)}, s32[]{:T(128)}, ...), condition=%wide.region_3.4_spmd, body=%wide.region_2.3_spmd.sunk | while | flops 131077 | bytes 2622083 | solution.py:104
  50.4 3.1 %dynamic_update_slice.15 = f32[2,4,128,512]{3,2,1,0:T(8,128)S(1)} dynamic-update-slice(f32[2,4,128,512]{3,2,1,0:T(8,128)S(1)} %get-tuple-element.333, f32[2,4,128,128]{3,2,1,0:T(8,128)S(1)} %fusion.129, s32[]{:T(128)} %constant.81.clone.1..sunk, s32[]{:T(128)} %constant.81.clone.1..sunk, s32[]{:T(128)} %constant.81.clone.1..sunk, s32[]{:T(128)S(6)} %select_n.94) | dynamic-update-slice | bytes 1048580 | tf_op jit(solution)/shard_map/while/body/eval_jaxpr/dynamic_update_slice | solution.py:102
  57.3 3.1 %dynamic_update_slice.15 = f32[2,4,128,512]{3,2,1,0:T(8,128)S(1)} dynamic-update-slice(f32[2,4,128,512]{3,2,1,0:T(8,128)S(1)} %get-tuple-element.333, f32[2,4,128,128]{3,2,1,0:T(8,128)S(1)} %fusion.129, s32[]{:T(128)} %constant.81.clone.1..sunk, s32[]{:T(128)} %constant.81.clone.1..sunk, s32[]{:T(128)} %constant.81.clone.1..sunk, s32[]{:T(128)S(6)} %select_n.94) | dynamic-update-slice | bytes 1048580 | tf_op jit(solution)/shard_map/while/body/eval_jaxpr/dynamic_update_slice | solution.py:102
  64.2 3.1 %dynamic_update_slice.15 = f32[2,4,128,512]{3,2,1,0:T(8,128)S(1)} dynamic-update-slice(f32[2,4,128,512]{3,2,1,0:T(8,128)S(1)} %get-tuple-element.333, f32[2,4,128,128]{3,2,1,0:T(8,128)S(1)} %fusion.129, s32[]{:T(128)} %constant.81.clone.1..sunk, s32[]{:T(128)} %constant.81.clone.1..sunk, s32[]{:T(128)} %constant.81.clone.1..sunk, s32[]{:T(128)S(6)} %select_n.94) | dynamic-update-slice | bytes 1048580 | tf_op jit(solution)/shard_map/while/body/eval_jaxpr/dynamic_update_slice | solution.py:102
  71.1 3.1 %dynamic_update_slice.15 = f32[2,4,128,512]{3,2,1,0:T(8,128)S(1)} dynamic-update-slice(f32[2,4,128,512]{3,2,1,0:T(8,128)S(1)} %get-tuple-element.333, f32[2,4,128,128]{3,2,1,0:T(8,128)S(1)} %fusion.129, s32[]{:T(128)} %constant.81.clone.1..sunk, s32[]{:T(128)} %constant.81.clone.1..sunk, s32[]{:T(128)} %constant.81.clone.1..sunk, s32[]{:T(128)S(6)} %select_n.94) | dynamic-update-slice | bytes 1048580 | tf_op jit(solution)/shard_map/while/body/eval_jaxpr/dynamic_update_slice | solution.py:102
  74.1 1.7 %reshape.972 = f32[2,4,8,16,4,128]{5,4,3,2,1,0:T(4,128)} reshape(f32[2,4,128,512]{3,2,1,0:T(8,128)S(1)} %get-tuple-element.116) | data formatting | bytes 4194304 | tf_op jit(solution)/shard_map/reshape | solution.py:109
  75.8 1.8 %copy.215 = f32[4,8,4,2,16,128]{5,4,3,2,1,0:T(8,128)S(1)} copy(f32[4,8,4,2,16,128]{5,2,4,1,0,3:T(4,128)} %bitcast.458) | data formatting | bytes 4194304 | tf_op jit(solution)/shard_map/transpose | solution.py:117
  79.6 5.1 %all-to-all-start.1 = ((f32[4,16,2,16,128]{4,3,2,1,0:T(8,128)}), f32[4,16,2,16,128]{4,3,2,1,0:T(8,128)S(1)}, u32[]{:S(2)}, u32[]{:S(2)}) async-start(f32[4,16,2,16,128]{4,3,2,1,0:T(8,128)} %broadcast_select_fusion), calls=%async_computation.1 | async-start | bytes 2097152 | tf_op jit(solution)/shard_map/all_to_all | solution.py:166
  85.0 23.9 %all-to-all-done.1 = f32[4,16,2,16,128]{4,3,2,1,0:T(8,128)S(1)} async-done(((f32[4,16,2,16,128]{4,3,2,1,0:T(8,128)}), f32[4,16,2,16,128]{4,3,2,1,0:T(8,128)S(1)}, u32[]{:S(2)}, u32[]{:S(2)}) %all-to-all-start.1) | async-done | bytes 1048608 | tf_op jit(solution)/shard_map/all_to_all | solution.py:166
  109.0 11.4 %while.25 = (s32[]{:T(128)}, f32[4,16,2,16,128]{4,3,2,1,0:T(8,128)S(1)}, f32[4,16,2,16,128]{4,3,2,1,0:T(8,128)S(1)}, s32[4,16,3]{1,2,0:T(4,128)S(1)}, f32[8,128,...) while((s32[]{:T(128)}, ...), condition=%wide.wide.region_5.6_spmd, body=%wide.wide.region_4.5_spmd.sunk | while | flops 138805504 | bytes 3842785 | solution.py:172
  109.8 1.3 fusion.137
  120.6 1.7 %fusion.91 = f32[64,4096]{1,0:T(8,128)} fusion(f32[64,4096]{1,0:T(8,128)S(1)} %reshape.974, s32[64]{0:T(128)S(1)} %eq.46, pred[64]{0:T(512)(128)(4,1)S(1)} %gt.16), kind=kOutput, calls=%fused_computation.166 | convolution fusion | flops 201334784 | bytes 2097472 | tf_op jit(solution)/shard_map/dot_general | solution.py:180
  122.3 24.1 %reduce-scatter.2.cloned.1.call-done = f32[16,4096]{1,0:T(8,128)} async-done(((f32[64,4096]{1,0:T(8,128)}), f32[16,4096]{1,0:T(8,128)}) %reduce-scatter.2.cloned.1.call-update) | async-done | bytes 262160 | tf_op jit(solution)/shard_map/reduce_scatter | solution.py:181
  146.4 1.7 %copy.289 = f32[2,8,32,128]{3,2,1,0:T(8,128)} copy(f32[2,8,32,128]{3,1,2,0:T(8,128)} %bitcast.467) | data formatting | bytes 524288
  (121 shorter events, 35.4 us)
Async XLA Ops:
  6.5 17.6 %copy-start.1 = (bf16[1,2,4,128,512]{4,3,2,1,0:T(8,128)(2,1)S(1)}, bf16[1,2,4,128,512]{4,3,2,1,0:T(8,128)(2,1)}, u32[]{:S(2)}) copy-start(bf16[1,2,4,128,512]{4,3,2,1,0:T(8,128)(2,1)} %param.13) | copy-start | bytes 3145732
  8.7 70.9 %all-to-all-start = ((s32[4,16,3]{1,2,0:T(4,128)}), s32[4,16,3]{1,2,0:T(4,128)S(1)}, u32[]{:S(2)}, u32[]{:S(2)}) async-start(s32[4,16,3]{1,2,0:T(4,128)} %copy.184), calls=%async_computation | async-start | bytes 16384 | tf_op jit(solution)/shard_map/all_to_all | solution.py:167
  16.0 8.9 %copy-start.12 = (s32[1,4]{1,0:T(1,128)S(1)}, s32[1,4]{1,0:T(1,128)}, u32[]{:S(2)}) copy-start(s32[1,4]{1,0:T(1,128)} %param.17) | copy-start | bytes 52
  26.4 2.4 %copy-start.7 = (bf16[2,128,128]{2,1,0:T(8,128)(2,1)S(1)}, bf16[2,128,128]{2,1,0:T(8,128)(2,1)}, u32[]{:S(2)}) copy-start(bf16[2,128,128]{2,1,0:T(8,128)(2,1)} %param.14) | copy-start | bytes 196612
  28.0 1.6 %copy-start.4 = (bf16[1,4,2,128,128]{4,3,2,1,0:T(8,128)(2,1)S(1)}, bf16[1,4,2,128,128]{4,3,2,1,0:T(8,128)(2,1)}, u32[]{:S(2)}) copy-start(bf16[1,4,2,128,128]{4,3,2,1,0:T(8,128)(2,1)} %param.16) | copy-start | bytes 786436
  28.8 3.2 %copy-start.3 = (f32[128,128]{1,0:T(8,128)}, f32[128,128]{1,0:T(8,128)S(1)}, u32[]{:S(2)}) copy-start(f32[128,128]{1,0:T(8,128)S(1)} %get-tuple-element.221) | copy-start | bytes 196612
  29.6 1.6 %copy-start.6 = (bf16[1,128,128]{1,2,0:T(8,128)(2,1)S(1)}, bf16[1,128,128]{1,2,0:T(8,128)(2,1)}, u32[]{:S(2)}) copy-start(bf16[1,128,128]{1,2,0:T(8,128)(2,1)} %bitcast_negate_fusion.1) | copy-start | bytes 98308
  30.4 1.0 copy-start.5
  31.3 3.5 %copy-start.8 = (bf16[1,2,128,128]{2,3,1,0:T(8,128)(2,1)}, bf16[1,2,128,128]{2,3,1,0:T(8,128)(2,1)S(1)}, u32[]{:S(2)}) copy-start(bf16[1,2,128,128]{2,3,1,0:T(8,128)(2,1)S(1)} %get-tuple-element.224) | copy-start | bytes 196612
  31.3 3.5 %copy-start.10 = (bf16[1,2,128,128]{2,3,1,0:T(8,128)(2,1)}, bf16[1,2,128,128]{2,3,1,0:T(8,128)(2,1)S(1)}, u32[]{:S(2)}) copy-start(bf16[1,2,128,128]{2,3,1,0:T(8,128)(2,1)S(1)} %get-tuple-element.225) | copy-start | bytes 196612
  40.2 2.5 %copy-start.9 = (bf16[1,2,128,128]{2,3,1,0:T(8,128)(2,1)S(1)}, bf16[1,2,128,128]{2,3,1,0:T(8,128)(2,1)}, u32[]{:S(2)}) copy-start(bf16[1,2,128,128]{2,3,1,0:T(8,128)(2,1)} %copy-done.8) | copy-start | bytes 196612
  42.7 1.7 %copy-start.2 = (f32[1,4,128,128]{3,2,1,0:T(8,128)S(1)}, f32[1,4,128,128]{3,2,1,0:T(8,128)}, u32[]{:S(2)}) copy-start(f32[1,4,128,128]{3,2,1,0:T(8,128)} %get-tuple-element.195) | copy-start | bytes 786436
  46.0 0.7 copy-start.13
  78.4 6.3 %copy-start.11 = (f32[8,16,16]{2,1,0:T(8,128)S(1)}, f32[8,16,16]{2,1,0:T(8,128)}, u32[]{:S(2)}) copy-start(f32[8,16,16]{2,1,0:T(8,128)} %param.20) | copy-start | bytes 24580
  78.5 30.5 %copy-start = (f32[8,128,128]{2,1,0:T(8,128)S(1)}, f32[8,128,128]{2,1,0:T(8,128)}, u32[]{:S(2)}) copy-start(f32[8,128,128]{2,1,0:T(8,128)} %param.21) | copy-start | bytes 1572868
  79.6 29.4 %all-to-all-start.1 = ((f32[4,16,2,16,128]{4,3,2,1,0:T(8,128)}), f32[4,16,2,16,128]{4,3,2,1,0:T(8,128)S(1)}, u32[]{:S(2)}, u32[]{:S(2)}) async-start(f32[4,16,2,16,128]{4,3,2,1,0:T(8,128)} %broadcast_select_fusion), calls=%async_computation.1 | async-start | bytes 2097152 | tf_op jit(solution)/shard_map/all_to_all | solution.py:166
  84.7 61.7 %reduce-scatter.2.cloned.1.call-start = ((), (), s32[]{:S(2)}) async-start(), calls=%async_computation.3 | async-start | bytes 1310720 | tf_op jit(solution)/shard_map/reduce_scatter | solution.py:181
Sparse Core Ops, SparseCore 0:
  122.4 23.9 reduce-scatter.1
where the time goes:
time: 156 us; the launch traced here: 155 us
  waiting for transfers between devices  48.1 us (31%)
  local copies, waits for them, and re-layouts  30.4 us (19%)
  matrix products  26.9 us (17%)
  other arithmetic  16.2 us (10%)
  between operations  13.9 us (9%)
  starting transfers between devices  11.4 us (7%)
  loops' own time  8.1 us (5%)
    reduce_scatter x1, waiting for transfers between devices, on_device(): lax.psum_scatter(volume_local, ('tilt', 'rep'), scatter_dimension=0, tile...  24.1 us
    all_to_all x1, waiting for transfers between devices, on_device(): lax.all_to_all(outgoing, 'slab', split_axis=0, concat_axis=0, tiled=True)  23.9 us
    dynamic_update_slice x4, local copies, waits for them, and re-layouts, accumulate(): lax.dynamic_update_slice_in_dim(running, current + updates[counter], colu...  12.2 us
    dot_general x6, matrix products, apply_right(): jnp.einsum('imk,iokn->omn', source, matrix, preferred_element_type=jnp.fl...  8.53 us
    another operation x1, loops' own time, band_gradient(): return lax.fori_loop(0, positions.shape[0], accumulate, initial)  7.89 us
    all_to_all x1, starting transfers between devices, on_device(): lax.all_to_all(details, 'slab', split_axis=0, concat_axis=0, tiled=True)  6.32 us
    unnamed x37, local copies, waits for them, and re-layouts  5.99 us
    dot_general x1, matrix products, propagators(): jnp.dot(selector, kernels, precision=lax.Precision.HIGHEST)  5.85 us
  transfers between devices with their start and end apart: 3, of which 2 were waited for; matrix products, arithmetic and copies ran while one was open for 36% of the time, Pallas kernels for 0%

commit v1 on v0

v1 whole, which is shorter than its diff:
```python
import functools
import math

import jax
import jax.numpy as jnp
import numpy as np
from jax import lax
from jax.experimental import pallas as pl
from jax.experimental.pallas import tpu as pltpu
from jax.sharding import PartitionSpec as P

VB_DEV = 64
REACH = 3
HIGH = lax.Precision.HIGHEST
SMEM = pltpu.SMEM
VMEM = pltpu.VMEM


def dot(left, right, precision=None):
    return jnp.dot(left, right, precision=precision, preferred_element_type=jnp.float32)


def slab_shifts(peers):
    if peers <= 2 * REACH + 1:
        return tuple(range(peers))
    return (0,) + tuple(s for k in range(1, REACH + 1) for s in (k, peers - k))


def angle_table(length):
    grid = np.arange(length)
    angles = (grid[:, None] * grid[None, :] % length) * (2.0 * math.pi / length)
    return np.concatenate([np.cos(angles), np.sin(angles)], axis=1).astype(np.float32)


def propagator_blocks(phases, table):
    length = phases.shape[-1]
    row = lax.broadcasted_iota(jnp.int32, (8, length), 0)
    waves = jnp.where(row == 0, jnp.cos(phases), jnp.sin(phases))
    sums = dot(waves, table, HIGH) * (1.0 / length)
    cc, cs = sums[0:1, :length], sums[0:1, length:]
    sc, ss = sums[1:2, :length], sums[1:2, length:]

    def circulant(line):
        wide = jnp.broadcast_to(line, (length, length))
        return pltpu.roll(wide, 0, 1, stride=1, stride_axis=0)

    kr, ki = circulant(cc + ss), circulant(sc - cs)
    krt, kit = circulant(cc - ss), circulant(sc + cs)
    whole = jnp.concatenate(
        [jnp.concatenate([kr, -ki], 1), jnp.concatenate([ki, kr], 1)], 0
    ).astype(jnp.bfloat16)
    turned = jnp.concatenate(
        [jnp.concatenate([krt, kit], 1), jnp.concatenate([-kit, krt], 1)], 0
    ).astype(jnp.bfloat16)
    return whole, turned


def frame_kernel(
    shifts,
    pos_ref,
    index_ref,
    count_ref,
    obj_ref,
    probe_ref,
    cot_ref,
    phase_ref,
    table_ref,
    mine_ref,
    other_ref,
    *rest,
):
    details, band, window = rest[:-2], rest[-2], rest[-1]
    me, core = lax.axis_index("slab"), lax.axis_index("rep")
    peers = lax.axis_size("slab")
    capacity = index_ref.shape[-1]
    for k, shift in enumerate(shifts):
        dest = lax.rem(me + shift, peers)
        live = count_ref[0, 0, dest]
        for slot in range(capacity):
            details[k][0, slot] = jnp.where(slot < live, index_ref[1, 0, 0, dest, slot], VB_DEV)
            details[k][1, slot] = index_ref[2, 0, 0, dest, slot]

    whole, turned = propagator_blocks(phase_ref[...], table_ref[...])
    size = probe_ref.shape[-1]
    _, _, slices, rows, cols = obj_ref.shape
    count = cot_ref.shape[1]
    wide = count * size
    group = 2 if count % 2 == 0 else 1
    f32, bf16 = jnp.float32, jnp.bfloat16

    col_down = lax.broadcasted_iota(jnp.int32, (cols, size), 0)
    lane = lax.broadcasted_iota(jnp.int32, (cols, size), 1)
    cut = jnp.concatenate(
        [(col_down == lane + pos_ref[0, w]).astype(bf16) for w in range(count)], 1
    )
    lane_down = lax.broadcasted_iota(jnp.int32, (size, cols), 0)
    col = lax.broadcasted_iota(jnp.int32, (size, cols), 1)
    paste = jnp.concatenate(
        [(col == lane_down + pos_ref[0, w]).astype(bf16) for w in range(count)], 0
    )

    for s in range(slices):
        source = jnp.concatenate([obj_ref[0, 0, s], obj_ref[0, 1, s]], 0)
        window[s] = dot(source, cut).astype(bf16)

    def tile(s, c, w):
        return window[s, c * rows : (c + 1) * rows, w * size : (w + 1) * size].astype(f32)

    def propagate(fields, first, second):
        result = []
        for g in range(0, count, group):
            stack = jnp.concatenate(
                [jnp.concatenate([fields[w][c] for w in range(g, g + group)], 1) for c in (0, 1)], 0
            )
            part = dot(first, stack).astype(bf16)
            turned_part = jnp.concatenate(
                [
                    jnp.concatenate(
                        [
                            part[c * size : (c + 1) * size, k * size : (k + 1) * size]
                            for c in (0, 1)
                        ],
                        1,
                    )
                    for k in range(group)
                ],
                0,
            )
            done = dot(turned_part, second).astype(bf16)
            for k in range(group):
                result.append(
                    tuple(
                        done[k * size : (k + 1) * size, c * size : (c + 1) * size] for c in (0, 1)
                    )
                )
        return result

    now = [(probe_ref[0], probe_ref[1])] * count
    kept = []
    for s in range(slices):
        kept.append(now)
        if s + 1 < slices:
            passed = []
            for w in range(count):
                o_re, o_im = tile(s, 0, w), tile(s, 1, w)
                p_re, p_im = now[w][0].astype(f32), now[w][1].astype(f32)
                passed.append(
                    (
                        (o_re * p_re - o_im * p_im).astype(bf16),
                        (o_re * p_im + o_im * p_re).astype(bf16),
                    )
                )
            now = propagate(passed, whole, turned)

    block_rows, block_cols = mine_ref.shape[-2:]
    across = cols // block_cols
    back = [(cot_ref[0, w, 0], cot_ref[0, w, 1]) for w in range(count)]
    for s in reversed(range(slices)):
        grads, rhos = [], []
        for w in range(count):
            c_re, c_im = back[w][0].astype(f32), back[w][1].astype(f32)
            p_re, p_im = kept[s][w][0].astype(f32), kept[s][w][1].astype(f32)
            grads.append(
                (
                    (p_re * c_re + p_im * c_im).astype(bf16),
                    (p_re * c_im - p_im * c_re).astype(bf16),
                )
            )
            if s > 0:
                o_re, o_im = tile(s, 0, w), tile(s, 1, w)
                rhos.append(
                    (
                        (o_re * c_re + o_im * c_im).astype(bf16),
                        (o_re * c_im - o_im * c_re).astype(bf16),
                    )
                )
        if s > 0:
            back = propagate(rhos, turned, whole)
        stack = jnp.concatenate(
            [jnp.concatenate([grads[w][c] for w in range(count)], 1) for c in (0, 1)], 0
        )
        spread = dot(stack, paste)
        for c in (0, 1):
            for i in range(rows // block_rows):
                top = c * rows + i * block_rows
                for j in range(across):
                    band[c, (s * (rows // block_rows) + i) * across + j] = spread[
                        top : top + block_rows, j * block_cols : (j + 1) * block_cols
                    ]

    for k, shift in enumerate(shifts):
        dest = lax.rem(me + shift, peers)
        for slot in range(capacity):
            block = index_ref[0, 0, 0, dest, slot]
            mine_ref[k * capacity + slot] = band[core, block]
            other_ref[k * capacity + slot] = band[1 - core, block]


def place_kernel(sources, owners, *refs):
    details, blocks = refs[:sources], refs[sources : 2 * sources]
    row_ref, col_ref = refs[2 * sources : 2 * sources + 2]
    outs = refs[2 * sources + 2 : -2]
    volume, col_bf = refs[-2:]
    f32, bf16 = jnp.float32, jnp.bfloat16
    tiles, block_rows, _ = row_ref.shape
    capacity = blocks[0].shape[0]
    wide = capacity * block_rows
    volume[...] = jnp.zeros_like(volume)
    col_bf[...] = col_ref[...].astype(bf16)
    down = lax.broadcasted_iota(jnp.int32, (block_rows, wide), 0)
    along = lax.broadcasted_iota(jnp.int32, (block_rows, wide), 1)
    repeat = (lax.rem(along, block_rows) == down).astype(bf16)
    row_wide = dot(row_ref[...].reshape(tiles * block_rows, block_rows).astype(bf16), repeat)
    row_scr = row_wide.reshape(tiles, block_rows, wide)
    strip = lax.div(along, block_rows)
    for p in range(sources):
        inner, rows = [], []
        for slot in range(capacity):
            t = details[p][1, slot]
            inner.append(dot(blocks[p][slot].astype(bf16), col_bf[t]).astype(bf16))
            picked = row_scr[0]
            for u in range(1, tiles):
                picked = jnp.where(t == u, row_scr[u], picked)
            rows.append(jnp.where(strip == slot, picked, 0.0).astype(bf16))
        mixed = dot(jnp.concatenate(rows, 0), jnp.concatenate(inner, 0))
        for slot in range(capacity):
            v = details[p][0, slot]
            volume[v] = volume[v] + mixed[slot * block_rows : (slot + 1) * block_rows]
    tilt, core = lax.axis_index("tilt"), lax.axis_index("rep")
    tilts, cores = lax.axis_size("tilt"), lax.axis_size("rep")
    each = VB_DEV // (tilts * cores)
    for out, (dt, dr) in zip(outs, owners):
        owner = lax.rem(tilt + dt, tilts) * cores + lax.rem(core + dr, cores)
        out[...] = volume[pl.ds(owner * each, each)]


def sum_kernel(owners, *refs):
    out_ref = refs[-1]
    core, cores = lax.axis_index("rep"), lax.axis_size("rep")
    for dr in range(cores):
        total = None
        for ref, (_, other) in zip(refs, owners):
            if other == dr:
                total = ref[...] if total is None else total + ref[...]
        out_ref[:, lax.rem(core + dr, cores)] = total


def on_device(
    object_slab,
    probe_field,
    phases,
    cotangent,
    positions,
    pair_index,
    pair_counts,
    row_interp,
    col_interp,
):
    peers = lax.axis_size("slab")
    tilts, cores = lax.axis_size("tilt"), lax.axis_size("rep")
    shifts = slab_shifts(peers)
    capacity = pair_index.shape[-1]
    block_rows, block_cols = row_interp.shape[-1], col_interp.shape[-1]
    _, _, slices, rows, cols = object_slab.shape
    windows, size = cotangent.shape[1], cotangent.shape[-1]
    f32 = jnp.float32
    smem, vmem = pl.BlockSpec(memory_space=SMEM), pl.BlockSpec(memory_space=VMEM)
    block_set = jax.ShapeDtypeStruct((len(shifts) * capacity, block_rows, block_cols), f32)
    detail = jax.ShapeDtypeStruct((2, capacity), jnp.int32)
    big = pltpu.CompilerParams(vmem_limit_bytes=40 * 1024 * 1024)

    mine, other, *details = pl.pallas_call(
        functools.partial(frame_kernel, shifts),
        out_shape=[block_set, block_set] + [detail] * len(shifts),
        in_specs=[smem] * 3 + [vmem] * 5,
        out_specs=[vmem, vmem] + [smem] * len(shifts),
        scratch_shapes=[
            pltpu.VMEM(
                (2, slices * (rows // block_rows) * (cols // block_cols), block_rows, block_cols),
                f32,
            ),
            pltpu.VMEM((slices, 2 * rows, windows * size), jnp.bfloat16),
        ],
        compiler_params=big,
        name="frame",
    )(
        positions,
        pair_index,
        pair_counts,
        object_slab,
        probe_field,
        cotangent,
        phases.reshape(1, -1),
        jnp.asarray(angle_table(size)),
    )

    swap = [(r, (r + 1) % cores) for r in range(cores)]
    got = lax.ppermute(other, "rep", swap)
    blocks, arrived_details = [], []
    for k, shift in enumerate(shifts):
        piece = slice(k * capacity, (k + 1) * capacity)
        summed = mine[piece] + got[piece]
        info = details[k]
        if shift:
            ring = [(p, (p + shift) % peers) for p in range(peers)]
            info = lax.ppermute(info, "slab", ring)
            summed = lax.ppermute(summed, "slab", ring)
        blocks.append(summed)
        arrived_details.append(info)

    owners = [(dt, dr) for dt in range(tilts) for dr in range(cores)]
    each = VB_DEV // len(owners)
    share = jax.ShapeDtypeStruct((each, block_rows, block_cols), f32)
    sources = len(shifts)
    parts = pl.pallas_call(
        functools.partial(place_kernel, sources, owners),
        out_shape=[share] * len(owners),
        in_specs=[smem] * sources + [vmem] * (sources + 2),
        out_specs=[vmem] * len(owners),
        scratch_shapes=[
            pltpu.VMEM((VB_DEV + 1, block_rows, block_cols), f32),
            pltpu.VMEM(col_interp.shape, jnp.bfloat16),
        ],
        compiler_params=big,
        name="place",
    )(*arrived_details, *blocks, row_interp, col_interp)

    arrived = []
    for part, (dt, dr) in zip(parts, owners):
        if dt or dr:
            route = [
                (t * cores + r, (t + dt) % tilts * cores + (r + dr) % cores)
                for t in range(tilts)
                for r in range(cores)
            ]
            part = lax.ppermute(part, ("tilt", "rep"), route)
        arrived.append(part)
    return pl.pallas_call(
        functools.partial(sum_kernel, owners),
        out_shape=jax.ShapeDtypeStruct((each, cores, block_rows, block_cols), f32),
        in_specs=[vmem] * len(owners),
        out_specs=vmem,
        name="total",
    )(*arrived)


def solution(mesh):
    in_specs = (
        P(("groups", "tilt"), None, None, "slab", None),
        P(),
        P(),
        P(("groups", "tilt"), ("slab", "rep"), None, None, None),
        P(("groups", "tilt"), ("slab", "rep")),
        P(None, ("groups", "tilt"), "slab", None, None),
        P(("groups", "tilt"), "slab", None),
        P(),
        P(),
    )
    out_specs = P(("groups", "slab", "tilt", "rep"), None, None, None)
    return jax.shard_map(
        on_device, mesh=mesh, in_specs=in_specs, out_specs=out_specs, check_vma=False
    )
```

time: 156 us -> 45 us (0.29)
  waiting for transfers between devices: 48.1 us -> 16.2 us
  matrix products: 26.9 us -> 0 us
  local copies, waits for them, and re-layouts: 30.4 us -> 6.59 us
  other arithmetic: 16.2 us -> 0.07 us
  between operations: 13.9 us -> 0.07 us
  Pallas kernels: 0 us -> 8.4 us
  loops' own time: 8.1 us -> 0 us
  starting transfers between devices: 11.4 us -> 13.1 us
    dot_general x24 -> x0, matrix products: 26.9 us -> none  [the longest x6 8.53 us: apply_right(): jnp.einsum('imk,iokn->omn', source, matrix, preferred_element_type=jnp.fl...]
    reduce_scatter x1 -> x0, waiting for transfers between devices: 24.1 us -> none  [on_device(): lax.psum_scatter(volume_local, ('tilt', 'rep'), scatter_dimension=0, tile...]
    all_to_all x2 -> x0, waiting for transfers between devices: 23.9 us -> none  [the longest x1 23.9 us: on_device(): lax.all_to_all(outgoing, 'slab', split_axis=0, concat_axis=0, tiled=True)]
    ppermute x0 -> x10, waiting for transfers between devices: none -> 16.2 us  [the longest x3 8.19 us: on_device(): info = lax.ppermute(info, 'slab', ring)]
    ppermute x0 -> x10, starting transfers between devices: none -> 13.1 us  [the longest x3 6.03 us: on_device(): summed = lax.ppermute(summed, 'slab', ring)]
    dynamic_update_slice x4 -> x0, local copies, waits for them, and re-layouts: 12.2 us -> none  [accumulate(): lax.dynamic_update_slice_in_dim(running, current + updates[counter], colu...]
    all_to_all x2 -> x0, starting transfers between devices: 11.4 us -> none  [the longest x1 6.32 us: on_device(): lax.all_to_all(details, 'slab', split_axis=0, concat_axis=0, tiled=True)]
    add x11 -> x1, other arithmetic: 8.7 us -> 0.07 us  [on_device(): summed = mine[piece] + got[piece]]
  transfers between devices with their start and end apart: 3 -> 10, of which waited for: 2 -> 6; matrix products, arithmetic and copies ran while one was open for 36% -> 0% of each run, Pallas kernels for 0% -> 0%
where the time goes in v1:
time: 45 us; the launch traced here: 44.4 us
  waiting for transfers between devices  16.2 us (36%)
  starting transfers between devices  13.1 us (29%)
  Pallas kernels  8.4 us (19%)
  local copies, waits for them, and re-layouts  6.59 us (15%)
    ppermute x3, waiting for transfers between devices, on_device(): info = lax.ppermute(info, 'slab', ring)  8.19 us
    unnamed x28, local copies, waits for them, and re-layouts  6.59 us
    ppermute x3, waiting for transfers between devices, on_device(): part = lax.ppermute(part, ('tilt', 'rep'), route)  6.46 us
    ppermute x3, starting transfers between devices, on_device(): summed = lax.ppermute(summed, 'slab', ring)  6.03 us
    ppermute x3, starting transfers between devices, on_device(): info = lax.ppermute(info, 'slab', ring)  4.67 us
    pallas_call x1, Pallas kernels, on_device(): pl.pallas_call(functools.partial(frame_kernel, shifts), out_shape=[block_...  4.53 us
    pallas_call x1, Pallas kernels, on_device(): pl.pallas_call(functools.partial(place_kernel, sources, owners), out_shap...  2.05 us
    ppermute x3, starting transfers between devices, on_device(): part = lax.ppermute(part, ('tilt', 'rep'), route)  1.86 us
  transfers between devices with their start and end apart: 10, of which 6 were waited for; matrix products, arithmetic and copies ran while one was open for 0% of the time, Pallas kernels for 0%

profile of v1, /device:TPU:0, one launch (start us, length us, event | category | flops | bytes accessed | tf_op | source)
XLA Modules:
  0.0 44.4 jit_solution(15356797926342247806)
XLA Ops:
  0.0 0.6 %copy-done.9 = s32[1,1,4]{2,1,0:T(1,128)S(1)} copy-done((s32[1,1,4]{2,1,0:T(1,128)S(1)}, s32[1,1,4]{2,1,0:T(1,128)}, u32[]{:S(2)}) %copy-start.9) | copy-done | bytes 40
  0.7 1.2 %copy-done = bf16[1,2,4,128,512]{4,3,2,1,0:T(8,128)(2,1)S(1)} copy-done((bf16[1,2,4,128,512]{4,3,2,1,0:T(8,128)(2,1)S(1)}, bf16[1,2,4,128,512]{4,3,2,1,0:T(8,128)(2,1)}, u32[]{:S(2)}) %copy-start) | copy-done | bytes 1048600
  1.9 0.9 %copy-done.2 = bf16[1,4,2,128,128]{4,3,2,1,0:T(8,128)(2,1)S(1)} copy-done((bf16[1,4,2,128,128]{4,3,2,1,0:T(8,128)(2,1)S(1)}, bf16[1,4,2,128,128]{4,3,2,1,0:T(8,128)(2,1)}, u32[]{:S(2)}) %copy-start.2) | copy-done | bytes 262168
  2.9 0.9 %copy-done.3 = f32[128,256]{1,0:T(8,128)S(1)} copy-done((f32[128,256]{1,0:T(8,128)S(1)}, f32[128,256]{1,0:T(8,128)}, u32[]{:S(2)}) %copy-start.3) | copy-done | bytes 131096
  3.8 0.8 %copy-done.5 = bf16[2,128,128]{2,1,0:T(8,128)(2,1)S(1)} copy-done((bf16[2,128,128]{2,1,0:T(8,128)(2,1)S(1)}, bf16[2,128,128]{2,1,0:T(8,128)(2,1)}, u32[]{:S(2)}) %copy-start.5) | copy-done | bytes 65560
  4.6 0.7 %copy-done.7 = s32[3,1,1,4,16]{4,3,2,1,0:T(4,128)S(1)} copy-done((s32[3,1,1,4,16]{4,3,2,1,0:T(4,128)S(1)}, s32[3,1,1,4,16]{4,3,2,1,0:T(4,128)}, u32[]{:S(2)}) %copy-start.7) | copy-done | bytes 792
  5.3 4.5 %frame.1 = (f32[64,16,128]{2,1,0:T(8,128)S(1)}, f32[64,16,128]{2,1,0:T(8,128)S(1)}, s32[2,16]{1,0:T(2,128)S(1)}, s32[2,16]{1,0:T(2,128)S(1)}, s32[2,16]{1,0:T(2,128)S(1)}, /*index=5*/s32[2,16]{1,0:T(2,128)S(1)}) custom-call(s32[1,4]{1,0:T(1,128)S(1)} %copy-done.8, s32[3,1,1,4,16]{4,3,2,1,0:T(4,128)S(1)} %copy-done.7, s32[1,1,4]{2,1,0:T(1,128)S(1)} %copy-done.9, ...), custom_call_target="tpu_custom_call" | custom-call | tf_op jit(solution)/shard_map/frame/pallas_call | solution.py:272
  9.8 0.5 %collective-permute-start.3 = (f32[64,16,128]{2,1,0:T(8,128)S(1)}, f32[64,16,128]{2,1,0:T(8,128)S(1)}, u32[]{:S(2)}, u32[]{:S(2)}) collective-permute-start(f32[64,16,128]{2,1,0:T(8,128)S(1)} %get-tuple-element.20), channel_id=1, source_target_pairs={{0,1},{1,0},{2,3},{3,2},{4,5},{5,4},{6,7},{7,6},{8,9},{9,8},{10,11... | collective-permute-start | bytes 1572872 | tf_op jit(solution)/shard_map/ppermute | solution.py:298
  10.4 1.5 %collective-permute-done.3 = f32[64,16,128]{2,1,0:T(8,128)S(1)} collective-permute-done((f32[64,16,128]{2,1,0:T(8,128)S(1)}, f32[64,16,128]{2,1,0:T(8,128)S(1)}, u32[]{:S(2)}, u32[]{:S(2)}) %collective-permute-start.3) | collective-permute-done | bytes 524320 | tf_op jit(solution)/shard_map/ppermute | solution.py:298
  12.0 5.0 %collective-permute-start.6 = (f32[16,16,128]{2,1,0:T(8,128)S(1)}, f32[16,16,128]{2,1,0:T(8,128)S(1)}, u32[]{:S(2)}, u32[]{:S(2)}) collective-permute-start(f32[16,16,128]{2,1,0:T(8,128)S(1)} %get-tuple-element.25), channel_id=1, source_target_pairs={{0,12},{4,0},{8,4},{12,8},{1,13},{5,1},{9,5},{13,9},{2,14},{6,2},{... | collective-permute-start | bytes 393224 | tf_op jit(solution)/shard_map/ppermute | solution.py:307
  17.0 1.0 %collective-permute-start.4 = (f32[16,16,128]{2,1,0:T(8,128)S(1)}, f32[16,16,128]{2,1,0:T(8,128)S(1)}, u32[]{:S(2)}, u32[]{:S(2)}) collective-permute-start(f32[16,16,128]{2,1,0:T(8,128)S(1)} %get-tuple-element.27), channel_id=1, source_target_pairs={{0,4},{4,8},{8,12},{12,0},{1,5},{5,9},{9,13},{13,1},{2,6},{6,10},{... | collective-permute-start | bytes 393224 | tf_op jit(solution)/shard_map/ppermute | solution.py:307
  18.0 2.5 %collective-permute-start = (s32[2,16]{1,0:T(2,128)S(1)}, s32[2,16]{1,0:T(2,128)S(1)}, u32[]{:S(2)}, u32[]{:S(2)}) collective-permute-start(s32[2,16]{1,0:T(2,128)S(1)} %get-tuple-element.16), channel_id=1, source_target_pairs={{0,4},{4,8},{8,12},{12,0},{1,5},{5,9},{9,13},{13,1},{2,6},{6,10},{... | collective-permute-start | bytes 392 | tf_op jit(solution)/shard_map/ppermute | solution.py:306
  20.5 0.9 %collective-permute-start.1 = (s32[2,16]{1,0:T(2,128)S(1)}, s32[2,16]{1,0:T(2,128)S(1)}, u32[]{:S(2)}, u32[]{:S(2)}) collective-permute-start(s32[2,16]{1,0:T(2,128)S(1)} %get-tuple-element.17), channel_id=1, source_target_pairs={{0,8},{4,12},{8,0},{12,4},{1,9},{5,13},{9,1},{13,5},{2,10},{6,14},... | collective-permute-start | bytes 392 | tf_op jit(solution)/shard_map/ppermute | solution.py:306
  21.4 5.4 %collective-permute-done.refs_1_ = s32[2,16]{1,0:T(2,128)S(1)} collective-permute-done((s32[2,16]{1,0:T(2,128)S(1)}, s32[2,16]{1,0:T(2,128)S(1)}, u32[]{:S(2)}, u32[]{:S(2)}) %collective-permute-start) | collective-permute-done | bytes 160 | tf_op jit(solution)/shard_map/ppermute | solution.py:306
  26.7 1.3 %collective-permute-start.2 = (s32[2,16]{1,0:T(2,128)S(1)}, s32[2,16]{1,0:T(2,128)S(1)}, u32[]{:S(2)}, u32[]{:S(2)}) collective-permute-start(s32[2,16]{1,0:T(2,128)S(1)} %get-tuple-element.18), channel_id=1, source_target_pairs={{0,12},{4,0},{8,4},{12,8},{1,13},{5,1},{9,5},{13,9},{2,14},{6,2},{... | collective-permute-start | bytes 392 | tf_op jit(solution)/shard_map/ppermute | solution.py:306
  28.0 0.7 %collective-permute-done.1.refs_2_ = s32[2,16]{1,0:T(2,128)S(1)} collective-permute-done((s32[2,16]{1,0:T(2,128)S(1)}, s32[2,16]{1,0:T(2,128)S(1)}, u32[]{:S(2)}, u32[]{:S(2)}) %collective-permute-start.1) | collective-permute-done | bytes 160 | tf_op jit(solution)/shard_map/ppermute | solution.py:306
  28.8 2.1 %collective-permute-done.2.refs_3_ = s32[2,16]{1,0:T(2,128)S(1)} collective-permute-done((s32[2,16]{1,0:T(2,128)S(1)}, s32[2,16]{1,0:T(2,128)S(1)}, u32[]{:S(2)}, u32[]{:S(2)}) %collective-permute-start.2) | collective-permute-done | bytes 160 | tf_op jit(solution)/shard_map/ppermute | solution.py:306
  30.9 2.0 %place.1 = (f32[16,16,128]{2,1,0:T(8,128)S(1)}, f32[16,16,128]{2,1,0:T(8,128)S(1)}, f32[16,16,128]{2,1,0:T(8,128)S(1)}, f32[16,16,128]{2,1,0:T(8,128)S(1)}) custom-call(s32[2,16]{1,0:T(2,128)S(1)} %get-tuple-element.15.refs_0_, s32[2,16]{1,0:T(2,128)S(1)} %collective-permute-done.refs_1_, s32[2,16]{1,0:T(2,128)S(1)} %collective-permute-done.1.refs_2_, ...), custom_call_target="tpu_custom_call" | custom-call | tf_op jit(solution)/shard_map/place/pallas_call | solution.py:315
  33.0 0.6 %copy-done.4 = f32[16,16,128]{2,1,0:T(8,128)} copy-done((f32[16,16,128]{2,1,0:T(8,128)}, f32[16,16,128]{2,1,0:T(8,128)S(1)}, u32[]{:S(2)}) %copy-start.4) | copy-done | bytes 131096
  33.6 1.5 %collective-permute-start.8 = (f32[16,16,128]{2,1,0:T(8,128)S(1)}, f32[16,16,128]{2,1,0:T(8,128)S(1)}, u32[]{:S(2)}, u32[]{:S(2)}) collective-permute-start(f32[16,16,128]{2,1,0:T(8,128)S(1)} %get-tuple-element.23), channel_id=1, source_target_pairs={{0,2},{1,3},{2,0},{3,1},{4,6},{5,7},{6,4},{7,5},{8,10},{9,11},{10,... | collective-permute-start | bytes 393224 | tf_op jit(solution)/shard_map/ppermute | solution.py:336
  35.5 4.4 %collective-permute-done.8.refs_2_ = f32[16,16,128]{2,1,0:T(8,128)S(1)} collective-permute-done((f32[16,16,128]{2,1,0:T(8,128)S(1)}, f32[16,16,128]{2,1,0:T(8,128)S(1)}, u32[]{:S(2)}, u32[]{:S(2)}) %collective-permute-start.8) | collective-permute-done | bytes 131104 | tf_op jit(solution)/shard_map/ppermute | solution.py:336
  39.9 2.0 %collective-permute-done.9.refs_3_ = f32[16,16,128]{2,1,0:T(8,128)S(1)} collective-permute-done((f32[16,16,128]{2,1,0:T(8,128)S(1)}, f32[16,16,128]{2,1,0:T(8,128)S(1)}, u32[]{:S(2)}, u32[]{:S(2)}) %collective-permute-start.9) | collective-permute-done | bytes 131104 | tf_op jit(solution)/shard_map/ppermute | solution.py:336
  42.0 0.6 %copy-done.13 = f32[16,16,128]{2,1,0:T(8,128)} copy-done((f32[16,16,128]{2,1,0:T(8,128)}, f32[16,16,128]{2,1,0:T(8,128)S(1)}, u32[]{:S(2)}) %copy-start.13) | copy-done | bytes 131096
  42.6 1.8 %total.1 = f32[16,2,16,128]{3,2,1,0:T(8,128)} custom-call(f32[16,16,128]{2,1,0:T(8,128)} %copy-done.4, f32[16,16,128]{2,1,0:T(8,128)} %copy-done.11, f32[16,16,128]{2,1,0:T(8,128)} %copy-done.12, f32[16,16,128]{2,1,0:T(8,128)} %copy-done.13), custom_call_target="tpu_custom_call" | custom-call | tf_op jit(solution)/shard_map/total/pallas_call | solution.py:338
  (28 shorter events, 0.5 us)
Async XLA Ops:
  0.0 0.7 %copy-start.9 = (s32[1,1,4]{2,1,0:T(1,128)S(1)}, s32[1,1,4]{2,1,0:T(1,128)}, u32[]{:S(2)}) copy-start(s32[1,1,4]{2,1,0:T(1,128)} %count_ref.1) | copy-start | bytes 52
  0.0 0.7 %copy-start.8 = (s32[1,4]{1,0:T(1,128)S(1)}, s32[1,4]{1,0:T(1,128)}, u32[]{:S(2)}) copy-start(s32[1,4]{1,0:T(1,128)} %pos_ref.1) | copy-start | bytes 52
  0.0 0.7 %copy-start.10 = (f32[128]{0:T(128)S(1)}, f32[128]{0:T(128)}, u32[]{:S(2)}) copy-start(f32[128]{0:T(128)} %param.12) | copy-start | bytes 1540
  0.7 1.2 %copy-start = (bf16[1,2,4,128,512]{4,3,2,1,0:T(8,128)(2,1)S(1)}, bf16[1,2,4,128,512]{4,3,2,1,0:T(8,128)(2,1)}, u32[]{:S(2)}) copy-start(bf16[1,2,4,128,512]{4,3,2,1,0:T(8,128)(2,1)} %obj_ref.1) | copy-start | bytes 3145732
  1.9 0.9 %copy-start.2 = (bf16[1,4,2,128,128]{4,3,2,1,0:T(8,128)(2,1)S(1)}, bf16[1,4,2,128,128]{4,3,2,1,0:T(8,128)(2,1)}, u32[]{:S(2)}) copy-start(bf16[1,4,2,128,128]{4,3,2,1,0:T(8,128)(2,1)} %cot_ref.1) | copy-start | bytes 786436
  2.9 0.9 %copy-start.3 = (f32[128,256]{1,0:T(8,128)S(1)}, f32[128,256]{1,0:T(8,128)}, u32[]{:S(2)}) copy-start(f32[128,256]{1,0:T(8,128)} %constant.2.clone.table_ref) | copy-start | bytes 393220
  3.8 0.8 %copy-start.5 = (bf16[2,128,128]{2,1,0:T(8,128)(2,1)S(1)}, bf16[2,128,128]{2,1,0:T(8,128)(2,1)}, u32[]{:S(2)}) copy-start(bf16[2,128,128]{2,1,0:T(8,128)(2,1)} %probe_ref.1) | copy-start | bytes 196612
  4.6 0.7 %copy-start.7 = (s32[3,1,1,4,16]{4,3,2,1,0:T(4,128)S(1)}, s32[3,1,1,4,16]{4,3,2,1,0:T(4,128)}, u32[]{:S(2)}) copy-start(s32[3,1,1,4,16]{4,3,2,1,0:T(4,128)} %index_ref.1) | copy-start | bytes 2308
  9.8 2.1 %collective-permute-start.3 = (f32[64,16,128]{2,1,0:T(8,128)S(1)}, f32[64,16,128]{2,1,0:T(8,128)S(1)}, u32[]{:S(2)}, u32[]{:S(2)}) collective-permute-start(f32[64,16,128]{2,1,0:T(8,128)S(1)} %get-tuple-element.20), channel_id=1, source_target_pairs={{0,1},{1,0},{2,3},{3,2},{4,5},{5,4},{6,7},{7,6},{8,9},{9,8},{10,11... | collective-permute-start | bytes 1572872 | tf_op jit(solution)/shard_map/ppermute | solution.py:298
  11.9 19.0 %copy-start.1 = (f32[8,128,128]{2,1,0:T(8,128)S(1)}, f32[8,128,128]{2,1,0:T(8,128)}, u32[]{:S(2)}) copy-start(f32[8,128,128]{2,1,0:T(8,128)} %refs_9_.1) | copy-start | bytes 1572868
  11.9 19.0 %copy-start.6 = (f32[8,16,16]{2,1,0:T(8,128)S(1)}, f32[8,16,16]{2,1,0:T(8,128)}, u32[]{:S(2)}) copy-start(f32[8,16,16]{2,1,0:T(8,128)} %refs_8_.1) | copy-start | bytes 24580
  12.0 18.9 %collective-permute-start.6 = (f32[16,16,128]{2,1,0:T(8,128)S(1)}, f32[16,16,128]{2,1,0:T(8,128)S(1)}, u32[]{:S(2)}, u32[]{:S(2)}) collective-permute-start(f32[16,16,128]{2,1,0:T(8,128)S(1)} %get-tuple-element.25), channel_id=1, source_target_pairs={{0,12},{4,0},{8,4},{12,8},{1,13},{5,1},{9,5},{13,9},{2,14},{6,2},{... | collective-permute-start | bytes 393224 | tf_op jit(solution)/shard_map/ppermute | solution.py:307
  17.0 13.9 %collective-permute-start.5 = (f32[16,16,128]{2,1,0:T(8,128)S(1)}, f32[16,16,128]{2,1,0:T(8,128)S(1)}, u32[]{:S(2)}, u32[]{:S(2)}) collective-permute-start(f32[16,16,128]{2,1,0:T(8,128)S(1)} %get-tuple-element.26), channel_id=1, source_target_pairs={{0,8},{4,12},{8,0},{12,4},{1,9},{5,13},{9,1},{13,5},{2,10},{6,14},... | collective-permute-start | bytes 393224 | tf_op jit(solution)/shard_map/ppermute | solution.py:307
  17.0 13.9 %collective-permute-start.4 = (f32[16,16,128]{2,1,0:T(8,128)S(1)}, f32[16,16,128]{2,1,0:T(8,128)S(1)}, u32[]{:S(2)}, u32[]{:S(2)}) collective-permute-start(f32[16,16,128]{2,1,0:T(8,128)S(1)} %get-tuple-element.27), channel_id=1, source_target_pairs={{0,4},{4,8},{8,12},{12,0},{1,5},{5,9},{9,13},{13,1},{2,6},{6,10},{... | collective-permute-start | bytes 393224 | tf_op jit(solution)/shard_map/ppermute | solution.py:307
  18.0 8.7 %collective-permute-start = (s32[2,16]{1,0:T(2,128)S(1)}, s32[2,16]{1,0:T(2,128)S(1)}, u32[]{:S(2)}, u32[]{:S(2)}) collective-permute-start(s32[2,16]{1,0:T(2,128)S(1)} %get-tuple-element.16), channel_id=1, source_target_pairs={{0,4},{4,8},{8,12},{12,0},{1,5},{5,9},{9,13},{13,1},{2,6},{6,10},{... | collective-permute-start | bytes 392 | tf_op jit(solution)/shard_map/ppermute | solution.py:306
  20.5 8.3 %collective-permute-start.1 = (s32[2,16]{1,0:T(2,128)S(1)}, s32[2,16]{1,0:T(2,128)S(1)}, u32[]{:S(2)}, u32[]{:S(2)}) collective-permute-start(s32[2,16]{1,0:T(2,128)S(1)} %get-tuple-element.17), channel_id=1, source_target_pairs={{0,8},{4,12},{8,0},{12,4},{1,9},{5,13},{9,1},{13,5},{2,10},{6,14},... | collective-permute-start | bytes 392 | tf_op jit(solution)/shard_map/ppermute | solution.py:306
  26.7 4.1 %collective-permute-start.2 = (s32[2,16]{1,0:T(2,128)S(1)}, s32[2,16]{1,0:T(2,128)S(1)}, u32[]{:S(2)}, u32[]{:S(2)}) collective-permute-start(s32[2,16]{1,0:T(2,128)S(1)} %get-tuple-element.18), channel_id=1, source_target_pairs={{0,12},{4,0},{8,4},{12,8},{1,13},{5,1},{9,5},{13,9},{2,14},{6,2},{... | collective-permute-start | bytes 392 | tf_op jit(solution)/shard_map/ppermute | solution.py:306
  33.0 0.7 %copy-start.4 = (f32[16,16,128]{2,1,0:T(8,128)}, f32[16,16,128]{2,1,0:T(8,128)S(1)}, u32[]{:S(2)}) copy-start(f32[16,16,128]{2,1,0:T(8,128)S(1)} %get-tuple-element.21.refs_0_) | copy-start | bytes 393220
  33.6 1.9 %collective-permute-start.7 = (f32[16,16,128]{2,1,0:T(8,128)S(1)}, f32[16,16,128]{2,1,0:T(8,128)S(1)}, u32[]{:S(2)}, u32[]{:S(2)}) collective-permute-start(f32[16,16,128]{2,1,0:T(8,128)S(1)} %get-tuple-element.22), channel_id=1, source_target_pairs={{0,1},{1,0},{2,3},{3,2},{4,5},{5,4},{6,7},{7,6},{8,9},{9,8},{10,11... | collective-permute-start | bytes 393224 | tf_op jit(solution)/shard_map/ppermute | solution.py:336
  33.6 6.3 %collective-permute-start.8 = (f32[16,16,128]{2,1,0:T(8,128)S(1)}, f32[16,16,128]{2,1,0:T(8,128)S(1)}, u32[]{:S(2)}, u32[]{:S(2)}) collective-permute-start(f32[16,16,128]{2,1,0:T(8,128)S(1)} %get-tuple-element.23), channel_id=1, source_target_pairs={{0,2},{1,3},{2,0},{3,1},{4,6},{5,7},{6,4},{7,5},{8,10},{9,11},{10,... | collective-permute-start | bytes 393224 | tf_op jit(solution)/shard_map/ppermute | solution.py:336
  35.1 6.8 %collective-permute-start.9 = (f32[16,16,128]{2,1,0:T(8,128)S(1)}, f32[16,16,128]{2,1,0:T(8,128)S(1)}, u32[]{:S(2)}, u32[]{:S(2)}) collective-permute-start(f32[16,16,128]{2,1,0:T(8,128)S(1)} %get-tuple-element.24), channel_id=1, source_target_pairs={{0,3},{1,2},{2,1},{3,0},{4,7},{5,6},{6,5},{7,4},{8,11},{9,10},{10,... | collective-permute-start | bytes 393224 | tf_op jit(solution)/shard_map/ppermute | solution.py:336
  35.5 6.5 %copy-start.11 = (f32[16,16,128]{2,1,0:T(8,128)}, f32[16,16,128]{2,1,0:T(8,128)S(1)}, u32[]{:S(2)}) copy-start(f32[16,16,128]{2,1,0:T(8,128)S(1)} %collective-permute-done.7.refs_1_) | copy-start | bytes 393220
  39.9 2.0 %copy-start.12 = (f32[16,16,128]{2,1,0:T(8,128)}, f32[16,16,128]{2,1,0:T(8,128)S(1)}, u32[]{:S(2)}) copy-start(f32[16,16,128]{2,1,0:T(8,128)S(1)} %collective-permute-done.8.refs_2_) | copy-start | bytes 393220
  41.9 0.6 %copy-start.13 = (f32[16,16,128]{2,1,0:T(8,128)}, f32[16,16,128]{2,1,0:T(8,128)S(1)}, u32[]{:S(2)}) copy-start(f32[16,16,128]{2,1,0:T(8,128)S(1)} %collective-permute-done.9.refs_3_) | copy-start | bytes 393220

commit v2 on v1

v2 whole, which is shorter than its diff:
```python
import functools
import math

import jax
import jax.numpy as jnp
import numpy as np
from jax import lax
from jax.experimental import pallas as pl
from jax.experimental.pallas import tpu as pltpu
from jax.sharding import PartitionSpec as P

VB_DEV = 64
REACH = 3
CHUNKS = 2
CHUNK_ROWS = 8
HIGH = lax.Precision.HIGHEST
SMEM = pltpu.SMEM
VMEM = pltpu.VMEM


def dot(left, right, precision=None):
    return jnp.dot(left, right, precision=precision, preferred_element_type=jnp.float32)


def slab_shifts(peers):
    if peers <= 2 * REACH + 1:
        return tuple(range(peers))
    return (0,) + tuple(s for k in range(1, REACH + 1) for s in (k, peers - k))


def angle_table(length):
    grid = np.arange(length)
    angles = (grid[:, None] * grid[None, :] % length) * (2.0 * math.pi / length)
    return np.concatenate([np.cos(angles), np.sin(angles)], axis=1).astype(np.float32)


def propagator_blocks(phases, table):
    length = phases.shape[-1]
    row = lax.broadcasted_iota(jnp.int32, (8, length), 0)
    waves = jnp.where(row == 0, jnp.cos(phases), jnp.sin(phases))
    sums = dot(waves, table, HIGH) * (1.0 / length)
    cc, cs = sums[0:1, :length], sums[0:1, length:]
    sc, ss = sums[1:2, :length], sums[1:2, length:]

    def circulant(line):
        wide = jnp.broadcast_to(line, (length, length))
        return pltpu.roll(wide, 0, 1, stride=1, stride_axis=0)

    kr, ki = circulant(cc + ss), circulant(sc - cs)
    krt, kit = circulant(cc - ss), circulant(sc + cs)
    whole = jnp.concatenate(
        [jnp.concatenate([kr, -ki], 1), jnp.concatenate([ki, kr], 1)], 0
    ).astype(jnp.bfloat16)
    turned = jnp.concatenate(
        [jnp.concatenate([krt, kit], 1), jnp.concatenate([-kit, krt], 1)], 0
    ).astype(jnp.bfloat16)
    return whole, turned


def frame_kernel(
    shifts,
    pos_hbm,
    index_hbm,
    count_hbm,
    phase_hbm,
    table_hbm,
    obj_hbm,
    probe_hbm,
    cot_hbm,
    row_hbm,
    col_hbm,
    *rest,
):
    mine, other = rest[: CHUNKS * len(shifts)], rest[CHUNKS * len(shifts)]
    scratch = rest[CHUNKS * len(shifts) + 1 :]
    pos_ref, index_ref, count_ref = scratch[0:3]
    phase_ref, table_ref, obj_ref, probe_ref, cot_ref, row_ref, col_ref = scratch[3:10]
    sems, band, window, col_bf = scratch[10:]
    slices = obj_ref.shape[2]
    copies = [
        pltpu.make_async_copy(src, dst, sems.at[i])
        for i, (src, dst) in enumerate(
            [
                (phase_hbm, phase_ref),
                (table_hbm, table_ref),
                (pos_hbm, pos_ref),
                (probe_hbm, probe_ref),
                (index_hbm, index_ref),
                (count_hbm, count_ref),
                (row_hbm, row_ref),
            ]
        )
    ]
    got_phase, got_table, got_pos, got_probe, got_index, got_count, got_row = copies
    got_obj = [
        pltpu.make_async_copy(obj_hbm.at[0, :, s], obj_ref.at[0, :, s], sems.at[len(copies) + s])
        for s in range(slices)
    ]
    got_cot = pltpu.make_async_copy(cot_hbm, cot_ref, sems.at[len(copies) + slices])
    got_col = pltpu.make_async_copy(col_hbm, col_ref, sems.at[len(copies) + slices + 1])
    for copy in (got_phase, got_table, got_pos, *got_obj, got_probe, got_cot):
        copy.start()
    for copy in (got_index, got_count, got_row, got_col):
        copy.start()

    me, core = lax.axis_index("slab"), lax.axis_index("rep")
    peers = lax.axis_size("slab")
    capacity = index_ref.shape[-1]
    size = probe_ref.shape[-1]
    rows, cols = obj_ref.shape[3:]
    count = cot_ref.shape[1]
    group = 2 if count % 2 == 0 else 1
    f32, bf16 = jnp.float32, jnp.bfloat16

    got_phase.wait()
    got_table.wait()
    whole, turned = propagator_blocks(phase_ref[...], table_ref[...])

    got_pos.wait()
    col_down = lax.broadcasted_iota(jnp.int32, (cols, size), 0)
    lane = lax.broadcasted_iota(jnp.int32, (cols, size), 1)
    cut = jnp.concatenate(
        [(col_down == lane + pos_ref[0, w]).astype(bf16) for w in range(count)], 1
    )
    lane_down = lax.broadcasted_iota(jnp.int32, (size, cols), 0)
    col = lax.broadcasted_iota(jnp.int32, (size, cols), 1)
    paste = jnp.concatenate(
        [(col == lane_down + pos_ref[0, w]).astype(bf16) for w in range(count)], 0
    )

    for s in range(slices):
        got_obj[s].wait()
        source = jnp.concatenate([obj_ref[0, 0, s], obj_ref[0, 1, s]], 0)
        window[s] = dot(source, cut).astype(bf16)

    def tile(s, c, w):
        return window[s, c * rows : (c + 1) * rows, w * size : (w + 1) * size].astype(f32)

    def propagate(fields, first, second):
        result = []
        for g in range(0, count, group):
            stack = jnp.concatenate(
                [jnp.concatenate([fields[w][c] for w in range(g, g + group)], 1) for c in (0, 1)], 0
            )
            part = dot(first, stack).astype(bf16)
            turned_part = jnp.concatenate(
                [
                    jnp.concatenate(
                        [
                            part[c * size : (c + 1) * size, k * size : (k + 1) * size]
                            for c in (0, 1)
                        ],
                        1,
                    )
                    for k in range(group)
                ],
                0,
            )
            done = dot(turned_part, second).astype(bf16)
            for k in range(group):
                result.append(
                    tuple(
                        done[k * size : (k + 1) * size, c * size : (c + 1) * size] for c in (0, 1)
                    )
                )
        return result

    got_probe.wait()
    now = [(probe_ref[0], probe_ref[1])] * count
    kept = []
    for s in range(slices):
        kept.append(now)
        if s + 1 < slices:
            passed = []
            for w in range(count):
                o_re, o_im = tile(s, 0, w), tile(s, 1, w)
                p_re, p_im = now[w][0].astype(f32), now[w][1].astype(f32)
                passed.append(
                    (
                        (o_re * p_re - o_im * p_im).astype(bf16),
                        (o_re * p_im + o_im * p_re).astype(bf16),
                    )
                )
            now = propagate(passed, whole, turned)

    block_rows, block_cols = row_ref.shape[-1], col_ref.shape[-1]
    across = cols // block_cols
    got_cot.wait()
    back = [(cot_ref[0, w, 0], cot_ref[0, w, 1]) for w in range(count)]
    for s in reversed(range(slices)):
        grads, rhos = [], []
        for w in range(count):
            c_re, c_im = back[w][0].astype(f32), back[w][1].astype(f32)
            p_re, p_im = kept[s][w][0].astype(f32), kept[s][w][1].astype(f32)
            grads.append(
                (
                    (p_re * c_re + p_im * c_im).astype(bf16),
                    (p_re * c_im - p_im * c_re).astype(bf16),
                )
            )
            if s > 0:
                o_re, o_im = tile(s, 0, w), tile(s, 1, w)
                rhos.append(
                    (
                        (o_re * c_re + o_im * c_im).astype(bf16),
                        (o_re * c_im - o_im * c_re).astype(bf16),
                    )
                )
        if s > 0:
            back = propagate(rhos, turned, whole)
        stack = jnp.concatenate(
            [jnp.concatenate([grads[w][c] for w in range(count)], 1) for c in (0, 1)], 0
        )
        spread = dot(stack, paste).astype(bf16)
        for c in (0, 1):
            for i in range(rows // block_rows):
                top = c * rows + i * block_rows
                for j in range(across):
                    band[c, (s * (rows // block_rows) + i) * across + j] = spread[
                        top : top + block_rows, j * block_cols : (j + 1) * block_cols
                    ]

    got_row.wait()
    got_col.wait()
    got_index.wait()
    got_count.wait()
    tiles = row_ref.shape[0]
    wide = capacity * block_rows
    col_bf[...] = col_ref[...].astype(bf16)
    down = lax.broadcasted_iota(jnp.int32, (block_rows, wide), 0)
    along = lax.broadcasted_iota(jnp.int32, (block_rows, wide), 1)
    repeat = (lax.rem(along, block_rows) == down).astype(bf16)
    row_wide = dot(row_ref[...].reshape(tiles * block_rows, block_rows).astype(bf16), repeat)
    row_wide = row_wide.reshape(tiles, block_rows, wide)
    strip = lax.div(along, block_rows)
    half = block_rows // CHUNKS
    mark_down = lax.broadcasted_iota(jnp.int32, (half, capacity * half), 0)
    mark_along = lax.broadcasted_iota(jnp.int32, (half, capacity * half), 1)
    mark_slot = jnp.where(lax.rem(mark_along, half) == mark_down, lax.div(mark_along, half), -1)
    starts = np.cumsum([0] + [ref.shape[0] for ref in mine])
    for k, shift in enumerate(shifts):
        dest = lax.rem(me + shift, peers)
        live = count_ref[0, 0, dest]
        inner, picks = [], []
        marks = jnp.full(mark_slot.shape, VB_DEV, jnp.int32)
        for slot in range(capacity):
            block = index_ref[0, 0, 0, dest, slot]
            target = index_ref[1, 0, 0, dest, slot]
            t = index_ref[2, 0, 0, dest, slot]
            target = jnp.where(slot < live, target, VB_DEV)
            marks = jnp.where(mark_slot == slot, target, marks)
            pair = jnp.concatenate([band[core, block], band[1 - core, block]], 0)
            mixed = dot(pair, col_bf[t]).astype(bf16)
            inner.append(jnp.concatenate([mixed[:block_rows], mixed[block_rows:]], 1))
            picked = row_wide[0]
            for u in range(1, tiles):
                picked = jnp.where(t == u, row_wide[u], picked)
            picks.append(jnp.where(strip == slot, picked, 0.0).astype(bf16))
        result = dot(jnp.concatenate(picks, 0), jnp.concatenate(inner, 0))
        for h in range(CHUNKS):
            for slot in range(capacity):
                top = slot * block_rows + h * half
                place = slice(slot * half, (slot + 1) * half)
                mine[h * len(shifts) + k][place] = result[top : top + half, :block_cols]
                begin = starts[h * len(shifts) + k] + slot * half
                other[begin : begin + half] = result[top : top + half, block_cols:]
        tail = capacity * half
        mine[k][tail : tail + half] = marks.astype(f32)
        begin = starts[k] + tail
        other[begin : begin + half] = jnp.zeros(marks.shape, f32)


def place_kernel(sources, owners, first, *refs):
    tilt, core = lax.axis_index("tilt"), lax.axis_index("rep")
    tilts, cores = lax.axis_size("tilt"), lax.axis_size("rep")
    each = VB_DEV // (tilts * cores)
    blocks = refs[:sources]
    half, lanes = CHUNK_ROWS, blocks[0].shape[-1]
    size = each * half
    if first:
        outs, mark_ref = refs[sources:-1], refs[-1]
        for k, block in enumerate(blocks):
            mark_ref[k] = block[lanes:]
    else:
        mark_ref, rest = refs[sources], refs[sources + 1 :]
        before, outs, done = rest[: len(owners)], rest[len(owners) : -1], rest[-1]
        for dr in range(cores):
            parts = [ref[...] for ref, (dt, r) in zip(before, owners) if r == dr]
            if dr:
                outs[dr][:size] = parts.pop(0)
            done[dr] = functools.reduce(jnp.add, parts, jnp.zeros((size, lanes), jnp.float32))
    data = jnp.concatenate([block[:lanes].astype(jnp.bfloat16) for block in blocks], 0)
    volume = lax.broadcasted_iota(jnp.int32, (each, half, lanes), 0).astype(jnp.float32)
    for out, (dt, dr) in zip(outs, owners):
        owner = lax.rem(tilt + dt, tilts) * cores + lax.rem(core + dr, cores)
        base = (owner * each).astype(jnp.float32)
        hot = []
        for k in range(sources):
            mark = mark_ref[k] - base
            hit = jnp.where(volume == mark[None], 1.0, 0.0)
            hot.append(hit.reshape(size, lanes).astype(jnp.bfloat16))
        begin = out.shape[0] - size
        out[begin : begin + size] = dot(jnp.concatenate(hot, 1), data)


def sum_kernel(owners, done_ref, *refs):
    parts, out_ref = refs[:-1], refs[-1]
    core, cores = lax.axis_index("rep"), lax.axis_size("rep")
    each, cols = out_ref.shape[0], out_ref.shape[-1]
    size = each * CHUNK_ROWS
    for dr in range(cores):
        at = lax.rem(core + dr, cores)
        early, late = done_ref[dr], None
        for ref, (dt, r) in zip(parts, owners):
            if r == dr:
                if dr and not dt:
                    early = early + ref[:size]
                value = ref[ref.shape[0] - size :]
                late = value if late is None else late + value
        for h, value in enumerate([early, late]):
            rows = pl.ds(h * CHUNK_ROWS, CHUNK_ROWS)
            out_ref[:, at, rows] = value.reshape(each, CHUNK_ROWS, cols)


def on_device(
    object_slab,
    probe_field,
    phases,
    cotangent,
    positions,
    pair_index,
    pair_counts,
    row_interp,
    col_interp,
):
    peers = lax.axis_size("slab")
    tilts, cores = lax.axis_size("tilt"), lax.axis_size("rep")
    shifts = slab_shifts(peers)
    capacity = pair_index.shape[-1]
    block_rows, block_cols = row_interp.shape[-1], col_interp.shape[-1]
    _, _, slices, rows, cols = object_slab.shape
    windows, size = cotangent.shape[1], cotangent.shape[-1]
    f32, bf16 = jnp.float32, jnp.bfloat16
    hbm, vmem = pl.BlockSpec(memory_space=pltpu.HBM), pl.BlockSpec(memory_space=VMEM)
    limit = pltpu.CompilerParams(vmem_limit_bytes=40 * 1024 * 1024)
    sources = len(shifts)
    lanes = capacity * CHUNK_ROWS

    phase_line = phases.reshape(1, -1)
    table = jnp.asarray(angle_table(size))
    frames = (slices * (rows // block_rows) * (cols // block_cols), block_rows, block_cols)
    marked = jax.ShapeDtypeStruct((lanes + CHUNK_ROWS, block_cols), f32)
    plain = jax.ShapeDtypeStruct((lanes, block_cols), f32)
    shapes = [marked] * sources + [plain] * (sources * (CHUNKS - 1))
    fetched = [
        (phase_line, VMEM),
        (table, VMEM),
        (object_slab, VMEM),
        (probe_field, VMEM),
        (cotangent, VMEM),
        (row_interp, VMEM),
        (col_interp, VMEM),
    ]
    scalars = [positions, pair_index, pair_counts]
    total = sum(shape.shape[0] for shape in shapes)
    *mine, other = pl.pallas_call(
        functools.partial(frame_kernel, shifts),
        out_shape=shapes + [jax.ShapeDtypeStruct((total, block_cols), f32)],
        in_specs=[hbm] * 10,
        out_specs=[vmem] * (len(shapes) + 1),
        scratch_shapes=[SMEM(x.shape, x.dtype) for x in scalars]
        + [space(x.shape, x.dtype) for x, space in fetched]
        + [
            pltpu.SemaphoreType.DMA((9 + slices,)),
            VMEM((2,) + frames, bf16),
            VMEM((slices, 2 * rows, windows * size), bf16),
            VMEM(col_interp.shape, bf16),
        ],
        compiler_params=limit,
        name="frame",
    )(*[pltpu.with_memory_space_constraint(x, pltpu.HBM) for x in scalars + [x for x, _ in fetched]])

    swap = [(r, (r + 1) % cores) for r in range(cores)]
    owners = [(dt, dr) for dt in range(tilts) for dr in range(cores)]
    each = VB_DEV // len(owners)
    share = jax.ShapeDtypeStruct((each * CHUNK_ROWS, block_cols), f32)
    got = lax.ppermute(other, "rep", swap)
    sent, start = [], 0
    for part in mine:
        sent.append(part + got[start : start + part.shape[0]])
        start += part.shape[0]

    mark = jax.ShapeDtypeStruct((sources, CHUNK_ROWS, block_cols), f32)
    double = jax.ShapeDtypeStruct((2 * each * CHUNK_ROWS, block_cols), f32)
    done = jax.ShapeDtypeStruct((cores, each * CHUNK_ROWS, block_cols), f32)
    extra = []
    for h in range(CHUNKS):
        blocks = [None] * sources
        for k in reversed(range(sources)):
            block = sent[h * sources + k]
            if shifts[k]:
                ring = [(p, (p + shifts[k]) % peers) for p in range(peers)]
                block = lax.ppermute(block, "slab", ring)
            blocks[k] = block
        *parts, more = pl.pallas_call(
            functools.partial(place_kernel, sources, owners, h == 0),
            out_shape=[double if h and dr and not dt else share for dt, dr in owners]
            + [done if h else mark],
            in_specs=[vmem] * (sources + len(extra)),
            out_specs=[vmem] * (len(owners) + 1),
            compiler_params=limit,
            name="place",
        )(*blocks, *extra)
        for i, (dt, dr) in enumerate(owners):
            if dt or (dr and h):
                route = [
                    (t * cores + r, (t + dt) % tilts * cores + (r + dr) % cores)
                    for t in range(tilts)
                    for r in range(cores)
                ]
                parts[i] = lax.ppermute(parts[i], ("tilt", "rep"), route)
        extra = [more, *parts]
    return pl.pallas_call(
        functools.partial(sum_kernel, owners),
        out_shape=jax.ShapeDtypeStruct((each, cores, block_rows, block_cols), f32),
        in_specs=[vmem] * len(extra),
        out_specs=vmem,
        compiler_params=limit,
        name="total",
    )(*extra)


def solution(mesh):
    in_specs = (
        P(("groups", "tilt"), None, None, "slab", None),
        P(),
        P(),
        P(("groups", "tilt"), ("slab", "rep"), None, None, None),
        P(("groups", "tilt"), ("slab", "rep")),
        P(None, ("groups", "tilt"), "slab", None, None),
        P(("groups", "tilt"), "slab", None),
        P(),
        P(),
    )
    out_specs = P(("groups", "slab", "tilt", "rep"), None, None, None)
    return jax.shard_map(
        on_device, mesh=mesh, in_specs=in_specs, out_specs=out_specs, check_vma=False
    )
```

time: 45 us -> 36.3 us (0.81)
  local copies, waits for them, and re-layouts: 6.59 us -> 0 us
  waiting for transfers between devices: 16.2 us -> 13.8 us
  starting transfers between devices: 13.1 us -> 14 us
    unnamed x28 -> x0, local copies, waits for them, and re-layouts: 6.59 us -> none
    ppermute x9 -> x11, waiting for transfers between devices: 14.7 us -> 12.2 us  [the longest x5 6.41 us: on_device(): parts[i] = lax.ppermute(parts[i], ('tilt', 'rep'), route)]
    pallas_call x1, Pallas kernels: 1.82 us -> 0.73 us  [on_device(): pl.pallas_call(functools.partial(sum_kernel, owners), out_shape=jax.Shape...]
    ppermute x9 -> x11, starting transfers between devices: 12.6 us -> 13.5 us  [the longest x6 10 us: on_device(): block = lax.ppermute(block, 'slab', ring)]
    pallas_call x2 -> x3, Pallas kernels: 6.58 us -> 7.42 us  [the longest x1 6.84 us: on_device(): pl.pallas_call(functools.partial(frame_kernel, shifts), out_shape=shapes...]
  transfers between devices with their start and end apart: 10 -> 12, of which waited for: 6 -> 7; matrix products, arithmetic and copies ran while one was open for 0% -> 0% of each run, Pallas kernels for 0% -> 1%
where the time goes in v2:
time: 36.3 us; the launch traced here: 36.1 us
  starting transfers between devices  14 us (39%)
  waiting for transfers between devices  13.8 us (38%)
  Pallas kernels  8.16 us (22%)
    ppermute x6, starting transfers between devices, on_device(): block = lax.ppermute(block, 'slab', ring)  10 us
    pallas_call x1, Pallas kernels, on_device(): pl.pallas_call(functools.partial(frame_kernel, shifts), out_shape=shapes...  6.84 us
    ppermute x5, waiting for transfers between devices, on_device(): parts[i] = lax.ppermute(parts[i], ('tilt', 'rep'), route)  6.41 us
    ppermute x6, waiting for transfers between devices, on_device(): block = lax.ppermute(block, 'slab', ring)  5.83 us
    ppermute x5, starting transfers between devices, on_device(): parts[i] = lax.ppermute(parts[i], ('tilt', 'rep'), route)  3.49 us
    ppermute x1, waiting for transfers between devices, on_device(): got = lax.ppermute(other, 'rep', swap)  1.56 us
    pallas_call x1, Pallas kernels, on_device(): pl.pallas_call(functools.partial(sum_kernel, owners), out_shape=jax.Shape...  0.73 us
  transfers between devices with their start and end apart: 12, of which 7 were waited for; matrix products, arithmetic and copies ran while one was open for 0% of the time, Pallas kernels for 1%

profile of v2, /device:TPU:0, one launch (start us, length us, event | category | flops | bytes accessed | tf_op | source)
XLA Modules:
  0.0 36.1 jit_solution(11746968230532671257)
XLA Ops:
  0.0 6.8 %frame.1 = (f32[136,128]{1,0:T(8,128)S(1)}, f32[136,128]{1,0:T(8,128)S(1)}, f32[136,128]{1,0:T(8,128)S(1)}, f32[136,128]{1,0:T(8,128)S(1)}, f32[128,128]{1,0:T(8...) custom-call(s32[1,4]{1,0:T(1,128)} %pos_hbm.1, ...), custom_call_target="tpu_custom_call" | custom-call | tf_op jit(solution)/shard_map/frame/pallas_call | solution.py:366
  6.8 0.5 %collective-permute-start = (f32[1056,128]{1,0:T(8,128)S(1)}, f32[1056,128]{1,0:T(8,128)S(1)}, u32[]{:S(2)}, u32[]{:S(2)}) collective-permute-start(f32[1056,128]{1,0:T(8,128)S(1)} %get-tuple-element.25), channel_id=1, source_target_pairs={{0,1},{1,0},{2,3},{3,2},{4,5},{5,4},{6,7},{7,6},{8,9},{9,8},{10,11... | collective-permute-start | bytes 1622024 | tf_op jit(solution)/shard_map/ppermute | solution.py:387
  7.4 1.6 %collective-permute-done = f32[1056,128]{1,0:T(8,128)S(1)} collective-permute-done((f32[1056,128]{1,0:T(8,128)S(1)}, f32[1056,128]{1,0:T(8,128)S(1)}, u32[]{:S(2)}, u32[]{:S(2)}) %collective-permute-start) | collective-permute-done | bytes 540704 | tf_op jit(solution)/shard_map/ppermute | solution.py:387
  9.0 5.0 %collective-permute-start.6 = (f32[136,128]{1,0:T(8,128)S(1)}, f32[136,128]{1,0:T(8,128)S(1)}, u32[]{:S(2)}, u32[]{:S(2)}) collective-permute-start(f32[136,128]{1,0:T(8,128)S(1)} %get-tuple-element.43), channel_id=1, source_target_pairs={{0,12},{4,0},{8,4},{12,8},{1,13},{5,1},{9,5},{13,9},{2,14},{6,2},{... | collective-permute-start | bytes 208904 | tf_op jit(solution)/shard_map/ppermute | solution.py:403
  14.0 0.0 collective-permute-start.5
  14.0 1.0 %collective-permute-start.4 = (f32[136,128]{1,0:T(8,128)S(1)}, f32[136,128]{1,0:T(8,128)S(1)}, u32[]{:S(2)}, u32[]{:S(2)}) collective-permute-start(f32[136,128]{1,0:T(8,128)S(1)} %get-tuple-element.45), channel_id=1, source_target_pairs={{0,4},{4,8},{8,12},{12,0},{1,5},{5,9},{9,13},{13,1},{2,6},{6,10},{... | collective-permute-start | bytes 208904 | tf_op jit(solution)/shard_map/ppermute | solution.py:403
  15.0 2.9 %collective-permute-start.3 = (f32[128,128]{1,0:T(8,128)S(1)}, f32[128,128]{1,0:T(8,128)S(1)}, u32[]{:S(2)}, u32[]{:S(2)}) collective-permute-start(f32[128,128]{1,0:T(8,128)S(1)} %get-tuple-element.47), channel_id=1, source_target_pairs={{0,12},{4,0},{8,4},{12,8},{1,13},{5,1},{9,5},{13,9},{2,14},{6,2},{... | collective-permute-start | bytes 196616 | tf_op jit(solution)/shard_map/ppermute | solution.py:403
  17.9 1.1 %collective-permute-start.2 = (f32[128,128]{1,0:T(8,128)S(1)}, f32[128,128]{1,0:T(8,128)S(1)}, u32[]{:S(2)}, u32[]{:S(2)}) collective-permute-start(f32[128,128]{1,0:T(8,128)S(1)} %get-tuple-element.48), channel_id=1, source_target_pairs={{0,8},{4,12},{8,0},{12,4},{1,9},{5,13},{9,1},{13,5},{2,10},{6,14},... | collective-permute-start | bytes 196616 | tf_op jit(solution)/shard_map/ppermute | solution.py:403
  19.0 0.0 collective-permute-done.6.refs_3_
  19.0 0.0 collective-permute-start.1
  19.0 4.3 %collective-permute-done.5.refs_2_ = f32[136,128]{1,0:T(8,128)S(1)} collective-permute-done((f32[136,128]{1,0:T(8,128)S(1)}, f32[136,128]{1,0:T(8,128)S(1)}, u32[]{:S(2)}, u32[]{:S(2)}) %collective-permute-start.5) | collective-permute-done | bytes 69664 | tf_op jit(solution)/shard_map/ppermute | solution.py:403
  23.4 0.0 collective-permute-done.4.refs_1_
  23.4 0.3 place.2
  23.7 1.6 %collective-permute-start.7 = (f32[128,128]{1,0:T(8,128)S(1)}, f32[128,128]{1,0:T(8,128)S(1)}, u32[]{:S(2)}, u32[]{:S(2)}) collective-permute-start(f32[128,128]{1,0:T(8,128)S(1)} %get-tuple-element.36), channel_id=1, source_target_pairs={{0,2},{1,3},{2,0},{3,1},{4,6},{5,7},{6,4},{7,5},{8,10},{9,11},{10,... | collective-permute-start | bytes 196616 | tf_op jit(solution)/shard_map/ppermute | solution.py:421
  25.2 1.5 %collective-permute-done.2.refs_2_ = f32[128,128]{1,0:T(8,128)S(1)} collective-permute-done((f32[128,128]{1,0:T(8,128)S(1)}, f32[128,128]{1,0:T(8,128)S(1)}, u32[]{:S(2)}, u32[]{:S(2)}) %collective-permute-start.2) | collective-permute-done | bytes 65568 | tf_op jit(solution)/shard_map/ppermute | solution.py:403
  26.7 1.3 %collective-permute-done.7.refs_7_ = f32[128,128]{1,0:T(8,128)S(1)} collective-permute-done((f32[128,128]{1,0:T(8,128)S(1)}, f32[128,128]{1,0:T(8,128)S(1)}, u32[]{:S(2)}, u32[]{:S(2)}) %collective-permute-start.7) | collective-permute-done | bytes 65568 | tf_op jit(solution)/shard_map/ppermute | solution.py:421
  28.0 1.4 %collective-permute-done.8.refs_8_ = f32[128,128]{1,0:T(8,128)S(1)} collective-permute-done((f32[128,128]{1,0:T(8,128)S(1)}, f32[128,128]{1,0:T(8,128)S(1)}, u32[]{:S(2)}, u32[]{:S(2)}) %collective-permute-start.8) | collective-permute-done | bytes 65568 | tf_op jit(solution)/shard_map/ppermute | solution.py:421
  29.4 0.3 place.3
  29.7 0.1 collective-permute-start.9
  29.8 1.3 %collective-permute-start.10 = (f32[128,128]{1,0:T(8,128)S(1)}, f32[128,128]{1,0:T(8,128)S(1)}, u32[]{:S(2)}, u32[]{:S(2)}) collective-permute-start(f32[128,128]{1,0:T(8,128)S(1)} %get-tuple-element.41), channel_id=1, source_target_pairs={{0,2},{1,3},{2,0},{3,1},{4,6},{5,7},{6,4},{7,5},{8,10},{9,11},{10,... | collective-permute-start | bytes 196616 | tf_op jit(solution)/shard_map/ppermute | solution.py:421
  31.0 0.6 %collective-permute-start.11 = (f32[128,128]{1,0:T(8,128)S(1)}, f32[128,128]{1,0:T(8,128)S(1)}, u32[]{:S(2)}, u32[]{:S(2)}) collective-permute-start(f32[128,128]{1,0:T(8,128)S(1)} %get-tuple-element.42), channel_id=1, source_target_pairs={{0,3},{1,2},{2,1},{3,0},{4,7},{5,6},{6,5},{7,4},{8,11},{9,10},{10,... | collective-permute-start | bytes 196616 | tf_op jit(solution)/shard_map/ppermute | solution.py:421
  31.7 3.0 %collective-permute-done.10.refs_2_ = f32[128,128]{1,0:T(8,128)S(1)} collective-permute-done((f32[128,128]{1,0:T(8,128)S(1)}, f32[128,128]{1,0:T(8,128)S(1)}, u32[]{:S(2)}, u32[]{:S(2)}) %collective-permute-start.10) | collective-permute-done | bytes 65568 | tf_op jit(solution)/shard_map/ppermute | solution.py:421
  34.6 0.8 %collective-permute-done.11.refs_3_ = f32[128,128]{1,0:T(8,128)S(1)} collective-permute-done((f32[128,128]{1,0:T(8,128)S(1)}, f32[128,128]{1,0:T(8,128)S(1)}, u32[]{:S(2)}, u32[]{:S(2)}) %collective-permute-start.11) | collective-permute-done | bytes 65568 | tf_op jit(solution)/shard_map/ppermute | solution.py:421
  35.4 0.7 %total.1 = f32[16,2,16,128]{3,2,1,0:T(8,128)} custom-call(f32[2,128,128]{2,1,0:T(8,128)S(1)} %get-tuple-element.38.done_ref, f32[128,128]{1,0:T(8,128)S(1)} %get-tuple-element.39.refs_0_, f32[256,128]{1,0:T(8,128)S(1)} %collective-permute-done.9.refs_1_, f32[128,128]{1,0:T(8,128)S(1)} %collective-permute-done.10.refs_2_, ...), custom_call_target="tpu_custom_call" | custom-call | tf_op jit(solution)/shard_map/total/pallas_call | solution.py:423
  (6 shorter events, 0.1 us)
Async XLA Ops:
  6.8 2.1 %collective-permute-start = (f32[1056,128]{1,0:T(8,128)S(1)}, f32[1056,128]{1,0:T(8,128)S(1)}, u32[]{:S(2)}, u32[]{:S(2)}) collective-permute-start(f32[1056,128]{1,0:T(8,128)S(1)} %get-tuple-element.25), channel_id=1, source_target_pairs={{0,1},{1,0},{2,3},{3,2},{4,5},{5,4},{6,7},{7,6},{8,9},{9,8},{10,11... | collective-permute-start | bytes 1622024 | tf_op jit(solution)/shard_map/ppermute | solution.py:387
  9.0 10.1 %collective-permute-start.6 = (f32[136,128]{1,0:T(8,128)S(1)}, f32[136,128]{1,0:T(8,128)S(1)}, u32[]{:S(2)}, u32[]{:S(2)}) collective-permute-start(f32[136,128]{1,0:T(8,128)S(1)} %get-tuple-element.43), channel_id=1, source_target_pairs={{0,12},{4,0},{8,4},{12,8},{1,13},{5,1},{9,5},{13,9},{2,14},{6,2},{... | collective-permute-start | bytes 208904 | tf_op jit(solution)/shard_map/ppermute | solution.py:403
  14.0 9.4 %collective-permute-start.5 = (f32[136,128]{1,0:T(8,128)S(1)}, f32[136,128]{1,0:T(8,128)S(1)}, u32[]{:S(2)}, u32[]{:S(2)}) collective-permute-start(f32[136,128]{1,0:T(8,128)S(1)} %get-tuple-element.44), channel_id=1, source_target_pairs={{0,8},{4,12},{8,0},{12,4},{1,9},{5,13},{9,1},{13,5},{2,10},{6,14},... | collective-permute-start | bytes 208904 | tf_op jit(solution)/shard_map/ppermute | solution.py:403
  14.0 9.4 %collective-permute-start.4 = (f32[136,128]{1,0:T(8,128)S(1)}, f32[136,128]{1,0:T(8,128)S(1)}, u32[]{:S(2)}, u32[]{:S(2)}) collective-permute-start(f32[136,128]{1,0:T(8,128)S(1)} %get-tuple-element.45), channel_id=1, source_target_pairs={{0,4},{4,8},{8,12},{12,0},{1,5},{5,9},{9,13},{13,1},{2,6},{6,10},{... | collective-permute-start | bytes 208904 | tf_op jit(solution)/shard_map/ppermute | solution.py:403
  15.0 10.2 %collective-permute-start.3 = (f32[128,128]{1,0:T(8,128)S(1)}, f32[128,128]{1,0:T(8,128)S(1)}, u32[]{:S(2)}, u32[]{:S(2)}) collective-permute-start(f32[128,128]{1,0:T(8,128)S(1)} %get-tuple-element.47), channel_id=1, source_target_pairs={{0,12},{4,0},{8,4},{12,8},{1,13},{5,1},{9,5},{13,9},{2,14},{6,2},{... | collective-permute-start | bytes 196616 | tf_op jit(solution)/shard_map/ppermute | solution.py:403
  17.9 8.8 %collective-permute-start.2 = (f32[128,128]{1,0:T(8,128)S(1)}, f32[128,128]{1,0:T(8,128)S(1)}, u32[]{:S(2)}, u32[]{:S(2)}) collective-permute-start(f32[128,128]{1,0:T(8,128)S(1)} %get-tuple-element.48), channel_id=1, source_target_pairs={{0,8},{4,12},{8,0},{12,4},{1,9},{5,13},{9,1},{13,5},{2,10},{6,14},... | collective-permute-start | bytes 196616 | tf_op jit(solution)/shard_map/ppermute | solution.py:403
  19.0 7.7 %collective-permute-start.1 = (f32[128,128]{1,0:T(8,128)S(1)}, f32[128,128]{1,0:T(8,128)S(1)}, u32[]{:S(2)}, u32[]{:S(2)}) collective-permute-start(f32[128,128]{1,0:T(8,128)S(1)} %get-tuple-element.49), channel_id=1, source_target_pairs={{0,4},{4,8},{8,12},{12,0},{1,5},{5,9},{9,13},{13,1},{2,6},{6,10},{... | collective-permute-start | bytes 196616 | tf_op jit(solution)/shard_map/ppermute | solution.py:403
  23.7 4.3 %collective-permute-start.7 = (f32[128,128]{1,0:T(8,128)S(1)}, f32[128,128]{1,0:T(8,128)S(1)}, u32[]{:S(2)}, u32[]{:S(2)}) collective-permute-start(f32[128,128]{1,0:T(8,128)S(1)} %get-tuple-element.36), channel_id=1, source_target_pairs={{0,2},{1,3},{2,0},{3,1},{4,6},{5,7},{6,4},{7,5},{8,10},{9,11},{10,... | collective-permute-start | bytes 196616 | tf_op jit(solution)/shard_map/ppermute | solution.py:421
  25.2 4.2 %collective-permute-start.8 = (f32[128,128]{1,0:T(8,128)S(1)}, f32[128,128]{1,0:T(8,128)S(1)}, u32[]{:S(2)}, u32[]{:S(2)}) collective-permute-start(f32[128,128]{1,0:T(8,128)S(1)} %get-tuple-element.37), channel_id=1, source_target_pairs={{0,3},{1,2},{2,1},{3,0},{4,7},{5,6},{6,5},{7,4},{8,11},{9,10},{10,... | collective-permute-start | bytes 196616 | tf_op jit(solution)/shard_map/ppermute | solution.py:421
  29.7 5.7 %collective-permute-start.9 = (f32[256,128]{1,0:T(8,128)S(1)}, f32[256,128]{1,0:T(8,128)S(1)}, u32[]{:S(2)}, u32[]{:S(2)}) collective-permute-start(f32[256,128]{1,0:T(8,128)S(1)} %get-tuple-element.40), channel_id=1, source_target_pairs={{0,1},{1,0},{2,3},{3,2},{4,5},{5,4},{6,7},{7,6},{8,9},{9,8},{10,11... | collective-permute-start | bytes 393224 | tf_op jit(solution)/shard_map/ppermute | solution.py:421
  29.8 4.8 %collective-permute-start.10 = (f32[128,128]{1,0:T(8,128)S(1)}, f32[128,128]{1,0:T(8,128)S(1)}, u32[]{:S(2)}, u32[]{:S(2)}) collective-permute-start(f32[128,128]{1,0:T(8,128)S(1)} %get-tuple-element.41), channel_id=1, source_target_pairs={{0,2},{1,3},{2,0},{3,1},{4,6},{5,7},{6,4},{7,5},{8,10},{9,11},{10,... | collective-permute-start | bytes 196616 | tf_op jit(solution)/shard_map/ppermute | solution.py:421
  31.0 4.3 %collective-permute-start.11 = (f32[128,128]{1,0:T(8,128)S(1)}, f32[128,128]{1,0:T(8,128)S(1)}, u32[]{:S(2)}, u32[]{:S(2)}) collective-permute-start(f32[128,128]{1,0:T(8,128)S(1)} %get-tuple-element.42), channel_id=1, source_target_pairs={{0,3},{1,2},{2,1},{3,0},{4,7},{5,6},{6,5},{7,4},{8,11},{9,10},{10,... | collective-permute-start | bytes 196616 | tf_op jit(solution)/shard_map/ppermute | solution.py:421

commit v3 on v2

--- a/solution.py
+++ b/solution.py
@@ -75,7 +75,7 @@
     scratch = rest[CHUNKS * len(shifts) + 1 :]
     pos_ref, index_ref, count_ref = scratch[0:3]
     phase_ref, table_ref, obj_ref, probe_ref, cot_ref, row_ref, col_ref = scratch[3:10]
-    sems, band, window, col_bf = scratch[10:]
+    sems, band, window, col_bf, row_scr = scratch[10:]
     slices = obj_ref.shape[2]
     copies = [
         pltpu.make_async_copy(src, dst, sems.at[i])
@@ -98,7 +98,8 @@
     ]
     got_cot = pltpu.make_async_copy(cot_hbm, cot_ref, sems.at[len(copies) + slices])
     got_col = pltpu.make_async_copy(col_hbm, col_ref, sems.at[len(copies) + slices + 1])
-    for copy in (got_phase, got_table, got_pos, *got_obj, got_probe, got_cot):
+    order = [s for i in range((slices + 1) // 2) for s in sorted({i, slices - 1 - i})]
+    for copy in (got_pos, got_phase, got_table, *[got_obj[s] for s in order], got_probe, got_cot):
         copy.start()
     for copy in (got_index, got_count, got_row, got_col):
         copy.start()
@@ -112,38 +113,40 @@
     group = 2 if count % 2 == 0 else 1
     f32, bf16 = jnp.float32, jnp.bfloat16
 
+    got_pos.wait()
     got_phase.wait()
     got_table.wait()
-    whole, turned = propagator_blocks(phase_ref[...], table_ref[...])
-
-    got_pos.wait()
     col_down = lax.broadcasted_iota(jnp.int32, (cols, size), 0)
     lane = lax.broadcasted_iota(jnp.int32, (cols, size), 1)
     cut = jnp.concatenate(
         [(col_down == lane + pos_ref[0, w]).astype(bf16) for w in range(count)], 1
     )
-    lane_down = lax.broadcasted_iota(jnp.int32, (size, cols), 0)
-    col = lax.broadcasted_iota(jnp.int32, (size, cols), 1)
-    paste = jnp.concatenate(
-        [(col == lane_down + pos_ref[0, w]).astype(bf16) for w in range(count)], 0
-    )
-
-    for s in range(slices):
-        got_obj[s].wait()
+    whole, turned = propagator_blocks(phase_ref[...], table_ref[...])
+
+    for copy in got_obj:
+        copy.wait()
+    got_probe.wait()
+    got_cot.wait()
+    for s in order:
         source = jnp.concatenate([obj_ref[0, 0, s], obj_ref[0, 1, s]], 0)
         window[s] = dot(source, cut).astype(bf16)
 
     def tile(s, c, w):
-        return window[s, c * rows : (c + 1) * rows, w * size : (w + 1) * size].astype(f32)
-
-    def propagate(fields, first, second):
-        result = []
+        return window[s, c * rows : (c + 1) * rows, w * size : (w + 1) * size]
+
+    def left(fields, matrix):
+        parts = []
         for g in range(0, count, group):
             stack = jnp.concatenate(
                 [jnp.concatenate([fields[w][c] for w in range(g, g + group)], 1) for c in (0, 1)], 0
             )
-            part = dot(first, stack).astype(bf16)
-            turned_part = jnp.concatenate(
+            parts.append(dot(matrix, stack).astype(bf16))
+        return parts
+
+    def right(parts, matrix):
+        result = []
+        for part in parts:
+            stack = jnp.concatenate(
                 [
                     jnp.concatenate(
                         [
@@ -156,82 +159,71 @@
                 ],
                 0,
             )
-            done = dot(turned_part, second).astype(bf16)
+            done = dot(stack, matrix).astype(bf16)
             for k in range(group):
-                result.append(
-                    tuple(
-                        done[k * size : (k + 1) * size, c * size : (c + 1) * size] for c in (0, 1)
-                    )
-                )
+                lines = done[k * size : (k + 1) * size]
+                result.append((lines[:, :size], lines[:, size:]))
         return result
 
-    got_probe.wait()
-    now = [(probe_ref[0], probe_ref[1])] * count
-    kept = []
-    for s in range(slices):
-        kept.append(now)
-        if s + 1 < slices:
-            passed = []
-            for w in range(count):
-                o_re, o_im = tile(s, 0, w), tile(s, 1, w)
-                p_re, p_im = now[w][0].astype(f32), now[w][1].astype(f32)
-                passed.append(
-                    (
-                        (o_re * p_re - o_im * p_im).astype(bf16),
-                        (o_re * p_im + o_im * p_re).astype(bf16),
-                    )
-                )
-            now = propagate(passed, whole, turned)
+    def product(one, two, conjugate):
+        a_re, a_im = one[0].astype(f32), one[1].astype(f32)
+        b_re, b_im = two[0].astype(f32), two[1].astype(f32)
+        if conjugate:
+            a_im = -a_im
+        return (
+            (a_re * b_re - a_im * b_im).astype(bf16),
+            (a_re * b_im + a_im * b_re).astype(bf16),
+        )
 
     block_rows, block_cols = row_ref.shape[-1], col_ref.shape[-1]
     across = cols // block_cols
-    got_cot.wait()
+    psi, chi = {}, {}
+    now = [(probe_ref[0], probe_ref[1])] * count
     back = [(cot_ref[0, w, 0], cot_ref[0, w, 1]) for w in range(count)]
-    for s in reversed(range(slices)):
-        grads, rhos = [], []
-        for w in range(count):
-            c_re, c_im = back[w][0].astype(f32), back[w][1].astype(f32)
-            p_re, p_im = kept[s][w][0].astype(f32), kept[s][w][1].astype(f32)
-            grads.append(
-                (
-                    (p_re * c_re + p_im * c_im).astype(bf16),
-                    (p_re * c_im - p_im * c_re).astype(bf16),
-                )
+    lane_down = lax.broadcasted_iota(jnp.int32, (size, cols), 0)
+    col = lax.broadcasted_iota(jnp.int32, (size, cols), 1)
+    paste = jnp.concatenate(
+        [(col == lane_down + pos_ref[0, w]).astype(bf16) for w in range(count)], 0
+    )
+    for i in range(slices):
+        s, e = i, slices - 1 - i
+        psi[s], chi[e] = now, back
+        if i + 1 < slices:
+            here = [(tile(s, 0, w), tile(s, 1, w)) for w in range(count)]
+            there = [(tile(e, 0, w), tile(e, 1, w)) for w in range(count)]
+            passed = [product(here[w], now[w], False) for w in range(count)]
+            rho = [product(there[w], back[w], True) for w in range(count)]
+            now, back = left(passed, whole), left(rho, turned)
+            now, back = right(now, turned), right(back, whole)
+        for t in sorted({s, e}):
+            if t not in psi or t not in chi or max(t, slices - 1 - t) != i:
+                continue
+            grads = [product(psi[t][w], chi[t][w], True) for w in range(count)]
+            stack = jnp.concatenate(
+                [jnp.concatenate([grads[w][c] for w in range(count)], 1) for c in (0, 1)], 0
             )
-            if s > 0:
-                o_re, o_im = tile(s, 0, w), tile(s, 1, w)
-                rhos.append(
-                    (
-                        (o_re * c_re + o_im * c_im).astype(bf16),
-                        (o_re * c_im - o_im * c_re).astype(bf16),
-                    )
-                )
-        if s > 0:
-            back = propagate(rhos, turned, whole)
-        stack = jnp.concatenate(
-            [jnp.concatenate([grads[w][c] for w in range(count)], 1) for c in (0, 1)], 0
-        )
-        spread = dot(stack, paste).astype(bf16)
-        for c in (0, 1):
-            for i in range(rows // block_rows):
-                top = c * rows + i * block_rows
-                for j in range(across):
-                    band[c, (s * (rows // block_rows) + i) * across + j] = spread[
-                        top : top + block_rows, j * block_cols : (j + 1) * block_cols
-                    ]
+            spread = dot(stack, paste).astype(bf16)
+            for c in (0, 1):
+                for k in range(rows // block_rows):
+                    top = c * rows + k * block_rows
+                    for j in range(across):
+                        band[c, (t * (rows // block_rows) + k) * across + j] = spread[
+                            top : top + block_rows, j * block_cols : (j + 1) * block_cols
+                        ]
 
     got_row.wait()
     got_col.wait()
     got_index.wait()
     got_count.wait()
     tiles = row_ref.shape[0]
-    wide = capacity * block_rows
+    batch = 8
+    wide = batch * block_rows
     col_bf[...] = col_ref[...].astype(bf16)
     down = lax.broadcasted_iota(jnp.int32, (block_rows, wide), 0)
     along = lax.broadcasted_iota(jnp.int32, (block_rows, wide), 1)
     repeat = (lax.rem(along, block_rows) == down).astype(bf16)
     row_wide = dot(row_ref[...].reshape(tiles * block_rows, block_rows).astype(bf16), repeat)
-    row_wide = row_wide.reshape(tiles, block_rows, wide)
+    row_scr[...] = row_wide.reshape(tiles, block_rows, wide)
     strip = lax.div(along, block_rows)
     half = block_rows // CHUNKS
     mark_down = lax.broadcasted_iota(jnp.int32, (half, capacity * half), 0)
@@ -241,29 +233,42 @@
     for k, shift in enumerate(shifts):
         dest = lax.rem(me + shift, peers)
         live = count_ref[0, 0, dest]
-        inner, picks = [], []
         marks = jnp.full(mark_slot.shape, VB_DEV, jnp.int32)
-        for slot in range(capacity):
-            block = index_ref[0, 0, 0, dest, slot]
-            target = index_ref[1, 0, 0, dest, slot]
-            t = index_ref[2, 0, 0, dest, slot]
-            target = jnp.where(slot < live, target, VB_DEV)
-            marks = jnp.where(mark_slot == slot, target, marks)
-            pair = jnp.concatenate([band[core, block], band[1 - core, block]], 0)
-            mixed = dot(pair, col_bf[t]).astype(bf16)
-            inner.append(jnp.concatenate([mixed[:block_rows], mixed[block_rows:]], 1))
-            picked = row_wide[0]
-            for u in range(1, tiles):
-                picked = jnp.where(t == u, row_wide[u], picked)
-            picks.append(jnp.where(strip == slot, picked, 0.0).astype(bf16))
-        result = dot(jnp.concatenate(picks, 0), jnp.concatenate(inner, 0))
-        for h in range(CHUNKS):
-            for slot in range(capacity):
-                top = slot * block_rows + h * half
-                place = slice(slot * half, (slot + 1) * half)
-                mine[h * len(shifts) + k][place] = result[top : top + half, :block_cols]
-                begin = starts[h * len(shifts) + k] + slot * half
-                other[begin : begin + half] = result[top : top + half, block_cols:]
+        for first in range(0, capacity, batch):
+            inner, picks = [], []
+            for slot in range(first, first + batch, 2):
+                pairs, factors = [], []
+                for one in (slot, slot + 1):
+                    block = index_ref[0, 0, 0, dest, one]
+                    target = index_ref[1, 0, 0, dest, one]
+                    t = index_ref[2, 0, 0, dest, one]
+                    target = jnp.where(one < live, target, VB_DEV)
+                    marks = jnp.where(mark_slot == one, target, marks)
+                    pairs += [band[core, block], band[1 - core, block]]
+                    factors.append(col_bf[t])
+                    picked = jnp.where(strip == one - first, row_scr[t], 0.0)
+                    picks.append(picked.astype(bf16))
+                mixed = dot(jnp.concatenate(pairs, 0), jnp.concatenate(factors, 1)).astype(bf16)
+                for n in (0, 1):
+                    lanes = slice(n * block_cols, (n + 1) * block_cols)
+                    top = 2 * n * block_rows
+                    inner.append(
+                        jnp.concatenate(
+                            [
+                                mixed[top : top + block_rows, lanes],
+                                mixed[top + block_rows : top + 2 * block_rows, lanes],
+                            ],
+                            1,
+                        )
+                    )
+            result = dot(jnp.concatenate(picks, 0), jnp.concatenate(inner, 0))
+            for h in range(CHUNKS):
+                for slot in range(first, first + batch):
+                    top = (slot - first) * block_rows + h * half
+                    place = slice(slot * half, (slot + 1) * half)
+                    mine[h * len(shifts) + k][place] = result[top : top + half, :block_cols]
+                    begin = starts[h * len(shifts) + k] + slot * half
+                    other[begin : begin + half] = result[top : top + half, block_cols:]
         tail = capacity * half
         mine[k][tail : tail + half] = marks.astype(f32)
         begin = starts[k] + tail
@@ -274,7 +279,7 @@
     tilt, core = lax.axis_index("tilt"), lax.axis_index("rep")
     tilts, cores = lax.axis_size("tilt"), lax.axis_size("rep")
     each = VB_DEV // (tilts * cores)
-    blocks = refs[:sources]
+    blocks = refs[sources - 1 :: -1]
     half, lanes = CHUNK_ROWS, blocks[0].shape[-1]
     size = each * half
     if first:
@@ -375,6 +380,7 @@
             VMEM((2,) + frames, bf16),
             VMEM((slices, 2 * rows, windows * size), bf16),
             VMEM(col_interp.shape, bf16),
+            VMEM((row_interp.shape[0], block_rows, 8 * block_rows), f32),
         ],
         compiler_params=limit,
         name="frame",
@@ -410,7 +416,7 @@
             out_specs=[vmem] * (len(owners) + 1),
             compiler_params=limit,
             name="place",
-        )(*blocks, *extra)
+        )(*blocks[::-1], *extra)
         for i, (dt, dr) in enumerate(owners):
             if dt or (dr and h):
                 route = [

time: 36.3 us -> 33.5 us (0.923)
  the two profiles are of different devices: /device:TPU:0 before, /device:TPU:9 now
where the time goes in v3:
time: 33.5 us; the launch traced here: 33.4 us
  waiting for transfers between devices  13.8 us (41%)
  starting transfers between devices  12.4 us (37%)
  Pallas kernels  7.05 us (21%)
    ppermute x6, starting transfers between devices, on_device(): block = lax.ppermute(block, 'slab', ring)  7.04 us
    ppermute x5, waiting for transfers between devices, on_device(): parts[i] = lax.ppermute(parts[i], ('tilt', 'rep'), route)  6.8 us
    pallas_call x1, Pallas kernels, on_device(): pl.pallas_call(functools.partial(frame_kernel, shifts), out_shape=shapes...  5.74 us
    ppermute x6, waiting for transfers between devices, on_device(): block = lax.ppermute(block, 'slab', ring)  5.43 us
    ppermute x5, starting transfers between devices, on_device(): parts[i] = lax.ppermute(parts[i], ('tilt', 'rep'), route)  4.63 us
    ppermute x1, waiting for transfers between devices, on_device(): got = lax.ppermute(other, 'rep', swap)  1.56 us
    ppermute x1, starting transfers between devices, on_device(): got = lax.ppermute(other, 'rep', swap)  0.74 us
    pallas_call x1, Pallas kernels, on_device(): pl.pallas_call(functools.partial(sum_kernel, owners), out_shape=jax.Shape...  0.73 us
  transfers between devices with their start and end apart: 12, of which 7 were waited for; matrix products, arithmetic and copies ran while one was open for 0% of the time, Pallas kernels for 1%

profile of v3, /device:TPU:9, one launch (start us, length us, event | category | flops | bytes accessed | tf_op | source)
XLA Modules:
  0.0 33.4 jit_solution(11710196935956700109)
XLA Ops:
  0.0 5.7 %frame.1 = (f32[136,128]{1,0:T(8,128)S(1)}, f32[136,128]{1,0:T(8,128)S(1)}, f32[136,128]{1,0:T(8,128)S(1)}, f32[136,128]{1,0:T(8,128)S(1)}, f32[128,128]{1,0:T(8...) custom-call(s32[1,4]{1,0:T(1,128)} %pos_hbm.1, ...), custom_call_target="tpu_custom_call" | custom-call | tf_op jit(solution)/shard_map/frame/pallas_call | solution.py:371
  5.7 0.7 %collective-permute-start = (f32[1056,128]{1,0:T(8,128)S(1)}, f32[1056,128]{1,0:T(8,128)S(1)}, u32[]{:S(2)}, u32[]{:S(2)}) collective-permute-start(f32[1056,128]{1,0:T(8,128)S(1)} %get-tuple-element.25), channel_id=1, source_target_pairs={{0,1},{1,0},{2,3},{3,2},{4,5},{5,4},{6,7},{7,6},{8,9},{9,8},{10,11... | collective-permute-start | bytes 1622024 | tf_op jit(solution)/shard_map/ppermute | solution.py:393
  6.5 1.6 %collective-permute-done = f32[1056,128]{1,0:T(8,128)S(1)} collective-permute-done((f32[1056,128]{1,0:T(8,128)S(1)}, f32[1056,128]{1,0:T(8,128)S(1)}, u32[]{:S(2)}, u32[]{:S(2)}) %collective-permute-start) | collective-permute-done | bytes 540704 | tf_op jit(solution)/shard_map/ppermute | solution.py:393
  8.1 1.4 %collective-permute-start.6 = (f32[136,128]{1,0:T(8,128)S(1)}, f32[136,128]{1,0:T(8,128)S(1)}, u32[]{:S(2)}, u32[]{:S(2)}) collective-permute-start(f32[136,128]{1,0:T(8,128)S(1)} %get-tuple-element.44), channel_id=1, source_target_pairs={{0,4},{4,8},{8,12},{12,0},{1,5},{5,9},{9,13},{13,1},{2,6},{6,10},{... | collective-permute-start | bytes 208904 | tf_op jit(solution)/shard_map/ppermute | solution.py:409
  9.4 1.1 %collective-permute-start.5 = (f32[136,128]{1,0:T(8,128)S(1)}, f32[136,128]{1,0:T(8,128)S(1)}, u32[]{:S(2)}, u32[]{:S(2)}) collective-permute-start(f32[136,128]{1,0:T(8,128)S(1)} %get-tuple-element.45), channel_id=1, source_target_pairs={{0,8},{4,12},{8,0},{12,4},{1,9},{5,13},{9,1},{13,5},{2,10},{6,14},... | collective-permute-start | bytes 208904 | tf_op jit(solution)/shard_map/ppermute | solution.py:409
  10.5 1.4 %collective-permute-start.4 = (f32[136,128]{1,0:T(8,128)S(1)}, f32[136,128]{1,0:T(8,128)S(1)}, u32[]{:S(2)}, u32[]{:S(2)}) collective-permute-start(f32[136,128]{1,0:T(8,128)S(1)} %get-tuple-element.46), channel_id=1, source_target_pairs={{0,12},{4,0},{8,4},{12,8},{1,13},{5,1},{9,5},{13,9},{2,14},{6,2},{... | collective-permute-start | bytes 208904 | tf_op jit(solution)/shard_map/ppermute | solution.py:409
  12.0 0.1 collective-permute-start.3
  12.1 3.1 %collective-permute-start.2 = (f32[128,128]{1,0:T(8,128)S(1)}, f32[128,128]{1,0:T(8,128)S(1)}, u32[]{:S(2)}, u32[]{:S(2)}) collective-permute-start(f32[128,128]{1,0:T(8,128)S(1)} %get-tuple-element.49), channel_id=1, source_target_pairs={{0,8},{4,12},{8,0},{12,4},{1,9},{5,13},{9,1},{13,5},{2,10},{6,14},... | collective-permute-start | bytes 196616 | tf_op jit(solution)/shard_map/ppermute | solution.py:409
  15.2 0.0 collective-permute-done.6.refs_2_
  15.2 0.0 collective-permute-start.1
  15.2 5.2 %collective-permute-done.4.refs_0_ = f32[136,128]{1,0:T(8,128)S(1)} collective-permute-done((f32[136,128]{1,0:T(8,128)S(1)}, f32[136,128]{1,0:T(8,128)S(1)}, u32[]{:S(2)}, u32[]{:S(2)}) %collective-permute-start.4) | collective-permute-done | bytes 69664 | tf_op jit(solution)/shard_map/ppermute | solution.py:409
  20.4 0.3 place.2
  20.7 1.3 %collective-permute-start.7 = (f32[128,128]{1,0:T(8,128)S(1)}, f32[128,128]{1,0:T(8,128)S(1)}, u32[]{:S(2)}, u32[]{:S(2)}) collective-permute-start(f32[128,128]{1,0:T(8,128)S(1)} %get-tuple-element.36), channel_id=1, source_target_pairs={{0,2},{1,3},{2,0},{3,1},{4,6},{5,7},{6,4},{7,5},{8,10},{9,11},{10,... | collective-permute-start | bytes 196616 | tf_op jit(solution)/shard_map/ppermute | solution.py:427
  21.9 1.0 %collective-permute-start.8 = (f32[128,128]{1,0:T(8,128)S(1)}, f32[128,128]{1,0:T(8,128)S(1)}, u32[]{:S(2)}, u32[]{:S(2)}) collective-permute-start(f32[128,128]{1,0:T(8,128)S(1)} %get-tuple-element.37), channel_id=1, source_target_pairs={{0,3},{1,2},{2,1},{3,0},{4,7},{5,6},{6,5},{7,4},{8,11},{9,10},{10,... | collective-permute-start | bytes 196616 | tf_op jit(solution)/shard_map/ppermute | solution.py:427
  23.0 0.2 collective-permute-done.1.refs_0_
  23.2 0.7 %collective-permute-done.7.refs_7_ = f32[128,128]{1,0:T(8,128)S(1)} collective-permute-done((f32[128,128]{1,0:T(8,128)S(1)}, f32[128,128]{1,0:T(8,128)S(1)}, u32[]{:S(2)}, u32[]{:S(2)}) %collective-permute-start.7) | collective-permute-done | bytes 65568 | tf_op jit(solution)/shard_map/ppermute | solution.py:427
  23.9 2.6 %collective-permute-done.8.refs_8_ = f32[128,128]{1,0:T(8,128)S(1)} collective-permute-done((f32[128,128]{1,0:T(8,128)S(1)}, f32[128,128]{1,0:T(8,128)S(1)}, u32[]{:S(2)}, u32[]{:S(2)}) %collective-permute-start.8) | collective-permute-done | bytes 65568 | tf_op jit(solution)/shard_map/ppermute | solution.py:427
  26.5 0.3 place.3
  26.8 0.6 %collective-permute-start.9 = (f32[256,128]{1,0:T(8,128)S(1)}, f32[256,128]{1,0:T(8,128)S(1)}, u32[]{:S(2)}, u32[]{:S(2)}) collective-permute-start(f32[256,128]{1,0:T(8,128)S(1)} %get-tuple-element.40), channel_id=1, source_target_pairs={{0,1},{1,0},{2,3},{3,2},{4,5},{5,4},{6,7},{7,6},{8,9},{9,8},{10,11... | collective-permute-start | bytes 393224 | tf_op jit(solution)/shard_map/ppermute | solution.py:427
  27.4 0.5 %collective-permute-start.10 = (f32[128,128]{1,0:T(8,128)S(1)}, f32[128,128]{1,0:T(8,128)S(1)}, u32[]{:S(2)}, u32[]{:S(2)}) collective-permute-start(f32[128,128]{1,0:T(8,128)S(1)} %get-tuple-element.41), channel_id=1, source_target_pairs={{0,2},{1,3},{2,0},{3,1},{4,6},{5,7},{6,4},{7,5},{8,10},{9,11},{10,... | collective-permute-start | bytes 196616 | tf_op jit(solution)/shard_map/ppermute | solution.py:427
  27.9 1.2 %collective-permute-start.11 = (f32[128,128]{1,0:T(8,128)S(1)}, f32[128,128]{1,0:T(8,128)S(1)}, u32[]{:S(2)}, u32[]{:S(2)}) collective-permute-start(f32[128,128]{1,0:T(8,128)S(1)} %get-tuple-element.42), channel_id=1, source_target_pairs={{0,3},{1,2},{2,1},{3,0},{4,7},{5,6},{6,5},{7,4},{8,11},{9,10},{10,... | collective-permute-start | bytes 196616 | tf_op jit(solution)/shard_map/ppermute | solution.py:427
  29.1 2.0 %collective-permute-done.10.refs_2_ = f32[128,128]{1,0:T(8,128)S(1)} collective-permute-done((f32[128,128]{1,0:T(8,128)S(1)}, f32[128,128]{1,0:T(8,128)S(1)}, u32[]{:S(2)}, u32[]{:S(2)}) %collective-permute-start.10) | collective-permute-done | bytes 65568 | tf_op jit(solution)/shard_map/ppermute | solution.py:427
  31.1 1.6 %collective-permute-done.11.refs_3_ = f32[128,128]{1,0:T(8,128)S(1)} collective-permute-done((f32[128,128]{1,0:T(8,128)S(1)}, f32[128,128]{1,0:T(8,128)S(1)}, u32[]{:S(2)}, u32[]{:S(2)}) %collective-permute-start.11) | collective-permute-done | bytes 65568 | tf_op jit(solution)/shard_map/ppermute | solution.py:427
  32.6 0.7 %total.1 = f32[16,2,16,128]{3,2,1,0:T(8,128)} custom-call(f32[2,128,128]{2,1,0:T(8,128)S(1)} %get-tuple-element.38.done_ref, f32[128,128]{1,0:T(8,128)S(1)} %get-tuple-element.39.refs_0_, f32[256,128]{1,0:T(8,128)S(1)} %collective-permute-done.9.refs_1_, f32[128,128]{1,0:T(8,128)S(1)} %collective-permute-done.10.refs_2_, ...), custom_call_target="tpu_custom_call" | custom-call | tf_op jit(solution)/shard_map/total/pallas_call | solution.py:429
  (6 shorter events, 0.1 us)
Async XLA Ops:
  5.7 2.3 %collective-permute-start = (f32[1056,128]{1,0:T(8,128)S(1)}, f32[1056,128]{1,0:T(8,128)S(1)}, u32[]{:S(2)}, u32[]{:S(2)}) collective-permute-start(f32[1056,128]{1,0:T(8,128)S(1)} %get-tuple-element.25), channel_id=1, source_target_pairs={{0,1},{1,0},{2,3},{3,2},{4,5},{5,4},{6,7},{7,6},{8,9},{9,8},{10,11... | collective-permute-start | bytes 1622024 | tf_op jit(solution)/shard_map/ppermute | solution.py:393
  8.1 7.1 %collective-permute-start.6 = (f32[136,128]{1,0:T(8,128)S(1)}, f32[136,128]{1,0:T(8,128)S(1)}, u32[]{:S(2)}, u32[]{:S(2)}) collective-permute-start(f32[136,128]{1,0:T(8,128)S(1)} %get-tuple-element.44), channel_id=1, source_target_pairs={{0,4},{4,8},{8,12},{12,0},{1,5},{5,9},{9,13},{13,1},{2,6},{6,10},{... | collective-permute-start | bytes 208904 | tf_op jit(solution)/shard_map/ppermute | solution.py:409
  9.4 5.7 %collective-permute-start.5 = (f32[136,128]{1,0:T(8,128)S(1)}, f32[136,128]{1,0:T(8,128)S(1)}, u32[]{:S(2)}, u32[]{:S(2)}) collective-permute-start(f32[136,128]{1,0:T(8,128)S(1)} %get-tuple-element.45), channel_id=1, source_target_pairs={{0,8},{4,12},{8,0},{12,4},{1,9},{5,13},{9,1},{13,5},{2,10},{6,14},... | collective-permute-start | bytes 208904 | tf_op jit(solution)/shard_map/ppermute | solution.py:409
  10.5 9.8 %collective-permute-start.4 = (f32[136,128]{1,0:T(8,128)S(1)}, f32[136,128]{1,0:T(8,128)S(1)}, u32[]{:S(2)}, u32[]{:S(2)}) collective-permute-start(f32[136,128]{1,0:T(8,128)S(1)} %get-tuple-element.46), channel_id=1, source_target_pairs={{0,12},{4,0},{8,4},{12,8},{1,13},{5,1},{9,5},{13,9},{2,14},{6,2},{... | collective-permute-start | bytes 208904 | tf_op jit(solution)/shard_map/ppermute | solution.py:409
  12.0 11.0 %collective-permute-start.3 = (f32[128,128]{1,0:T(8,128)S(1)}, f32[128,128]{1,0:T(8,128)S(1)}, u32[]{:S(2)}, u32[]{:S(2)}) collective-permute-start(f32[128,128]{1,0:T(8,128)S(1)} %get-tuple-element.48), channel_id=1, source_target_pairs={{0,4},{4,8},{8,12},{12,0},{1,5},{5,9},{9,13},{13,1},{2,6},{6,10},{... | collective-permute-start | bytes 196616 | tf_op jit(solution)/shard_map/ppermute | solution.py:409
  12.1 10.9 %collective-permute-start.2 = (f32[128,128]{1,0:T(8,128)S(1)}, f32[128,128]{1,0:T(8,128)S(1)}, u32[]{:S(2)}, u32[]{:S(2)}) collective-permute-start(f32[128,128]{1,0:T(8,128)S(1)} %get-tuple-element.49), channel_id=1, source_target_pairs={{0,8},{4,12},{8,0},{12,4},{1,9},{5,13},{9,1},{13,5},{2,10},{6,14},... | collective-permute-start | bytes 196616 | tf_op jit(solution)/shard_map/ppermute | solution.py:409
  15.2 8.0 %collective-permute-start.1 = (f32[128,128]{1,0:T(8,128)S(1)}, f32[128,128]{1,0:T(8,128)S(1)}, u32[]{:S(2)}, u32[]{:S(2)}) collective-permute-start(f32[128,128]{1,0:T(8,128)S(1)} %get-tuple-element.50), channel_id=1, source_target_pairs={{0,12},{4,0},{8,4},{12,8},{1,13},{5,1},{9,5},{13,9},{2,14},{6,2},{... | collective-permute-start | bytes 196616 | tf_op jit(solution)/shard_map/ppermute | solution.py:409
  20.7 3.2 %collective-permute-start.7 = (f32[128,128]{1,0:T(8,128)S(1)}, f32[128,128]{1,0:T(8,128)S(1)}, u32[]{:S(2)}, u32[]{:S(2)}) collective-permute-start(f32[128,128]{1,0:T(8,128)S(1)} %get-tuple-element.36), channel_id=1, source_target_pairs={{0,2},{1,3},{2,0},{3,1},{4,6},{5,7},{6,4},{7,5},{8,10},{9,11},{10,... | collective-permute-start | bytes 196616 | tf_op jit(solution)/shard_map/ppermute | solution.py:427
  21.9 4.5 %collective-permute-start.8 = (f32[128,128]{1,0:T(8,128)S(1)}, f32[128,128]{1,0:T(8,128)S(1)}, u32[]{:S(2)}, u32[]{:S(2)}) collective-permute-start(f32[128,128]{1,0:T(8,128)S(1)} %get-tuple-element.37), channel_id=1, source_target_pairs={{0,3},{1,2},{2,1},{3,0},{4,7},{5,6},{6,5},{7,4},{8,11},{9,10},{10,... | collective-permute-start | bytes 196616 | tf_op jit(solution)/shard_map/ppermute | solution.py:427
  26.8 5.9 %collective-permute-start.9 = (f32[256,128]{1,0:T(8,128)S(1)}, f32[256,128]{1,0:T(8,128)S(1)}, u32[]{:S(2)}, u32[]{:S(2)}) collective-permute-start(f32[256,128]{1,0:T(8,128)S(1)} %get-tuple-element.40), channel_id=1, source_target_pairs={{0,1},{1,0},{2,3},{3,2},{4,5},{5,4},{6,7},{7,6},{8,9},{9,8},{10,11... | collective-permute-start | bytes 393224 | tf_op jit(solution)/shard_map/ppermute | solution.py:427
  27.4 3.7 %collective-permute-start.10 = (f32[128,128]{1,0:T(8,128)S(1)}, f32[128,128]{1,0:T(8,128)S(1)}, u32[]{:S(2)}, u32[]{:S(2)}) collective-permute-start(f32[128,128]{1,0:T(8,128)S(1)} %get-tuple-element.41), channel_id=1, source_target_pairs={{0,2},{1,3},{2,0},{3,1},{4,6},{5,7},{6,4},{7,5},{8,10},{9,11},{10,... | collective-permute-start | bytes 196616 | tf_op jit(solution)/shard_map/ppermute | solution.py:427
  27.9 4.7 %collective-permute-start.11 = (f32[128,128]{1,0:T(8,128)S(1)}, f32[128,128]{1,0:T(8,128)S(1)}, u32[]{:S(2)}, u32[]{:S(2)}) collective-permute-start(f32[128,128]{1,0:T(8,128)S(1)} %get-tuple-element.42), channel_id=1, source_target_pairs={{0,3},{1,2},{2,1},{3,0},{4,7},{5,6},{6,5},{7,4},{8,11},{9,10},{10,... | collective-permute-start | bytes 196616 | tf_op jit(solution)/shard_map/ppermute | solution.py:427

commit v4 on v3

--- a/solution.py
+++ b/solution.py
@@ -22,10 +22,16 @@
     return jnp.dot(left, right, precision=precision, preferred_element_type=jnp.float32)
 
 
-def slab_shifts(peers):
-    if peers <= 2 * REACH + 1:
-        return tuple(range(peers))
+def slab_steps(peers):
+    if peers <= REACH + 1:
+        return (0,) + tuple(sorted(range(1, peers), key=lambda k: (k < peers // 2, k)))
     return (0,) + tuple(s for k in range(1, REACH + 1) for s in (k, peers - k))
+
+
+def partner(slab, step, peers):
+    if peers <= REACH + 1 and peers & (peers - 1) == 0:
+        return slab ^ step
+    return (slab + step) % peers
 
 
 def angle_table(length):
@@ -71,8 +77,9 @@
     col_hbm,
     *rest,
 ):
-    mine, other = rest[: CHUNKS * len(shifts)], rest[CHUNKS * len(shifts)]
-    scratch = rest[CHUNKS * len(shifts) + 1 :]
+    mine = rest[: CHUNKS * len(shifts)]
+    other = rest[CHUNKS * len(shifts) :][:CHUNKS]
+    scratch = rest[CHUNKS * (len(shifts) + 1) :]
     pos_ref, index_ref, count_ref = scratch[0:3]
     phase_ref, table_ref, obj_ref, probe_ref, cot_ref, row_ref, col_ref = scratch[3:10]
     sems, band, window, col_bf, row_scr = scratch[10:]
@@ -229,9 +236,8 @@
     mark_down = lax.broadcasted_iota(jnp.int32, (half, capacity * half), 0)
     mark_along = lax.broadcasted_iota(jnp.int32, (half, capacity * half), 1)
     mark_slot = jnp.where(lax.rem(mark_along, half) == mark_down, lax.div(mark_along, half), -1)
-    starts = np.cumsum([0] + [ref.shape[0] for ref in mine])
     for k, shift in enumerate(shifts):
-        dest = lax.rem(me + shift, peers)
+        dest = partner(me, shift, peers)
         live = count_ref[0, 0, dest]
         marks = jnp.full(mark_slot.shape, VB_DEV, jnp.int32)
         for first in range(0, capacity, batch):
@@ -267,12 +273,12 @@
                     top = (slot - first) * block_rows + h * half
                     place = slice(slot * half, (slot + 1) * half)
                     mine[h * len(shifts) + k][place] = result[top : top + half, :block_cols]
-                    begin = starts[h * len(shifts) + k] + slot * half
-                    other[begin : begin + half] = result[top : top + half, block_cols:]
+                    begin = k * mine[h * len(shifts)].shape[0] + slot * half
+                    other[h][begin : begin + half] = result[top : top + half, block_cols:]
         tail = capacity * half
         mine[k][tail : tail + half] = marks.astype(f32)
-        begin = starts[k] + tail
-        other[begin : begin + half] = jnp.zeros(marks.shape, f32)
+        begin = k * mine[0].shape[0] + tail
+        other[0][begin : begin + half] = jnp.zeros(marks.shape, f32)
 
 
 def place_kernel(sources, owners, first, *refs):
@@ -340,7 +346,7 @@
 ):
     peers = lax.axis_size("slab")
     tilts, cores = lax.axis_size("tilt"), lax.axis_size("rep")
-    shifts = slab_shifts(peers)
+    shifts = slab_steps(peers)
     capacity = pair_index.shape[-1]
     block_rows, block_cols = row_interp.shape[-1], col_interp.shape[-1]
     _, _, slices, rows, cols = object_slab.shape
@@ -367,12 +373,15 @@
         (col_interp, VMEM),
     ]
     scalars = [positions, pair_index, pair_counts]
-    total = sum(shape.shape[0] for shape in shapes)
-    *mine, other = pl.pallas_call(
+    wholes = [
+        jax.ShapeDtypeStruct((sources * shapes[h * sources].shape[0], block_cols), f32)
+        for h in range(CHUNKS)
+    ]
+    held = pl.pallas_call(
         functools.partial(frame_kernel, shifts),
-        out_shape=shapes + [jax.ShapeDtypeStruct((total, block_cols), f32)],
+        out_shape=shapes + wholes,
         in_specs=[hbm] * 10,
-        out_specs=[vmem] * (len(shapes) + 1),
+        out_specs=[vmem] * (len(shapes) + CHUNKS),
         scratch_shapes=[SMEM(x.shape, x.dtype) for x in scalars]
         + [space(x.shape, x.dtype) for x, space in fetched]
         + [
@@ -387,15 +396,18 @@
     )(*[pltpu.with_memory_space_constraint(x, pltpu.HBM) for x in scalars + [x for x, _ in fetched]])
 
     swap = [(r, (r + 1) % cores) for r in range(cores)]
+    mine, other = held[: len(shapes)], held[len(shapes) :]
+    sent = []
+    for h in range(CHUNKS):
+        got = lax.ppermute(other[h], "rep", swap)
+        for k in range(sources):
+            part = mine[h * sources + k]
+            tall = part.shape[0]
+            sent.append(part + got[k * tall : (k + 1) * tall])
+
     owners = [(dt, dr) for dt in range(tilts) for dr in range(cores)]
     each = VB_DEV // len(owners)
     share = jax.ShapeDtypeStruct((each * CHUNK_ROWS, block_cols), f32)
-    got = lax.ppermute(other, "rep", swap)
-    sent, start = [], 0
-    for part in mine:
-        sent.append(part + got[start : start + part.shape[0]])
-        start += part.shape[0]
-
     mark = jax.ShapeDtypeStruct((sources, CHUNK_ROWS, block_cols), f32)
     double = jax.ShapeDtypeStruct((2 * each * CHUNK_ROWS, block_cols), f32)
     done = jax.ShapeDtypeStruct((cores, each * CHUNK_ROWS, block_cols), f32)
@@ -405,7 +417,7 @@
         for k in reversed(range(sources)):
             block = sent[h * sources + k]
             if shifts[k]:
-                ring = [(p, (p + shifts[k]) % peers) for p in range(peers)]
+                ring = [(p, partner(p, shifts[k], peers)) for p in range(peers)]
                 block = lax.ppermute(block, "slab", ring)
             blocks[k] = block
         *parts, more = pl.pallas_call(

time: 33.5 us -> 33.2 us (level)
  the two profiles are of different devices: /device:TPU:9 before, /device:TPU:17 now
where the time goes in v4:
time: 33.2 us; the launch traced here: 33.1 us
  starting transfers between devices  15.1 us (45%)
  waiting for transfers between devices  10.8 us (33%)
  Pallas kernels  7.05 us (21%)
    ppermute x6, starting transfers between devices, on_device(): block = lax.ppermute(block, 'slab', ring)  9.68 us
    ppermute x5, waiting for transfers between devices, on_device(): parts[i] = lax.ppermute(parts[i], ('tilt', 'rep'), route)  6.8 us
    pallas_call x1, Pallas kernels, on_device(): pl.pallas_call(functools.partial(frame_kernel, shifts), out_shape=shapes...  5.73 us
    ppermute x5, starting transfers between devices, on_device(): parts[i] = lax.ppermute(parts[i], ('tilt', 'rep'), route)  4.64 us
    ppermute x6, waiting for transfers between devices, on_device(): block = lax.ppermute(block, 'slab', ring)  2.89 us
    ppermute x2, waiting for transfers between devices, on_device(): got = lax.ppermute(other[h], 'rep', swap)  1.11 us
    ppermute x2, starting transfers between devices, on_device(): got = lax.ppermute(other[h], 'rep', swap)  0.82 us
    pallas_call x1, Pallas kernels, on_device(): pl.pallas_call(functools.partial(sum_kernel, owners), out_shape=jax.Shape...  0.73 us
  transfers between devices with their start and end apart: 13, of which 7 were waited for; matrix products, arithmetic and copies ran while one was open for 0% of the time, Pallas kernels for 1%

profile of v4, /device:TPU:17, one launch (start us, length us, event | category | flops | bytes accessed | tf_op | source)
XLA Modules:
  0.0 33.1 jit_solution(13669186316021719969)
XLA Ops:
  0.0 5.7 %frame.1 = (f32[136,128]{1,0:T(8,128)S(1)}, f32[136,128]{1,0:T(8,128)S(1)}, f32[136,128]{1,0:T(8,128)S(1)}, f32[136,128]{1,0:T(8,128)S(1)}, f32[128,128]{1,0:T(8...) custom-call(s32[1,4]{1,0:T(1,128)} %pos_hbm.1, ...), custom_call_target="tpu_custom_call" | custom-call | tf_op jit(solution)/shard_map/frame/pallas_call | solution.py:380
  5.7 0.7 %collective-permute-start.4 = (f32[544,128]{1,0:T(8,128)S(1)}, f32[544,128]{1,0:T(8,128)S(1)}, u32[]{:S(2)}, u32[]{:S(2)}) collective-permute-start(f32[544,128]{1,0:T(8,128)S(1)} %get-tuple-element.31), channel_id=1, source_target_pairs={{0,1},{1,0},{2,3},{3,2},{4,5},{5,4},{6,7},{7,6},{8,9},{9,8},{10,11... | collective-permute-start | bytes 835592 | tf_op jit(solution)/shard_map/ppermute | solution.py:402
  6.5 0.1 collective-permute-start
  6.6 1.1 %collective-permute-done.4 = f32[544,128]{1,0:T(8,128)S(1)} collective-permute-done((f32[544,128]{1,0:T(8,128)S(1)}, f32[544,128]{1,0:T(8,128)S(1)}, u32[]{:S(2)}, u32[]{:S(2)}) %collective-permute-start.4) | collective-permute-done | bytes 278560 | tf_op jit(solution)/shard_map/ppermute | solution.py:402
  7.7 0.1 collective-permute-start.7
  7.8 2.5 %collective-permute-start.6 = (f32[136,128]{1,0:T(8,128)S(1)}, f32[136,128]{1,0:T(8,128)S(1)}, u32[]{:S(2)}, u32[]{:S(2)}) collective-permute-start(f32[136,128]{1,0:T(8,128)S(1)} %get-tuple-element.47), channel_id=1, source_target_pairs={{0,12},{4,8},{8,4},{12,0},{1,13},{5,9},{9,5},{13,1},{2,14},{6,10},... | collective-permute-start | bytes 208904 | tf_op jit(solution)/shard_map/ppermute | solution.py:421
  10.3 1.1 %collective-permute-start.5 = (f32[136,128]{1,0:T(8,128)S(1)}, f32[136,128]{1,0:T(8,128)S(1)}, u32[]{:S(2)}, u32[]{:S(2)}) collective-permute-start(f32[136,128]{1,0:T(8,128)S(1)} %get-tuple-element.48), channel_id=1, source_target_pairs={{0,4},{4,0},{8,12},{12,8},{1,5},{5,1},{9,13},{13,9},{2,6},{6,2},{1... | collective-permute-start | bytes 208904 | tf_op jit(solution)/shard_map/ppermute | solution.py:421
  11.4 0.2 collective-permute-start.3
  11.5 1.5 %collective-permute-start.2 = (f32[128,128]{1,0:T(8,128)S(1)}, f32[128,128]{1,0:T(8,128)S(1)}, u32[]{:S(2)}, u32[]{:S(2)}) collective-permute-start(f32[128,128]{1,0:T(8,128)S(1)} %get-tuple-element.51), channel_id=1, source_target_pairs={{0,12},{4,8},{8,4},{12,0},{1,13},{5,9},{9,5},{13,1},{2,14},{6,10},... | collective-permute-start | bytes 196616 | tf_op jit(solution)/shard_map/ppermute | solution.py:421
  13.0 4.4 %collective-permute-start.1 = (f32[128,128]{1,0:T(8,128)S(1)}, f32[128,128]{1,0:T(8,128)S(1)}, u32[]{:S(2)}, u32[]{:S(2)}) collective-permute-start(f32[128,128]{1,0:T(8,128)S(1)} %get-tuple-element.52), channel_id=1, source_target_pairs={{0,4},{4,0},{8,12},{12,8},{1,5},{5,1},{9,13},{13,9},{2,6},{6,2},{1... | collective-permute-start | bytes 196616 | tf_op jit(solution)/shard_map/ppermute | solution.py:421
  17.4 2.7 %collective-permute-done.6.refs_1_ = f32[136,128]{1,0:T(8,128)S(1)} collective-permute-done((f32[136,128]{1,0:T(8,128)S(1)}, f32[136,128]{1,0:T(8,128)S(1)}, u32[]{:S(2)}, u32[]{:S(2)}) %collective-permute-start.6) | collective-permute-done | bytes 69664 | tf_op jit(solution)/shard_map/ppermute | solution.py:421
  20.1 0.3 place.2
  20.4 1.3 %collective-permute-start.8 = (f32[128,128]{1,0:T(8,128)S(1)}, f32[128,128]{1,0:T(8,128)S(1)}, u32[]{:S(2)}, u32[]{:S(2)}) collective-permute-start(f32[128,128]{1,0:T(8,128)S(1)} %get-tuple-element.38), channel_id=1, source_target_pairs={{0,2},{1,3},{2,0},{3,1},{4,6},{5,7},{6,4},{7,5},{8,10},{9,11},{10,... | collective-permute-start | bytes 196616 | tf_op jit(solution)/shard_map/ppermute | solution.py:439
  21.7 1.0 %collective-permute-start.9 = (f32[128,128]{1,0:T(8,128)S(1)}, f32[128,128]{1,0:T(8,128)S(1)}, u32[]{:S(2)}, u32[]{:S(2)}) collective-permute-start(f32[128,128]{1,0:T(8,128)S(1)} %get-tuple-element.39), channel_id=1, source_target_pairs={{0,3},{1,2},{2,1},{3,0},{4,7},{5,6},{6,5},{7,4},{8,11},{9,10},{10,... | collective-permute-start | bytes 196616 | tf_op jit(solution)/shard_map/ppermute | solution.py:439
  22.7 0.2 collective-permute-done.2.refs_1_
  22.9 0.7 %collective-permute-done.8.refs_7_ = f32[128,128]{1,0:T(8,128)S(1)} collective-permute-done((f32[128,128]{1,0:T(8,128)S(1)}, f32[128,128]{1,0:T(8,128)S(1)}, u32[]{:S(2)}, u32[]{:S(2)}) %collective-permute-start.8) | collective-permute-done | bytes 65568 | tf_op jit(solution)/shard_map/ppermute | solution.py:439
  23.6 2.6 %collective-permute-done.9.refs_8_ = f32[128,128]{1,0:T(8,128)S(1)} collective-permute-done((f32[128,128]{1,0:T(8,128)S(1)}, f32[128,128]{1,0:T(8,128)S(1)}, u32[]{:S(2)}, u32[]{:S(2)}) %collective-permute-start.9) | collective-permute-done | bytes 65568 | tf_op jit(solution)/shard_map/ppermute | solution.py:439
  26.2 0.3 place.3
  26.5 0.6 %collective-permute-start.10 = (f32[256,128]{1,0:T(8,128)S(1)}, f32[256,128]{1,0:T(8,128)S(1)}, u32[]{:S(2)}, u32[]{:S(2)}) collective-permute-start(f32[256,128]{1,0:T(8,128)S(1)} %get-tuple-element.42), channel_id=1, source_target_pairs={{0,1},{1,0},{2,3},{3,2},{4,5},{5,4},{6,7},{7,6},{8,9},{9,8},{10,11... | collective-permute-start | bytes 393224 | tf_op jit(solution)/shard_map/ppermute | solution.py:439
  27.1 0.5 %collective-permute-start.11 = (f32[128,128]{1,0:T(8,128)S(1)}, f32[128,128]{1,0:T(8,128)S(1)}, u32[]{:S(2)}, u32[]{:S(2)}) collective-permute-start(f32[128,128]{1,0:T(8,128)S(1)} %get-tuple-element.43), channel_id=1, source_target_pairs={{0,2},{1,3},{2,0},{3,1},{4,6},{5,7},{6,4},{7,5},{8,10},{9,11},{10,... | collective-permute-start | bytes 196616 | tf_op jit(solution)/shard_map/ppermute | solution.py:439
  27.7 1.2 %collective-permute-start.12 = (f32[128,128]{1,0:T(8,128)S(1)}, f32[128,128]{1,0:T(8,128)S(1)}, u32[]{:S(2)}, u32[]{:S(2)}) collective-permute-start(f32[128,128]{1,0:T(8,128)S(1)} %get-tuple-element.44), channel_id=1, source_target_pairs={{0,3},{1,2},{2,1},{3,0},{4,7},{5,6},{6,5},{7,4},{8,11},{9,10},{10,... | collective-permute-start | bytes 196616 | tf_op jit(solution)/shard_map/ppermute | solution.py:439
  28.8 2.0 %collective-permute-done.11.refs_2_ = f32[128,128]{1,0:T(8,128)S(1)} collective-permute-done((f32[128,128]{1,0:T(8,128)S(1)}, f32[128,128]{1,0:T(8,128)S(1)}, u32[]{:S(2)}, u32[]{:S(2)}) %collective-permute-start.11) | collective-permute-done | bytes 65568 | tf_op jit(solution)/shard_map/ppermute | solution.py:439
  30.8 1.6 %collective-permute-done.12.refs_3_ = f32[128,128]{1,0:T(8,128)S(1)} collective-permute-done((f32[128,128]{1,0:T(8,128)S(1)}, f32[128,128]{1,0:T(8,128)S(1)}, u32[]{:S(2)}, u32[]{:S(2)}) %collective-permute-start.12) | collective-permute-done | bytes 65568 | tf_op jit(solution)/shard_map/ppermute | solution.py:439
  32.4 0.7 %total.1 = f32[16,2,16,128]{3,2,1,0:T(8,128)} custom-call(f32[2,128,128]{2,1,0:T(8,128)S(1)} %get-tuple-element.40.done_ref, f32[128,128]{1,0:T(8,128)S(1)} %get-tuple-element.41.refs_0_, f32[256,128]{1,0:T(8,128)S(1)} %collective-permute-done.10.refs_1_, f32[128,128]{1,0:T(8,128)S(1)} %collective-permute-done.11.refs_2_, ...), custom_call_target="tpu_custom_call" | custom-call | tf_op jit(solution)/shard_map/total/pallas_call | solution.py:441
  (8 shorter events, 0.1 us)
Async XLA Ops:
  5.7 1.9 %collective-permute-start.4 = (f32[544,128]{1,0:T(8,128)S(1)}, f32[544,128]{1,0:T(8,128)S(1)}, u32[]{:S(2)}, u32[]{:S(2)}) collective-permute-start(f32[544,128]{1,0:T(8,128)S(1)} %get-tuple-element.31), channel_id=1, source_target_pairs={{0,1},{1,0},{2,3},{3,2},{4,5},{5,4},{6,7},{7,6},{8,9},{9,8},{10,11... | collective-permute-start | bytes 835592 | tf_op jit(solution)/shard_map/ppermute | solution.py:402
  6.5 4.8 %collective-permute-start = (f32[512,128]{1,0:T(8,128)S(1)}, f32[512,128]{1,0:T(8,128)S(1)}, u32[]{:S(2)}, u32[]{:S(2)}) collective-permute-start(f32[512,128]{1,0:T(8,128)S(1)} %get-tuple-element.26), channel_id=1, source_target_pairs={{0,1},{1,0},{2,3},{3,2},{4,5},{5,4},{6,7},{7,6},{8,9},{9,8},{10,11... | collective-permute-start | bytes 786440 | tf_op jit(solution)/shard_map/ppermute | solution.py:402
  7.7 5.3 %collective-permute-start.7 = (f32[136,128]{1,0:T(8,128)S(1)}, f32[136,128]{1,0:T(8,128)S(1)}, u32[]{:S(2)}, u32[]{:S(2)}) collective-permute-start(f32[136,128]{1,0:T(8,128)S(1)} %get-tuple-element.46), channel_id=1, source_target_pairs={{0,8},{4,12},{8,0},{12,4},{1,9},{5,13},{9,1},{13,5},{2,10},{6,14},... | collective-permute-start | bytes 208904 | tf_op jit(solution)/shard_map/ppermute | solution.py:421
  7.8 12.3 %collective-permute-start.6 = (f32[136,128]{1,0:T(8,128)S(1)}, f32[136,128]{1,0:T(8,128)S(1)}, u32[]{:S(2)}, u32[]{:S(2)}) collective-permute-start(f32[136,128]{1,0:T(8,128)S(1)} %get-tuple-element.47), channel_id=1, source_target_pairs={{0,12},{4,8},{8,4},{12,0},{1,13},{5,9},{9,5},{13,1},{2,14},{6,10},... | collective-permute-start | bytes 208904 | tf_op jit(solution)/shard_map/ppermute | solution.py:421
  10.3 9.9 %collective-permute-start.5 = (f32[136,128]{1,0:T(8,128)S(1)}, f32[136,128]{1,0:T(8,128)S(1)}, u32[]{:S(2)}, u32[]{:S(2)}) collective-permute-start(f32[136,128]{1,0:T(8,128)S(1)} %get-tuple-element.48), channel_id=1, source_target_pairs={{0,4},{4,0},{8,12},{12,8},{1,5},{5,1},{9,13},{13,9},{2,6},{6,2},{1... | collective-permute-start | bytes 208904 | tf_op jit(solution)/shard_map/ppermute | solution.py:421
  11.4 11.3 %collective-permute-start.3 = (f32[128,128]{1,0:T(8,128)S(1)}, f32[128,128]{1,0:T(8,128)S(1)}, u32[]{:S(2)}, u32[]{:S(2)}) collective-permute-start(f32[128,128]{1,0:T(8,128)S(1)} %get-tuple-element.50), channel_id=1, source_target_pairs={{0,8},{4,12},{8,0},{12,4},{1,9},{5,13},{9,1},{13,5},{2,10},{6,14},... | collective-permute-start | bytes 196616 | tf_op jit(solution)/shard_map/ppermute | solution.py:421
  11.5 11.4 %collective-permute-start.2 = (f32[128,128]{1,0:T(8,128)S(1)}, f32[128,128]{1,0:T(8,128)S(1)}, u32[]{:S(2)}, u32[]{:S(2)}) collective-permute-start(f32[128,128]{1,0:T(8,128)S(1)} %get-tuple-element.51), channel_id=1, source_target_pairs={{0,12},{4,8},{8,4},{12,0},{1,13},{5,9},{9,5},{13,1},{2,14},{6,10},... | collective-permute-start | bytes 196616 | tf_op jit(solution)/shard_map/ppermute | solution.py:421
  13.0 9.9 %collective-permute-start.1 = (f32[128,128]{1,0:T(8,128)S(1)}, f32[128,128]{1,0:T(8,128)S(1)}, u32[]{:S(2)}, u32[]{:S(2)}) collective-permute-start(f32[128,128]{1,0:T(8,128)S(1)} %get-tuple-element.52), channel_id=1, source_target_pairs={{0,4},{4,0},{8,12},{12,8},{1,5},{5,1},{9,13},{13,9},{2,6},{6,2},{1... | collective-permute-start | bytes 196616 | tf_op jit(solution)/shard_map/ppermute | solution.py:421
  20.4 3.2 %collective-permute-start.8 = (f32[128,128]{1,0:T(8,128)S(1)}, f32[128,128]{1,0:T(8,128)S(1)}, u32[]{:S(2)}, u32[]{:S(2)}) collective-permute-start(f32[128,128]{1,0:T(8,128)S(1)} %get-tuple-element.38), channel_id=1, source_target_pairs={{0,2},{1,3},{2,0},{3,1},{4,6},{5,7},{6,4},{7,5},{8,10},{9,11},{10,... | collective-permute-start | bytes 196616 | tf_op jit(solution)/shard_map/ppermute | solution.py:439
  21.7 4.5 %collective-permute-start.9 = (f32[128,128]{1,0:T(8,128)S(1)}, f32[128,128]{1,0:T(8,128)S(1)}, u32[]{:S(2)}, u32[]{:S(2)}) collective-permute-start(f32[128,128]{1,0:T(8,128)S(1)} %get-tuple-element.39), channel_id=1, source_target_pairs={{0,3},{1,2},{2,1},{3,0},{4,7},{5,6},{6,5},{7,4},{8,11},{9,10},{10,... | collective-permute-start | bytes 196616 | tf_op jit(solution)/shard_map/ppermute | solution.py:439
  26.5 5.9 %collective-permute-start.10 = (f32[256,128]{1,0:T(8,128)S(1)}, f32[256,128]{1,0:T(8,128)S(1)}, u32[]{:S(2)}, u32[]{:S(2)}) collective-permute-start(f32[256,128]{1,0:T(8,128)S(1)} %get-tuple-element.42), channel_id=1, source_target_pairs={{0,1},{1,0},{2,3},{3,2},{4,5},{5,4},{6,7},{7,6},{8,9},{9,8},{10,11... | collective-permute-start | bytes 393224 | tf_op jit(solution)/shard_map/ppermute | solution.py:439
  27.1 3.7 %collective-permute-start.11 = (f32[128,128]{1,0:T(8,128)S(1)}, f32[128,128]{1,0:T(8,128)S(1)}, u32[]{:S(2)}, u32[]{:S(2)}) collective-permute-start(f32[128,128]{1,0:T(8,128)S(1)} %get-tuple-element.43), channel_id=1, source_target_pairs={{0,2},{1,3},{2,0},{3,1},{4,6},{5,7},{6,4},{7,5},{8,10},{9,11},{10,... | collective-permute-start | bytes 196616 | tf_op jit(solution)/shard_map/ppermute | solution.py:439
  27.7 4.7 %collective-permute-start.12 = (f32[128,128]{1,0:T(8,128)S(1)}, f32[128,128]{1,0:T(8,128)S(1)}, u32[]{:S(2)}, u32[]{:S(2)}) collective-permute-start(f32[128,128]{1,0:T(8,128)S(1)} %get-tuple-element.44), channel_id=1, source_target_pairs={{0,3},{1,2},{2,1},{3,0},{4,7},{5,6},{6,5},{7,4},{8,11},{9,10},{10,... | collective-permute-start | bytes 196616 | tf_op jit(solution)/shard_map/ppermute | solution.py:439

commit v5 on v3

--- a/solution.py
+++ b/solution.py
@@ -10,7 +10,6 @@
 from jax.sharding import PartitionSpec as P
 
 VB_DEV = 64
-REACH = 3
 CHUNKS = 2
 CHUNK_ROWS = 8
 HIGH = lax.Precision.HIGHEST
@@ -20,12 +19,6 @@
 
 def dot(left, right, precision=None):
     return jnp.dot(left, right, precision=precision, preferred_element_type=jnp.float32)
-
-
-def slab_shifts(peers):
-    if peers <= 2 * REACH + 1:
-        return tuple(range(peers))
-    return (0,) + tuple(s for k in range(1, REACH + 1) for s in (k, peers - k))
 
 
 def angle_table(length):
@@ -58,7 +51,7 @@
 
 
 def frame_kernel(
-    shifts,
+    peers,
     pos_hbm,
     index_hbm,
     count_hbm,
@@ -71,8 +64,7 @@
     col_hbm,
     *rest,
 ):
-    mine, other = rest[: CHUNKS * len(shifts)], rest[CHUNKS * len(shifts)]
-    scratch = rest[CHUNKS * len(shifts) + 1 :]
+    mine, other, scratch = rest[:CHUNKS], rest[CHUNKS : 2 * CHUNKS], rest[2 * CHUNKS :]
     pos_ref, index_ref, count_ref = scratch[0:3]
     phase_ref, table_ref, obj_ref, probe_ref, cot_ref, row_ref, col_ref = scratch[3:10]
     sems, band, window, col_bf, row_scr = scratch[10:]
@@ -104,8 +96,7 @@
     for copy in (got_index, got_count, got_row, got_col):
         copy.start()
 
-    me, core = lax.axis_index("slab"), lax.axis_index("rep")
-    peers = lax.axis_size("slab")
+    core = lax.axis_index("rep")
     capacity = index_ref.shape[-1]
     size = probe_ref.shape[-1]
     rows, cols = obj_ref.shape[3:]
@@ -229,9 +220,7 @@
     mark_down = lax.broadcasted_iota(jnp.int32, (half, capacity * half), 0)
     mark_along = lax.broadcasted_iota(jnp.int32, (half, capacity * half), 1)
     mark_slot = jnp.where(lax.rem(mark_along, half) == mark_down, lax.div(mark_along, half), -1)
-    starts = np.cumsum([0] + [ref.shape[0] for ref in mine])
-    for k, shift in enumerate(shifts):
-        dest = lax.rem(me + shift, peers)
+    for dest in range(peers):
         live = count_ref[0, 0, dest]
         marks = jnp.full(mark_slot.shape, VB_DEV, jnp.int32)
         for first in range(0, capacity, batch):
@@ -266,35 +255,32 @@
                 for slot in range(first, first + batch):
                     top = (slot - first) * block_rows + h * half
                     place = slice(slot * half, (slot + 1) * half)
-                    mine[h * len(shifts) + k][place] = result[top : top + half, :block_cols]
-                    begin = starts[h * len(shifts) + k] + slot * half
-                    other[begin : begin + half] = result[top : top + half, block_cols:]
-        tail = capacity * half
-        mine[k][tail : tail + half] = marks.astype(f32)
-        begin = starts[k] + tail
-        other[begin : begin + half] = jnp.zeros(marks.shape, f32)
+                    mine[h][dest, place] = result[top : top + half, :block_cols]
+                    other[h][dest, place] = result[top : top + half, block_cols:]
+        tail = slice(capacity * half, (capacity + 1) * half)
+        mine[0][dest, tail] = marks.astype(f32)
+        other[0][dest, tail] = jnp.zeros(marks.shape, f32)
 
 
 def place_kernel(sources, owners, first, *refs):
     tilt, core = lax.axis_index("tilt"), lax.axis_index("rep")
     tilts, cores = lax.axis_size("tilt"), lax.axis_size("rep")
     each = VB_DEV // (tilts * cores)
-    blocks = refs[sources - 1 :: -1]
-    half, lanes = CHUNK_ROWS, blocks[0].shape[-1]
+    block_ref, refs = refs[0], refs[1:]
+    half, lanes = CHUNK_ROWS, block_ref.shape[-1]
     size = each * half
     if first:
-        outs, mark_ref = refs[sources:-1], refs[-1]
-        for k, block in enumerate(blocks):
-            mark_ref[k] = block[lanes:]
+        outs, mark_ref = refs[:-1], refs[-1]
+        mark_ref[...] = block_ref[:, lanes:]
     else:
-        mark_ref, rest = refs[sources], refs[sources + 1 :]
+        mark_ref, rest = refs[0], refs[1:]
         before, outs, done = rest[: len(owners)], rest[len(owners) : -1], rest[-1]
         for dr in range(cores):
             parts = [ref[...] for ref, (dt, r) in zip(before, owners) if r == dr]
             if dr:
                 outs[dr][:size] = parts.pop(0)
             done[dr] = functools.reduce(jnp.add, parts, jnp.zeros((size, lanes), jnp.float32))
-    data = jnp.concatenate([block[:lanes].astype(jnp.bfloat16) for block in blocks], 0)
+    data = block_ref[:, :lanes].astype(jnp.bfloat16).reshape(sources * lanes, -1)
     volume = lax.broadcasted_iota(jnp.int32, (each, half, lanes), 0).astype(jnp.float32)
     for out, (dt, dr) in zip(outs, owners):
         owner = lax.rem(tilt + dt, tilts) * cores + lax.rem(core + dr, cores)
@@ -340,7 +326,6 @@
 ):
     peers = lax.axis_size("slab")
     tilts, cores = lax.axis_size("tilt"), lax.axis_size("rep")
-    shifts = slab_shifts(peers)
     capacity = pair_index.shape[-1]
     block_rows, block_cols = row_interp.shape[-1], col_interp.shape[-1]
     _, _, slices, rows, cols = object_slab.shape
@@ -348,15 +333,16 @@
     f32, bf16 = jnp.float32, jnp.bfloat16
     hbm, vmem = pl.BlockSpec(memory_space=pltpu.HBM), pl.BlockSpec(memory_space=VMEM)
     limit = pltpu.CompilerParams(vmem_limit_bytes=40 * 1024 * 1024)
-    sources = len(shifts)
+    sources = peers
     lanes = capacity * CHUNK_ROWS
 
     phase_line = phases.reshape(1, -1)
     table = jnp.asarray(angle_table(size))
     frames = (slices * (rows // block_rows) * (cols // block_cols), block_rows, block_cols)
-    marked = jax.ShapeDtypeStruct((lanes + CHUNK_ROWS, block_cols), f32)
-    plain = jax.ShapeDtypeStruct((lanes, block_cols), f32)
-    shapes = [marked] * sources + [plain] * (sources * (CHUNKS - 1))
+    shapes = [
+        jax.ShapeDtypeStruct((peers, lanes + CHUNK_ROWS * (h == 0), block_cols), f32)
+        for h in range(CHUNKS)
+    ]
     fetched = [
         (phase_line, VMEM),
         (table, VMEM),
@@ -367,12 +353,11 @@
         (col_interp, VMEM),
     ]
     scalars = [positions, pair_index, pair_counts]
-    total = sum(shape.shape[0] for shape in shapes)
-    *mine, other = pl.pallas_call(
-        functools.partial(frame_kernel, shifts),
-        out_shape=shapes + [jax.ShapeDtypeStruct((total, block_cols), f32)],
+    held = pl.pallas_call(
+        functools.partial(frame_kernel, peers),
+        out_shape=shapes + shapes,
         in_specs=[hbm] * 10,
-        out_specs=[vmem] * (len(shapes) + 1),
+        out_specs=[vmem] * (2 * CHUNKS),
         scratch_shapes=[SMEM(x.shape, x.dtype) for x in scalars]
         + [space(x.shape, x.dtype) for x, space in fetched]
         + [
@@ -387,36 +372,27 @@
     )(*[pltpu.with_memory_space_constraint(x, pltpu.HBM) for x in scalars + [x for x, _ in fetched]])
 
     swap = [(r, (r + 1) % cores) for r in range(cores)]
+    mine, other = held[:CHUNKS], held[CHUNKS:]
+    sent = [mine[h] + lax.ppermute(other[h], "rep", swap) for h in range(CHUNKS)]
+
     owners = [(dt, dr) for dt in range(tilts) for dr in range(cores)]
     each = VB_DEV // len(owners)
     share = jax.ShapeDtypeStruct((each * CHUNK_ROWS, block_cols), f32)
-    got = lax.ppermute(other, "rep", swap)
-    sent, start = [], 0
-    for part in mine:
-        sent.append(part + got[start : start + part.shape[0]])
-        start += part.shape[0]
-
     mark = jax.ShapeDtypeStruct((sources, CHUNK_ROWS, block_cols), f32)
     double = jax.ShapeDtypeStruct((2 * each * CHUNK_ROWS, block_cols), f32)
     done = jax.ShapeDtypeStruct((cores, each * CHUNK_ROWS, block_cols), f32)
     extra = []
     for h in range(CHUNKS):
-        blocks = [None] * sources
-        for k in reversed(range(sources)):
-            block = sent[h * sources + k]
-            if shifts[k]:
-                ring = [(p, (p + shifts[k]) % peers) for p in range(peers)]
-                block = lax.ppermute(block, "slab", ring)
-            blocks[k] = block
+        blocks = lax.all_to_all(sent[h], "slab", split_axis=0, concat_axis=0, tiled=True)
         *parts, more = pl.pallas_call(
             functools.partial(place_kernel, sources, owners, h == 0),
             out_shape=[double if h and dr and not dt else share for dt, dr in owners]
             + [done if h else mark],
-            in_specs=[vmem] * (sources + len(extra)),
+            in_specs=[vmem] * (1 + len(extra)),
             out_specs=[vmem] * (len(owners) + 1),
             compiler_params=limit,
             name="place",
-        )(*blocks[::-1], *extra)
+        )(blocks, *extra)
         for i, (dt, dr) in enumerate(owners):
             if dt or (dr and h):
                 route = [

time: 33.5 us -> 41.3 us (1.23)
  the two profiles are of different devices: /device:TPU:9 before, /device:TPU:0 now
where the time goes in v5:
time: 41.3 us; the launch traced here: 41 us
  waiting for transfers between devices  18.8 us (46%)
  starting transfers between devices  13.7 us (33%)
  Pallas kernels  7.04 us (17%)
  other arithmetic  1.49 us (4%)
    all_to_all x2, waiting for transfers between devices, on_device(): lax.all_to_all(sent[h], 'slab', split_axis=0, concat_axis=0, tiled=True)  12.3 us
    all_to_all x2, starting transfers between devices, on_device(): lax.all_to_all(sent[h], 'slab', split_axis=0, concat_axis=0, tiled=True)  9.65 us
    pallas_call x1, Pallas kernels, on_device(): pl.pallas_call(functools.partial(frame_kernel, peers), out_shape=shapes +...  5.73 us
    ppermute x5, waiting for transfers between devices, on_device(): parts[i] = lax.ppermute(parts[i], ('tilt', 'rep'), route)  3.75 us
    ppermute x5, starting transfers between devices, on_device(): parts[i] = lax.ppermute(parts[i], ('tilt', 'rep'), route)  3.49 us
    ppermute x2, waiting for transfers between devices, on_device(): lax.ppermute(other[h], 'rep', swap)  2.72 us
    add x2, other arithmetic, on_device(): mine[h] + lax.ppermute(other[h], 'rep', swap)  1.49 us
  transfers between devices with their start and end apart: 9, of which 6 were waited for; matrix products, arithmetic and copies ran while one was open for 2% of the time, Pallas kernels for 1%

profile of v5, /device:TPU:0, one launch (start us, length us, event | category | flops | bytes accessed | tf_op | source)
XLA Modules:
  0.0 41.0 jit_solution(7913936109638097661)
XLA Ops:
  0.0 5.7 %frame.1 = (f32[4,136,128]{2,1,0:T(8,128)S(1)}, f32[4,128,128]{2,1,0:T(8,128)S(1)}, f32[4,136,128]{2,1,0:T(8,128)S(1)}, f32[4,128,128]{2,1,0:T(8,128)S(1)}) custom-call(s32[1,4]{1,0:T(1,128)} %pos_hbm.1, s32[3,1,1,4,16]{4,3,2,1,0:T(4,128)} %index_hbm.1, s32[1,1,4]{2,1,0:T(1,128)} %count_hbm.1, f32[1,128]{1,0:T(1,128)} %bitcast.1, ...), custom_call_target="tpu_custom_call" | custom-call | tf_op jit(solution)/shard_map/frame/pallas_call | solution.py:356
  5.7 0.5 %collective-permute-start.1 = (f32[4,136,128]{2,1,0:T(8,128)S(1)}, f32[4,136,128]{2,1,0:T(8,128)S(1)}, u32[]{:S(2)}, u32[]{:S(2)}) collective-permute-start(f32[4,136,128]{2,1,0:T(8,128)S(1)} %get-tuple-element.22), channel_id=1, source_target_pairs={{0,1},{1,0},{2,3},{3,2},{4,5},{5,4},{6,7},{7,6},{8,9},{9,8},{10,11... | collective-permute-start | bytes 835592 | tf_op jit(solution)/shard_map/ppermute | solution.py:376
  6.3 1.2 %collective-permute-done.1 = f32[4,136,128]{2,1,0:T(8,128)S(1)} collective-permute-done((f32[4,136,128]{2,1,0:T(8,128)S(1)}, f32[4,136,128]{2,1,0:T(8,128)S(1)}, u32[]{:S(2)}, u32[]{:S(2)}) %collective-permute-start.1) | collective-permute-done | bytes 278560 | tf_op jit(solution)/shard_map/ppermute | solution.py:376
  7.5 0.7 %add.7 = f32[4,136,128]{2,1,0:T(8,128)} add(f32[4,136,128]{2,1,0:T(8,128)S(1)} %get-tuple-element.21, f32[4,136,128]{2,1,0:T(8,128)S(1)} %collective-permute-done.1) | non-fusion elementwise | flops 69632 | bytes 835584 | tf_op jit(solution)/shard_map/add | solution.py:376
  8.2 6.2 %all-to-all-start.1 = ((f32[4,136,128]{2,1,0:T(8,128)}), f32[4,136,128]{2,1,0:T(8,128)S(1)}, u32[]{:S(2)}, u32[]{:S(2)}) async-start(f32[4,136,128]{2,1,0:T(8,128)} %add.7), calls=%async_computation.1 | async-start | bytes 557056 | tf_op jit(solution)/shard_map/all_to_all | solution.py:386
  14.4 0.0 collective-permute-start
  14.4 1.5 %collective-permute-done = f32[4,128,128]{2,1,0:T(8,128)S(1)} collective-permute-done((f32[4,128,128]{2,1,0:T(8,128)S(1)}, f32[4,128,128]{2,1,0:T(8,128)S(1)}, u32[]{:S(2)}, u32[]{:S(2)}) %collective-permute-start) | collective-permute-done | bytes 262176 | tf_op jit(solution)/shard_map/ppermute | solution.py:376
  16.0 0.7 %add.6 = f32[4,128,128]{2,1,0:T(8,128)} add(f32[4,128,128]{2,1,0:T(8,128)S(1)} %get-tuple-element.19, f32[4,128,128]{2,1,0:T(8,128)S(1)} %collective-permute-done) | non-fusion elementwise | flops 65536 | bytes 786432 | tf_op jit(solution)/shard_map/add | solution.py:376
  16.7 7.3 %all-to-all-done.1.refs_0_ = f32[4,136,128]{2,1,0:T(8,128)S(1)} async-done(((f32[4,136,128]{2,1,0:T(8,128)}), f32[4,136,128]{2,1,0:T(8,128)S(1)}, u32[]{:S(2)}, u32[]{:S(2)}) %all-to-all-start.1) | async-done | bytes 278560 | tf_op jit(solution)/shard_map/all_to_all | solution.py:386
  24.0 3.4 %all-to-all-start = ((f32[4,128,128]{2,1,0:T(8,128)}), f32[4,128,128]{2,1,0:T(8,128)S(1)}, u32[]{:S(2)}, u32[]{:S(2)}) async-start(f32[4,128,128]{2,1,0:T(8,128)} %add.6), calls=%async_computation | async-start | bytes 524288 | tf_op jit(solution)/shard_map/all_to_all | solution.py:386
  27.4 0.3 place.2
  27.7 1.6 %collective-permute-start.2 = (f32[128,128]{1,0:T(8,128)S(1)}, f32[128,128]{1,0:T(8,128)S(1)}, u32[]{:S(2)}, u32[]{:S(2)}) collective-permute-start(f32[128,128]{1,0:T(8,128)S(1)} %get-tuple-element.26), channel_id=1, source_target_pairs={{0,2},{1,3},{2,0},{3,1},{4,6},{5,7},{6,4},{7,5},{8,10},{9,11},{10,... | collective-permute-start | bytes 196616 | tf_op jit(solution)/shard_map/ppermute | solution.py:403
  29.3 0.0 collective-permute-start.3
  29.3 5.0 %all-to-all-done.refs_0_ = f32[4,128,128]{2,1,0:T(8,128)S(1)} async-done(((f32[4,128,128]{2,1,0:T(8,128)}), f32[4,128,128]{2,1,0:T(8,128)S(1)}, u32[]{:S(2)}, u32[]{:S(2)}) %all-to-all-start) | async-done | bytes 262176 | tf_op jit(solution)/shard_map/all_to_all | solution.py:386
  34.3 0.0 collective-permute-done.2.refs_4_
  34.3 0.0 collective-permute-done.3.refs_5_
  34.3 0.3 place.3
  34.6 0.1 collective-permute-start.4
  34.7 1.6 %collective-permute-start.5 = (f32[128,128]{1,0:T(8,128)S(1)}, f32[128,128]{1,0:T(8,128)S(1)}, u32[]{:S(2)}, u32[]{:S(2)}) collective-permute-start(f32[128,128]{1,0:T(8,128)S(1)} %get-tuple-element.31), channel_id=1, source_target_pairs={{0,2},{1,3},{2,0},{3,1},{4,6},{5,7},{6,4},{7,5},{8,10},{9,11},{10,... | collective-permute-start | bytes 196616 | tf_op jit(solution)/shard_map/ppermute | solution.py:403
  36.2 0.3 collective-permute-start.6
  36.5 2.6 %collective-permute-done.5.refs_2_ = f32[128,128]{1,0:T(8,128)S(1)} collective-permute-done((f32[128,128]{1,0:T(8,128)S(1)}, f32[128,128]{1,0:T(8,128)S(1)}, u32[]{:S(2)}, u32[]{:S(2)}) %collective-permute-start.5) | collective-permute-done | bytes 65568 | tf_op jit(solution)/shard_map/ppermute | solution.py:403
  39.2 1.1 %collective-permute-done.6.refs_3_ = f32[128,128]{1,0:T(8,128)S(1)} collective-permute-done((f32[128,128]{1,0:T(8,128)S(1)}, f32[128,128]{1,0:T(8,128)S(1)}, u32[]{:S(2)}, u32[]{:S(2)}) %collective-permute-start.6) | collective-permute-done | bytes 65568 | tf_op jit(solution)/shard_map/ppermute | solution.py:403
  40.3 0.0 collective-permute-done.4.refs_1_
  40.3 0.7 %total.1 = f32[16,2,16,128]{3,2,1,0:T(8,128)} custom-call(f32[2,128,128]{2,1,0:T(8,128)S(1)} %get-tuple-element.28.done_ref, f32[128,128]{1,0:T(8,128)S(1)} %get-tuple-element.29.refs_0_, f32[256,128]{1,0:T(8,128)S(1)} %collective-permute-done.4.refs_1_, f32[128,128]{1,0:T(8,128)S(1)} %collective-permute-done.5.refs_2_, ...), custom_call_target="tpu_custom_call" | custom-call | tf_op jit(solution)/shard_map/total/pallas_call | solution.py:405
Async XLA Ops:
  5.7 1.7 %collective-permute-start.1 = (f32[4,136,128]{2,1,0:T(8,128)S(1)}, f32[4,136,128]{2,1,0:T(8,128)S(1)}, u32[]{:S(2)}, u32[]{:S(2)}) collective-permute-start(f32[4,136,128]{2,1,0:T(8,128)S(1)} %get-tuple-element.22), channel_id=1, source_target_pairs={{0,1},{1,0},{2,3},{3,2},{4,5},{5,4},{6,7},{7,6},{8,9},{9,8},{10,11... | collective-permute-start | bytes 835592 | tf_op jit(solution)/shard_map/ppermute | solution.py:376
  8.2 15.8 %all-to-all-start.1 = ((f32[4,136,128]{2,1,0:T(8,128)}), f32[4,136,128]{2,1,0:T(8,128)S(1)}, u32[]{:S(2)}, u32[]{:S(2)}) async-start(f32[4,136,128]{2,1,0:T(8,128)} %add.7), calls=%async_computation.1 | async-start | bytes 557056 | tf_op jit(solution)/shard_map/all_to_all | solution.py:386
  14.4 1.5 %collective-permute-start = (f32[4,128,128]{2,1,0:T(8,128)S(1)}, f32[4,128,128]{2,1,0:T(8,128)S(1)}, u32[]{:S(2)}, u32[]{:S(2)}) collective-permute-start(f32[4,128,128]{2,1,0:T(8,128)S(1)} %get-tuple-element.20), channel_id=1, source_target_pairs={{0,1},{1,0},{2,3},{3,2},{4,5},{5,4},{6,7},{7,6},{8,9},{9,8},{10,11... | collective-permute-start | bytes 786440 | tf_op jit(solution)/shard_map/ppermute | solution.py:376
  24.0 10.3 %all-to-all-start = ((f32[4,128,128]{2,1,0:T(8,128)}), f32[4,128,128]{2,1,0:T(8,128)S(1)}, u32[]{:S(2)}, u32[]{:S(2)}) async-start(f32[4,128,128]{2,1,0:T(8,128)} %add.6), calls=%async_computation | async-start | bytes 524288 | tf_op jit(solution)/shard_map/all_to_all | solution.py:386
  27.7 6.6 %collective-permute-start.2 = (f32[128,128]{1,0:T(8,128)S(1)}, f32[128,128]{1,0:T(8,128)S(1)}, u32[]{:S(2)}, u32[]{:S(2)}) collective-permute-start(f32[128,128]{1,0:T(8,128)S(1)} %get-tuple-element.26), channel_id=1, source_target_pairs={{0,2},{1,3},{2,0},{3,1},{4,6},{5,7},{6,4},{7,5},{8,10},{9,11},{10,... | collective-permute-start | bytes 196616 | tf_op jit(solution)/shard_map/ppermute | solution.py:403
  29.3 5.0 %collective-permute-start.3 = (f32[128,128]{1,0:T(8,128)S(1)}, f32[128,128]{1,0:T(8,128)S(1)}, u32[]{:S(2)}, u32[]{:S(2)}) collective-permute-start(f32[128,128]{1,0:T(8,128)S(1)} %get-tuple-element.27), channel_id=1, source_target_pairs={{0,3},{1,2},{2,1},{3,0},{4,7},{5,6},{6,5},{7,4},{8,11},{9,10},{10,... | collective-permute-start | bytes 196616 | tf_op jit(solution)/shard_map/ppermute | solution.py:403
  34.6 5.7 %collective-permute-start.4 = (f32[256,128]{1,0:T(8,128)S(1)}, f32[256,128]{1,0:T(8,128)S(1)}, u32[]{:S(2)}, u32[]{:S(2)}) collective-permute-start(f32[256,128]{1,0:T(8,128)S(1)} %get-tuple-element.30), channel_id=1, source_target_pairs={{0,1},{1,0},{2,3},{3,2},{4,5},{5,4},{6,7},{7,6},{8,9},{9,8},{10,11... | collective-permute-start | bytes 393224 | tf_op jit(solution)/shard_map/ppermute | solution.py:403
  34.7 4.5 %collective-permute-start.5 = (f32[128,128]{1,0:T(8,128)S(1)}, f32[128,128]{1,0:T(8,128)S(1)}, u32[]{:S(2)}, u32[]{:S(2)}) collective-permute-start(f32[128,128]{1,0:T(8,128)S(1)} %get-tuple-element.31), channel_id=1, source_target_pairs={{0,2},{1,3},{2,0},{3,1},{4,6},{5,7},{6,4},{7,5},{8,10},{9,11},{10,... | collective-permute-start | bytes 196616 | tf_op jit(solution)/shard_map/ppermute | solution.py:403
  36.2 4.0 %collective-permute-start.6 = (f32[128,128]{1,0:T(8,128)S(1)}, f32[128,128]{1,0:T(8,128)S(1)}, u32[]{:S(2)}, u32[]{:S(2)}) collective-permute-start(f32[128,128]{1,0:T(8,128)S(1)} %get-tuple-element.32), channel_id=1, source_target_pairs={{0,3},{1,2},{2,1},{3,0},{4,7},{5,6},{6,5},{7,4},{8,11},{9,10},{10,... | collective-permute-start | bytes 196616 | tf_op jit(solution)/shard_map/ppermute | solution.py:403

commit v6 on v4

--- a/solution.py
+++ b/solution.py
@@ -24,8 +24,9 @@
 
 def slab_steps(peers):
     if peers <= REACH + 1:
-        return (0,) + tuple(sorted(range(1, peers), key=lambda k: (k < peers // 2, k)))
-    return (0,) + tuple(s for k in range(1, REACH + 1) for s in (k, peers - k))
+        return tuple(sorted(range(peers), key=lambda k: (k == 0, k < peers // 2, k)))
+    ring = [s for k in range(REACH, 0, -1) for s in (peers - k, k)]
+    return (*ring, 0)
 
 
 def partner(slab, step, peers):
@@ -77,9 +78,8 @@
     col_hbm,
     *rest,
 ):
-    mine = rest[: CHUNKS * len(shifts)]
-    other = rest[CHUNKS * len(shifts) :][:CHUNKS]
-    scratch = rest[CHUNKS * (len(shifts) + 1) :]
+    far, steps = len(shifts) - 2, len(shifts)
+    mine, other, scratch = rest[: 2 * steps], rest[2 * steps : 2 * steps + 2], rest[2 * steps + 2 :]
     pos_ref, index_ref, count_ref = scratch[0:3]
     phase_ref, table_ref, obj_ref, probe_ref, cot_ref, row_ref, col_ref = scratch[3:10]
     sems, band, window, col_bf, row_scr = scratch[10:]
@@ -236,6 +236,20 @@
     mark_down = lax.broadcasted_iota(jnp.int32, (half, capacity * half), 0)
     mark_along = lax.broadcasted_iota(jnp.int32, (half, capacity * half), 1)
     mark_slot = jnp.where(lax.rem(mark_along, half) == mark_down, lax.div(mark_along, half), -1)
+    lines = capacity * half
+    late = (steps - far) * (lines + half)
+
+    def put(k, h, slot, value):
+        at = slot * half
+        if h:
+            swap, base = other[1], late + k * lines
+        elif k < far:
+            swap, base = other[0], k * (lines + half)
+        else:
+            swap, base = other[1], (k - far) * (lines + half)
+        mine[h * steps + k][at : at + half] = value[:, :block_cols]
+        swap[base + at : base + at + half] = value[:, block_cols:]
+
     for k, shift in enumerate(shifts):
         dest = partner(me, shift, peers)
         live = count_ref[0, 0, dest]
@@ -268,24 +282,27 @@
                         )
                     )
             result = dot(jnp.concatenate(picks, 0), jnp.concatenate(inner, 0))
-            for h in range(CHUNKS):
-                for slot in range(first, first + batch):
+            for slot in range(first, first + batch):
+                for h in range(CHUNKS):
                     top = (slot - first) * block_rows + h * half
-                    place = slice(slot * half, (slot + 1) * half)
-                    mine[h * len(shifts) + k][place] = result[top : top + half, :block_cols]
-                    begin = k * mine[h * len(shifts)].shape[0] + slot * half
-                    other[h][begin : begin + half] = result[top : top + half, block_cols:]
-        tail = capacity * half
-        mine[k][tail : tail + half] = marks.astype(f32)
-        begin = k * mine[0].shape[0] + tail
-        other[0][begin : begin + half] = jnp.zeros(marks.shape, f32)
+                    put(k, h, slot, result[top : top + half])
+        marks = marks.astype(f32)
+        put(k, 0, capacity, jnp.concatenate([marks, jnp.zeros_like(marks)], 1))
+
+
+def join_kernel(base, first_ref, got_ref, *refs):
+    count = len(refs) // 2
+    for part, out in zip(refs[:count], refs[count:]):
+        tall = part.shape[0]
+        out[...] = part[...] + got_ref[base : base + tall]
+        base += tall
 
 
 def place_kernel(sources, owners, first, *refs):
     tilt, core = lax.axis_index("tilt"), lax.axis_index("rep")
     tilts, cores = lax.axis_size("tilt"), lax.axis_size("rep")
     each = VB_DEV // (tilts * cores)
-    blocks = refs[sources - 1 :: -1]
+    blocks = refs[:sources]
     half, lanes = CHUNK_ROWS, blocks[0].shape[-1]
     size = each * half
     if first:
@@ -297,9 +314,7 @@
         before, outs, done = rest[: len(owners)], rest[len(owners) : -1], rest[-1]
         for dr in range(cores):
             parts = [ref[...] for ref, (dt, r) in zip(before, owners) if r == dr]
-            if dr:
-                outs[dr][:size] = parts.pop(0)
-            done[dr] = functools.reduce(jnp.add, parts, jnp.zeros((size, lanes), jnp.float32))
+            done[dr] = functools.reduce(jnp.add, parts)
     data = jnp.concatenate([block[:lanes].astype(jnp.bfloat16) for block in blocks], 0)
     volume = lax.broadcasted_iota(jnp.int32, (each, half, lanes), 0).astype(jnp.float32)
     for out, (dt, dr) in zip(outs, owners):
@@ -310,25 +325,17 @@
             mark = mark_ref[k] - base
             hit = jnp.where(volume == mark[None], 1.0, 0.0)
             hot.append(hit.reshape(size, lanes).astype(jnp.bfloat16))
-        begin = out.shape[0] - size
-        out[begin : begin + size] = dot(jnp.concatenate(hot, 1), data)
+        out[...] = dot(jnp.concatenate(hot, 1), data)
 
 
 def sum_kernel(owners, done_ref, *refs):
     parts, out_ref = refs[:-1], refs[-1]
     core, cores = lax.axis_index("rep"), lax.axis_size("rep")
     each, cols = out_ref.shape[0], out_ref.shape[-1]
-    size = each * CHUNK_ROWS
     for dr in range(cores):
         at = lax.rem(core + dr, cores)
-        early, late = done_ref[dr], None
-        for ref, (dt, r) in zip(parts, owners):
-            if r == dr:
-                if dr and not dt:
-                    early = early + ref[:size]
-                value = ref[ref.shape[0] - size :]
-                late = value if late is None else late + value
-        for h, value in enumerate([early, late]):
+        late = functools.reduce(jnp.add, [ref[...] for ref, (_, r) in zip(parts, owners) if r == dr])
+        for h, value in enumerate([done_ref[dr], late]):
             rows = pl.ds(h * CHUNK_ROWS, CHUNK_ROWS)
             out_ref[:, at, rows] = value.reshape(each, CHUNK_ROWS, cols)
 
@@ -360,9 +367,11 @@
     phase_line = phases.reshape(1, -1)
     table = jnp.asarray(angle_table(size))
     frames = (slices * (rows // block_rows) * (cols // block_cols), block_rows, block_cols)
-    marked = jax.ShapeDtypeStruct((lanes + CHUNK_ROWS, block_cols), f32)
-    plain = jax.ShapeDtypeStruct((lanes, block_cols), f32)
-    shapes = [marked] * sources + [plain] * (sources * (CHUNKS - 1))
+    far = sources - 2
+    tall = lanes + CHUNK_ROWS
+    heights = [tall] * sources + [lanes] * sources
+    swapped = [far * tall, (sources - far) * tall + sources * lanes]
+    shapes = [jax.ShapeDtypeStruct((tall, block_cols), f32) for tall in heights + swapped]
     fetched = [
         (phase_line, VMEM),
         (table, VMEM),
@@ -373,15 +382,11 @@
         (col_interp, VMEM),
     ]
     scalars = [positions, pair_index, pair_counts]
-    wholes = [
-        jax.ShapeDtypeStruct((sources * shapes[h * sources].shape[0], block_cols), f32)
-        for h in range(CHUNKS)
-    ]
     held = pl.pallas_call(
         functools.partial(frame_kernel, shifts),
-        out_shape=shapes + wholes,
+        out_shape=shapes,
         in_specs=[hbm] * 10,
-        out_specs=[vmem] * (len(shapes) + CHUNKS),
+        out_specs=[vmem] * len(shapes),
         scratch_shapes=[SMEM(x.shape, x.dtype) for x in scalars]
         + [space(x.shape, x.dtype) for x, space in fetched]
         + [
@@ -396,41 +401,51 @@
     )(*[pltpu.with_memory_space_constraint(x, pltpu.HBM) for x in scalars + [x for x, _ in fetched]])
 
     swap = [(r, (r + 1) % cores) for r in range(cores)]
-    mine, other = held[: len(shapes)], held[len(shapes) :]
-    sent = []
-    for h in range(CHUNKS):
-        got = lax.ppermute(other[h], "rep", swap)
-        for k in range(sources):
-            part = mine[h * sources + k]
-            tall = part.shape[0]
-            sent.append(part + got[k * tall : (k + 1) * tall])
-
-    owners = [(dt, dr) for dt in range(tilts) for dr in range(cores)]
+    owners = sorted(
+        ((dt, dr) for dt in range(tilts) for dr in range(cores)), key=lambda o: (o[0] == 0, o)
+    )
     each = VB_DEV // len(owners)
     share = jax.ShapeDtypeStruct((each * CHUNK_ROWS, block_cols), f32)
     mark = jax.ShapeDtypeStruct((sources, CHUNK_ROWS, block_cols), f32)
-    double = jax.ShapeDtypeStruct((2 * each * CHUNK_ROWS, block_cols), f32)
     done = jax.ShapeDtypeStruct((cores, each * CHUNK_ROWS, block_cols), f32)
+    mine, other = held[: len(heights)], held[len(heights) :]
+    got = [lax.ppermute(half, "rep", swap) for half in other]
+
+    def send(block, step):
+        ring = [(p, partner(p, step, peers)) for p in range(peers)]
+        return lax.ppermute(block, "slab", ring)
+
+    first = []
+    for k in range(sources):
+        h, at = (0, k * tall) if k < far else (1, (k - far) * tall)
+        block = mine[k] + got[h][at : at + tall]
+        first.append(send(block, shifts[k]) if shifts[k] else block)
+    joined = []
+    for k in range(far):
+        part = slice(k, k + 1) if k + 1 < far else slice(k, sources)
+        late = mine[sources:][part]
+        joined += pl.pallas_call(
+            functools.partial(join_kernel, (sources - far) * tall + k * lanes),
+            out_shape=shapes[sources : 2 * sources][part],
+            in_specs=[vmem] * (len(late) + 2),
+            out_specs=[vmem] * len(late),
+            compiler_params=limit,
+            name="join",
+        )(first[k], got[1], *late)
+    second = [send(block, k) if k else block for block, k in zip(joined, shifts)]
+
     extra = []
-    for h in range(CHUNKS):
-        blocks = [None] * sources
-        for k in reversed(range(sources)):
-            block = sent[h * sources + k]
-            if shifts[k]:
-                ring = [(p, partner(p, shifts[k], peers)) for p in range(peers)]
-                block = lax.ppermute(block, "slab", ring)
-            blocks[k] = block
+    for h, blocks in enumerate([first, second]):
         *parts, more = pl.pallas_call(
             functools.partial(place_kernel, sources, owners, h == 0),
-            out_shape=[double if h and dr and not dt else share for dt, dr in owners]
-            + [done if h else mark],
+            out_shape=[share] * len(owners) + [done if h else mark],
             in_specs=[vmem] * (sources + len(extra)),
             out_specs=[vmem] * (len(owners) + 1),
             compiler_params=limit,
             name="place",
-        )(*blocks[::-1], *extra)
+        )(*blocks, *extra)
         for i, (dt, dr) in enumerate(owners):
-            if dt or (dr and h):
+            if dt or dr:
                 route = [
                     (t * cores + r, (t + dt) % tilts * cores + (r + dr) % cores)
                     for t in range(tilts)

time: 33.2 us -> 33 us (level)
  the two profiles are of different devices: /device:TPU:17 before, /device:TPU:0 now
where the time goes in v6:
time: 33 us; the launch traced here: 32.9 us
  starting transfers between devices  15.1 us (46%)
  waiting for transfers between devices  10.6 us (32%)
  Pallas kernels  7.09 us (21%)
    ppermute x6, starting transfers between devices, send(): return lax.ppermute(block, 'slab', ring)  10.1 us
    pallas_call x1, Pallas kernels, on_device(): pl.pallas_call(functools.partial(frame_kernel, shifts), out_shape=shapes,...  5.72 us
    ppermute x6, waiting for transfers between devices, send(): return lax.ppermute(block, 'slab', ring)  5.14 us
    ppermute x6, starting transfers between devices, on_device(): parts[i] = lax.ppermute(parts[i], ('tilt', 'rep'), route)  4.41 us
    ppermute x6, waiting for transfers between devices, on_device(): parts[i] = lax.ppermute(parts[i], ('tilt', 'rep'), route)  3.99 us
    ppermute x2, waiting for transfers between devices, on_device(): got = [lax.ppermute(half, 'rep', swap) for half in other]  1.48 us
    pallas_call x1, Pallas kernels, on_device(): pl.pallas_call(functools.partial(sum_kernel, owners), out_shape=jax.Shape...  0.73 us
  transfers between devices with their start and end apart: 14, of which 8 were waited for; matrix products, arithmetic and copies ran while one was open for 0% of the time, Pallas kernels for 1%

profile of v6, /device:TPU:0, one launch (start us, length us, event | category | flops | bytes accessed | tf_op | source)
XLA Modules:
  0.0 32.9 jit_solution(1237089909695697727)
XLA Ops:
  0.0 5.7 %frame.1 = (f32[136,128]{1,0:T(8,128)S(1)}, f32[136,128]{1,0:T(8,128)S(1)}, f32[136,128]{1,0:T(8,128)S(1)}, f32[136,128]{1,0:T(8,128)S(1)}, f32[128,128]{1,0:T(8...) custom-call(s32[1,4]{1,0:T(1,128)} %pos_hbm.1, ...), custom_call_target="tpu_custom_call" | custom-call | tf_op jit(solution)/shard_map/frame/pallas_call | solution.py:385
  5.7 0.5 %collective-permute-start.2 = (f32[784,128]{1,0:T(8,128)S(1)}, f32[784,128]{1,0:T(8,128)S(1)}, u32[]{:S(2)}, u32[]{:S(2)}) collective-permute-start(f32[784,128]{1,0:T(8,128)S(1)} %get-tuple-element.30), channel_id=1, source_target_pairs={{0,1},{1,0},{2,3},{3,2},{4,5},{5,4},{6,7},{7,6},{8,9},{9,8},{10,11... | collective-permute-start | bytes 1204232 | tf_op jit(solution)/shard_map/ppermute | solution.py:412
  6.3 0.1 collective-permute-start
  6.3 1.5 %collective-permute-done = f32[272,128]{1,0:T(8,128)S(1)} collective-permute-done((f32[272,128]{1,0:T(8,128)S(1)}, f32[272,128]{1,0:T(8,128)S(1)}, u32[]{:S(2)}, u32[]{:S(2)}) %collective-permute-start) | collective-permute-done | bytes 139296 | tf_op jit(solution)/shard_map/ppermute | solution.py:412
  7.8 5.0 %collective-permute-start.4 = (f32[136,128]{1,0:T(8,128)S(1)}, f32[136,128]{1,0:T(8,128)S(1)}, u32[]{:S(2)}, u32[]{:S(2)}) collective-permute-start(f32[136,128]{1,0:T(8,128)S(1)} %get-tuple-element.53), channel_id=1, source_target_pairs={{0,12},{4,8},{8,4},{12,0},{1,13},{5,9},{9,5},{13,1},{2,14},{6,10},... | collective-permute-start | bytes 208904 | tf_op jit(solution)/shard_map/ppermute | solution.py:416
  12.9 0.0 collective-permute-start.1
  12.9 0.7 %collective-permute-start.7 = (f32[136,128]{1,0:T(8,128)S(1)}, f32[136,128]{1,0:T(8,128)S(1)}, u32[]{:S(2)}, u32[]{:S(2)}) collective-permute-start(f32[136,128]{1,0:T(8,128)S(1)} %get-tuple-element.52), channel_id=1, source_target_pairs={{0,4},{4,0},{8,12},{12,8},{1,5},{5,1},{9,13},{13,9},{2,6},{6,2},{1... | collective-permute-start | bytes 208904 | tf_op jit(solution)/shard_map/ppermute | solution.py:416
  13.6 2.1 %collective-permute-done.4.first_ref.refs_1_ = f32[136,128]{1,0:T(8,128)S(1)} collective-permute-done((f32[136,128]{1,0:T(8,128)S(1)}, f32[136,128]{1,0:T(8,128)S(1)}, u32[]{:S(2)}, u32[]{:S(2)}) %collective-permute-start.4) | collective-permute-done | bytes 69664 | tf_op jit(solution)/shard_map/ppermute | solution.py:416
  15.7 4.1 %collective-permute-start.5 = (f32[128,128]{1,0:T(8,128)S(1)}, f32[128,128]{1,0:T(8,128)S(1)}, u32[]{:S(2)}, u32[]{:S(2)}) collective-permute-start(f32[128,128]{1,0:T(8,128)S(1)} %get-tuple-element.36), channel_id=1, source_target_pairs={{0,12},{4,8},{8,4},{12,0},{1,13},{5,9},{9,5},{13,1},{2,14},{6,10},... | collective-permute-start | bytes 196616 | tf_op jit(solution)/shard_map/ppermute | solution.py:416
  19.9 0.5 %collective-permute-done.1.first_ref.refs_0_ = f32[136,128]{1,0:T(8,128)S(1)} collective-permute-done((f32[136,128]{1,0:T(8,128)S(1)}, f32[136,128]{1,0:T(8,128)S(1)}, u32[]{:S(2)}, u32[]{:S(2)}) %collective-permute-start.1) | collective-permute-done | bytes 69664 | tf_op jit(solution)/shard_map/ppermute | solution.py:416
  20.4 0.2 collective-permute-start.3
  20.6 0.3 place.2
  20.9 1.6 %collective-permute-start.8 = (f32[128,128]{1,0:T(8,128)S(1)}, f32[128,128]{1,0:T(8,128)S(1)}, u32[]{:S(2)}, u32[]{:S(2)}) collective-permute-start(f32[128,128]{1,0:T(8,128)S(1)} %get-tuple-element.42), channel_id=1, source_target_pairs={{0,2},{1,3},{2,0},{3,1},{4,6},{5,7},{6,4},{7,5},{8,10},{9,11},{10,... | collective-permute-start | bytes 196616 | tf_op jit(solution)/shard_map/ppermute | solution.py:454
  22.4 0.7 %collective-permute-start.10 = (f32[128,128]{1,0:T(8,128)S(1)}, f32[128,128]{1,0:T(8,128)S(1)}, u32[]{:S(2)}, u32[]{:S(2)}) collective-permute-start(f32[128,128]{1,0:T(8,128)S(1)} %get-tuple-element.45), channel_id=1, source_target_pairs={{0,1},{1,0},{2,3},{3,2},{4,5},{5,4},{6,7},{7,6},{8,9},{9,8},{10,11... | collective-permute-start | bytes 196616 | tf_op jit(solution)/shard_map/ppermute | solution.py:454
  23.1 1.4 %collective-permute-done.6.refs_2_ = f32[128,128]{1,0:T(8,128)S(1)} collective-permute-done((f32[128,128]{1,0:T(8,128)S(1)}, f32[128,128]{1,0:T(8,128)S(1)}, u32[]{:S(2)}, u32[]{:S(2)}) %collective-permute-start.6) | collective-permute-done | bytes 65568 | tf_op jit(solution)/shard_map/ppermute | solution.py:416
  24.5 1.1 %collective-permute-done.3.refs_0_ = f32[128,128]{1,0:T(8,128)S(1)} collective-permute-done((f32[128,128]{1,0:T(8,128)S(1)}, f32[128,128]{1,0:T(8,128)S(1)}, u32[]{:S(2)}, u32[]{:S(2)}) %collective-permute-start.3) | collective-permute-done | bytes 65568 | tf_op jit(solution)/shard_map/ppermute | solution.py:416
  25.6 1.0 %collective-permute-done.9.refs_6_ = f32[128,128]{1,0:T(8,128)S(1)} collective-permute-done((f32[128,128]{1,0:T(8,128)S(1)}, f32[128,128]{1,0:T(8,128)S(1)}, u32[]{:S(2)}, u32[]{:S(2)}) %collective-permute-start.9) | collective-permute-done | bytes 65568 | tf_op jit(solution)/shard_map/ppermute | solution.py:454
  26.6 0.3 place.3
  26.9 0.8 %collective-permute-start.11 = (f32[128,128]{1,0:T(8,128)S(1)}, f32[128,128]{1,0:T(8,128)S(1)}, u32[]{:S(2)}, u32[]{:S(2)}) collective-permute-start(f32[128,128]{1,0:T(8,128)S(1)} %get-tuple-element.47), channel_id=1, source_target_pairs={{0,2},{1,3},{2,0},{3,1},{4,6},{5,7},{6,4},{7,5},{8,10},{9,11},{10,... | collective-permute-start | bytes 196616 | tf_op jit(solution)/shard_map/ppermute | solution.py:454
  27.7 0.5 %collective-permute-start.12 = (f32[128,128]{1,0:T(8,128)S(1)}, f32[128,128]{1,0:T(8,128)S(1)}, u32[]{:S(2)}, u32[]{:S(2)}) collective-permute-start(f32[128,128]{1,0:T(8,128)S(1)} %get-tuple-element.48), channel_id=1, source_target_pairs={{0,3},{1,2},{2,1},{3,0},{4,7},{5,6},{6,5},{7,4},{8,11},{9,10},{10,... | collective-permute-start | bytes 196616 | tf_op jit(solution)/shard_map/ppermute | solution.py:454
  28.3 0.9 %collective-permute-start.13 = (f32[128,128]{1,0:T(8,128)S(1)}, f32[128,128]{1,0:T(8,128)S(1)}, u32[]{:S(2)}, u32[]{:S(2)}) collective-permute-start(f32[128,128]{1,0:T(8,128)S(1)} %get-tuple-element.50), channel_id=1, source_target_pairs={{0,1},{1,0},{2,3},{3,2},{4,5},{5,4},{6,7},{7,6},{8,9},{9,8},{10,11... | collective-permute-start | bytes 196616 | tf_op jit(solution)/shard_map/ppermute | solution.py:454
  29.1 2.6 %collective-permute-done.11.refs_0_ = f32[128,128]{1,0:T(8,128)S(1)} collective-permute-done((f32[128,128]{1,0:T(8,128)S(1)}, f32[128,128]{1,0:T(8,128)S(1)}, u32[]{:S(2)}, u32[]{:S(2)}) %collective-permute-start.11) | collective-permute-done | bytes 65568 | tf_op jit(solution)/shard_map/ppermute | solution.py:454
  31.8 0.4 %collective-permute-done.12.refs_1_ = f32[128,128]{1,0:T(8,128)S(1)} collective-permute-done((f32[128,128]{1,0:T(8,128)S(1)}, f32[128,128]{1,0:T(8,128)S(1)}, u32[]{:S(2)}, u32[]{:S(2)}) %collective-permute-start.12) | collective-permute-done | bytes 65568 | tf_op jit(solution)/shard_map/ppermute | solution.py:454
  32.1 0.7 %total.1 = f32[16,2,16,128]{3,2,1,0:T(8,128)} custom-call(f32[2,128,128]{2,1,0:T(8,128)S(1)} %get-tuple-element.46.done_ref, f32[128,128]{1,0:T(8,128)S(1)} %collective-permute-done.11.refs_0_, f32[128,128]{1,0:T(8,128)S(1)} %collective-permute-done.12.refs_1_, f32[128,128]{1,0:T(8,128)S(1)} %get-tuple-element.49.refs_2_, ...), custom_call_target="tpu_custom_call" | custom-call | tf_op jit(solution)/shard_map/total/pallas_call | solution.py:456
  (12 shorter events, 0.1 us)
Async XLA Ops:
  5.7 7.2 %collective-permute-start.2 = (f32[784,128]{1,0:T(8,128)S(1)}, f32[784,128]{1,0:T(8,128)S(1)}, u32[]{:S(2)}, u32[]{:S(2)}) collective-permute-start(f32[784,128]{1,0:T(8,128)S(1)} %get-tuple-element.30), channel_id=1, source_target_pairs={{0,1},{1,0},{2,3},{3,2},{4,5},{5,4},{6,7},{7,6},{8,9},{9,8},{10,11... | collective-permute-start | bytes 1204232 | tf_op jit(solution)/shard_map/ppermute | solution.py:412
  6.3 1.6 %collective-permute-start = (f32[272,128]{1,0:T(8,128)S(1)}, f32[272,128]{1,0:T(8,128)S(1)}, u32[]{:S(2)}, u32[]{:S(2)}) collective-permute-start(f32[272,128]{1,0:T(8,128)S(1)} %get-tuple-element.29), channel_id=1, source_target_pairs={{0,1},{1,0},{2,3},{3,2},{4,5},{5,4},{6,7},{7,6},{8,9},{9,8},{10,11... | collective-permute-start | bytes 417800 | tf_op jit(solution)/shard_map/ppermute | solution.py:412
  7.8 7.9 %collective-permute-start.4 = (f32[136,128]{1,0:T(8,128)S(1)}, f32[136,128]{1,0:T(8,128)S(1)}, u32[]{:S(2)}, u32[]{:S(2)}) collective-permute-start(f32[136,128]{1,0:T(8,128)S(1)} %get-tuple-element.53), channel_id=1, source_target_pairs={{0,12},{4,8},{8,4},{12,0},{1,13},{5,9},{9,5},{13,1},{2,14},{6,10},... | collective-permute-start | bytes 208904 | tf_op jit(solution)/shard_map/ppermute | solution.py:416
  12.9 7.5 %collective-permute-start.1 = (f32[136,128]{1,0:T(8,128)S(1)}, f32[136,128]{1,0:T(8,128)S(1)}, u32[]{:S(2)}, u32[]{:S(2)}) collective-permute-start(f32[136,128]{1,0:T(8,128)S(1)} %get-tuple-element.54), channel_id=1, source_target_pairs={{0,8},{4,12},{8,0},{12,4},{1,9},{5,13},{9,1},{13,5},{2,10},{6,14},... | collective-permute-start | bytes 208904 | tf_op jit(solution)/shard_map/ppermute | solution.py:416
  12.9 7.7 %collective-permute-start.7 = (f32[136,128]{1,0:T(8,128)S(1)}, f32[136,128]{1,0:T(8,128)S(1)}, u32[]{:S(2)}, u32[]{:S(2)}) collective-permute-start(f32[136,128]{1,0:T(8,128)S(1)} %get-tuple-element.52), channel_id=1, source_target_pairs={{0,4},{4,0},{8,12},{12,8},{1,5},{5,1},{9,13},{13,9},{2,6},{6,2},{1... | collective-permute-start | bytes 208904 | tf_op jit(solution)/shard_map/ppermute | solution.py:416
  15.7 6.7 %collective-permute-start.5 = (f32[128,128]{1,0:T(8,128)S(1)}, f32[128,128]{1,0:T(8,128)S(1)}, u32[]{:S(2)}, u32[]{:S(2)}) collective-permute-start(f32[128,128]{1,0:T(8,128)S(1)} %get-tuple-element.36), channel_id=1, source_target_pairs={{0,12},{4,8},{8,4},{12,0},{1,13},{5,9},{9,5},{13,1},{2,14},{6,10},... | collective-permute-start | bytes 196616 | tf_op jit(solution)/shard_map/ppermute | solution.py:416
  19.9 4.6 %collective-permute-start.6 = (f32[128,128]{1,0:T(8,128)S(1)}, f32[128,128]{1,0:T(8,128)S(1)}, u32[]{:S(2)}, u32[]{:S(2)}) collective-permute-start(f32[128,128]{1,0:T(8,128)S(1)} %get-tuple-element.37), channel_id=1, source_target_pairs={{0,4},{4,0},{8,12},{12,8},{1,5},{5,1},{9,13},{13,9},{2,6},{6,2},{1... | collective-permute-start | bytes 196616 | tf_op jit(solution)/shard_map/ppermute | solution.py:416
  20.4 5.2 %collective-permute-start.3 = (f32[128,128]{1,0:T(8,128)S(1)}, f32[128,128]{1,0:T(8,128)S(1)}, u32[]{:S(2)}, u32[]{:S(2)}) collective-permute-start(f32[128,128]{1,0:T(8,128)S(1)} %join.2), channel_id=1, source_target_pairs={{0,8},{4,12},{8,0},{12,4},{1,9},{5,13},{9,1},{13,5},{2,10},{6,14},... | collective-permute-start | bytes 196616 | tf_op jit(solution)/shard_map/ppermute | solution.py:416
  20.9 4.8 %collective-permute-start.8 = (f32[128,128]{1,0:T(8,128)S(1)}, f32[128,128]{1,0:T(8,128)S(1)}, u32[]{:S(2)}, u32[]{:S(2)}) collective-permute-start(f32[128,128]{1,0:T(8,128)S(1)} %get-tuple-element.42), channel_id=1, source_target_pairs={{0,2},{1,3},{2,0},{3,1},{4,6},{5,7},{6,4},{7,5},{8,10},{9,11},{10,... | collective-permute-start | bytes 196616 | tf_op jit(solution)/shard_map/ppermute | solution.py:454
  22.4 4.2 %collective-permute-start.9 = (f32[128,128]{1,0:T(8,128)S(1)}, f32[128,128]{1,0:T(8,128)S(1)}, u32[]{:S(2)}, u32[]{:S(2)}) collective-permute-start(f32[128,128]{1,0:T(8,128)S(1)} %get-tuple-element.43), channel_id=1, source_target_pairs={{0,3},{1,2},{2,1},{3,0},{4,7},{5,6},{6,5},{7,4},{8,11},{9,10},{10,... | collective-permute-start | bytes 196616 | tf_op jit(solution)/shard_map/ppermute | solution.py:454
  22.4 4.2 %collective-permute-start.10 = (f32[128,128]{1,0:T(8,128)S(1)}, f32[128,128]{1,0:T(8,128)S(1)}, u32[]{:S(2)}, u32[]{:S(2)}) collective-permute-start(f32[128,128]{1,0:T(8,128)S(1)} %get-tuple-element.45), channel_id=1, source_target_pairs={{0,1},{1,0},{2,3},{3,2},{4,5},{5,4},{6,7},{7,6},{8,9},{9,8},{10,11... | collective-permute-start | bytes 196616 | tf_op jit(solution)/shard_map/ppermute | solution.py:454
  26.9 4.9 %collective-permute-start.11 = (f32[128,128]{1,0:T(8,128)S(1)}, f32[128,128]{1,0:T(8,128)S(1)}, u32[]{:S(2)}, u32[]{:S(2)}) collective-permute-start(f32[128,128]{1,0:T(8,128)S(1)} %get-tuple-element.47), channel_id=1, source_target_pairs={{0,2},{1,3},{2,0},{3,1},{4,6},{5,7},{6,4},{7,5},{8,10},{9,11},{10,... | collective-permute-start | bytes 196616 | tf_op jit(solution)/shard_map/ppermute | solution.py:454
  27.7 4.4 %collective-permute-start.12 = (f32[128,128]{1,0:T(8,128)S(1)}, f32[128,128]{1,0:T(8,128)S(1)}, u32[]{:S(2)}, u32[]{:S(2)}) collective-permute-start(f32[128,128]{1,0:T(8,128)S(1)} %get-tuple-element.48), channel_id=1, source_target_pairs={{0,3},{1,2},{2,1},{3,0},{4,7},{5,6},{6,5},{7,4},{8,11},{9,10},{10,... | collective-permute-start | bytes 196616 | tf_op jit(solution)/shard_map/ppermute | solution.py:454
  28.3 3.9 %collective-permute-start.13 = (f32[128,128]{1,0:T(8,128)S(1)}, f32[128,128]{1,0:T(8,128)S(1)}, u32[]{:S(2)}, u32[]{:S(2)}) collective-permute-start(f32[128,128]{1,0:T(8,128)S(1)} %get-tuple-element.50), channel_id=1, source_target_pairs={{0,1},{1,0},{2,3},{3,2},{4,5},{5,4},{6,7},{7,6},{8,9},{9,8},{10,11... | collective-permute-start | bytes 196616 | tf_op jit(solution)/shard_map/ppermute | solution.py:454

commit v7 on v6

--- a/solution.py
+++ b/solution.py
@@ -312,8 +312,11 @@
     else:
         mark_ref, rest = refs[sources], refs[sources + 1 :]
         before, outs, done = rest[: len(owners)], rest[len(owners) : -1], rest[-1]
+        for ref, out, (dt, dr) in zip(before, outs, owners):
+            if dr and not dt:
+                out[:size] = ref[...]
         for dr in range(cores):
-            parts = [ref[...] for ref, (dt, r) in zip(before, owners) if r == dr]
+            parts = [ref[...] for ref, (dt, r) in zip(before, owners) if r == dr and (dt or not r)]
             done[dr] = functools.reduce(jnp.add, parts)
     data = jnp.concatenate([block[:lanes].astype(jnp.bfloat16) for block in blocks], 0)
     volume = lax.broadcasted_iota(jnp.int32, (each, half, lanes), 0).astype(jnp.float32)
@@ -325,17 +328,25 @@
             mark = mark_ref[k] - base
             hit = jnp.where(volume == mark[None], 1.0, 0.0)
             hot.append(hit.reshape(size, lanes).astype(jnp.bfloat16))
-        out[...] = dot(jnp.concatenate(hot, 1), data)
+        begin = out.shape[0] - size
+        out[begin : begin + size] = dot(jnp.concatenate(hot, 1), data)
 
 
 def sum_kernel(owners, done_ref, *refs):
     parts, out_ref = refs[:-1], refs[-1]
     core, cores = lax.axis_index("rep"), lax.axis_size("rep")
     each, cols = out_ref.shape[0], out_ref.shape[-1]
+    size = each * CHUNK_ROWS
     for dr in range(cores):
         at = lax.rem(core + dr, cores)
-        late = functools.reduce(jnp.add, [ref[...] for ref, (_, r) in zip(parts, owners) if r == dr])
-        for h, value in enumerate([done_ref[dr], late]):
+        early, late = done_ref[dr], None
+        for ref, (dt, r) in zip(parts, owners):
+            if r == dr:
+                if dr and not dt:
+                    early = early + ref[:size]
+                value = ref[ref.shape[0] - size :]
+                late = value if late is None else late + value
+        for h, value in enumerate([early, late]):
             rows = pl.ds(h * CHUNK_ROWS, CHUNK_ROWS)
             out_ref[:, at, rows] = value.reshape(each, CHUNK_ROWS, cols)
 
@@ -407,6 +418,7 @@
     each = VB_DEV // len(owners)
     share = jax.ShapeDtypeStruct((each * CHUNK_ROWS, block_cols), f32)
     mark = jax.ShapeDtypeStruct((sources, CHUNK_ROWS, block_cols), f32)
+    double = jax.ShapeDtypeStruct((2 * each * CHUNK_ROWS, block_cols), f32)
     done = jax.ShapeDtypeStruct((cores, each * CHUNK_ROWS, block_cols), f32)
     mine, other = held[: len(heights)], held[len(heights) :]
     got = [lax.ppermute(half, "rep", swap) for half in other]
@@ -420,39 +432,48 @@
         h, at = (0, k * tall) if k < far else (1, (k - far) * tall)
         block = mine[k] + got[h][at : at + tall]
         first.append(send(block, shifts[k]) if shifts[k] else block)
-    joined = []
-    for k in range(far):
-        part = slice(k, k + 1) if k + 1 < far else slice(k, sources)
+    def join(after, part):
         late = mine[sources:][part]
-        joined += pl.pallas_call(
-            functools.partial(join_kernel, (sources - far) * tall + k * lanes),
+        return pl.pallas_call(
+            functools.partial(join_kernel, (sources - far) * tall + part.start * lanes),
             out_shape=shapes[sources : 2 * sources][part],
             in_specs=[vmem] * (len(late) + 2),
             out_specs=[vmem] * len(late),
             compiler_params=limit,
             name="join",
-        )(first[k], got[1], *late)
-    second = [send(block, k) if k else block for block, k in zip(joined, shifts)]
-
-    extra = []
-    for h, blocks in enumerate([first, second]):
-        *parts, more = pl.pallas_call(
+        )(after, got[1], *late)
+
+    def place(blocks, extra, h):
+        return pl.pallas_call(
             functools.partial(place_kernel, sources, owners, h == 0),
-            out_shape=[share] * len(owners) + [done if h else mark],
+            out_shape=[double if h and dr and not dt else share for dt, dr in owners]
+            + [done if h else mark],
             in_specs=[vmem] * (sources + len(extra)),
             out_specs=[vmem] * (len(owners) + 1),
             compiler_params=limit,
             name="place",
         )(*blocks, *extra)
-        for i, (dt, dr) in enumerate(owners):
-            if dt or dr:
+
+    def share_out(parts, h):
+        sent = []
+        for part, (dt, dr) in zip(parts, owners):
+            if dt or (dr and h):
                 route = [
                     (t * cores + r, (t + dt) % tilts * cores + (r + dr) % cores)
                     for t in range(tilts)
                     for r in range(cores)
                 ]
-                parts[i] = lax.ppermute(parts[i], ("tilt", "rep"), route)
-        extra = [more, *parts]
+                part = lax.ppermute(part, ("tilt", "rep"), route)
+            sent.append(part)
+        return sent
+
+    joined = [block for k in range(far) for block in join(first[k], slice(k, k + 1))]
+    *parts, marks = place(first, [], 0)
+    parts = share_out(parts, 0)
+    joined += join(marks, slice(far, sources))
+    second = [send(block, k) if k else block for block, k in zip(joined, shifts)]
+    *late_parts, sums = place(second, [marks, *parts], 1)
+    extra = [sums, *share_out(late_parts, 1)]
     return pl.pallas_call(
         functools.partial(sum_kernel, owners),
         out_shape=jax.ShapeDtypeStruct((each, cores, block_rows, block_cols), f32),

time: 33 us -> 35.1 us (1.064)
  waiting for transfers between devices: 10.6 us -> 14.3 us
  starting transfers between devices: 15.1 us -> 13.5 us
    ppermute x6, waiting for transfers between devices: 5.14 us -> 8.19 us  [send(): return lax.ppermute(block, 'slab', ring)]
    ppermute x6 -> x5, starting transfers between devices: 4.41 us -> 3.48 us  [share_out(): part = lax.ppermute(part, ('tilt', 'rep'), route)]
    ppermute x6, starting transfers between devices: 10.1 us -> 9.42 us  [send(): return lax.ppermute(block, 'slab', ring)]
    ppermute x6 -> x5, waiting for transfers between devices: 3.99 us -> 4.62 us  [share_out(): part = lax.ppermute(part, ('tilt', 'rep'), route)]
  transfers between devices with their start and end apart: 14 -> 13, of which waited for: 8 -> 7; matrix products, arithmetic and copies ran while one was open for 0% -> 0% of each run, Pallas kernels for 1% -> 1%
where the time goes in v7:
time: 35.1 us; the launch traced here: 35 us
  waiting for transfers between devices  14.3 us (41%)
  starting transfers between devices  13.5 us (38%)
  Pallas kernels  7.09 us (20%)
    ppermute x6, starting transfers between devices, send(): return lax.ppermute(block, 'slab', ring)  9.42 us
    ppermute x6, waiting for transfers between devices, send(): return lax.ppermute(block, 'slab', ring)  8.19 us
    pallas_call x1, Pallas kernels, on_device(): pl.pallas_call(functools.partial(frame_kernel, shifts), out_shape=shapes,...  5.72 us
    ppermute x5, waiting for transfers between devices, share_out(): part = lax.ppermute(part, ('tilt', 'rep'), route)  4.62 us
    ppermute x5, starting transfers between devices, share_out(): part = lax.ppermute(part, ('tilt', 'rep'), route)  3.48 us
    ppermute x2, waiting for transfers between devices, on_device(): got = [lax.ppermute(half, 'rep', swap) for half in other]  1.48 us
    pallas_call x1, Pallas kernels, on_device(): pl.pallas_call(functools.partial(sum_kernel, owners), out_shape=jax.Shape...  0.73 us
  transfers between devices with their start and end apart: 13, of which 7 were waited for; matrix products, arithmetic and copies ran while one was open for 0% of the time, Pallas kernels for 1%

profile of v7, /device:TPU:0, one launch (start us, length us, event | category | flops | bytes accessed | tf_op | source)
XLA Modules:
  0.0 35.0 jit_solution(1786041406580310592)
XLA Ops:
  0.0 5.7 %frame.1 = (f32[136,128]{1,0:T(8,128)S(1)}, f32[136,128]{1,0:T(8,128)S(1)}, f32[136,128]{1,0:T(8,128)S(1)}, f32[136,128]{1,0:T(8,128)S(1)}, f32[128,128]{1,0:T(8...) custom-call(s32[1,4]{1,0:T(1,128)} %pos_hbm.1, ...), custom_call_target="tpu_custom_call" | custom-call | tf_op jit(solution)/shard_map/frame/pallas_call | solution.py:396
  5.7 0.5 %collective-permute-start.2 = (f32[784,128]{1,0:T(8,128)S(1)}, f32[784,128]{1,0:T(8,128)S(1)}, u32[]{:S(2)}, u32[]{:S(2)}) collective-permute-start(f32[784,128]{1,0:T(8,128)S(1)} %get-tuple-element.29), channel_id=1, source_target_pairs={{0,1},{1,0},{2,3},{3,2},{4,5},{5,4},{6,7},{7,6},{8,9},{9,8},{10,11... | collective-permute-start | bytes 1204232 | tf_op jit(solution)/shard_map/ppermute | solution.py:424
  6.3 0.1 collective-permute-start
  6.3 1.5 %collective-permute-done = f32[272,128]{1,0:T(8,128)S(1)} collective-permute-done((f32[272,128]{1,0:T(8,128)S(1)}, f32[272,128]{1,0:T(8,128)S(1)}, u32[]{:S(2)}, u32[]{:S(2)}) %collective-permute-start) | collective-permute-done | bytes 139296 | tf_op jit(solution)/shard_map/ppermute | solution.py:424
  7.8 5.0 %collective-permute-start.4 = (f32[136,128]{1,0:T(8,128)S(1)}, f32[136,128]{1,0:T(8,128)S(1)}, u32[]{:S(2)}, u32[]{:S(2)}) collective-permute-start(f32[136,128]{1,0:T(8,128)S(1)} %get-tuple-element.51), channel_id=1, source_target_pairs={{0,12},{4,8},{8,4},{12,0},{1,13},{5,9},{9,5},{13,1},{2,14},{6,10},... | collective-permute-start | bytes 208904 | tf_op jit(solution)/shard_map/ppermute | solution.py:428
  12.9 0.0 collective-permute-start.1
  12.9 0.7 %collective-permute-start.6 = (f32[136,128]{1,0:T(8,128)S(1)}, f32[136,128]{1,0:T(8,128)S(1)}, u32[]{:S(2)}, u32[]{:S(2)}) collective-permute-start(f32[136,128]{1,0:T(8,128)S(1)} %get-tuple-element.50), channel_id=1, source_target_pairs={{0,4},{4,0},{8,12},{12,8},{1,5},{5,1},{9,13},{13,9},{2,6},{6,2},{1... | collective-permute-start | bytes 208904 | tf_op jit(solution)/shard_map/ppermute | solution.py:428
  13.6 5.5 %collective-permute-done.1.first_ref.refs_0_ = f32[136,128]{1,0:T(8,128)S(1)} collective-permute-done((f32[136,128]{1,0:T(8,128)S(1)}, f32[136,128]{1,0:T(8,128)S(1)}, u32[]{:S(2)}, u32[]{:S(2)}) %collective-permute-start.1) | collective-permute-done | bytes 69664 | tf_op jit(solution)/shard_map/ppermute | solution.py:428
  19.1 1.3 %collective-permute-start.3 = (f32[128,128]{1,0:T(8,128)S(1)}, f32[128,128]{1,0:T(8,128)S(1)}, u32[]{:S(2)}, u32[]{:S(2)}) collective-permute-start(f32[128,128]{1,0:T(8,128)S(1)} %join.3), channel_id=1, source_target_pairs={{0,8},{4,12},{8,0},{12,4},{1,9},{5,13},{9,1},{13,5},{2,10},{6,14},... | collective-permute-start | bytes 196616 | tf_op jit(solution)/shard_map/ppermute | solution.py:428
  20.4 1.4 %collective-permute-start.5 = (f32[128,128]{1,0:T(8,128)S(1)}, f32[128,128]{1,0:T(8,128)S(1)}, u32[]{:S(2)}, u32[]{:S(2)}) collective-permute-start(f32[128,128]{1,0:T(8,128)S(1)} %join.4), channel_id=1, source_target_pairs={{0,12},{4,8},{8,4},{12,0},{1,13},{5,9},{9,5},{13,1},{2,14},{6,10},... | collective-permute-start | bytes 196616 | tf_op jit(solution)/shard_map/ppermute | solution.py:428
  21.7 0.0 collective-permute-done.6.refs_2_
  21.7 0.3 place.2
  22.0 1.5 %collective-permute-start.8 = (f32[128,128]{1,0:T(8,128)S(1)}, f32[128,128]{1,0:T(8,128)S(1)}, u32[]{:S(2)}, u32[]{:S(2)}) collective-permute-start(f32[128,128]{1,0:T(8,128)S(1)} %get-tuple-element.40), channel_id=1, source_target_pairs={{0,2},{1,3},{2,0},{3,1},{4,6},{5,7},{6,4},{7,5},{8,10},{9,11},{10,... | collective-permute-start | bytes 196616 | tf_op jit(solution)/shard_map/ppermute | solution.py:466
  23.6 1.0 %collective-permute-start.7 = (f32[128,128]{1,0:T(8,128)S(1)}, f32[128,128]{1,0:T(8,128)S(1)}, u32[]{:S(2)}, u32[]{:S(2)}) collective-permute-start(f32[128,128]{1,0:T(8,128)S(1)} %get-tuple-element.38), channel_id=1, source_target_pairs={{0,4},{4,0},{8,12},{12,8},{1,5},{5,1},{9,13},{13,9},{2,6},{6,2},{1... | collective-permute-start | bytes 196616 | tf_op jit(solution)/shard_map/ppermute | solution.py:428
  24.7 2.2 %collective-permute-done.3.refs_0_ = f32[128,128]{1,0:T(8,128)S(1)} collective-permute-done((f32[128,128]{1,0:T(8,128)S(1)}, f32[128,128]{1,0:T(8,128)S(1)}, u32[]{:S(2)}, u32[]{:S(2)}) %collective-permute-start.3) | collective-permute-done | bytes 65568 | tf_op jit(solution)/shard_map/ppermute | solution.py:428
  26.8 1.0 %collective-permute-done.9.refs_6_ = f32[128,128]{1,0:T(8,128)S(1)} collective-permute-done((f32[128,128]{1,0:T(8,128)S(1)}, f32[128,128]{1,0:T(8,128)S(1)}, u32[]{:S(2)}, u32[]{:S(2)}) %collective-permute-start.9) | collective-permute-done | bytes 65568 | tf_op jit(solution)/shard_map/ppermute | solution.py:466
  27.8 0.6 %collective-permute-done.7.refs_2_ = f32[128,128]{1,0:T(8,128)S(1)} collective-permute-done((f32[128,128]{1,0:T(8,128)S(1)}, f32[128,128]{1,0:T(8,128)S(1)}, u32[]{:S(2)}, u32[]{:S(2)}) %collective-permute-start.7) | collective-permute-done | bytes 65568 | tf_op jit(solution)/shard_map/ppermute | solution.py:428
  28.3 0.3 place.3
  28.7 0.1 collective-permute-start.12
  28.7 1.2 %collective-permute-start.10 = (f32[128,128]{1,0:T(8,128)S(1)}, f32[128,128]{1,0:T(8,128)S(1)}, u32[]{:S(2)}, u32[]{:S(2)}) collective-permute-start(f32[128,128]{1,0:T(8,128)S(1)} %get-tuple-element.45), channel_id=1, source_target_pairs={{0,2},{1,3},{2,0},{3,1},{4,6},{5,7},{6,4},{7,5},{8,10},{9,11},{10,... | collective-permute-start | bytes 196616 | tf_op jit(solution)/shard_map/ppermute | solution.py:466
  29.9 0.7 %collective-permute-start.11 = (f32[128,128]{1,0:T(8,128)S(1)}, f32[128,128]{1,0:T(8,128)S(1)}, u32[]{:S(2)}, u32[]{:S(2)}) collective-permute-start(f32[128,128]{1,0:T(8,128)S(1)} %get-tuple-element.46), channel_id=1, source_target_pairs={{0,3},{1,2},{2,1},{3,0},{4,7},{5,6},{6,5},{7,4},{8,11},{9,10},{10,... | collective-permute-start | bytes 196616 | tf_op jit(solution)/shard_map/ppermute | solution.py:466
  30.6 3.0 %collective-permute-done.10.refs_0_ = f32[128,128]{1,0:T(8,128)S(1)} collective-permute-done((f32[128,128]{1,0:T(8,128)S(1)}, f32[128,128]{1,0:T(8,128)S(1)}, u32[]{:S(2)}, u32[]{:S(2)}) %collective-permute-start.10) | collective-permute-done | bytes 65568 | tf_op jit(solution)/shard_map/ppermute | solution.py:466
  33.6 0.6 %collective-permute-done.11.refs_1_ = f32[128,128]{1,0:T(8,128)S(1)} collective-permute-done((f32[128,128]{1,0:T(8,128)S(1)}, f32[128,128]{1,0:T(8,128)S(1)}, u32[]{:S(2)}, u32[]{:S(2)}) %collective-permute-start.11) | collective-permute-done | bytes 65568 | tf_op jit(solution)/shard_map/ppermute | solution.py:466
  34.3 0.7 %total.1 = f32[16,2,16,128]{3,2,1,0:T(8,128)} custom-call(f32[2,128,128]{2,1,0:T(8,128)S(1)} %get-tuple-element.44.done_ref, f32[128,128]{1,0:T(8,128)S(1)} %collective-permute-done.10.refs_0_, f32[128,128]{1,0:T(8,128)S(1)} %collective-permute-done.11.refs_1_, f32[128,128]{1,0:T(8,128)S(1)} %get-tuple-element.47.refs_2_, ...), custom_call_target="tpu_custom_call" | custom-call | tf_op jit(solution)/shard_map/total/pallas_call | solution.py:477
  (11 shorter events, 0.1 us)
Async XLA Ops:
  5.7 7.2 %collective-permute-start.2 = (f32[784,128]{1,0:T(8,128)S(1)}, f32[784,128]{1,0:T(8,128)S(1)}, u32[]{:S(2)}, u32[]{:S(2)}) collective-permute-start(f32[784,128]{1,0:T(8,128)S(1)} %get-tuple-element.29), channel_id=1, source_target_pairs={{0,1},{1,0},{2,3},{3,2},{4,5},{5,4},{6,7},{7,6},{8,9},{9,8},{10,11... | collective-permute-start | bytes 1204232 | tf_op jit(solution)/shard_map/ppermute | solution.py:424
  6.3 1.6 %collective-permute-start = (f32[272,128]{1,0:T(8,128)S(1)}, f32[272,128]{1,0:T(8,128)S(1)}, u32[]{:S(2)}, u32[]{:S(2)}) collective-permute-start(f32[272,128]{1,0:T(8,128)S(1)} %get-tuple-element.28), channel_id=1, source_target_pairs={{0,1},{1,0},{2,3},{3,2},{4,5},{5,4},{6,7},{7,6},{8,9},{9,8},{10,11... | collective-permute-start | bytes 417800 | tf_op jit(solution)/shard_map/ppermute | solution.py:424
  7.8 12.5 %collective-permute-start.4 = (f32[136,128]{1,0:T(8,128)S(1)}, f32[136,128]{1,0:T(8,128)S(1)}, u32[]{:S(2)}, u32[]{:S(2)}) collective-permute-start(f32[136,128]{1,0:T(8,128)S(1)} %get-tuple-element.51), channel_id=1, source_target_pairs={{0,12},{4,8},{8,4},{12,0},{1,13},{5,9},{9,5},{13,1},{2,14},{6,10},... | collective-permute-start | bytes 208904 | tf_op jit(solution)/shard_map/ppermute | solution.py:428
  12.9 6.2 %collective-permute-start.1 = (f32[136,128]{1,0:T(8,128)S(1)}, f32[136,128]{1,0:T(8,128)S(1)}, u32[]{:S(2)}, u32[]{:S(2)}) collective-permute-start(f32[136,128]{1,0:T(8,128)S(1)} %get-tuple-element.52), channel_id=1, source_target_pairs={{0,8},{4,12},{8,0},{12,4},{1,9},{5,13},{9,1},{13,5},{2,10},{6,14},... | collective-permute-start | bytes 208904 | tf_op jit(solution)/shard_map/ppermute | solution.py:428
  12.9 8.8 %collective-permute-start.6 = (f32[136,128]{1,0:T(8,128)S(1)}, f32[136,128]{1,0:T(8,128)S(1)}, u32[]{:S(2)}, u32[]{:S(2)}) collective-permute-start(f32[136,128]{1,0:T(8,128)S(1)} %get-tuple-element.50), channel_id=1, source_target_pairs={{0,4},{4,0},{8,12},{12,8},{1,5},{5,1},{9,13},{13,9},{2,6},{6,2},{1... | collective-permute-start | bytes 208904 | tf_op jit(solution)/shard_map/ppermute | solution.py:428
  19.1 7.7 %collective-permute-start.3 = (f32[128,128]{1,0:T(8,128)S(1)}, f32[128,128]{1,0:T(8,128)S(1)}, u32[]{:S(2)}, u32[]{:S(2)}) collective-permute-start(f32[128,128]{1,0:T(8,128)S(1)} %join.3), channel_id=1, source_target_pairs={{0,8},{4,12},{8,0},{12,4},{1,9},{5,13},{9,1},{13,5},{2,10},{6,14},... | collective-permute-start | bytes 196616 | tf_op jit(solution)/shard_map/ppermute | solution.py:428
  20.4 6.5 %collective-permute-start.5 = (f32[128,128]{1,0:T(8,128)S(1)}, f32[128,128]{1,0:T(8,128)S(1)}, u32[]{:S(2)}, u32[]{:S(2)}) collective-permute-start(f32[128,128]{1,0:T(8,128)S(1)} %join.4), channel_id=1, source_target_pairs={{0,12},{4,8},{8,4},{12,0},{1,13},{5,9},{9,5},{13,1},{2,14},{6,10},... | collective-permute-start | bytes 196616 | tf_op jit(solution)/shard_map/ppermute | solution.py:428
  22.0 4.8 %collective-permute-start.8 = (f32[128,128]{1,0:T(8,128)S(1)}, f32[128,128]{1,0:T(8,128)S(1)}, u32[]{:S(2)}, u32[]{:S(2)}) collective-permute-start(f32[128,128]{1,0:T(8,128)S(1)} %get-tuple-element.40), channel_id=1, source_target_pairs={{0,2},{1,3},{2,0},{3,1},{4,6},{5,7},{6,4},{7,5},{8,10},{9,11},{10,... | collective-permute-start | bytes 196616 | tf_op jit(solution)/shard_map/ppermute | solution.py:466
  23.6 4.2 %collective-permute-start.9 = (f32[128,128]{1,0:T(8,128)S(1)}, f32[128,128]{1,0:T(8,128)S(1)}, u32[]{:S(2)}, u32[]{:S(2)}) collective-permute-start(f32[128,128]{1,0:T(8,128)S(1)} %get-tuple-element.41), channel_id=1, source_target_pairs={{0,3},{1,2},{2,1},{3,0},{4,7},{5,6},{6,5},{7,4},{8,11},{9,10},{10,... | collective-permute-start | bytes 196616 | tf_op jit(solution)/shard_map/ppermute | solution.py:466
  23.6 4.7 %collective-permute-start.7 = (f32[128,128]{1,0:T(8,128)S(1)}, f32[128,128]{1,0:T(8,128)S(1)}, u32[]{:S(2)}, u32[]{:S(2)}) collective-permute-start(f32[128,128]{1,0:T(8,128)S(1)} %get-tuple-element.38), channel_id=1, source_target_pairs={{0,4},{4,0},{8,12},{12,8},{1,5},{5,1},{9,13},{13,9},{2,6},{6,2},{1... | collective-permute-start | bytes 196616 | tf_op jit(solution)/shard_map/ppermute | solution.py:428
  28.7 5.6 %collective-permute-start.12 = (f32[256,128]{1,0:T(8,128)S(1)}, f32[256,128]{1,0:T(8,128)S(1)}, u32[]{:S(2)}, u32[]{:S(2)}) collective-permute-start(f32[256,128]{1,0:T(8,128)S(1)} %get-tuple-element.48), channel_id=1, source_target_pairs={{0,1},{1,0},{2,3},{3,2},{4,5},{5,4},{6,7},{7,6},{8,9},{9,8},{10,11... | collective-permute-start | bytes 393224 | tf_op jit(solution)/shard_map/ppermute | solution.py:466
  28.7 4.9 %collective-permute-start.10 = (f32[128,128]{1,0:T(8,128)S(1)}, f32[128,128]{1,0:T(8,128)S(1)}, u32[]{:S(2)}, u32[]{:S(2)}) collective-permute-start(f32[128,128]{1,0:T(8,128)S(1)} %get-tuple-element.45), channel_id=1, source_target_pairs={{0,2},{1,3},{2,0},{3,1},{4,6},{5,7},{6,4},{7,5},{8,10},{9,11},{10,... | collective-permute-start | bytes 196616 | tf_op jit(solution)/shard_map/ppermute | solution.py:466
  29.9 4.3 %collective-permute-start.11 = (f32[128,128]{1,0:T(8,128)S(1)}, f32[128,128]{1,0:T(8,128)S(1)}, u32[]{:S(2)}, u32[]{:S(2)}) collective-permute-start(f32[128,128]{1,0:T(8,128)S(1)} %get-tuple-element.46), channel_id=1, source_target_pairs={{0,3},{1,2},{2,1},{3,0},{4,7},{5,6},{6,5},{7,4},{8,11},{9,10},{10,... | collective-permute-start | bytes 196616 | tf_op jit(solution)/shard_map/ppermute | solution.py:466

commit v8 on v6

--- a/solution.py
+++ b/solution.py
@@ -310,11 +310,7 @@
         for k, block in enumerate(blocks):
             mark_ref[k] = block[lanes:]
     else:
-        mark_ref, rest = refs[sources], refs[sources + 1 :]
-        before, outs, done = rest[: len(owners)], rest[len(owners) : -1], rest[-1]
-        for dr in range(cores):
-            parts = [ref[...] for ref, (dt, r) in zip(before, owners) if r == dr]
-            done[dr] = functools.reduce(jnp.add, parts)
+        mark_ref, outs = refs[sources], refs[sources + cores :]
     data = jnp.concatenate([block[:lanes].astype(jnp.bfloat16) for block in blocks], 0)
     volume = lax.broadcasted_iota(jnp.int32, (each, half, lanes), 0).astype(jnp.float32)
     for out, (dt, dr) in zip(outs, owners):
@@ -325,19 +321,22 @@
             mark = mark_ref[k] - base
             hit = jnp.where(volume == mark[None], 1.0, 0.0)
             hot.append(hit.reshape(size, lanes).astype(jnp.bfloat16))
-        out[...] = dot(jnp.concatenate(hot, 1), data)
-
-
-def sum_kernel(owners, done_ref, *refs):
-    parts, out_ref = refs[:-1], refs[-1]
+        out[:size] = dot(jnp.concatenate(hot, 1), data)
+        if out.shape[0] > size:
+            out[size:] = jnp.zeros((out.shape[0] - size, out.shape[1]), jnp.float32)
+
+
+def sum_kernel(owners, *refs):
+    out_ref = refs[-1]
     core, cores = lax.axis_index("rep"), lax.axis_size("rep")
     each, cols = out_ref.shape[0], out_ref.shape[-1]
-    for dr in range(cores):
-        at = lax.rem(core + dr, cores)
-        late = functools.reduce(jnp.add, [ref[...] for ref, (_, r) in zip(parts, owners) if r == dr])
-        for h, value in enumerate([done_ref[dr], late]):
-            rows = pl.ds(h * CHUNK_ROWS, CHUNK_ROWS)
-            out_ref[:, at, rows] = value.reshape(each, CHUNK_ROWS, cols)
+    size = each * CHUNK_ROWS
+    for h in range(CHUNKS):
+        parts = refs[h * len(owners) : (h + 1) * len(owners)]
+        for dr in range(cores):
+            values = [ref[:size] for ref, (_, r) in zip(parts, owners) if r == dr]
+            total = functools.reduce(jnp.add, values).reshape(each, CHUNK_ROWS, cols)
+            out_ref[:, lax.rem(core + dr, cores), pl.ds(h * CHUNK_ROWS, CHUNK_ROWS)] = total
 
 
 def on_device(
@@ -407,7 +406,7 @@
     each = VB_DEV // len(owners)
     share = jax.ShapeDtypeStruct((each * CHUNK_ROWS, block_cols), f32)
     mark = jax.ShapeDtypeStruct((sources, CHUNK_ROWS, block_cols), f32)
-    done = jax.ShapeDtypeStruct((cores, each * CHUNK_ROWS, block_cols), f32)
+    padded = jax.ShapeDtypeStruct(((each + 1) * CHUNK_ROWS, block_cols), f32)
     mine, other = held[: len(heights)], held[len(heights) :]
     got = [lax.ppermute(half, "rep", swap) for half in other]
 
@@ -420,39 +419,50 @@
         h, at = (0, k * tall) if k < far else (1, (k - far) * tall)
         block = mine[k] + got[h][at : at + tall]
         first.append(send(block, shifts[k]) if shifts[k] else block)
-    joined = []
-    for k in range(far):
-        part = slice(k, k + 1) if k + 1 < far else slice(k, sources)
+    def join(after, part):
         late = mine[sources:][part]
-        joined += pl.pallas_call(
-            functools.partial(join_kernel, (sources - far) * tall + k * lanes),
+        return pl.pallas_call(
+            functools.partial(join_kernel, (sources - far) * tall + part.start * lanes),
             out_shape=shapes[sources : 2 * sources][part],
             in_specs=[vmem] * (len(late) + 2),
             out_specs=[vmem] * len(late),
             compiler_params=limit,
             name="join",
-        )(first[k], got[1], *late)
-    second = [send(block, k) if k else block for block, k in zip(joined, shifts)]
-
-    extra = []
-    for h, blocks in enumerate([first, second]):
-        *parts, more = pl.pallas_call(
+        )(after, got[1], *late)
+
+    def place(blocks, extra, h):
+        shapes = [padded if dt else share for dt, dr in owners] + [mark]
+        if h:
+            shapes = [share] * len(owners)
+        return pl.pallas_call(
             functools.partial(place_kernel, sources, owners, h == 0),
-            out_shape=[share] * len(owners) + [done if h else mark],
+            out_shape=shapes,
             in_specs=[vmem] * (sources + len(extra)),
-            out_specs=[vmem] * (len(owners) + 1),
+            out_specs=[vmem] * len(shapes),
             compiler_params=limit,
             name="place",
         )(*blocks, *extra)
-        for i, (dt, dr) in enumerate(owners):
-            if dt or dr:
-                route = [
-                    (t * cores + r, (t + dt) % tilts * cores + (r + dr) % cores)
-                    for t in range(tilts)
-                    for r in range(cores)
-                ]
-                parts[i] = lax.ppermute(parts[i], ("tilt", "rep"), route)
-        extra = [more, *parts]
+
+    def share_out(part, owner):
+        dt, dr = owner
+        if not (dt or dr):
+            return part
+        route = [
+            (t * cores + r, (t + dt) % tilts * cores + (r + dr) % cores)
+            for t in range(tilts)
+            for r in range(cores)
+        ]
+        return lax.ppermute(part, ("tilt", "rep"), route)
+
+    joined = []
+    for k in range(far):
+        joined += join(first[k], slice(k, k + 1 if k + 1 < far else sources))
+    second = [send(block, k) if k else block for block, k in zip(joined, shifts)]
+    *parts, marks = place(first, [], 0)
+    extra = [share_out(part, owner) for part, owner in zip(parts, owners)]
+    held = [part for part, (dt, dr) in zip(extra, owners) if dr and not dt]
+    late = place(second, [marks, *held], 1)
+    extra += [share_out(part, owner) for part, owner in zip(late, owners)]
     return pl.pallas_call(
         functools.partial(sum_kernel, owners),
         out_shape=jax.ShapeDtypeStruct((each, cores, block_rows, block_cols), f32),

time: 33 us -> 32.6 us (0.988)
    ppermute x6, waiting for transfers between devices: 3.99 us -> 3.53 us  [share_out(): return lax.ppermute(part, ('tilt', 'rep'), route)]
  transfers between devices with their start and end apart: 14 -> 14, of which waited for: 8 -> 7; matrix products, arithmetic and copies ran while one was open for 0% -> 0% of each run, Pallas kernels for 1% -> 2%
where the time goes in v8:
time: 32.6 us; the launch traced here: 32.4 us
  starting transfers between devices  14.8 us (45%)
  waiting for transfers between devices  10.4 us (32%)
  Pallas kernels  7.11 us (22%)
    ppermute x6, starting transfers between devices, send(): return lax.ppermute(block, 'slab', ring)  10.1 us
    pallas_call x1, Pallas kernels, on_device(): pl.pallas_call(functools.partial(frame_kernel, shifts), out_shape=shapes,...  5.72 us
    ppermute x6, waiting for transfers between devices, send(): return lax.ppermute(block, 'slab', ring)  5.4 us
    ppermute x6, starting transfers between devices, share_out(): return lax.ppermute(part, ('tilt', 'rep'), route)  4.14 us
    ppermute x6, waiting for transfers between devices, share_out(): return lax.ppermute(part, ('tilt', 'rep'), route)  3.53 us
    ppermute x2, waiting for transfers between devices, on_device(): got = [lax.ppermute(half, 'rep', swap) for half in other]  1.48 us
    pallas_call x1, Pallas kernels, on_device(): pl.pallas_call(functools.partial(sum_kernel, owners), out_shape=jax.Shape...  0.75 us
  transfers between devices with their start and end apart: 14, of which 7 were waited for; matrix products, arithmetic and copies ran while one was open for 0% of the time, Pallas kernels for 2%

profile of v8, /device:TPU:0, one launch (start us, length us, event | category | flops | bytes accessed | tf_op | source)
XLA Modules:
  0.0 32.4 jit_solution(4392499442513880668)
XLA Ops:
  0.0 5.7 %frame.1 = (f32[136,128]{1,0:T(8,128)S(1)}, f32[136,128]{1,0:T(8,128)S(1)}, f32[136,128]{1,0:T(8,128)S(1)}, f32[136,128]{1,0:T(8,128)S(1)}, f32[128,128]{1,0:T(8...) custom-call(s32[1,4]{1,0:T(1,128)} %pos_hbm.1, ...), custom_call_target="tpu_custom_call" | custom-call | tf_op jit(solution)/shard_map/frame/pallas_call | solution.py:384
  5.7 0.5 %collective-permute-start.3 = (f32[784,128]{1,0:T(8,128)S(1)}, f32[784,128]{1,0:T(8,128)S(1)}, u32[]{:S(2)}, u32[]{:S(2)}) collective-permute-start(f32[784,128]{1,0:T(8,128)S(1)} %get-tuple-element.31), channel_id=1, source_target_pairs={{0,1},{1,0},{2,3},{3,2},{4,5},{5,4},{6,7},{7,6},{8,9},{9,8},{10,11... | collective-permute-start | bytes 1204232 | tf_op jit(solution)/shard_map/ppermute | solution.py:411
  6.3 0.1 collective-permute-start
  6.3 1.5 %collective-permute-done = f32[272,128]{1,0:T(8,128)S(1)} collective-permute-done((f32[272,128]{1,0:T(8,128)S(1)}, f32[272,128]{1,0:T(8,128)S(1)}, u32[]{:S(2)}, u32[]{:S(2)}) %collective-permute-start) | collective-permute-done | bytes 139296 | tf_op jit(solution)/shard_map/ppermute | solution.py:411
  7.8 5.0 %collective-permute-start.2 = (f32[136,128]{1,0:T(8,128)S(1)}, f32[136,128]{1,0:T(8,128)S(1)}, u32[]{:S(2)}, u32[]{:S(2)}) collective-permute-start(f32[136,128]{1,0:T(8,128)S(1)} %get-tuple-element.51), channel_id=1, source_target_pairs={{0,12},{4,8},{8,4},{12,0},{1,13},{5,9},{9,5},{13,1},{2,14},{6,10},... | collective-permute-start | bytes 208904 | tf_op jit(solution)/shard_map/ppermute | solution.py:415
  12.9 0.0 collective-permute-start.1
  12.9 0.7 %collective-permute-start.4 = (f32[136,128]{1,0:T(8,128)S(1)}, f32[136,128]{1,0:T(8,128)S(1)}, u32[]{:S(2)}, u32[]{:S(2)}) collective-permute-start(f32[136,128]{1,0:T(8,128)S(1)} %get-tuple-element.50), channel_id=1, source_target_pairs={{0,4},{4,0},{8,12},{12,8},{1,5},{5,1},{9,13},{13,9},{2,6},{6,2},{1... | collective-permute-start | bytes 208904 | tf_op jit(solution)/shard_map/ppermute | solution.py:415
  13.6 2.1 %collective-permute-done.2.refs_1_.first_ref = f32[136,128]{1,0:T(8,128)S(1)} collective-permute-done((f32[136,128]{1,0:T(8,128)S(1)}, f32[136,128]{1,0:T(8,128)S(1)}, u32[]{:S(2)}, u32[]{:S(2)}) %collective-permute-start.2) | collective-permute-done | bytes 69664 | tf_op jit(solution)/shard_map/ppermute | solution.py:415
  15.7 4.1 %collective-permute-start.9 = (f32[128,128]{1,0:T(8,128)S(1)}, f32[128,128]{1,0:T(8,128)S(1)}, u32[]{:S(2)}, u32[]{:S(2)}) collective-permute-start(f32[128,128]{1,0:T(8,128)S(1)} %get-tuple-element.41), channel_id=1, source_target_pairs={{0,12},{4,8},{8,4},{12,0},{1,13},{5,9},{9,5},{13,1},{2,14},{6,10},... | collective-permute-start | bytes 196616 | tf_op jit(solution)/shard_map/ppermute | solution.py:415
  19.9 0.0 collective-permute-start.10
  19.9 0.5 %collective-permute-done.1.refs_0_.first_ref = f32[136,128]{1,0:T(8,128)S(1)} collective-permute-done((f32[136,128]{1,0:T(8,128)S(1)}, f32[136,128]{1,0:T(8,128)S(1)}, u32[]{:S(2)}, u32[]{:S(2)}) %collective-permute-start.1) | collective-permute-done | bytes 69664 | tf_op jit(solution)/shard_map/ppermute | solution.py:415
  20.4 0.2 collective-permute-start.8
  20.6 0.3 place.2
  20.9 0.1 collective-permute-start.7
  21.0 1.6 %collective-permute-start.5 = (f32[136,128]{1,0:T(8,128)S(1)}, f32[136,128]{1,0:T(8,128)S(1)}, u32[]{:S(2)}, u32[]{:S(2)}) collective-permute-start(f32[136,128]{1,0:T(8,128)S(1)} %get-tuple-element.33), channel_id=1, source_target_pairs={{0,2},{1,3},{2,0},{3,1},{4,6},{5,7},{6,4},{7,5},{8,10},{9,11},{10,... | collective-permute-start | bytes 208904 | tf_op jit(solution)/shard_map/ppermute | solution.py:455
  22.5 0.3 collective-permute-start.6
  22.8 1.7 %collective-permute-done.10.refs_2_ = f32[128,128]{1,0:T(8,128)S(1)} collective-permute-done((f32[128,128]{1,0:T(8,128)S(1)}, f32[128,128]{1,0:T(8,128)S(1)}, u32[]{:S(2)}, u32[]{:S(2)}) %collective-permute-start.10) | collective-permute-done | bytes 65568 | tf_op jit(solution)/shard_map/ppermute | solution.py:415
  24.5 1.1 %collective-permute-done.8.refs_0_ = f32[128,128]{1,0:T(8,128)S(1)} collective-permute-done((f32[128,128]{1,0:T(8,128)S(1)}, f32[128,128]{1,0:T(8,128)S(1)}, u32[]{:S(2)}, u32[]{:S(2)}) %collective-permute-start.8) | collective-permute-done | bytes 65568 | tf_op jit(solution)/shard_map/ppermute | solution.py:415
  25.6 0.3 place.3
  25.9 1.4 %collective-permute-start.11 = (f32[128,128]{1,0:T(8,128)S(1)}, f32[128,128]{1,0:T(8,128)S(1)}, u32[]{:S(2)}, u32[]{:S(2)}) collective-permute-start(f32[128,128]{1,0:T(8,128)S(1)} %get-tuple-element.45), channel_id=1, source_target_pairs={{0,2},{1,3},{2,0},{3,1},{4,6},{5,7},{6,4},{7,5},{8,10},{9,11},{10,... | collective-permute-start | bytes 196616 | tf_op jit(solution)/shard_map/ppermute | solution.py:455
  27.3 0.8 %collective-permute-start.13 = (f32[128,128]{1,0:T(8,128)S(1)}, f32[128,128]{1,0:T(8,128)S(1)}, u32[]{:S(2)}, u32[]{:S(2)}) collective-permute-start(f32[128,128]{1,0:T(8,128)S(1)} %get-tuple-element.48), channel_id=1, source_target_pairs={{0,1},{1,0},{2,3},{3,2},{4,5},{5,4},{6,7},{7,6},{8,9},{9,8},{10,11... | collective-permute-start | bytes 196616 | tf_op jit(solution)/shard_map/ppermute | solution.py:455
  28.1 2.1 %collective-permute-done.11.refs_4_ = f32[128,128]{1,0:T(8,128)S(1)} collective-permute-done((f32[128,128]{1,0:T(8,128)S(1)}, f32[128,128]{1,0:T(8,128)S(1)}, u32[]{:S(2)}, u32[]{:S(2)}) %collective-permute-start.11) | collective-permute-done | bytes 65568 | tf_op jit(solution)/shard_map/ppermute | solution.py:455
  30.3 1.4 %collective-permute-done.12.refs_5_ = f32[128,128]{1,0:T(8,128)S(1)} collective-permute-done((f32[128,128]{1,0:T(8,128)S(1)}, f32[128,128]{1,0:T(8,128)S(1)}, u32[]{:S(2)}, u32[]{:S(2)}) %collective-permute-start.12) | collective-permute-done | bytes 65568 | tf_op jit(solution)/shard_map/ppermute | solution.py:455
  31.7 0.7 %total.1 = f32[16,2,16,128]{3,2,1,0:T(8,128)} custom-call(f32[136,128]{1,0:T(8,128)S(1)} %collective-permute-done.5.refs_0_, f32[136,128]{1,0:T(8,128)S(1)} %collective-permute-done.6.refs_1_, f32[128,128]{1,0:T(8,128)S(1)} %get-tuple-element.35.refs_2_, f32[128,128]{1,0:T(8,128)S(1)} %collective-permute-done.7.refs_5_.refs_3_, ...), custom_call_target="tpu_custom_call" | custom-call | tf_op jit(solution)/shard_map/total/pallas_call | solution.py:466
  (12 shorter events, 0.1 us)
Async XLA Ops:
  5.7 7.2 %collective-permute-start.3 = (f32[784,128]{1,0:T(8,128)S(1)}, f32[784,128]{1,0:T(8,128)S(1)}, u32[]{:S(2)}, u32[]{:S(2)}) collective-permute-start(f32[784,128]{1,0:T(8,128)S(1)} %get-tuple-element.31), channel_id=1, source_target_pairs={{0,1},{1,0},{2,3},{3,2},{4,5},{5,4},{6,7},{7,6},{8,9},{9,8},{10,11... | collective-permute-start | bytes 1204232 | tf_op jit(solution)/shard_map/ppermute | solution.py:411
  6.3 1.6 %collective-permute-start = (f32[272,128]{1,0:T(8,128)S(1)}, f32[272,128]{1,0:T(8,128)S(1)}, u32[]{:S(2)}, u32[]{:S(2)}) collective-permute-start(f32[272,128]{1,0:T(8,128)S(1)} %get-tuple-element.28), channel_id=1, source_target_pairs={{0,1},{1,0},{2,3},{3,2},{4,5},{5,4},{6,7},{7,6},{8,9},{9,8},{10,11... | collective-permute-start | bytes 417800 | tf_op jit(solution)/shard_map/ppermute | solution.py:411
  7.8 7.9 %collective-permute-start.2 = (f32[136,128]{1,0:T(8,128)S(1)}, f32[136,128]{1,0:T(8,128)S(1)}, u32[]{:S(2)}, u32[]{:S(2)}) collective-permute-start(f32[136,128]{1,0:T(8,128)S(1)} %get-tuple-element.51), channel_id=1, source_target_pairs={{0,12},{4,8},{8,4},{12,0},{1,13},{5,9},{9,5},{13,1},{2,14},{6,10},... | collective-permute-start | bytes 208904 | tf_op jit(solution)/shard_map/ppermute | solution.py:415
  12.9 7.5 %collective-permute-start.1 = (f32[136,128]{1,0:T(8,128)S(1)}, f32[136,128]{1,0:T(8,128)S(1)}, u32[]{:S(2)}, u32[]{:S(2)}) collective-permute-start(f32[136,128]{1,0:T(8,128)S(1)} %get-tuple-element.52), channel_id=1, source_target_pairs={{0,8},{4,12},{8,0},{12,4},{1,9},{5,13},{9,1},{13,5},{2,10},{6,14},... | collective-permute-start | bytes 208904 | tf_op jit(solution)/shard_map/ppermute | solution.py:415
  12.9 7.7 %collective-permute-start.4 = (f32[136,128]{1,0:T(8,128)S(1)}, f32[136,128]{1,0:T(8,128)S(1)}, u32[]{:S(2)}, u32[]{:S(2)}) collective-permute-start(f32[136,128]{1,0:T(8,128)S(1)} %get-tuple-element.50), channel_id=1, source_target_pairs={{0,4},{4,0},{8,12},{12,8},{1,5},{5,1},{9,13},{13,9},{2,6},{6,2},{1... | collective-permute-start | bytes 208904 | tf_op jit(solution)/shard_map/ppermute | solution.py:415
  15.7 6.8 %collective-permute-start.9 = (f32[128,128]{1,0:T(8,128)S(1)}, f32[128,128]{1,0:T(8,128)S(1)}, u32[]{:S(2)}, u32[]{:S(2)}) collective-permute-start(f32[128,128]{1,0:T(8,128)S(1)} %get-tuple-element.41), channel_id=1, source_target_pairs={{0,12},{4,8},{8,4},{12,0},{1,13},{5,9},{9,5},{13,1},{2,14},{6,10},... | collective-permute-start | bytes 196616 | tf_op jit(solution)/shard_map/ppermute | solution.py:415
  19.9 4.6 %collective-permute-start.10 = (f32[128,128]{1,0:T(8,128)S(1)}, f32[128,128]{1,0:T(8,128)S(1)}, u32[]{:S(2)}, u32[]{:S(2)}) collective-permute-start(f32[128,128]{1,0:T(8,128)S(1)} %get-tuple-element.42), channel_id=1, source_target_pairs={{0,4},{4,0},{8,12},{12,8},{1,5},{5,1},{9,13},{13,9},{2,6},{6,2},{1... | collective-permute-start | bytes 196616 | tf_op jit(solution)/shard_map/ppermute | solution.py:415
  20.4 5.2 %collective-permute-start.8 = (f32[128,128]{1,0:T(8,128)S(1)}, f32[128,128]{1,0:T(8,128)S(1)}, u32[]{:S(2)}, u32[]{:S(2)}) collective-permute-start(f32[128,128]{1,0:T(8,128)S(1)} %join.2), channel_id=1, source_target_pairs={{0,8},{4,12},{8,0},{12,4},{1,9},{5,13},{9,1},{13,5},{2,10},{6,14},... | collective-permute-start | bytes 196616 | tf_op jit(solution)/shard_map/ppermute | solution.py:415
  20.9 4.7 %collective-permute-start.7 = (f32[128,128]{1,0:T(8,128)S(1)}, f32[128,128]{1,0:T(8,128)S(1)}, u32[]{:S(2)}, u32[]{:S(2)}) collective-permute-start(f32[128,128]{1,0:T(8,128)S(1)} %get-tuple-element.36), channel_id=1, source_target_pairs={{0,1},{1,0},{2,3},{3,2},{4,5},{5,4},{6,7},{7,6},{8,9},{9,8},{10,11... | collective-permute-start | bytes 196616 | tf_op jit(solution)/shard_map/ppermute | solution.py:455
  21.0 7.2 %collective-permute-start.5 = (f32[136,128]{1,0:T(8,128)S(1)}, f32[136,128]{1,0:T(8,128)S(1)}, u32[]{:S(2)}, u32[]{:S(2)}) collective-permute-start(f32[136,128]{1,0:T(8,128)S(1)} %get-tuple-element.33), channel_id=1, source_target_pairs={{0,2},{1,3},{2,0},{3,1},{4,6},{5,7},{6,4},{7,5},{8,10},{9,11},{10,... | collective-permute-start | bytes 208904 | tf_op jit(solution)/shard_map/ppermute | solution.py:455
  22.5 5.6 %collective-permute-start.6 = (f32[136,128]{1,0:T(8,128)S(1)}, f32[136,128]{1,0:T(8,128)S(1)}, u32[]{:S(2)}, u32[]{:S(2)}) collective-permute-start(f32[136,128]{1,0:T(8,128)S(1)} %get-tuple-element.34), channel_id=1, source_target_pairs={{0,3},{1,2},{2,1},{3,0},{4,7},{5,6},{6,5},{7,4},{8,11},{9,10},{10,... | collective-permute-start | bytes 208904 | tf_op jit(solution)/shard_map/ppermute | solution.py:455
  25.9 4.3 %collective-permute-start.11 = (f32[128,128]{1,0:T(8,128)S(1)}, f32[128,128]{1,0:T(8,128)S(1)}, u32[]{:S(2)}, u32[]{:S(2)}) collective-permute-start(f32[128,128]{1,0:T(8,128)S(1)} %get-tuple-element.45), channel_id=1, source_target_pairs={{0,2},{1,3},{2,0},{3,1},{4,6},{5,7},{6,4},{7,5},{8,10},{9,11},{10,... | collective-permute-start | bytes 196616 | tf_op jit(solution)/shard_map/ppermute | solution.py:455
  27.3 4.3 %collective-permute-start.12 = (f32[128,128]{1,0:T(8,128)S(1)}, f32[128,128]{1,0:T(8,128)S(1)}, u32[]{:S(2)}, u32[]{:S(2)}) collective-permute-start(f32[128,128]{1,0:T(8,128)S(1)} %get-tuple-element.46), channel_id=1, source_target_pairs={{0,3},{1,2},{2,1},{3,0},{4,7},{5,6},{6,5},{7,4},{8,11},{9,10},{10,... | collective-permute-start | bytes 196616 | tf_op jit(solution)/shard_map/ppermute | solution.py:455
  27.3 4.3 %collective-permute-start.13 = (f32[128,128]{1,0:T(8,128)S(1)}, f32[128,128]{1,0:T(8,128)S(1)}, u32[]{:S(2)}, u32[]{:S(2)}) collective-permute-start(f32[128,128]{1,0:T(8,128)S(1)} %get-tuple-element.48), channel_id=1, source_target_pairs={{0,1},{1,0},{2,3},{3,2},{4,5},{5,4},{6,7},{7,6},{8,9},{9,8},{10,11... | collective-permute-start | bytes 196616 | tf_op jit(solution)/shard_map/ppermute | solution.py:455

commit v9 on v8

--- a/solution.py
+++ b/solution.py
@@ -79,10 +79,10 @@
     *rest,
 ):
     far, steps = len(shifts) - 2, len(shifts)
-    mine, other, scratch = rest[: 2 * steps], rest[2 * steps : 2 * steps + 2], rest[2 * steps + 2 :]
+    mine, other, scratch = rest[: 2 * steps], rest[2 * steps : 2 * steps + 3], rest[2 * steps + 3 :]
     pos_ref, index_ref, count_ref = scratch[0:3]
     phase_ref, table_ref, obj_ref, probe_ref, cot_ref, row_ref, col_ref = scratch[3:10]
-    sems, band, window, col_bf, row_scr = scratch[10:]
+    sems, band, window, col_bf, row_scr, row_mix = scratch[10:]
     slices = obj_ref.shape[2]
     copies = [
         pltpu.make_async_copy(src, dst, sems.at[i])
@@ -134,9 +134,52 @@
         copy.wait()
     got_probe.wait()
     got_cot.wait()
+    got_row.wait()
+    got_col.wait()
+    got_index.wait()
+    got_count.wait()
     for s in order:
         source = jnp.concatenate([obj_ref[0, 0, s], obj_ref[0, 1, s]], 0)
         window[s] = dot(source, cut).astype(bf16)
+
+    block_rows, block_cols = row_ref.shape[-1], col_ref.shape[-1]
+    tiles = row_ref.shape[0]
+    batch = 8
+    wide = batch * block_rows
+    col_bf[...] = col_ref[...].astype(bf16)
+    down = lax.broadcasted_iota(jnp.int32, (block_rows, wide), 0)
+    along = lax.broadcasted_iota(jnp.int32, (block_rows, wide), 1)
+    repeat = (lax.rem(along, block_rows) == down).astype(bf16)
+    row_wide = dot(row_ref[...].reshape(tiles * block_rows, block_rows).astype(bf16), repeat)
+    row_scr[...] = row_wide.reshape(tiles, block_rows, wide)
+    strip = lax.div(along, block_rows)
+    half = block_rows // CHUNKS
+    mark_down = lax.broadcasted_iota(jnp.int32, (half, capacity * half), 0)
+    mark_along = lax.broadcasted_iota(jnp.int32, (half, capacity * half), 1)
+    mark_slot = jnp.where(lax.rem(mark_along, half) == mark_down, lax.div(mark_along, half), -1)
+    lines = capacity * half
+
+    def put(k, h, slot, value):
+        at = slot * half
+        late = h and k >= far
+        base = (k - far if late else k) * mine[h * steps].shape[0]
+        mine[h * steps + k][at : at + half] = value[:, :block_cols]
+        other[h + late][base + at : base + at + half] = value[:, block_cols:]
+
+    for k, shift in enumerate(shifts):
+        dest = partner(me, shift, peers)
+        live = count_ref[0, 0, dest]
+        marks = jnp.full(mark_slot.shape, VB_DEV, jnp.int32)
+        for slot in range(capacity):
+            target = jnp.where(slot < live, index_ref[1, 0, 0, dest, slot], VB_DEV)
+            marks = jnp.where(mark_slot == slot, target, marks)
+            group, at = divmod(slot, batch)
+            picked = jnp.where(strip == at, row_scr[index_ref[2, 0, 0, dest, slot]], 0.0)
+            row_mix[
+                k * (capacity // batch) + group, at * block_rows : (at + 1) * block_rows
+            ] = picked.astype(bf16)
+        marks = marks.astype(f32)
+        put(k, 0, capacity, jnp.concatenate([marks, jnp.zeros_like(marks)], 1))
 
     def tile(s, c, w):
         return window[s, c * rows : (c + 1) * rows, w * size : (w + 1) * size]
@@ -176,13 +219,11 @@
         a_re, a_im = one[0].astype(f32), one[1].astype(f32)
         b_re, b_im = two[0].astype(f32), two[1].astype(f32)
         if conjugate:
-            a_im = -a_im
-        return (
-            (a_re * b_re - a_im * b_im).astype(bf16),
-            (a_re * b_im + a_im * b_re).astype(bf16),
-        )
-
-    block_rows, block_cols = row_ref.shape[-1], col_ref.shape[-1]
+            re, im = a_re * b_re + a_im * b_im, a_re * b_im - a_im * b_re
+        else:
+            re, im = a_re * b_re - a_im * b_im, a_re * b_im + a_im * b_re
+        return re.astype(bf16), im.astype(bf16)
+
     across = cols // block_cols
     psi, chi = {}, {}
     now = [(probe_ref[0], probe_ref[1])] * count
@@ -218,56 +259,16 @@
                             top : top + block_rows, j * block_cols : (j + 1) * block_cols
                         ]
 
-    got_row.wait()
-    got_col.wait()
-    got_index.wait()
-    got_count.wait()
-    tiles = row_ref.shape[0]
-    batch = 8
-    wide = batch * block_rows
-    col_bf[...] = col_ref[...].astype(bf16)
-    down = lax.broadcasted_iota(jnp.int32, (block_rows, wide), 0)
-    along = lax.broadcasted_iota(jnp.int32, (block_rows, wide), 1)
-    repeat = (lax.rem(along, block_rows) == down).astype(bf16)
-    row_wide = dot(row_ref[...].reshape(tiles * block_rows, block_rows).astype(bf16), repeat)
-    row_scr[...] = row_wide.reshape(tiles, block_rows, wide)
-    strip = lax.div(along, block_rows)
-    half = block_rows // CHUNKS
-    mark_down = lax.broadcasted_iota(jnp.int32, (half, capacity * half), 0)
-    mark_along = lax.broadcasted_iota(jnp.int32, (half, capacity * half), 1)
-    mark_slot = jnp.where(lax.rem(mark_along, half) == mark_down, lax.div(mark_along, half), -1)
-    lines = capacity * half
-    late = (steps - far) * (lines + half)
-
-    def put(k, h, slot, value):
-        at = slot * half
-        if h:
-            swap, base = other[1], late + k * lines
-        elif k < far:
-            swap, base = other[0], k * (lines + half)
-        else:
-            swap, base = other[1], (k - far) * (lines + half)
-        mine[h * steps + k][at : at + half] = value[:, :block_cols]
-        swap[base + at : base + at + half] = value[:, block_cols:]
-
     for k, shift in enumerate(shifts):
         dest = partner(me, shift, peers)
-        live = count_ref[0, 0, dest]
-        marks = jnp.full(mark_slot.shape, VB_DEV, jnp.int32)
         for first in range(0, capacity, batch):
-            inner, picks = [], []
+            inner = []
             for slot in range(first, first + batch, 2):
                 pairs, factors = [], []
                 for one in (slot, slot + 1):
                     block = index_ref[0, 0, 0, dest, one]
-                    target = index_ref[1, 0, 0, dest, one]
-                    t = index_ref[2, 0, 0, dest, one]
-                    target = jnp.where(one < live, target, VB_DEV)
-                    marks = jnp.where(mark_slot == one, target, marks)
                     pairs += [band[core, block], band[1 - core, block]]
-                    factors.append(col_bf[t])
-                    picked = jnp.where(strip == one - first, row_scr[t], 0.0)
-                    picks.append(picked.astype(bf16))
+                    factors.append(col_bf[index_ref[2, 0, 0, dest, one]])
                 mixed = dot(jnp.concatenate(pairs, 0), jnp.concatenate(factors, 1)).astype(bf16)
                 for n in (0, 1):
                     lanes = slice(n * block_cols, (n + 1) * block_cols)
@@ -281,21 +282,15 @@
                             1,
                         )
                     )
-            result = dot(jnp.concatenate(picks, 0), jnp.concatenate(inner, 0))
+            result = dot(row_mix[k * (capacity // batch) + first // batch], jnp.concatenate(inner, 0))
             for slot in range(first, first + batch):
                 for h in range(CHUNKS):
                     top = (slot - first) * block_rows + h * half
                     put(k, h, slot, result[top : top + half])
-        marks = marks.astype(f32)
-        put(k, 0, capacity, jnp.concatenate([marks, jnp.zeros_like(marks)], 1))
-
-
-def join_kernel(base, first_ref, got_ref, *refs):
-    count = len(refs) // 2
-    for part, out in zip(refs[:count], refs[count:]):
-        tall = part.shape[0]
-        out[...] = part[...] + got_ref[base : base + tall]
-        base += tall
+
+
+def join_kernel(base, after_ref, got_ref, part_ref, out_ref):
+    out_ref[...] = part_ref[...] + got_ref[base : base + out_ref.shape[0]]
 
 
 def place_kernel(sources, owners, first, *refs):
@@ -369,7 +364,7 @@
     far = sources - 2
     tall = lanes + CHUNK_ROWS
     heights = [tall] * sources + [lanes] * sources
-    swapped = [far * tall, (sources - far) * tall + sources * lanes]
+    swapped = [sources * tall, far * lanes, (sources - far) * lanes]
     shapes = [jax.ShapeDtypeStruct((tall, block_cols), f32) for tall in heights + swapped]
     fetched = [
         (phase_line, VMEM),
@@ -394,6 +389,7 @@
             VMEM((slices, 2 * rows, windows * size), bf16),
             VMEM(col_interp.shape, bf16),
             VMEM((row_interp.shape[0], block_rows, 8 * block_rows), f32),
+            VMEM((sources * capacity // 8, 8 * block_rows, 8 * block_rows), bf16),
         ],
         compiler_params=limit,
         name="frame",
@@ -414,21 +410,27 @@
         ring = [(p, partner(p, step, peers)) for p in range(peers)]
         return lax.ppermute(block, "slab", ring)
 
-    first = []
-    for k in range(sources):
-        h, at = (0, k * tall) if k < far else (1, (k - far) * tall)
-        block = mine[k] + got[h][at : at + tall]
-        first.append(send(block, shifts[k]) if shifts[k] else block)
-    def join(after, part):
-        late = mine[sources:][part]
+    def near_sum(h, k):
+        part = mine[h * sources + k]
+        late = h and k >= far
+        at = (k - far if late else k) * part.shape[0]
+        return part + got[h + late][at : at + part.shape[0]]
+
+    def join(after, k):
         return pl.pallas_call(
-            functools.partial(join_kernel, (sources - far) * tall + part.start * lanes),
-            out_shape=shapes[sources : 2 * sources][part],
-            in_specs=[vmem] * (len(late) + 2),
-            out_specs=[vmem] * len(late),
+            functools.partial(join_kernel, k * lanes),
+            out_shape=shapes[sources],
+            in_specs=[vmem] * 3,
+            out_specs=vmem,
             compiler_params=limit,
             name="join",
-        )(after, got[1], *late)
+        )(after, got[1], mine[sources + k])
+
+    first = [send(near_sum(0, k), step) if step else near_sum(0, k) for k, step in enumerate(shifts)]
+    second = [
+        send(join(first[k], k) if k < far else near_sum(1, k), step) if step else near_sum(1, k)
+        for k, step in enumerate(shifts)
+    ]
 
     def place(blocks, extra, h):
         shapes = [padded if dt else share for dt, dr in owners] + [mark]
@@ -454,10 +456,6 @@
         ]
         return lax.ppermute(part, ("tilt", "rep"), route)
 
-    joined = []
-    for k in range(far):
-        joined += join(first[k], slice(k, k + 1 if k + 1 < far else sources))
-    second = [send(block, k) if k else block for block, k in zip(joined, shifts)]
     *parts, marks = place(first, [], 0)
     extra = [share_out(part, owner) for part, owner in zip(parts, owners)]
     held = [part for part, (dt, dr) in zip(extra, owners) if dr and not dt]

time: 32.6 us -> 34.4 us (1.055)
  starting transfers between devices: 14.8 us -> 15.9 us
  waiting for transfers between devices: 10.4 us -> 10.9 us
    ppermute x6, waiting for transfers between devices: 5.4 us -> 6.72 us  [send(): return lax.ppermute(block, 'slab', ring)]
    ppermute x6, starting transfers between devices: 10.1 us -> 11 us  [send(): return lax.ppermute(block, 'slab', ring)]
    ppermute x2 -> x3, waiting for transfers between devices: 1.48 us -> 0.68 us  [on_device(): got = [lax.ppermute(half, 'rep', swap) for half in other]]
    ppermute x2 -> x3, starting transfers between devices: 0.6 us -> 1.03 us  [on_device(): got = [lax.ppermute(half, 'rep', swap) for half in other]]
  transfers between devices with their start and end apart: 14 -> 15, of which waited for: 7 -> 6; matrix products, arithmetic and copies ran while one was open for 0% -> 0% of each run, Pallas kernels for 2% -> 2%
where the time goes in v9:
time: 34.4 us; the launch traced here: 34.2 us
  starting transfers between devices  15.9 us (46%)
  waiting for transfers between devices  10.9 us (32%)
  Pallas kernels  7.35 us (21%)
    ppermute x6, starting transfers between devices, send(): return lax.ppermute(block, 'slab', ring)  11 us
    ppermute x6, waiting for transfers between devices, send(): return lax.ppermute(block, 'slab', ring)  6.72 us
    pallas_call x1, Pallas kernels, on_device(): pl.pallas_call(functools.partial(frame_kernel, shifts), out_shape=shapes,...  6 us
    ppermute x6, starting transfers between devices, share_out(): return lax.ppermute(part, ('tilt', 'rep'), route)  3.84 us
    ppermute x6, waiting for transfers between devices, share_out(): return lax.ppermute(part, ('tilt', 'rep'), route)  3.53 us
    ppermute x3, starting transfers between devices, on_device(): got = [lax.ppermute(half, 'rep', swap) for half in other]  1.03 us
    pallas_call x1, Pallas kernels, on_device(): pl.pallas_call(functools.partial(sum_kernel, owners), out_shape=jax.Shape...  0.74 us
  transfers between devices with their start and end apart: 15, of which 6 were waited for; matrix products, arithmetic and copies ran while one was open for 0% of the time, Pallas kernels for 2%

profile of v9, /device:TPU:0, one launch (start us, length us, event | category | flops | bytes accessed | tf_op | source)
XLA Modules:
  0.0 34.2 jit_solution(17921234967024936879)
XLA Ops:
  0.0 6.0 %frame.1 = (f32[136,128]{1,0:T(8,128)S(1)}, f32[136,128]{1,0:T(8,128)S(1)}, f32[136,128]{1,0:T(8,128)S(1)}, f32[136,128]{1,0:T(8,128)S(1)}, f32[128,128]{1,0:T(8...) custom-call(s32[1,4]{1,0:T(1,128)} %pos_hbm.1, ...), custom_call_target="tpu_custom_call" | custom-call | tf_op jit(solution)/shard_map/frame/pallas_call | solution.py:379
  6.0 0.5 %collective-permute-start = (f32[544,128]{1,0:T(8,128)S(1)}, f32[544,128]{1,0:T(8,128)S(1)}, u32[]{:S(2)}, u32[]{:S(2)}) collective-permute-start(f32[544,128]{1,0:T(8,128)S(1)} %get-tuple-element.26), channel_id=1, source_target_pairs={{0,1},{1,0},{2,3},{3,2},{4,5},{5,4},{6,7},{7,6},{8,9},{9,8},{10,11... | collective-permute-start | bytes 835592 | tf_op jit(solution)/shard_map/ppermute | solution.py:407
  6.5 0.1 collective-permute-start.7
  6.6 0.4 %collective-permute-start.10 = (f32[256,128]{1,0:T(8,128)S(1)}, f32[256,128]{1,0:T(8,128)S(1)}, u32[]{:S(2)}, u32[]{:S(2)}) collective-permute-start(f32[256,128]{1,0:T(8,128)S(1)} %get-tuple-element.38), channel_id=1, source_target_pairs={{0,1},{1,0},{2,3},{3,2},{4,5},{5,4},{6,7},{7,6},{8,9},{9,8},{10,11... | collective-permute-start | bytes 393224 | tf_op jit(solution)/shard_map/ppermute | solution.py:407
  7.0 0.7 %collective-permute-done = f32[544,128]{1,0:T(8,128)S(1)} collective-permute-done((f32[544,128]{1,0:T(8,128)S(1)}, f32[544,128]{1,0:T(8,128)S(1)}, u32[]{:S(2)}, u32[]{:S(2)}) %collective-permute-start) | collective-permute-done | bytes 278560 | tf_op jit(solution)/shard_map/ppermute | solution.py:407
  7.8 3.0 %collective-permute-start.3 = (f32[136,128]{1,0:T(8,128)S(1)}, f32[136,128]{1,0:T(8,128)S(1)}, u32[]{:S(2)}, u32[]{:S(2)}) collective-permute-start(f32[136,128]{1,0:T(8,128)S(1)} %get-tuple-element.46), channel_id=1, source_target_pairs={{0,4},{4,0},{8,12},{12,8},{1,5},{5,1},{9,13},{13,9},{2,6},{6,2},{1... | collective-permute-start | bytes 208904 | tf_op jit(solution)/shard_map/ppermute | solution.py:411
  10.8 2.5 %collective-permute-start.2 = (f32[136,128]{1,0:T(8,128)S(1)}, f32[136,128]{1,0:T(8,128)S(1)}, u32[]{:S(2)}, u32[]{:S(2)}) collective-permute-start(f32[136,128]{1,0:T(8,128)S(1)} %get-tuple-element.47), channel_id=1, source_target_pairs={{0,12},{4,8},{8,4},{12,0},{1,13},{5,9},{9,5},{13,1},{2,14},{6,10},... | collective-permute-start | bytes 208904 | tf_op jit(solution)/shard_map/ppermute | solution.py:411
  13.2 0.1 collective-permute-start.1
  13.4 1.9 %collective-permute-start.11 = (f32[128,128]{1,0:T(8,128)S(1)}, f32[128,128]{1,0:T(8,128)S(1)}, u32[]{:S(2)}, u32[]{:S(2)}) collective-permute-start(f32[128,128]{1,0:T(8,128)S(1)} %get-tuple-element.50), channel_id=1, source_target_pairs={{0,4},{4,0},{8,12},{12,8},{1,5},{5,1},{9,13},{13,9},{2,6},{6,2},{1... | collective-permute-start | bytes 196616 | tf_op jit(solution)/shard_map/ppermute | solution.py:411
  15.3 2.5 %collective-permute-done.2.refs_1_.after_ref = f32[136,128]{1,0:T(8,128)S(1)} collective-permute-done((f32[136,128]{1,0:T(8,128)S(1)}, f32[136,128]{1,0:T(8,128)S(1)}, u32[]{:S(2)}, u32[]{:S(2)}) %collective-permute-start.2) | collective-permute-done | bytes 69664 | tf_op jit(solution)/shard_map/ppermute | solution.py:411
  17.7 2.5 %collective-permute-start.9 = (f32[128,128]{1,0:T(8,128)S(1)}, f32[128,128]{1,0:T(8,128)S(1)}, u32[]{:S(2)}, u32[]{:S(2)}) collective-permute-start(f32[128,128]{1,0:T(8,128)S(1)} %join.3), channel_id=1, source_target_pairs={{0,12},{4,8},{8,4},{12,0},{1,13},{5,9},{9,5},{13,1},{2,14},{6,10},... | collective-permute-start | bytes 196616 | tf_op jit(solution)/shard_map/ppermute | solution.py:411
  20.2 0.3 place.2
  20.5 0.1 collective-permute-start.6
  20.6 1.0 %collective-permute-start.8 = (f32[128,128]{1,0:T(8,128)S(1)}, f32[128,128]{1,0:T(8,128)S(1)}, u32[]{:S(2)}, u32[]{:S(2)}) collective-permute-start(f32[128,128]{1,0:T(8,128)S(1)} %join.2), channel_id=1, source_target_pairs={{0,8},{4,12},{8,0},{12,4},{1,9},{5,13},{9,1},{13,5},{2,10},{6,14},... | collective-permute-start | bytes 196616 | tf_op jit(solution)/shard_map/ppermute | solution.py:411
  21.7 1.5 %collective-permute-start.4 = (f32[136,128]{1,0:T(8,128)S(1)}, f32[136,128]{1,0:T(8,128)S(1)}, u32[]{:S(2)}, u32[]{:S(2)}) collective-permute-start(f32[136,128]{1,0:T(8,128)S(1)} %get-tuple-element.30), channel_id=1, source_target_pairs={{0,2},{1,3},{2,0},{3,1},{4,6},{5,7},{6,4},{7,5},{8,10},{9,11},{10,... | collective-permute-start | bytes 208904 | tf_op jit(solution)/shard_map/ppermute | solution.py:457
  23.1 0.1 collective-permute-start.5
  23.2 0.7 %collective-permute-done.9.refs_1_ = f32[128,128]{1,0:T(8,128)S(1)} collective-permute-done((f32[128,128]{1,0:T(8,128)S(1)}, f32[128,128]{1,0:T(8,128)S(1)}, u32[]{:S(2)}, u32[]{:S(2)}) %collective-permute-start.9) | collective-permute-done | bytes 65568 | tf_op jit(solution)/shard_map/ppermute | solution.py:411
  24.0 3.5 %collective-permute-done.8.refs_0_ = f32[128,128]{1,0:T(8,128)S(1)} collective-permute-done((f32[128,128]{1,0:T(8,128)S(1)}, f32[128,128]{1,0:T(8,128)S(1)}, u32[]{:S(2)}, u32[]{:S(2)}) %collective-permute-start.8) | collective-permute-done | bytes 65568 | tf_op jit(solution)/shard_map/ppermute | solution.py:411
  27.5 0.3 place.3
  27.8 1.6 %collective-permute-start.12 = (f32[128,128]{1,0:T(8,128)S(1)}, f32[128,128]{1,0:T(8,128)S(1)}, u32[]{:S(2)}, u32[]{:S(2)}) collective-permute-start(f32[128,128]{1,0:T(8,128)S(1)} %get-tuple-element.41), channel_id=1, source_target_pairs={{0,2},{1,3},{2,0},{3,1},{4,6},{5,7},{6,4},{7,5},{8,10},{9,11},{10,... | collective-permute-start | bytes 196616 | tf_op jit(solution)/shard_map/ppermute | solution.py:457
  29.3 0.6 %collective-permute-start.14 = (f32[128,128]{1,0:T(8,128)S(1)}, f32[128,128]{1,0:T(8,128)S(1)}, u32[]{:S(2)}, u32[]{:S(2)}) collective-permute-start(f32[128,128]{1,0:T(8,128)S(1)} %get-tuple-element.44), channel_id=1, source_target_pairs={{0,1},{1,0},{2,3},{3,2},{4,5},{5,4},{6,7},{7,6},{8,9},{9,8},{10,11... | collective-permute-start | bytes 196616 | tf_op jit(solution)/shard_map/ppermute | solution.py:457
  30.0 2.1 %collective-permute-done.12.refs_4_ = f32[128,128]{1,0:T(8,128)S(1)} collective-permute-done((f32[128,128]{1,0:T(8,128)S(1)}, f32[128,128]{1,0:T(8,128)S(1)}, u32[]{:S(2)}, u32[]{:S(2)}) %collective-permute-start.12) | collective-permute-done | bytes 65568 | tf_op jit(solution)/shard_map/ppermute | solution.py:457
  32.1 1.4 %collective-permute-done.13.refs_5_ = f32[128,128]{1,0:T(8,128)S(1)} collective-permute-done((f32[128,128]{1,0:T(8,128)S(1)}, f32[128,128]{1,0:T(8,128)S(1)}, u32[]{:S(2)}, u32[]{:S(2)}) %collective-permute-start.13) | collective-permute-done | bytes 65568 | tf_op jit(solution)/shard_map/ppermute | solution.py:457
  33.5 0.7 %total.1 = f32[16,2,16,128]{3,2,1,0:T(8,128)} custom-call(f32[136,128]{1,0:T(8,128)S(1)} %collective-permute-done.4.refs_0_, f32[136,128]{1,0:T(8,128)S(1)} %collective-permute-done.5.refs_1_, f32[128,128]{1,0:T(8,128)S(1)} %get-tuple-element.32.refs_2_, f32[128,128]{1,0:T(8,128)S(1)} %collective-permute-done.6.refs_5_.refs_3_, ...), custom_call_target="tpu_custom_call" | custom-call | tf_op jit(solution)/shard_map/total/pallas_call | solution.py:464
  (14 shorter events, 0.1 us)
Async XLA Ops:
  6.0 1.7 %collective-permute-start = (f32[544,128]{1,0:T(8,128)S(1)}, f32[544,128]{1,0:T(8,128)S(1)}, u32[]{:S(2)}, u32[]{:S(2)}) collective-permute-start(f32[544,128]{1,0:T(8,128)S(1)} %get-tuple-element.26), channel_id=1, source_target_pairs={{0,1},{1,0},{2,3},{3,2},{4,5},{5,4},{6,7},{7,6},{8,9},{9,8},{10,11... | collective-permute-start | bytes 835592 | tf_op jit(solution)/shard_map/ppermute | solution.py:407
  6.5 8.7 %collective-permute-start.7 = (f32[256,128]{1,0:T(8,128)S(1)}, f32[256,128]{1,0:T(8,128)S(1)}, u32[]{:S(2)}, u32[]{:S(2)}) collective-permute-start(f32[256,128]{1,0:T(8,128)S(1)} %get-tuple-element.34), channel_id=1, source_target_pairs={{0,1},{1,0},{2,3},{3,2},{4,5},{5,4},{6,7},{7,6},{8,9},{9,8},{10,11... | collective-permute-start | bytes 393224 | tf_op jit(solution)/shard_map/ppermute | solution.py:407
  6.6 6.8 %collective-permute-start.10 = (f32[256,128]{1,0:T(8,128)S(1)}, f32[256,128]{1,0:T(8,128)S(1)}, u32[]{:S(2)}, u32[]{:S(2)}) collective-permute-start(f32[256,128]{1,0:T(8,128)S(1)} %get-tuple-element.38), channel_id=1, source_target_pairs={{0,1},{1,0},{2,3},{3,2},{4,5},{5,4},{6,7},{7,6},{8,9},{9,8},{10,11... | collective-permute-start | bytes 393224 | tf_op jit(solution)/shard_map/ppermute | solution.py:407
  7.8 12.5 %collective-permute-start.3 = (f32[136,128]{1,0:T(8,128)S(1)}, f32[136,128]{1,0:T(8,128)S(1)}, u32[]{:S(2)}, u32[]{:S(2)}) collective-permute-start(f32[136,128]{1,0:T(8,128)S(1)} %get-tuple-element.46), channel_id=1, source_target_pairs={{0,4},{4,0},{8,12},{12,8},{1,5},{5,1},{9,13},{13,9},{2,6},{6,2},{1... | collective-permute-start | bytes 208904 | tf_op jit(solution)/shard_map/ppermute | solution.py:411
  10.8 6.9 %collective-permute-start.2 = (f32[136,128]{1,0:T(8,128)S(1)}, f32[136,128]{1,0:T(8,128)S(1)}, u32[]{:S(2)}, u32[]{:S(2)}) collective-permute-start(f32[136,128]{1,0:T(8,128)S(1)} %get-tuple-element.47), channel_id=1, source_target_pairs={{0,12},{4,8},{8,4},{12,0},{1,13},{5,9},{9,5},{13,1},{2,14},{6,10},... | collective-permute-start | bytes 208904 | tf_op jit(solution)/shard_map/ppermute | solution.py:411
  13.2 7.0 %collective-permute-start.1 = (f32[136,128]{1,0:T(8,128)S(1)}, f32[136,128]{1,0:T(8,128)S(1)}, u32[]{:S(2)}, u32[]{:S(2)}) collective-permute-start(f32[136,128]{1,0:T(8,128)S(1)} %get-tuple-element.48), channel_id=1, source_target_pairs={{0,8},{4,12},{8,0},{12,4},{1,9},{5,13},{9,1},{13,5},{2,10},{6,14},... | collective-permute-start | bytes 208904 | tf_op jit(solution)/shard_map/ppermute | solution.py:411
  13.4 9.8 %collective-permute-start.11 = (f32[128,128]{1,0:T(8,128)S(1)}, f32[128,128]{1,0:T(8,128)S(1)}, u32[]{:S(2)}, u32[]{:S(2)}) collective-permute-start(f32[128,128]{1,0:T(8,128)S(1)} %get-tuple-element.50), channel_id=1, source_target_pairs={{0,4},{4,0},{8,12},{12,8},{1,5},{5,1},{9,13},{13,9},{2,6},{6,2},{1... | collective-permute-start | bytes 196616 | tf_op jit(solution)/shard_map/ppermute | solution.py:411
  17.7 6.2 %collective-permute-start.9 = (f32[128,128]{1,0:T(8,128)S(1)}, f32[128,128]{1,0:T(8,128)S(1)}, u32[]{:S(2)}, u32[]{:S(2)}) collective-permute-start(f32[128,128]{1,0:T(8,128)S(1)} %join.3), channel_id=1, source_target_pairs={{0,12},{4,8},{8,4},{12,0},{1,13},{5,9},{9,5},{13,1},{2,14},{6,10},... | collective-permute-start | bytes 196616 | tf_op jit(solution)/shard_map/ppermute | solution.py:411
  20.5 3.4 %collective-permute-start.6 = (f32[128,128]{1,0:T(8,128)S(1)}, f32[128,128]{1,0:T(8,128)S(1)}, u32[]{:S(2)}, u32[]{:S(2)}) collective-permute-start(f32[128,128]{1,0:T(8,128)S(1)} %get-tuple-element.33), channel_id=1, source_target_pairs={{0,1},{1,0},{2,3},{3,2},{4,5},{5,4},{6,7},{7,6},{8,9},{9,8},{10,11... | collective-permute-start | bytes 196616 | tf_op jit(solution)/shard_map/ppermute | solution.py:457
  20.6 6.9 %collective-permute-start.8 = (f32[128,128]{1,0:T(8,128)S(1)}, f32[128,128]{1,0:T(8,128)S(1)}, u32[]{:S(2)}, u32[]{:S(2)}) collective-permute-start(f32[128,128]{1,0:T(8,128)S(1)} %join.2), channel_id=1, source_target_pairs={{0,8},{4,12},{8,0},{12,4},{1,9},{5,13},{9,1},{13,5},{2,10},{6,14},... | collective-permute-start | bytes 196616 | tf_op jit(solution)/shard_map/ppermute | solution.py:411
  21.7 8.3 %collective-permute-start.4 = (f32[136,128]{1,0:T(8,128)S(1)}, f32[136,128]{1,0:T(8,128)S(1)}, u32[]{:S(2)}, u32[]{:S(2)}) collective-permute-start(f32[136,128]{1,0:T(8,128)S(1)} %get-tuple-element.30), channel_id=1, source_target_pairs={{0,2},{1,3},{2,0},{3,1},{4,6},{5,7},{6,4},{7,5},{8,10},{9,11},{10,... | collective-permute-start | bytes 208904 | tf_op jit(solution)/shard_map/ppermute | solution.py:457
  23.1 6.8 %collective-permute-start.5 = (f32[136,128]{1,0:T(8,128)S(1)}, f32[136,128]{1,0:T(8,128)S(1)}, u32[]{:S(2)}, u32[]{:S(2)}) collective-permute-start(f32[136,128]{1,0:T(8,128)S(1)} %get-tuple-element.31), channel_id=1, source_target_pairs={{0,3},{1,2},{2,1},{3,0},{4,7},{5,6},{6,5},{7,4},{8,11},{9,10},{10,... | collective-permute-start | bytes 208904 | tf_op jit(solution)/shard_map/ppermute | solution.py:457
  27.8 4.3 %collective-permute-start.12 = (f32[128,128]{1,0:T(8,128)S(1)}, f32[128,128]{1,0:T(8,128)S(1)}, u32[]{:S(2)}, u32[]{:S(2)}) collective-permute-start(f32[128,128]{1,0:T(8,128)S(1)} %get-tuple-element.41), channel_id=1, source_target_pairs={{0,2},{1,3},{2,0},{3,1},{4,6},{5,7},{6,4},{7,5},{8,10},{9,11},{10,... | collective-permute-start | bytes 196616 | tf_op jit(solution)/shard_map/ppermute | solution.py:457
  29.3 4.2 %collective-permute-start.13 = (f32[128,128]{1,0:T(8,128)S(1)}, f32[128,128]{1,0:T(8,128)S(1)}, u32[]{:S(2)}, u32[]{:S(2)}) collective-permute-start(f32[128,128]{1,0:T(8,128)S(1)} %get-tuple-element.42), channel_id=1, source_target_pairs={{0,3},{1,2},{2,1},{3,0},{4,7},{5,6},{6,5},{7,4},{8,11},{9,10},{10,... | collective-permute-start | bytes 196616 | tf_op jit(solution)/shard_map/ppermute | solution.py:457
  29.3 4.2 %collective-permute-start.14 = (f32[128,128]{1,0:T(8,128)S(1)}, f32[128,128]{1,0:T(8,128)S(1)}, u32[]{:S(2)}, u32[]{:S(2)}) collective-permute-start(f32[128,128]{1,0:T(8,128)S(1)} %get-tuple-element.44), channel_id=1, source_target_pairs={{0,1},{1,0},{2,3},{3,2},{4,5},{5,4},{6,7},{7,6},{8,9},{9,8},{10,11... | collective-permute-start | bytes 196616 | tf_op jit(solution)/shard_map/ppermute | solution.py:457

commit v10 on v8

--- a/solution.py
+++ b/solution.py
@@ -79,7 +79,7 @@
     *rest,
 ):
     far, steps = len(shifts) - 2, len(shifts)
-    mine, other, scratch = rest[: 2 * steps], rest[2 * steps : 2 * steps + 2], rest[2 * steps + 2 :]
+    mine, other, scratch = rest[: 2 * steps], rest[2 * steps : 2 * steps + 3], rest[2 * steps + 3 :]
     pos_ref, index_ref, count_ref = scratch[0:3]
     phase_ref, table_ref, obj_ref, probe_ref, cot_ref, row_ref, col_ref = scratch[3:10]
     sems, band, window, col_bf, row_scr = scratch[10:]
@@ -130,11 +130,8 @@
     )
     whole, turned = propagator_blocks(phase_ref[...], table_ref[...])
 
-    for copy in got_obj:
-        copy.wait()
-    got_probe.wait()
-    got_cot.wait()
     for s in order:
+        got_obj[s].wait()
         source = jnp.concatenate([obj_ref[0, 0, s], obj_ref[0, 1, s]], 0)
         window[s] = dot(source, cut).astype(bf16)
 
@@ -176,15 +173,16 @@
         a_re, a_im = one[0].astype(f32), one[1].astype(f32)
         b_re, b_im = two[0].astype(f32), two[1].astype(f32)
         if conjugate:
-            a_im = -a_im
-        return (
-            (a_re * b_re - a_im * b_im).astype(bf16),
-            (a_re * b_im + a_im * b_re).astype(bf16),
-        )
+            re, im = a_re * b_re + a_im * b_im, a_re * b_im - a_im * b_re
+        else:
+            re, im = a_re * b_re - a_im * b_im, a_re * b_im + a_im * b_re
+        return re.astype(bf16), im.astype(bf16)
 
     block_rows, block_cols = row_ref.shape[-1], col_ref.shape[-1]
     across = cols // block_cols
     psi, chi = {}, {}
+    got_probe.wait()
+    got_cot.wait()
     now = [(probe_ref[0], probe_ref[1])] * count
     back = [(cot_ref[0, w, 0], cot_ref[0, w, 1]) for w in range(count)]
     lane_down = lax.broadcasted_iota(jnp.int32, (size, cols), 0)
@@ -237,18 +235,13 @@
     mark_along = lax.broadcasted_iota(jnp.int32, (half, capacity * half), 1)
     mark_slot = jnp.where(lax.rem(mark_along, half) == mark_down, lax.div(mark_along, half), -1)
     lines = capacity * half
-    late = (steps - far) * (lines + half)
 
     def put(k, h, slot, value):
         at = slot * half
-        if h:
-            swap, base = other[1], late + k * lines
-        elif k < far:
-            swap, base = other[0], k * (lines + half)
-        else:
-            swap, base = other[1], (k - far) * (lines + half)
+        late = h and k >= far
+        base = (k - far if late else k) * mine[h * steps].shape[0]
         mine[h * steps + k][at : at + half] = value[:, :block_cols]
-        swap[base + at : base + at + half] = value[:, block_cols:]
+        other[h + late][base + at : base + at + half] = value[:, block_cols:]
 
     for k, shift in enumerate(shifts):
         dest = partner(me, shift, peers)
@@ -290,12 +283,11 @@
         put(k, 0, capacity, jnp.concatenate([marks, jnp.zeros_like(marks)], 1))
 
 
-def join_kernel(base, first_ref, got_ref, *refs):
+def join_kernel(after_ref, got_ref, *refs):
     count = len(refs) // 2
-    for part, out in zip(refs[:count], refs[count:]):
+    for k, (part, out) in enumerate(zip(refs[:count], refs[count:])):
         tall = part.shape[0]
-        out[...] = part[...] + got_ref[base : base + tall]
-        base += tall
+        out[...] = part[...] + got_ref[k * tall : (k + 1) * tall]
 
 
 def place_kernel(sources, owners, first, *refs):
@@ -369,7 +361,7 @@
     far = sources - 2
     tall = lanes + CHUNK_ROWS
     heights = [tall] * sources + [lanes] * sources
-    swapped = [far * tall, (sources - far) * tall + sources * lanes]
+    swapped = [sources * tall, far * lanes, (sources - far) * lanes]
     shapes = [jax.ShapeDtypeStruct((tall, block_cols), f32) for tall in heights + swapped]
     fetched = [
         (phase_line, VMEM),
@@ -414,21 +406,25 @@
         ring = [(p, partner(p, step, peers)) for p in range(peers)]
         return lax.ppermute(block, "slab", ring)
 
-    first = []
-    for k in range(sources):
-        h, at = (0, k * tall) if k < far else (1, (k - far) * tall)
-        block = mine[k] + got[h][at : at + tall]
-        first.append(send(block, shifts[k]) if shifts[k] else block)
-    def join(after, part):
-        late = mine[sources:][part]
-        return pl.pallas_call(
-            functools.partial(join_kernel, (sources - far) * tall + part.start * lanes),
-            out_shape=shapes[sources : 2 * sources][part],
-            in_specs=[vmem] * (len(late) + 2),
-            out_specs=[vmem] * len(late),
-            compiler_params=limit,
-            name="join",
-        )(after, got[1], *late)
+    def core_sum(h, k):
+        part = mine[h * sources + k]
+        late = h and k >= far
+        at = (k - far if late else k) * part.shape[0]
+        return part + got[h + late][at : at + part.shape[0]]
+
+    def send_all(blocks):
+        return [send(block, step) if step else block for block, step in zip(blocks, shifts)]
+
+    first = send_all([core_sum(0, k) for k in range(sources)])
+    joined = pl.pallas_call(
+        join_kernel,
+        out_shape=[shapes[sources]] * far,
+        in_specs=[vmem] * (far + 2),
+        out_specs=[vmem] * far,
+        compiler_params=limit,
+        name="join",
+    )(first[far - 1], got[1], *mine[sources : sources + far])
+    second = send_all([*joined, *[core_sum(1, k) for k in range(far, sources)]])
 
     def place(blocks, extra, h):
         shapes = [padded if dt else share for dt, dr in owners] + [mark]
@@ -454,10 +450,6 @@
         ]
         return lax.ppermute(part, ("tilt", "rep"), route)
 
-    joined = []
-    for k in range(far):
-        joined += join(first[k], slice(k, k + 1 if k + 1 < far else sources))
-    second = [send(block, k) if k else block for block, k in zip(joined, shifts)]
     *parts, marks = place(first, [], 0)
     extra = [share_out(part, owner) for part, owner in zip(parts, owners)]
     held = [part for part, (dt, dr) in zip(extra, owners) if dr and not dt]

time: 32.6 us -> 36 us (1.10)
  starting transfers between devices: 14.8 us -> 17.5 us
  Pallas kernels: 7.11 us -> 7.76 us
    ppermute x6, starting transfers between devices: 10.1 us -> 12.3 us  [send(): return lax.ppermute(block, 'slab', ring)]
    ppermute x6, waiting for transfers between devices: 5.4 us -> 6.25 us  [send(): return lax.ppermute(block, 'slab', ring)]
    ppermute x2 -> x3, waiting for transfers between devices: 1.48 us -> 0.68 us  [on_device(): got = [lax.ppermute(half, 'rep', swap) for half in other]]
    pallas_call x1, Pallas kernels: 5.72 us -> 6.41 us  [on_device(): pl.pallas_call(functools.partial(frame_kernel, shifts), out_shape=shapes,...]
    ppermute x2 -> x3, starting transfers between devices: 0.6 us -> 1.03 us  [on_device(): got = [lax.ppermute(half, 'rep', swap) for half in other]]
  transfers between devices with their start and end apart: 14 -> 15, of which waited for: 7 -> 6; matrix products, arithmetic and copies ran while one was open for 0% -> 0% of each run, Pallas kernels for 2% -> 2%
where the time goes in v10:
time: 36 us; the launch traced here: 35.8 us
  starting transfers between devices  17.5 us (49%)
  waiting for transfers between devices  10.5 us (29%)
  Pallas kernels  7.76 us (22%)
    ppermute x6, starting transfers between devices, send(): return lax.ppermute(block, 'slab', ring)  12.3 us
    pallas_call x1, Pallas kernels, on_device(): pl.pallas_call(functools.partial(frame_kernel, shifts), out_shape=shapes,...  6.41 us
    ppermute x6, waiting for transfers between devices, send(): return lax.ppermute(block, 'slab', ring)  6.25 us
    ppermute x6, starting transfers between devices, share_out(): return lax.ppermute(part, ('tilt', 'rep'), route)  4.14 us
    ppermute x6, waiting for transfers between devices, share_out(): return lax.ppermute(part, ('tilt', 'rep'), route)  3.53 us
    ppermute x3, starting transfers between devices, on_device(): got = [lax.ppermute(half, 'rep', swap) for half in other]  1.03 us
    pallas_call x1, Pallas kernels, on_device(): pl.pallas_call(functools.partial(sum_kernel, owners), out_shape=jax.Shape...  0.74 us
  transfers between devices with their start and end apart: 15, of which 6 were waited for; matrix products, arithmetic and copies ran while one was open for 0% of the time, Pallas kernels for 2%

profile of v10, /device:TPU:0, one launch (start us, length us, event | category | flops | bytes accessed | tf_op | source)
XLA Modules:
  0.0 35.8 jit_solution(10278335408307984505)
XLA Ops:
  0.0 6.4 %frame.1 = (f32[136,128]{1,0:T(8,128)S(1)}, f32[136,128]{1,0:T(8,128)S(1)}, f32[136,128]{1,0:T(8,128)S(1)}, f32[136,128]{1,0:T(8,128)S(1)}, f32[128,128]{1,0:T(8...) custom-call(s32[1,4]{1,0:T(1,128)} %pos_hbm.1, ...), custom_call_target="tpu_custom_call" | custom-call | tf_op jit(solution)/shard_map/frame/pallas_call | solution.py:376
  6.4 0.5 %collective-permute-start = (f32[544,128]{1,0:T(8,128)S(1)}, f32[544,128]{1,0:T(8,128)S(1)}, u32[]{:S(2)}, u32[]{:S(2)}) collective-permute-start(f32[544,128]{1,0:T(8,128)S(1)} %get-tuple-element.28), channel_id=1, source_target_pairs={{0,1},{1,0},{2,3},{3,2},{4,5},{5,4},{6,7},{7,6},{8,9},{9,8},{10,11... | collective-permute-start | bytes 835592 | tf_op jit(solution)/shard_map/ppermute | solution.py:403
  6.9 0.1 collective-permute-start.7
  7.0 0.4 %collective-permute-start.10 = (f32[256,128]{1,0:T(8,128)S(1)}, f32[256,128]{1,0:T(8,128)S(1)}, u32[]{:S(2)}, u32[]{:S(2)}) collective-permute-start(f32[256,128]{1,0:T(8,128)S(1)} %get-tuple-element.42), channel_id=1, source_target_pairs={{0,1},{1,0},{2,3},{3,2},{4,5},{5,4},{6,7},{7,6},{8,9},{9,8},{10,11... | collective-permute-start | bytes 393224 | tf_op jit(solution)/shard_map/ppermute | solution.py:403
  7.5 0.7 %collective-permute-done = f32[544,128]{1,0:T(8,128)S(1)} collective-permute-done((f32[544,128]{1,0:T(8,128)S(1)}, f32[544,128]{1,0:T(8,128)S(1)}, u32[]{:S(2)}, u32[]{:S(2)}) %collective-permute-start) | collective-permute-done | bytes 278560 | tf_op jit(solution)/shard_map/ppermute | solution.py:403
  8.2 3.0 %collective-permute-start.3 = (f32[136,128]{1,0:T(8,128)S(1)}, f32[136,128]{1,0:T(8,128)S(1)}, u32[]{:S(2)}, u32[]{:S(2)}) collective-permute-start(f32[136,128]{1,0:T(8,128)S(1)} %get-tuple-element.50), channel_id=1, source_target_pairs={{0,4},{4,0},{8,12},{12,8},{1,5},{5,1},{9,13},{13,9},{2,6},{6,2},{1... | collective-permute-start | bytes 208904 | tf_op jit(solution)/shard_map/ppermute | solution.py:407
  11.2 2.5 %collective-permute-start.2 = (f32[136,128]{1,0:T(8,128)S(1)}, f32[136,128]{1,0:T(8,128)S(1)}, u32[]{:S(2)}, u32[]{:S(2)}) collective-permute-start(f32[136,128]{1,0:T(8,128)S(1)} %get-tuple-element.51), channel_id=1, source_target_pairs={{0,12},{4,8},{8,4},{12,0},{1,13},{5,9},{9,5},{13,1},{2,14},{6,10},... | collective-permute-start | bytes 208904 | tf_op jit(solution)/shard_map/ppermute | solution.py:407
  13.7 0.1 collective-permute-start.1
  13.8 1.9 %collective-permute-start.11 = (f32[128,128]{1,0:T(8,128)S(1)}, f32[128,128]{1,0:T(8,128)S(1)}, u32[]{:S(2)}, u32[]{:S(2)}) collective-permute-start(f32[128,128]{1,0:T(8,128)S(1)} %get-tuple-element.54), channel_id=1, source_target_pairs={{0,4},{4,0},{8,12},{12,8},{1,5},{5,1},{9,13},{13,9},{2,6},{6,2},{1... | collective-permute-start | bytes 196616 | tf_op jit(solution)/shard_map/ppermute | solution.py:407
  15.7 2.4 %collective-permute-done.2.refs_1_.after_ref = f32[136,128]{1,0:T(8,128)S(1)} collective-permute-done((f32[136,128]{1,0:T(8,128)S(1)}, f32[136,128]{1,0:T(8,128)S(1)}, u32[]{:S(2)}, u32[]{:S(2)}) %collective-permute-start.2) | collective-permute-done | bytes 69664 | tf_op jit(solution)/shard_map/ppermute | solution.py:407
  18.1 4.9 %collective-permute-start.8 = (f32[128,128]{1,0:T(8,128)S(1)}, f32[128,128]{1,0:T(8,128)S(1)}, u32[]{:S(2)}, u32[]{:S(2)}) collective-permute-start(f32[128,128]{1,0:T(8,128)S(1)} %get-tuple-element.39), channel_id=1, source_target_pairs={{0,8},{4,12},{8,0},{12,4},{1,9},{5,13},{9,1},{13,5},{2,10},{6,14},... | collective-permute-start | bytes 196616 | tf_op jit(solution)/shard_map/ppermute | solution.py:407
  23.0 0.0 collective-permute-start.9
  23.0 0.3 place.2
  23.3 0.1 collective-permute-start.6
  23.4 1.6 %collective-permute-start.4 = (f32[136,128]{1,0:T(8,128)S(1)}, f32[136,128]{1,0:T(8,128)S(1)}, u32[]{:S(2)}, u32[]{:S(2)}) collective-permute-start(f32[136,128]{1,0:T(8,128)S(1)} %get-tuple-element.32), channel_id=1, source_target_pairs={{0,2},{1,3},{2,0},{3,1},{4,6},{5,7},{6,4},{7,5},{8,10},{9,11},{10,... | collective-permute-start | bytes 208904 | tf_op jit(solution)/shard_map/ppermute | solution.py:451
  24.9 0.3 collective-permute-start.5
  25.2 0.2 collective-permute-done.8.refs_0_
  25.4 3.6 %collective-permute-done.9.refs_1_ = f32[128,128]{1,0:T(8,128)S(1)} collective-permute-done((f32[128,128]{1,0:T(8,128)S(1)}, f32[128,128]{1,0:T(8,128)S(1)}, u32[]{:S(2)}, u32[]{:S(2)}) %collective-permute-start.9) | collective-permute-done | bytes 65568 | tf_op jit(solution)/shard_map/ppermute | solution.py:407
  29.1 0.3 place.3
  29.4 1.6 %collective-permute-start.12 = (f32[128,128]{1,0:T(8,128)S(1)}, f32[128,128]{1,0:T(8,128)S(1)}, u32[]{:S(2)}, u32[]{:S(2)}) collective-permute-start(f32[128,128]{1,0:T(8,128)S(1)} %get-tuple-element.45), channel_id=1, source_target_pairs={{0,2},{1,3},{2,0},{3,1},{4,6},{5,7},{6,4},{7,5},{8,10},{9,11},{10,... | collective-permute-start | bytes 196616 | tf_op jit(solution)/shard_map/ppermute | solution.py:451
  30.9 0.6 %collective-permute-start.14 = (f32[128,128]{1,0:T(8,128)S(1)}, f32[128,128]{1,0:T(8,128)S(1)}, u32[]{:S(2)}, u32[]{:S(2)}) collective-permute-start(f32[128,128]{1,0:T(8,128)S(1)} %get-tuple-element.48), channel_id=1, source_target_pairs={{0,1},{1,0},{2,3},{3,2},{4,5},{5,4},{6,7},{7,6},{8,9},{9,8},{10,11... | collective-permute-start | bytes 196616 | tf_op jit(solution)/shard_map/ppermute | solution.py:451
  31.6 2.1 %collective-permute-done.12.refs_4_ = f32[128,128]{1,0:T(8,128)S(1)} collective-permute-done((f32[128,128]{1,0:T(8,128)S(1)}, f32[128,128]{1,0:T(8,128)S(1)}, u32[]{:S(2)}, u32[]{:S(2)}) %collective-permute-start.12) | collective-permute-done | bytes 65568 | tf_op jit(solution)/shard_map/ppermute | solution.py:451
  33.7 1.4 %collective-permute-done.13.refs_5_ = f32[128,128]{1,0:T(8,128)S(1)} collective-permute-done((f32[128,128]{1,0:T(8,128)S(1)}, f32[128,128]{1,0:T(8,128)S(1)}, u32[]{:S(2)}, u32[]{:S(2)}) %collective-permute-start.13) | collective-permute-done | bytes 65568 | tf_op jit(solution)/shard_map/ppermute | solution.py:451
  35.1 0.7 %total.1 = f32[16,2,16,128]{3,2,1,0:T(8,128)} custom-call(f32[136,128]{1,0:T(8,128)S(1)} %collective-permute-done.4.refs_0_, f32[136,128]{1,0:T(8,128)S(1)} %collective-permute-done.5.refs_1_, f32[128,128]{1,0:T(8,128)S(1)} %get-tuple-element.34.refs_2_, f32[128,128]{1,0:T(8,128)S(1)} %collective-permute-done.6.refs_5_.refs_3_, ...), custom_call_target="tpu_custom_call" | custom-call | tf_op jit(solution)/shard_map/total/pallas_call | solution.py:458
  (13 shorter events, 0.1 us)
Async XLA Ops:
  6.4 1.7 %collective-permute-start = (f32[544,128]{1,0:T(8,128)S(1)}, f32[544,128]{1,0:T(8,128)S(1)}, u32[]{:S(2)}, u32[]{:S(2)}) collective-permute-start(f32[544,128]{1,0:T(8,128)S(1)} %get-tuple-element.28), channel_id=1, source_target_pairs={{0,1},{1,0},{2,3},{3,2},{4,5},{5,4},{6,7},{7,6},{8,9},{9,8},{10,11... | collective-permute-start | bytes 835592 | tf_op jit(solution)/shard_map/ppermute | solution.py:403
  6.9 8.7 %collective-permute-start.7 = (f32[256,128]{1,0:T(8,128)S(1)}, f32[256,128]{1,0:T(8,128)S(1)}, u32[]{:S(2)}, u32[]{:S(2)}) collective-permute-start(f32[256,128]{1,0:T(8,128)S(1)} %get-tuple-element.36), channel_id=1, source_target_pairs={{0,1},{1,0},{2,3},{3,2},{4,5},{5,4},{6,7},{7,6},{8,9},{9,8},{10,11... | collective-permute-start | bytes 393224 | tf_op jit(solution)/shard_map/ppermute | solution.py:403
  7.0 6.8 %collective-permute-start.10 = (f32[256,128]{1,0:T(8,128)S(1)}, f32[256,128]{1,0:T(8,128)S(1)}, u32[]{:S(2)}, u32[]{:S(2)}) collective-permute-start(f32[256,128]{1,0:T(8,128)S(1)} %get-tuple-element.42), channel_id=1, source_target_pairs={{0,1},{1,0},{2,3},{3,2},{4,5},{5,4},{6,7},{7,6},{8,9},{9,8},{10,11... | collective-permute-start | bytes 393224 | tf_op jit(solution)/shard_map/ppermute | solution.py:403
  8.2 14.8 %collective-permute-start.3 = (f32[136,128]{1,0:T(8,128)S(1)}, f32[136,128]{1,0:T(8,128)S(1)}, u32[]{:S(2)}, u32[]{:S(2)}) collective-permute-start(f32[136,128]{1,0:T(8,128)S(1)} %get-tuple-element.50), channel_id=1, source_target_pairs={{0,4},{4,0},{8,12},{12,8},{1,5},{5,1},{9,13},{13,9},{2,6},{6,2},{1... | collective-permute-start | bytes 208904 | tf_op jit(solution)/shard_map/ppermute | solution.py:407
  11.2 6.9 %collective-permute-start.2 = (f32[136,128]{1,0:T(8,128)S(1)}, f32[136,128]{1,0:T(8,128)S(1)}, u32[]{:S(2)}, u32[]{:S(2)}) collective-permute-start(f32[136,128]{1,0:T(8,128)S(1)} %get-tuple-element.51), channel_id=1, source_target_pairs={{0,12},{4,8},{8,4},{12,0},{1,13},{5,9},{9,5},{13,1},{2,14},{6,10},... | collective-permute-start | bytes 208904 | tf_op jit(solution)/shard_map/ppermute | solution.py:407
  13.7 9.3 %collective-permute-start.1 = (f32[136,128]{1,0:T(8,128)S(1)}, f32[136,128]{1,0:T(8,128)S(1)}, u32[]{:S(2)}, u32[]{:S(2)}) collective-permute-start(f32[136,128]{1,0:T(8,128)S(1)} %get-tuple-element.52), channel_id=1, source_target_pairs={{0,8},{4,12},{8,0},{12,4},{1,9},{5,13},{9,1},{13,5},{2,10},{6,14},... | collective-permute-start | bytes 208904 | tf_op jit(solution)/shard_map/ppermute | solution.py:407
  13.8 11.1 %collective-permute-start.11 = (f32[128,128]{1,0:T(8,128)S(1)}, f32[128,128]{1,0:T(8,128)S(1)}, u32[]{:S(2)}, u32[]{:S(2)}) collective-permute-start(f32[128,128]{1,0:T(8,128)S(1)} %get-tuple-element.54), channel_id=1, source_target_pairs={{0,4},{4,0},{8,12},{12,8},{1,5},{5,1},{9,13},{13,9},{2,6},{6,2},{1... | collective-permute-start | bytes 196616 | tf_op jit(solution)/shard_map/ppermute | solution.py:407
  18.1 7.3 %collective-permute-start.8 = (f32[128,128]{1,0:T(8,128)S(1)}, f32[128,128]{1,0:T(8,128)S(1)}, u32[]{:S(2)}, u32[]{:S(2)}) collective-permute-start(f32[128,128]{1,0:T(8,128)S(1)} %get-tuple-element.39), channel_id=1, source_target_pairs={{0,8},{4,12},{8,0},{12,4},{1,9},{5,13},{9,1},{13,5},{2,10},{6,14},... | collective-permute-start | bytes 196616 | tf_op jit(solution)/shard_map/ppermute | solution.py:407
  23.0 6.1 %collective-permute-start.9 = (f32[128,128]{1,0:T(8,128)S(1)}, f32[128,128]{1,0:T(8,128)S(1)}, u32[]{:S(2)}, u32[]{:S(2)}) collective-permute-start(f32[128,128]{1,0:T(8,128)S(1)} %get-tuple-element.40), channel_id=1, source_target_pairs={{0,12},{4,8},{8,4},{12,0},{1,13},{5,9},{9,5},{13,1},{2,14},{6,10},... | collective-permute-start | bytes 196616 | tf_op jit(solution)/shard_map/ppermute | solution.py:407
  23.3 5.8 %collective-permute-start.6 = (f32[128,128]{1,0:T(8,128)S(1)}, f32[128,128]{1,0:T(8,128)S(1)}, u32[]{:S(2)}, u32[]{:S(2)}) collective-permute-start(f32[128,128]{1,0:T(8,128)S(1)} %get-tuple-element.35), channel_id=1, source_target_pairs={{0,1},{1,0},{2,3},{3,2},{4,5},{5,4},{6,7},{7,6},{8,9},{9,8},{10,11... | collective-permute-start | bytes 196616 | tf_op jit(solution)/shard_map/ppermute | solution.py:451
  23.4 8.2 %collective-permute-start.4 = (f32[136,128]{1,0:T(8,128)S(1)}, f32[136,128]{1,0:T(8,128)S(1)}, u32[]{:S(2)}, u32[]{:S(2)}) collective-permute-start(f32[136,128]{1,0:T(8,128)S(1)} %get-tuple-element.32), channel_id=1, source_target_pairs={{0,2},{1,3},{2,0},{3,1},{4,6},{5,7},{6,4},{7,5},{8,10},{9,11},{10,... | collective-permute-start | bytes 208904 | tf_op jit(solution)/shard_map/ppermute | solution.py:451
  24.9 6.6 %collective-permute-start.5 = (f32[136,128]{1,0:T(8,128)S(1)}, f32[136,128]{1,0:T(8,128)S(1)}, u32[]{:S(2)}, u32[]{:S(2)}) collective-permute-start(f32[136,128]{1,0:T(8,128)S(1)} %get-tuple-element.33), channel_id=1, source_target_pairs={{0,3},{1,2},{2,1},{3,0},{4,7},{5,6},{6,5},{7,4},{8,11},{9,10},{10,... | collective-permute-start | bytes 208904 | tf_op jit(solution)/shard_map/ppermute | solution.py:451
  29.4 4.3 %collective-permute-start.12 = (f32[128,128]{1,0:T(8,128)S(1)}, f32[128,128]{1,0:T(8,128)S(1)}, u32[]{:S(2)}, u32[]{:S(2)}) collective-permute-start(f32[128,128]{1,0:T(8,128)S(1)} %get-tuple-element.45), channel_id=1, source_target_pairs={{0,2},{1,3},{2,0},{3,1},{4,6},{5,7},{6,4},{7,5},{8,10},{9,11},{10,... | collective-permute-start | bytes 196616 | tf_op jit(solution)/shard_map/ppermute | solution.py:451
  30.9 4.2 %collective-permute-start.13 = (f32[128,128]{1,0:T(8,128)S(1)}, f32[128,128]{1,0:T(8,128)S(1)}, u32[]{:S(2)}, u32[]{:S(2)}) collective-permute-start(f32[128,128]{1,0:T(8,128)S(1)} %get-tuple-element.46), channel_id=1, source_target_pairs={{0,3},{1,2},{2,1},{3,0},{4,7},{5,6},{6,5},{7,4},{8,11},{9,10},{10,... | collective-permute-start | bytes 196616 | tf_op jit(solution)/shard_map/ppermute | solution.py:451
  30.9 4.2 %collective-permute-start.14 = (f32[128,128]{1,0:T(8,128)S(1)}, f32[128,128]{1,0:T(8,128)S(1)}, u32[]{:S(2)}, u32[]{:S(2)}) collective-permute-start(f32[128,128]{1,0:T(8,128)S(1)} %get-tuple-element.48), channel_id=1, source_target_pairs={{0,1},{1,0},{2,3},{3,2},{4,5},{5,4},{6,7},{7,6},{8,9},{9,8},{10,11... | collective-permute-start | bytes 196616 | tf_op jit(solution)/shard_map/ppermute | solution.py:451

commit v11 on v8

--- a/solution.py
+++ b/solution.py
@@ -134,6 +134,10 @@
         copy.wait()
     got_probe.wait()
     got_cot.wait()
+    got_row.wait()
+    got_col.wait()
+    got_index.wait()
+    got_count.wait()
     for s in order:
         source = jnp.concatenate([obj_ref[0, 0, s], obj_ref[0, 1, s]], 0)
         window[s] = dot(source, cut).astype(bf16)
@@ -218,10 +222,6 @@
                             top : top + block_rows, j * block_cols : (j + 1) * block_cols
                         ]
 
-    got_row.wait()
-    got_col.wait()
-    got_index.wait()
-    got_count.wait()
     tiles = row_ref.shape[0]
     batch = 8
     wide = batch * block_rows
@@ -290,6 +290,22 @@
         put(k, 0, capacity, jnp.concatenate([marks, jnp.zeros_like(marks)], 1))
 
 
+def keep_until(value, after):
+    anywhere = pl.BlockSpec(memory_space=pl.ANY)
+
+    def kernel(value_ref, after_ref, out_ref):
+        pass
+
+    return pl.pallas_call(
+        kernel,
+        out_shape=jax.ShapeDtypeStruct(value.shape, value.dtype),
+        in_specs=[anywhere] * 2,
+        out_specs=anywhere,
+        input_output_aliases={0: 0},
+        name="keep",
+    )(value, after)
+
+
 def join_kernel(base, first_ref, got_ref, *refs):
     count = len(refs) // 2
     for part, out in zip(refs[:count], refs[count:]):
@@ -408,7 +424,8 @@
     mark = jax.ShapeDtypeStruct((sources, CHUNK_ROWS, block_cols), f32)
     padded = jax.ShapeDtypeStruct(((each + 1) * CHUNK_ROWS, block_cols), f32)
     mine, other = held[: len(heights)], held[len(heights) :]
-    got = [lax.ppermute(half, "rep", swap) for half in other]
+    got = [lax.ppermute(other[0], "rep", swap)]
+    got.append(lax.ppermute(keep_until(other[1], got[0]), "rep", swap))
 
     def send(block, step):
         ring = [(p, partner(p, step, peers)) for p in range(peers)]

time: 32.6 us -> 34.1 us (1.046)
  local copies, waits for them, and re-layouts: 0 us -> 1.4 us
  waiting for transfers between devices: 10.4 us -> 9.08 us
  other arithmetic: 0.04 us -> 0.96 us
  starting transfers between devices: 14.8 us -> 15.2 us
    unnamed x0 -> x4, local copies, waits for them, and re-layouts: none -> 1.4 us
    add x2, other arithmetic: 0.04 us -> 0.96 us  [on_device(): block = mine[k] + got[h][at:at + tall]]
    ppermute x6, waiting for transfers between devices: 5.4 us -> 4.55 us  [send(): return lax.ppermute(block, 'slab', ring)]
    ppermute x2, waiting for transfers between devices: 1.48 us -> 1 us  [the longest x1 1 us: on_device(): got = [lax.ppermute(other[0], 'rep', swap)]]
  transfers between devices with their start and end apart: 14 -> 14, of which waited for: 7 -> 6; matrix products, arithmetic and copies ran while one was open for 0% -> 3% of each run, Pallas kernels for 2% -> 2%
where the time goes in v11:
time: 34.1 us; the launch traced here: 33.9 us
  starting transfers between devices  15.2 us (45%)
  waiting for transfers between devices  9.08 us (27%)
  Pallas kernels  7.2 us (21%)
  local copies, waits for them, and re-layouts  1.4 us (4%)
  other arithmetic  0.96 us (3%)
    ppermute x6, starting transfers between devices, send(): return lax.ppermute(block, 'slab', ring)  10.2 us
    pallas_call x1, Pallas kernels, on_device(): pl.pallas_call(functools.partial(frame_kernel, shifts), out_shape=shapes,...  5.84 us
    ppermute x6, waiting for transfers between devices, send(): return lax.ppermute(block, 'slab', ring)  4.55 us
    ppermute x6, starting transfers between devices, share_out(): return lax.ppermute(part, ('tilt', 'rep'), route)  4.14 us
    ppermute x6, waiting for transfers between devices, share_out(): return lax.ppermute(part, ('tilt', 'rep'), route)  3.53 us
    unnamed x4, local copies, waits for them, and re-layouts  1.4 us
    ppermute x1, waiting for transfers between devices, on_device(): got = [lax.ppermute(other[0], 'rep', swap)]  1 us
    add x2, other arithmetic, on_device(): block = mine[k] + got[h][at:at + tall]  0.96 us
  transfers between devices with their start and end apart: 14, of which 6 were waited for; matrix products, arithmetic and copies ran while one was open for 3% of the time, Pallas kernels for 2%

profile of v11, /device:TPU:0, one launch (start us, length us, event | category | flops | bytes accessed | tf_op | source)
XLA Modules:
  0.0 33.9 jit_solution(3558002327623418466)
XLA Ops:
  0.0 5.8 %frame.1 = (f32[136,128]{1,0:T(8,128)S(1)}, f32[136,128]{1,0:T(8,128)S(1)}, f32[136,128]{1,0:T(8,128)S(1)}, f32[136,128]{1,0:T(8,128)S(1)}, f32[128,128]{1,0:T(8...) custom-call(s32[1,4]{1,0:T(1,128)} %pos_hbm.1, ...), custom_call_target="tpu_custom_call" | custom-call | tf_op jit(solution)/shard_map/frame/pallas_call | solution.py:400
  5.9 0.7 %copy-done = f32[784,128]{1,0:T(8,128)} copy-done((f32[784,128]{1,0:T(8,128)}, f32[784,128]{1,0:T(8,128)S(1)}, u32[]{:S(2)}) %copy-start) | copy-done | bytes 401432
  6.6 0.5 %collective-permute-start = (f32[272,128]{1,0:T(8,128)S(1)}, f32[272,128]{1,0:T(8,128)S(1)}, u32[]{:S(2)}, u32[]{:S(2)}) collective-permute-start(f32[272,128]{1,0:T(8,128)S(1)} %get-tuple-element.28), channel_id=1, source_target_pairs={{0,1},{1,0},{2,3},{3,2},{4,5},{5,4},{6,7},{7,6},{8,9},{9,8},{10,11... | collective-permute-start | bytes 417800 | tf_op jit(solution)/shard_map/ppermute | solution.py:427
  7.1 1.0 %collective-permute-done.after_ref = f32[272,128]{1,0:T(8,128)S(1)} collective-permute-done((f32[272,128]{1,0:T(8,128)S(1)}, f32[272,128]{1,0:T(8,128)S(1)}, u32[]{:S(2)}, u32[]{:S(2)}) %collective-permute-start) | collective-permute-done | bytes 139296 | tf_op jit(solution)/shard_map/ppermute | solution.py:427
  8.1 0.7 %copy-done.1 = f32[272,128]{1,0:T(8,128)} copy-done((f32[272,128]{1,0:T(8,128)}, f32[272,128]{1,0:T(8,128)S(1)}, u32[]{:S(2)}) %copy-start.1) | copy-done | bytes 139288
  8.7 0.4 %collective-permute-start.3 = (f32[784,128]{1,0:T(8,128)}, f32[784,128]{1,0:T(8,128)S(1)}, u32[]{:S(2)}, u32[]{:S(2)}) collective-permute-start(f32[784,128]{1,0:T(8,128)} %keep.1), channel_id=1, source_target_pairs={{0,1},{1,0},{2,3},{3,2},{4,5},{5,4},{6,7},{7,6},{8,9},{9,8},{10,11... | collective-permute-start | bytes 1204232 | tf_op jit(solution)/shard_map/ppermute | solution.py:428
  9.1 0.9 %slice_add_fusion.2 = (f32[136,128]{1,0:T(8,128)S(1)}, f32[136,128]{1,0:T(8,128)S(1)}) fusion(f32[136,128]{1,0:T(8,128)S(1)} %get-tuple-element.29, f32[272,128]{1,0:T(8,128)} %copy-done.1, f32[136,128]{1,0:T(8,128)S(1)} %get-tuple-element.27), kind=kLoop, calls=%fused_computation.2 | loop fusion | flops 34816 | bytes 417792 | tf_op jit(solution)/shard_map/add | solution.py:437
  10.0 4.8 %collective-permute-start.2 = (f32[136,128]{1,0:T(8,128)S(1)}, f32[136,128]{1,0:T(8,128)S(1)}, u32[]{:S(2)}, u32[]{:S(2)}) collective-permute-start(f32[136,128]{1,0:T(8,128)S(1)} %get-tuple-element.51), channel_id=1, source_target_pairs={{0,12},{4,8},{8,4},{12,0},{1,13},{5,9},{9,5},{13,1},{2,14},{6,10},... | collective-permute-start | bytes 208904 | tf_op jit(solution)/shard_map/ppermute | solution.py:432
  14.9 0.7 %collective-permute-start.4 = (f32[136,128]{1,0:T(8,128)S(1)}, f32[136,128]{1,0:T(8,128)S(1)}, u32[]{:S(2)}, u32[]{:S(2)}) collective-permute-start(f32[136,128]{1,0:T(8,128)S(1)} %get-tuple-element.50), channel_id=1, source_target_pairs={{0,4},{4,0},{8,12},{12,8},{1,5},{5,1},{9,13},{13,9},{2,6},{6,2},{1... | collective-permute-start | bytes 208904 | tf_op jit(solution)/shard_map/ppermute | solution.py:432
  15.6 2.2 %collective-permute-done.2.refs_1_.first_ref = f32[136,128]{1,0:T(8,128)S(1)} collective-permute-done((f32[136,128]{1,0:T(8,128)S(1)}, f32[136,128]{1,0:T(8,128)S(1)}, u32[]{:S(2)}, u32[]{:S(2)}) %collective-permute-start.2) | collective-permute-done | bytes 69664 | tf_op jit(solution)/shard_map/ppermute | solution.py:432
  17.8 4.0 %collective-permute-start.9 = (f32[128,128]{1,0:T(8,128)S(1)}, f32[128,128]{1,0:T(8,128)S(1)}, u32[]{:S(2)}, u32[]{:S(2)}) collective-permute-start(f32[128,128]{1,0:T(8,128)S(1)} %get-tuple-element.41), channel_id=1, source_target_pairs={{0,12},{4,8},{8,4},{12,0},{1,13},{5,9},{9,5},{13,1},{2,14},{6,10},... | collective-permute-start | bytes 196616 | tf_op jit(solution)/shard_map/ppermute | solution.py:432
  21.8 0.7 %collective-permute-start.8 = (f32[128,128]{1,0:T(8,128)S(1)}, f32[128,128]{1,0:T(8,128)S(1)}, u32[]{:S(2)}, u32[]{:S(2)}) collective-permute-start(f32[128,128]{1,0:T(8,128)S(1)} %join.2), channel_id=1, source_target_pairs={{0,8},{4,12},{8,0},{12,4},{1,9},{5,13},{9,1},{13,5},{2,10},{6,14},... | collective-permute-start | bytes 196616 | tf_op jit(solution)/shard_map/ppermute | solution.py:432
  22.6 0.3 place.2
  22.9 0.1 collective-permute-start.7
  22.9 1.6 %collective-permute-start.5 = (f32[136,128]{1,0:T(8,128)S(1)}, f32[136,128]{1,0:T(8,128)S(1)}, u32[]{:S(2)}, u32[]{:S(2)}) collective-permute-start(f32[136,128]{1,0:T(8,128)S(1)} %get-tuple-element.33), channel_id=1, source_target_pairs={{0,2},{1,3},{2,0},{3,1},{4,6},{5,7},{6,4},{7,5},{8,10},{9,11},{10,... | collective-permute-start | bytes 208904 | tf_op jit(solution)/shard_map/ppermute | solution.py:472
  24.5 0.3 collective-permute-start.6
  24.8 1.5 %collective-permute-done.10.refs_2_ = f32[128,128]{1,0:T(8,128)S(1)} collective-permute-done((f32[128,128]{1,0:T(8,128)S(1)}, f32[128,128]{1,0:T(8,128)S(1)}, u32[]{:S(2)}, u32[]{:S(2)}) %collective-permute-start.10) | collective-permute-done | bytes 65568 | tf_op jit(solution)/shard_map/ppermute | solution.py:432
  26.3 0.8 %collective-permute-done.8.refs_0_ = f32[128,128]{1,0:T(8,128)S(1)} collective-permute-done((f32[128,128]{1,0:T(8,128)S(1)}, f32[128,128]{1,0:T(8,128)S(1)}, u32[]{:S(2)}, u32[]{:S(2)}) %collective-permute-start.8) | collective-permute-done | bytes 65568 | tf_op jit(solution)/shard_map/ppermute | solution.py:432
  27.1 0.3 place.3
  27.4 1.6 %collective-permute-start.11 = (f32[128,128]{1,0:T(8,128)S(1)}, f32[128,128]{1,0:T(8,128)S(1)}, u32[]{:S(2)}, u32[]{:S(2)}) collective-permute-start(f32[128,128]{1,0:T(8,128)S(1)} %get-tuple-element.45), channel_id=1, source_target_pairs={{0,2},{1,3},{2,0},{3,1},{4,6},{5,7},{6,4},{7,5},{8,10},{9,11},{10,... | collective-permute-start | bytes 196616 | tf_op jit(solution)/shard_map/ppermute | solution.py:472
  29.0 0.6 %collective-permute-start.13 = (f32[128,128]{1,0:T(8,128)S(1)}, f32[128,128]{1,0:T(8,128)S(1)}, u32[]{:S(2)}, u32[]{:S(2)}) collective-permute-start(f32[128,128]{1,0:T(8,128)S(1)} %get-tuple-element.48), channel_id=1, source_target_pairs={{0,1},{1,0},{2,3},{3,2},{4,5},{5,4},{6,7},{7,6},{8,9},{9,8},{10,11... | collective-permute-start | bytes 196616 | tf_op jit(solution)/shard_map/ppermute | solution.py:472
  29.6 2.1 %collective-permute-done.11.refs_4_ = f32[128,128]{1,0:T(8,128)S(1)} collective-permute-done((f32[128,128]{1,0:T(8,128)S(1)}, f32[128,128]{1,0:T(8,128)S(1)}, u32[]{:S(2)}, u32[]{:S(2)}) %collective-permute-start.11) | collective-permute-done | bytes 65568 | tf_op jit(solution)/shard_map/ppermute | solution.py:472
  31.7 1.4 %collective-permute-done.12.refs_5_ = f32[128,128]{1,0:T(8,128)S(1)} collective-permute-done((f32[128,128]{1,0:T(8,128)S(1)}, f32[128,128]{1,0:T(8,128)S(1)}, u32[]{:S(2)}, u32[]{:S(2)}) %collective-permute-start.12) | collective-permute-done | bytes 65568 | tf_op jit(solution)/shard_map/ppermute | solution.py:472
  33.1 0.7 %total.1 = f32[16,2,16,128]{3,2,1,0:T(8,128)} custom-call(f32[136,128]{1,0:T(8,128)S(1)} %collective-permute-done.5.refs_0_, f32[136,128]{1,0:T(8,128)S(1)} %collective-permute-done.6.refs_1_, f32[128,128]{1,0:T(8,128)S(1)} %get-tuple-element.35.refs_2_, f32[128,128]{1,0:T(8,128)S(1)} %collective-permute-done.7.refs_5_.refs_3_, ...), custom_call_target="tpu_custom_call" | custom-call | tf_op jit(solution)/shard_map/total/pallas_call | solution.py:483
  (17 shorter events, 0.1 us)
Async XLA Ops:
  5.8 0.8 %copy-start = (f32[784,128]{1,0:T(8,128)}, f32[784,128]{1,0:T(8,128)S(1)}, u32[]{:S(2)}) copy-start(f32[784,128]{1,0:T(8,128)S(1)} %get-tuple-element.31.value_ref) | copy-start | bytes 1204228
  6.6 1.4 %collective-permute-start = (f32[272,128]{1,0:T(8,128)S(1)}, f32[272,128]{1,0:T(8,128)S(1)}, u32[]{:S(2)}, u32[]{:S(2)}) collective-permute-start(f32[272,128]{1,0:T(8,128)S(1)} %get-tuple-element.28), channel_id=1, source_target_pairs={{0,1},{1,0},{2,3},{3,2},{4,5},{5,4},{6,7},{7,6},{8,9},{9,8},{10,11... | collective-permute-start | bytes 417800 | tf_op jit(solution)/shard_map/ppermute | solution.py:427
  8.1 0.7 %copy-start.1 = (f32[272,128]{1,0:T(8,128)}, f32[272,128]{1,0:T(8,128)S(1)}, u32[]{:S(2)}) copy-start(f32[272,128]{1,0:T(8,128)S(1)} %collective-permute-done.after_ref) | copy-start | bytes 417796
  8.7 6.1 %collective-permute-start.3 = (f32[784,128]{1,0:T(8,128)}, f32[784,128]{1,0:T(8,128)S(1)}, u32[]{:S(2)}, u32[]{:S(2)}) collective-permute-start(f32[784,128]{1,0:T(8,128)} %keep.1), channel_id=1, source_target_pairs={{0,1},{1,0},{2,3},{3,2},{4,5},{5,4},{6,7},{7,6},{8,9},{9,8},{10,11... | collective-permute-start | bytes 1204232 | tf_op jit(solution)/shard_map/ppermute | solution.py:428
  10.0 7.8 %collective-permute-start.2 = (f32[136,128]{1,0:T(8,128)S(1)}, f32[136,128]{1,0:T(8,128)S(1)}, u32[]{:S(2)}, u32[]{:S(2)}) collective-permute-start(f32[136,128]{1,0:T(8,128)S(1)} %get-tuple-element.51), channel_id=1, source_target_pairs={{0,12},{4,8},{8,4},{12,0},{1,13},{5,9},{9,5},{13,1},{2,14},{6,10},... | collective-permute-start | bytes 208904 | tf_op jit(solution)/shard_map/ppermute | solution.py:432
  14.8 7.0 %collective-permute-start.1 = (f32[136,128]{1,0:T(8,128)S(1)}, f32[136,128]{1,0:T(8,128)S(1)}, u32[]{:S(2)}, u32[]{:S(2)}) collective-permute-start(f32[136,128]{1,0:T(8,128)S(1)} %get-tuple-element.52), channel_id=1, source_target_pairs={{0,8},{4,12},{8,0},{12,4},{1,9},{5,13},{9,1},{13,5},{2,10},{6,14},... | collective-permute-start | bytes 208904 | tf_op jit(solution)/shard_map/ppermute | solution.py:432
  14.9 7.7 %collective-permute-start.4 = (f32[136,128]{1,0:T(8,128)S(1)}, f32[136,128]{1,0:T(8,128)S(1)}, u32[]{:S(2)}, u32[]{:S(2)}) collective-permute-start(f32[136,128]{1,0:T(8,128)S(1)} %get-tuple-element.50), channel_id=1, source_target_pairs={{0,4},{4,0},{8,12},{12,8},{1,5},{5,1},{9,13},{13,9},{2,6},{6,2},{1... | collective-permute-start | bytes 208904 | tf_op jit(solution)/shard_map/ppermute | solution.py:432
  17.8 6.7 %collective-permute-start.9 = (f32[128,128]{1,0:T(8,128)S(1)}, f32[128,128]{1,0:T(8,128)S(1)}, u32[]{:S(2)}, u32[]{:S(2)}) collective-permute-start(f32[128,128]{1,0:T(8,128)S(1)} %get-tuple-element.41), channel_id=1, source_target_pairs={{0,12},{4,8},{8,4},{12,0},{1,13},{5,9},{9,5},{13,1},{2,14},{6,10},... | collective-permute-start | bytes 196616 | tf_op jit(solution)/shard_map/ppermute | solution.py:432
  21.8 4.5 %collective-permute-start.10 = (f32[128,128]{1,0:T(8,128)S(1)}, f32[128,128]{1,0:T(8,128)S(1)}, u32[]{:S(2)}, u32[]{:S(2)}) collective-permute-start(f32[128,128]{1,0:T(8,128)S(1)} %get-tuple-element.42), channel_id=1, source_target_pairs={{0,4},{4,0},{8,12},{12,8},{1,5},{5,1},{9,13},{13,9},{2,6},{6,2},{1... | collective-permute-start | bytes 196616 | tf_op jit(solution)/shard_map/ppermute | solution.py:432
  21.8 5.2 %collective-permute-start.8 = (f32[128,128]{1,0:T(8,128)S(1)}, f32[128,128]{1,0:T(8,128)S(1)}, u32[]{:S(2)}, u32[]{:S(2)}) collective-permute-start(f32[128,128]{1,0:T(8,128)S(1)} %join.2), channel_id=1, source_target_pairs={{0,8},{4,12},{8,0},{12,4},{1,9},{5,13},{9,1},{13,5},{2,10},{6,14},... | collective-permute-start | bytes 196616 | tf_op jit(solution)/shard_map/ppermute | solution.py:432
  22.9 4.2 %collective-permute-start.7 = (f32[128,128]{1,0:T(8,128)S(1)}, f32[128,128]{1,0:T(8,128)S(1)}, u32[]{:S(2)}, u32[]{:S(2)}) collective-permute-start(f32[128,128]{1,0:T(8,128)S(1)} %get-tuple-element.36), channel_id=1, source_target_pairs={{0,1},{1,0},{2,3},{3,2},{4,5},{5,4},{6,7},{7,6},{8,9},{9,8},{10,11... | collective-permute-start | bytes 196616 | tf_op jit(solution)/shard_map/ppermute | solution.py:472
  22.9 6.7 %collective-permute-start.5 = (f32[136,128]{1,0:T(8,128)S(1)}, f32[136,128]{1,0:T(8,128)S(1)}, u32[]{:S(2)}, u32[]{:S(2)}) collective-permute-start(f32[136,128]{1,0:T(8,128)S(1)} %get-tuple-element.33), channel_id=1, source_target_pairs={{0,2},{1,3},{2,0},{3,1},{4,6},{5,7},{6,4},{7,5},{8,10},{9,11},{10,... | collective-permute-start | bytes 208904 | tf_op jit(solution)/shard_map/ppermute | solution.py:472
  24.5 5.1 %collective-permute-start.6 = (f32[136,128]{1,0:T(8,128)S(1)}, f32[136,128]{1,0:T(8,128)S(1)}, u32[]{:S(2)}, u32[]{:S(2)}) collective-permute-start(f32[136,128]{1,0:T(8,128)S(1)} %get-tuple-element.34), channel_id=1, source_target_pairs={{0,3},{1,2},{2,1},{3,0},{4,7},{5,6},{6,5},{7,4},{8,11},{9,10},{10,... | collective-permute-start | bytes 208904 | tf_op jit(solution)/shard_map/ppermute | solution.py:472
  27.4 4.3 %collective-permute-start.11 = (f32[128,128]{1,0:T(8,128)S(1)}, f32[128,128]{1,0:T(8,128)S(1)}, u32[]{:S(2)}, u32[]{:S(2)}) collective-permute-start(f32[128,128]{1,0:T(8,128)S(1)} %get-tuple-element.45), channel_id=1, source_target_pairs={{0,2},{1,3},{2,0},{3,1},{4,6},{5,7},{6,4},{7,5},{8,10},{9,11},{10,... | collective-permute-start | bytes 196616 | tf_op jit(solution)/shard_map/ppermute | solution.py:472
  29.0 4.2 %collective-permute-start.12 = (f32[128,128]{1,0:T(8,128)S(1)}, f32[128,128]{1,0:T(8,128)S(1)}, u32[]{:S(2)}, u32[]{:S(2)}) collective-permute-start(f32[128,128]{1,0:T(8,128)S(1)} %get-tuple-element.46), channel_id=1, source_target_pairs={{0,3},{1,2},{2,1},{3,0},{4,7},{5,6},{6,5},{7,4},{8,11},{9,10},{10,... | collective-permute-start | bytes 196616 | tf_op jit(solution)/shard_map/ppermute | solution.py:472
  29.0 4.2 %collective-permute-start.13 = (f32[128,128]{1,0:T(8,128)S(1)}, f32[128,128]{1,0:T(8,128)S(1)}, u32[]{:S(2)}, u32[]{:S(2)}) collective-permute-start(f32[128,128]{1,0:T(8,128)S(1)} %get-tuple-element.48), channel_id=1, source_target_pairs={{0,1},{1,0},{2,3},{3,2},{4,5},{5,4},{6,7},{7,6},{8,9},{9,8},{10,11... | collective-permute-start | bytes 196616 | tf_op jit(solution)/shard_map/ppermute | solution.py:472

commit v12 on v11

--- a/solution.py
+++ b/solution.py
@@ -16,6 +16,7 @@
 HIGH = lax.Precision.HIGHEST
 SMEM = pltpu.SMEM
 VMEM = pltpu.VMEM
+LIMIT = pltpu.CompilerParams(vmem_limit_bytes=40 * 1024 * 1024)
 
 
 def dot(left, right, precision=None):
@@ -302,6 +303,7 @@
         in_specs=[anywhere] * 2,
         out_specs=anywhere,
         input_output_aliases={0: 0},
+        compiler_params=LIMIT,
         name="keep",
     )(value, after)
 
@@ -375,7 +377,6 @@
     windows, size = cotangent.shape[1], cotangent.shape[-1]
     f32, bf16 = jnp.float32, jnp.bfloat16
     hbm, vmem = pl.BlockSpec(memory_space=pltpu.HBM), pl.BlockSpec(memory_space=VMEM)
-    limit = pltpu.CompilerParams(vmem_limit_bytes=40 * 1024 * 1024)
     sources = len(shifts)
     lanes = capacity * CHUNK_ROWS
 
@@ -411,7 +412,7 @@
             VMEM(col_interp.shape, bf16),
             VMEM((row_interp.shape[0], block_rows, 8 * block_rows), f32),
         ],
-        compiler_params=limit,
+        compiler_params=LIMIT,
         name="frame",
     )(*[pltpu.with_memory_space_constraint(x, pltpu.HBM) for x in scalars + [x for x, _ in fetched]])
 
@@ -443,7 +444,7 @@
             out_shape=shapes[sources : 2 * sources][part],
             in_specs=[vmem] * (len(late) + 2),
             out_specs=[vmem] * len(late),
-            compiler_params=limit,
+            compiler_params=LIMIT,
             name="join",
         )(after, got[1], *late)
 
@@ -456,7 +457,7 @@
             out_shape=shapes,
             in_specs=[vmem] * (sources + len(extra)),
             out_specs=[vmem] * len(shapes),
-            compiler_params=limit,
+            compiler_params=LIMIT,
             name="place",
         )(*blocks, *extra)
 
@@ -485,7 +486,7 @@
         out_shape=jax.ShapeDtypeStruct((each, cores, block_rows, block_cols), f32),
         in_specs=[vmem] * len(extra),
         out_specs=vmem,
-        compiler_params=limit,
+        compiler_params=LIMIT,
         name="total",
     )(*extra)
 

time: 34.1 us -> 31.8 us (0.933)
  local copies, waits for them, and re-layouts: 1.4 us -> 0 us
  other arithmetic: 0.96 us -> 0.04 us
    unnamed x4 -> x0, local copies, waits for them, and re-layouts: 1.4 us -> none
    add x2, other arithmetic: 0.96 us -> 0.04 us  [on_device(): block = mine[k] + got[h][at:at + tall]]
  transfers between devices with their start and end apart: 14 -> 14, of which waited for: 6 -> 6; matrix products, arithmetic and copies ran while one was open for 3% -> 0% of each run, Pallas kernels for 2% -> 2%
where the time goes in v12:
time: 31.8 us; the launch traced here: 31.6 us
  starting transfers between devices  15.2 us (48%)
  waiting for transfers between devices  9.08 us (29%)
  Pallas kernels  7.24 us (23%)
    ppermute x6, starting transfers between devices, send(): return lax.ppermute(block, 'slab', ring)  10.2 us
    pallas_call x1, Pallas kernels, on_device(): pl.pallas_call(functools.partial(frame_kernel, shifts), out_shape=shapes,...  5.86 us
    ppermute x6, waiting for transfers between devices, send(): return lax.ppermute(block, 'slab', ring)  4.55 us
    ppermute x6, starting transfers between devices, share_out(): return lax.ppermute(part, ('tilt', 'rep'), route)  4.14 us
    ppermute x6, waiting for transfers between devices, share_out(): return lax.ppermute(part, ('tilt', 'rep'), route)  3.53 us
    ppermute x1, waiting for transfers between devices, on_device(): got = [lax.ppermute(other[0], 'rep', swap)]  1 us
    pallas_call x1, Pallas kernels, on_device(): pl.pallas_call(functools.partial(sum_kernel, owners), out_shape=jax.Shape...  0.75 us
  transfers between devices with their start and end apart: 14, of which 6 were waited for; matrix products, arithmetic and copies ran while one was open for 0% of the time, Pallas kernels for 2%

profile of v12, /device:TPU:0, one launch (start us, length us, event | category | flops | bytes accessed | tf_op | source)
XLA Modules:
  0.0 31.6 jit_solution(17341591488033332066)
XLA Ops:
  0.0 5.9 %frame.1 = (f32[136,128]{1,0:T(8,128)S(1)}, f32[136,128]{1,0:T(8,128)S(1)}, f32[136,128]{1,0:T(8,128)S(1)}, f32[136,128]{1,0:T(8,128)S(1)}, f32[128,128]{1,0:T(8...) custom-call(s32[1,4]{1,0:T(1,128)} %pos_hbm.1, ...), custom_call_target="tpu_custom_call" | custom-call | tf_op jit(solution)/shard_map/frame/pallas_call | solution.py:401
  5.9 0.5 %collective-permute-start = (f32[272,128]{1,0:T(8,128)S(1)}, f32[272,128]{1,0:T(8,128)S(1)}, u32[]{:S(2)}, u32[]{:S(2)}) collective-permute-start(f32[272,128]{1,0:T(8,128)S(1)} %get-tuple-element.28), channel_id=1, source_target_pairs={{0,1},{1,0},{2,3},{3,2},{4,5},{5,4},{6,7},{7,6},{8,9},{9,8},{10,11... | collective-permute-start | bytes 417800 | tf_op jit(solution)/shard_map/ppermute | solution.py:428
  6.4 1.0 %collective-permute-done.after_ref = f32[272,128]{1,0:T(8,128)S(1)} collective-permute-done((f32[272,128]{1,0:T(8,128)S(1)}, f32[272,128]{1,0:T(8,128)S(1)}, u32[]{:S(2)}, u32[]{:S(2)}) %collective-permute-start) | collective-permute-done | bytes 139296 | tf_op jit(solution)/shard_map/ppermute | solution.py:428
  7.4 0.4 %collective-permute-start.3 = (f32[784,128]{1,0:T(8,128)S(1)}, f32[784,128]{1,0:T(8,128)S(1)}, u32[]{:S(2)}, u32[]{:S(2)}) collective-permute-start(f32[784,128]{1,0:T(8,128)S(1)} %keep.1), channel_id=1, source_target_pairs={{0,1},{1,0},{2,3},{3,2},{4,5},{5,4},{6,7},{7,6},{8,9},{9,8},{10,11... | collective-permute-start | bytes 1204232 | tf_op jit(solution)/shard_map/ppermute | solution.py:429
  7.8 4.8 %collective-permute-start.2 = (f32[136,128]{1,0:T(8,128)S(1)}, f32[136,128]{1,0:T(8,128)S(1)}, u32[]{:S(2)}, u32[]{:S(2)}) collective-permute-start(f32[136,128]{1,0:T(8,128)S(1)} %get-tuple-element.51), channel_id=1, source_target_pairs={{0,12},{4,8},{8,4},{12,0},{1,13},{5,9},{9,5},{13,1},{2,14},{6,10},... | collective-permute-start | bytes 208904 | tf_op jit(solution)/shard_map/ppermute | solution.py:433
  12.6 0.0 collective-permute-start.1
  12.6 0.0 collective-permute-done.3.got_ref
  12.6 0.7 %collective-permute-start.4 = (f32[136,128]{1,0:T(8,128)S(1)}, f32[136,128]{1,0:T(8,128)S(1)}, u32[]{:S(2)}, u32[]{:S(2)}) collective-permute-start(f32[136,128]{1,0:T(8,128)S(1)} %get-tuple-element.50), channel_id=1, source_target_pairs={{0,4},{4,0},{8,12},{12,8},{1,5},{5,1},{9,13},{13,9},{2,6},{6,2},{1... | collective-permute-start | bytes 208904 | tf_op jit(solution)/shard_map/ppermute | solution.py:433
  13.3 2.2 %collective-permute-done.2.refs_1_.first_ref = f32[136,128]{1,0:T(8,128)S(1)} collective-permute-done((f32[136,128]{1,0:T(8,128)S(1)}, f32[136,128]{1,0:T(8,128)S(1)}, u32[]{:S(2)}, u32[]{:S(2)}) %collective-permute-start.2) | collective-permute-done | bytes 69664 | tf_op jit(solution)/shard_map/ppermute | solution.py:433
  15.6 4.0 %collective-permute-start.9 = (f32[128,128]{1,0:T(8,128)S(1)}, f32[128,128]{1,0:T(8,128)S(1)}, u32[]{:S(2)}, u32[]{:S(2)}) collective-permute-start(f32[128,128]{1,0:T(8,128)S(1)} %get-tuple-element.41), channel_id=1, source_target_pairs={{0,12},{4,8},{8,4},{12,0},{1,13},{5,9},{9,5},{13,1},{2,14},{6,10},... | collective-permute-start | bytes 196616 | tf_op jit(solution)/shard_map/ppermute | solution.py:433
  19.6 0.0 collective-permute-start.10
  19.6 0.7 %collective-permute-start.8 = (f32[128,128]{1,0:T(8,128)S(1)}, f32[128,128]{1,0:T(8,128)S(1)}, u32[]{:S(2)}, u32[]{:S(2)}) collective-permute-start(f32[128,128]{1,0:T(8,128)S(1)} %join.2), channel_id=1, source_target_pairs={{0,8},{4,12},{8,0},{12,4},{1,9},{5,13},{9,1},{13,5},{2,10},{6,14},... | collective-permute-start | bytes 196616 | tf_op jit(solution)/shard_map/ppermute | solution.py:433
  20.3 0.3 place.2
  20.6 0.1 collective-permute-start.7
  20.7 1.6 %collective-permute-start.5 = (f32[136,128]{1,0:T(8,128)S(1)}, f32[136,128]{1,0:T(8,128)S(1)}, u32[]{:S(2)}, u32[]{:S(2)}) collective-permute-start(f32[136,128]{1,0:T(8,128)S(1)} %get-tuple-element.33), channel_id=1, source_target_pairs={{0,2},{1,3},{2,0},{3,1},{4,6},{5,7},{6,4},{7,5},{8,10},{9,11},{10,... | collective-permute-start | bytes 208904 | tf_op jit(solution)/shard_map/ppermute | solution.py:473
  22.2 0.3 collective-permute-start.6
  22.5 1.5 %collective-permute-done.10.refs_2_ = f32[128,128]{1,0:T(8,128)S(1)} collective-permute-done((f32[128,128]{1,0:T(8,128)S(1)}, f32[128,128]{1,0:T(8,128)S(1)}, u32[]{:S(2)}, u32[]{:S(2)}) %collective-permute-start.10) | collective-permute-done | bytes 65568 | tf_op jit(solution)/shard_map/ppermute | solution.py:433
  24.0 0.8 %collective-permute-done.8.refs_0_ = f32[128,128]{1,0:T(8,128)S(1)} collective-permute-done((f32[128,128]{1,0:T(8,128)S(1)}, f32[128,128]{1,0:T(8,128)S(1)}, u32[]{:S(2)}, u32[]{:S(2)}) %collective-permute-start.8) | collective-permute-done | bytes 65568 | tf_op jit(solution)/shard_map/ppermute | solution.py:433
  24.8 0.3 place.3
  25.1 1.6 %collective-permute-start.11 = (f32[128,128]{1,0:T(8,128)S(1)}, f32[128,128]{1,0:T(8,128)S(1)}, u32[]{:S(2)}, u32[]{:S(2)}) collective-permute-start(f32[128,128]{1,0:T(8,128)S(1)} %get-tuple-element.45), channel_id=1, source_target_pairs={{0,2},{1,3},{2,0},{3,1},{4,6},{5,7},{6,4},{7,5},{8,10},{9,11},{10,... | collective-permute-start | bytes 196616 | tf_op jit(solution)/shard_map/ppermute | solution.py:473
  26.7 0.6 %collective-permute-start.13 = (f32[128,128]{1,0:T(8,128)S(1)}, f32[128,128]{1,0:T(8,128)S(1)}, u32[]{:S(2)}, u32[]{:S(2)}) collective-permute-start(f32[128,128]{1,0:T(8,128)S(1)} %get-tuple-element.48), channel_id=1, source_target_pairs={{0,1},{1,0},{2,3},{3,2},{4,5},{5,4},{6,7},{7,6},{8,9},{9,8},{10,11... | collective-permute-start | bytes 196616 | tf_op jit(solution)/shard_map/ppermute | solution.py:473
  27.4 2.1 %collective-permute-done.11.refs_4_ = f32[128,128]{1,0:T(8,128)S(1)} collective-permute-done((f32[128,128]{1,0:T(8,128)S(1)}, f32[128,128]{1,0:T(8,128)S(1)}, u32[]{:S(2)}, u32[]{:S(2)}) %collective-permute-start.11) | collective-permute-done | bytes 65568 | tf_op jit(solution)/shard_map/ppermute | solution.py:473
  29.5 1.4 %collective-permute-done.12.refs_5_ = f32[128,128]{1,0:T(8,128)S(1)} collective-permute-done((f32[128,128]{1,0:T(8,128)S(1)}, f32[128,128]{1,0:T(8,128)S(1)}, u32[]{:S(2)}, u32[]{:S(2)}) %collective-permute-start.12) | collective-permute-done | bytes 65568 | tf_op jit(solution)/shard_map/ppermute | solution.py:473
  30.9 0.7 %total.1 = f32[16,2,16,128]{3,2,1,0:T(8,128)} custom-call(f32[136,128]{1,0:T(8,128)S(1)} %collective-permute-done.5.refs_0_, f32[136,128]{1,0:T(8,128)S(1)} %collective-permute-done.6.refs_1_, f32[128,128]{1,0:T(8,128)S(1)} %get-tuple-element.35.refs_2_, f32[128,128]{1,0:T(8,128)S(1)} %collective-permute-done.7.refs_5_.refs_3_, ...), custom_call_target="tpu_custom_call" | custom-call | tf_op jit(solution)/shard_map/total/pallas_call | solution.py:484
  (13 shorter events, 0.1 us)
Async XLA Ops:
  5.9 1.5 %collective-permute-start = (f32[272,128]{1,0:T(8,128)S(1)}, f32[272,128]{1,0:T(8,128)S(1)}, u32[]{:S(2)}, u32[]{:S(2)}) collective-permute-start(f32[272,128]{1,0:T(8,128)S(1)} %get-tuple-element.28), channel_id=1, source_target_pairs={{0,1},{1,0},{2,3},{3,2},{4,5},{5,4},{6,7},{7,6},{8,9},{9,8},{10,11... | collective-permute-start | bytes 417800 | tf_op jit(solution)/shard_map/ppermute | solution.py:428
  7.4 5.2 %collective-permute-start.3 = (f32[784,128]{1,0:T(8,128)S(1)}, f32[784,128]{1,0:T(8,128)S(1)}, u32[]{:S(2)}, u32[]{:S(2)}) collective-permute-start(f32[784,128]{1,0:T(8,128)S(1)} %keep.1), channel_id=1, source_target_pairs={{0,1},{1,0},{2,3},{3,2},{4,5},{5,4},{6,7},{7,6},{8,9},{9,8},{10,11... | collective-permute-start | bytes 1204232 | tf_op jit(solution)/shard_map/ppermute | solution.py:429
  7.8 7.8 %collective-permute-start.2 = (f32[136,128]{1,0:T(8,128)S(1)}, f32[136,128]{1,0:T(8,128)S(1)}, u32[]{:S(2)}, u32[]{:S(2)}) collective-permute-start(f32[136,128]{1,0:T(8,128)S(1)} %get-tuple-element.51), channel_id=1, source_target_pairs={{0,12},{4,8},{8,4},{12,0},{1,13},{5,9},{9,5},{13,1},{2,14},{6,10},... | collective-permute-start | bytes 208904 | tf_op jit(solution)/shard_map/ppermute | solution.py:433
  12.6 7.0 %collective-permute-start.1 = (f32[136,128]{1,0:T(8,128)S(1)}, f32[136,128]{1,0:T(8,128)S(1)}, u32[]{:S(2)}, u32[]{:S(2)}) collective-permute-start(f32[136,128]{1,0:T(8,128)S(1)} %get-tuple-element.52), channel_id=1, source_target_pairs={{0,8},{4,12},{8,0},{12,4},{1,9},{5,13},{9,1},{13,5},{2,10},{6,14},... | collective-permute-start | bytes 208904 | tf_op jit(solution)/shard_map/ppermute | solution.py:433
  12.6 7.7 %collective-permute-start.4 = (f32[136,128]{1,0:T(8,128)S(1)}, f32[136,128]{1,0:T(8,128)S(1)}, u32[]{:S(2)}, u32[]{:S(2)}) collective-permute-start(f32[136,128]{1,0:T(8,128)S(1)} %get-tuple-element.50), channel_id=1, source_target_pairs={{0,4},{4,0},{8,12},{12,8},{1,5},{5,1},{9,13},{13,9},{2,6},{6,2},{1... | collective-permute-start | bytes 208904 | tf_op jit(solution)/shard_map/ppermute | solution.py:433
  15.6 6.7 %collective-permute-start.9 = (f32[128,128]{1,0:T(8,128)S(1)}, f32[128,128]{1,0:T(8,128)S(1)}, u32[]{:S(2)}, u32[]{:S(2)}) collective-permute-start(f32[128,128]{1,0:T(8,128)S(1)} %get-tuple-element.41), channel_id=1, source_target_pairs={{0,12},{4,8},{8,4},{12,0},{1,13},{5,9},{9,5},{13,1},{2,14},{6,10},... | collective-permute-start | bytes 196616 | tf_op jit(solution)/shard_map/ppermute | solution.py:433
  19.6 4.5 %collective-permute-start.10 = (f32[128,128]{1,0:T(8,128)S(1)}, f32[128,128]{1,0:T(8,128)S(1)}, u32[]{:S(2)}, u32[]{:S(2)}) collective-permute-start(f32[128,128]{1,0:T(8,128)S(1)} %get-tuple-element.42), channel_id=1, source_target_pairs={{0,4},{4,0},{8,12},{12,8},{1,5},{5,1},{9,13},{13,9},{2,6},{6,2},{1... | collective-permute-start | bytes 196616 | tf_op jit(solution)/shard_map/ppermute | solution.py:433
  19.6 5.3 %collective-permute-start.8 = (f32[128,128]{1,0:T(8,128)S(1)}, f32[128,128]{1,0:T(8,128)S(1)}, u32[]{:S(2)}, u32[]{:S(2)}) collective-permute-start(f32[128,128]{1,0:T(8,128)S(1)} %join.2), channel_id=1, source_target_pairs={{0,8},{4,12},{8,0},{12,4},{1,9},{5,13},{9,1},{13,5},{2,10},{6,14},... | collective-permute-start | bytes 196616 | tf_op jit(solution)/shard_map/ppermute | solution.py:433
  20.6 4.2 %collective-permute-start.7 = (f32[128,128]{1,0:T(8,128)S(1)}, f32[128,128]{1,0:T(8,128)S(1)}, u32[]{:S(2)}, u32[]{:S(2)}) collective-permute-start(f32[128,128]{1,0:T(8,128)S(1)} %get-tuple-element.36), channel_id=1, source_target_pairs={{0,1},{1,0},{2,3},{3,2},{4,5},{5,4},{6,7},{7,6},{8,9},{9,8},{10,11... | collective-permute-start | bytes 196616 | tf_op jit(solution)/shard_map/ppermute | solution.py:473
  20.7 6.7 %collective-permute-start.5 = (f32[136,128]{1,0:T(8,128)S(1)}, f32[136,128]{1,0:T(8,128)S(1)}, u32[]{:S(2)}, u32[]{:S(2)}) collective-permute-start(f32[136,128]{1,0:T(8,128)S(1)} %get-tuple-element.33), channel_id=1, source_target_pairs={{0,2},{1,3},{2,0},{3,1},{4,6},{5,7},{6,4},{7,5},{8,10},{9,11},{10,... | collective-permute-start | bytes 208904 | tf_op jit(solution)/shard_map/ppermute | solution.py:473
  22.2 5.1 %collective-permute-start.6 = (f32[136,128]{1,0:T(8,128)S(1)}, f32[136,128]{1,0:T(8,128)S(1)}, u32[]{:S(2)}, u32[]{:S(2)}) collective-permute-start(f32[136,128]{1,0:T(8,128)S(1)} %get-tuple-element.34), channel_id=1, source_target_pairs={{0,3},{1,2},{2,1},{3,0},{4,7},{5,6},{6,5},{7,4},{8,11},{9,10},{10,... | collective-permute-start | bytes 208904 | tf_op jit(solution)/shard_map/ppermute | solution.py:473
  25.1 4.3 %collective-permute-start.11 = (f32[128,128]{1,0:T(8,128)S(1)}, f32[128,128]{1,0:T(8,128)S(1)}, u32[]{:S(2)}, u32[]{:S(2)}) collective-permute-start(f32[128,128]{1,0:T(8,128)S(1)} %get-tuple-element.45), channel_id=1, source_target_pairs={{0,2},{1,3},{2,0},{3,1},{4,6},{5,7},{6,4},{7,5},{8,10},{9,11},{10,... | collective-permute-start | bytes 196616 | tf_op jit(solution)/shard_map/ppermute | solution.py:473
  26.7 4.2 %collective-permute-start.12 = (f32[128,128]{1,0:T(8,128)S(1)}, f32[128,128]{1,0:T(8,128)S(1)}, u32[]{:S(2)}, u32[]{:S(2)}) collective-permute-start(f32[128,128]{1,0:T(8,128)S(1)} %get-tuple-element.46), channel_id=1, source_target_pairs={{0,3},{1,2},{2,1},{3,0},{4,7},{5,6},{6,5},{7,4},{8,11},{9,10},{10,... | collective-permute-start | bytes 196616 | tf_op jit(solution)/shard_map/ppermute | solution.py:473
  26.7 4.2 %collective-permute-start.13 = (f32[128,128]{1,0:T(8,128)S(1)}, f32[128,128]{1,0:T(8,128)S(1)}, u32[]{:S(2)}, u32[]{:S(2)}) collective-permute-start(f32[128,128]{1,0:T(8,128)S(1)} %get-tuple-element.48), channel_id=1, source_target_pairs={{0,1},{1,0},{2,3},{3,2},{4,5},{5,4},{6,7},{7,6},{8,9},{9,8},{10,11... | collective-permute-start | bytes 196616 | tf_op jit(solution)/shard_map/ppermute | solution.py:473

commit v13 on v12

--- a/solution.py
+++ b/solution.py
@@ -472,11 +472,10 @@
         ]
         return lax.ppermute(part, ("tilt", "rep"), route)
 
-    joined = []
-    for k in range(far):
-        joined += join(first[k], slice(k, k + 1 if k + 1 < far else sources))
+    joined = [block for k in range(far) for block in join(first[k], slice(k, k + 1))]
+    *parts, marks = place(first, [], 0)
+    joined += join(marks, slice(far, sources))
     second = [send(block, k) if k else block for block, k in zip(joined, shifts)]
-    *parts, marks = place(first, [], 0)
     extra = [share_out(part, owner) for part, owner in zip(parts, owners)]
     held = [part for part, (dt, dr) in zip(extra, owners) if dr and not dt]
     late = place(second, [marks, *held], 1)

time: 31.8 us -> 34.7 us (1.091)
  waiting for transfers between devices: 9.08 us -> 13.4 us
  starting transfers between devices: 15.2 us -> 13.9 us
    ppermute x6, waiting for transfers between devices: 4.55 us -> 8.66 us  [send(): return lax.ppermute(block, 'slab', ring)]
    ppermute x6, starting transfers between devices: 10.2 us -> 9.2 us  [send(): return lax.ppermute(block, 'slab', ring)]
    ppermute x6, starting transfers between devices: 4.14 us -> 3.77 us  [share_out(): return lax.ppermute(part, ('tilt', 'rep'), route)]
  transfers between devices with their start and end apart: 14 -> 14, of which waited for: 6 -> 7; matrix products, arithmetic and copies ran while one was open for 0% -> 0% of each run, Pallas kernels for 2% -> 2%
where the time goes in v13:
time: 34.7 us; the launch traced here: 34.6 us
  starting transfers between devices  13.9 us (40%)
  waiting for transfers between devices  13.4 us (39%)
  Pallas kernels  7.22 us (21%)
    ppermute x6, starting transfers between devices, send(): return lax.ppermute(block, 'slab', ring)  9.2 us
    ppermute x6, waiting for transfers between devices, send(): return lax.ppermute(block, 'slab', ring)  8.66 us
    pallas_call x1, Pallas kernels, on_device(): pl.pallas_call(functools.partial(frame_kernel, shifts), out_shape=shapes,...  5.86 us
    ppermute x6, starting transfers between devices, share_out(): return lax.ppermute(part, ('tilt', 'rep'), route)  3.77 us
    ppermute x6, waiting for transfers between devices, share_out(): return lax.ppermute(part, ('tilt', 'rep'), route)  3.74 us
    ppermute x1, waiting for transfers between devices, on_device(): got = [lax.ppermute(other[0], 'rep', swap)]  1 us
    pallas_call x1, Pallas kernels, on_device(): pl.pallas_call(functools.partial(sum_kernel, owners), out_shape=jax.Shape...  0.74 us
  transfers between devices with their start and end apart: 14, of which 7 were waited for; matrix products, arithmetic and copies ran while one was open for 0% of the time, Pallas kernels for 2%

profile of v13, /device:TPU:0, one launch (start us, length us, event | category | flops | bytes accessed | tf_op | source)
XLA Modules:
  0.0 34.6 jit_solution(8950075833265320790)
XLA Ops:
  0.0 5.9 %frame.1 = (f32[136,128]{1,0:T(8,128)S(1)}, f32[136,128]{1,0:T(8,128)S(1)}, f32[136,128]{1,0:T(8,128)S(1)}, f32[136,128]{1,0:T(8,128)S(1)}, f32[128,128]{1,0:T(8...) custom-call(s32[1,4]{1,0:T(1,128)} %pos_hbm.1, ...), custom_call_target="tpu_custom_call" | custom-call | tf_op jit(solution)/shard_map/frame/pallas_call | solution.py:401
  5.9 0.5 %collective-permute-start = (f32[272,128]{1,0:T(8,128)S(1)}, f32[272,128]{1,0:T(8,128)S(1)}, u32[]{:S(2)}, u32[]{:S(2)}) collective-permute-start(f32[272,128]{1,0:T(8,128)S(1)} %get-tuple-element.27), channel_id=1, source_target_pairs={{0,1},{1,0},{2,3},{3,2},{4,5},{5,4},{6,7},{7,6},{8,9},{9,8},{10,11... | collective-permute-start | bytes 417800 | tf_op jit(solution)/shard_map/ppermute | solution.py:428
  6.4 1.0 %collective-permute-done.after_ref = f32[272,128]{1,0:T(8,128)S(1)} collective-permute-done((f32[272,128]{1,0:T(8,128)S(1)}, f32[272,128]{1,0:T(8,128)S(1)}, u32[]{:S(2)}, u32[]{:S(2)}) %collective-permute-start) | collective-permute-done | bytes 139296 | tf_op jit(solution)/shard_map/ppermute | solution.py:428
  7.4 0.4 %collective-permute-start.3 = (f32[784,128]{1,0:T(8,128)S(1)}, f32[784,128]{1,0:T(8,128)S(1)}, u32[]{:S(2)}, u32[]{:S(2)}) collective-permute-start(f32[784,128]{1,0:T(8,128)S(1)} %keep.1), channel_id=1, source_target_pairs={{0,1},{1,0},{2,3},{3,2},{4,5},{5,4},{6,7},{7,6},{8,9},{9,8},{10,11... | collective-permute-start | bytes 1204232 | tf_op jit(solution)/shard_map/ppermute | solution.py:429
  7.8 4.8 %collective-permute-start.2 = (f32[136,128]{1,0:T(8,128)S(1)}, f32[136,128]{1,0:T(8,128)S(1)}, u32[]{:S(2)}, u32[]{:S(2)}) collective-permute-start(f32[136,128]{1,0:T(8,128)S(1)} %get-tuple-element.49), channel_id=1, source_target_pairs={{0,12},{4,8},{8,4},{12,0},{1,13},{5,9},{9,5},{13,1},{2,14},{6,10},... | collective-permute-start | bytes 208904 | tf_op jit(solution)/shard_map/ppermute | solution.py:433
  12.6 0.7 %collective-permute-start.4 = (f32[136,128]{1,0:T(8,128)S(1)}, f32[136,128]{1,0:T(8,128)S(1)}, u32[]{:S(2)}, u32[]{:S(2)}) collective-permute-start(f32[136,128]{1,0:T(8,128)S(1)} %get-tuple-element.48), channel_id=1, source_target_pairs={{0,4},{4,0},{8,12},{12,8},{1,5},{5,1},{9,13},{13,9},{2,6},{6,2},{1... | collective-permute-start | bytes 208904 | tf_op jit(solution)/shard_map/ppermute | solution.py:433
  13.3 5.6 %collective-permute-done.1.refs_0_.first_ref = f32[136,128]{1,0:T(8,128)S(1)} collective-permute-done((f32[136,128]{1,0:T(8,128)S(1)}, f32[136,128]{1,0:T(8,128)S(1)}, u32[]{:S(2)}, u32[]{:S(2)}) %collective-permute-start.1) | collective-permute-done | bytes 69664 | tf_op jit(solution)/shard_map/ppermute | solution.py:433
  18.9 1.2 %collective-permute-start.8 = (f32[128,128]{1,0:T(8,128)S(1)}, f32[128,128]{1,0:T(8,128)S(1)}, u32[]{:S(2)}, u32[]{:S(2)}) collective-permute-start(f32[128,128]{1,0:T(8,128)S(1)} %join.3), channel_id=1, source_target_pairs={{0,8},{4,12},{8,0},{12,4},{1,9},{5,13},{9,1},{13,5},{2,10},{6,14},... | collective-permute-start | bytes 196616 | tf_op jit(solution)/shard_map/ppermute | solution.py:433
  20.1 0.0 collective-permute-done.2.refs_1_.first_ref
  20.1 1.4 %collective-permute-start.9 = (f32[128,128]{1,0:T(8,128)S(1)}, f32[128,128]{1,0:T(8,128)S(1)}, u32[]{:S(2)}, u32[]{:S(2)}) collective-permute-start(f32[128,128]{1,0:T(8,128)S(1)} %join.4), channel_id=1, source_target_pairs={{0,12},{4,8},{8,4},{12,0},{1,13},{5,9},{9,5},{13,1},{2,14},{6,10},... | collective-permute-start | bytes 196616 | tf_op jit(solution)/shard_map/ppermute | solution.py:433
  21.6 0.3 place.2
  21.9 0.1 collective-permute-start.7
  22.0 1.1 %collective-permute-start.10 = (f32[128,128]{1,0:T(8,128)S(1)}, f32[128,128]{1,0:T(8,128)S(1)}, u32[]{:S(2)}, u32[]{:S(2)}) collective-permute-start(f32[128,128]{1,0:T(8,128)S(1)} %get-tuple-element.41), channel_id=1, source_target_pairs={{0,4},{4,0},{8,12},{12,8},{1,5},{5,1},{9,13},{13,9},{2,6},{6,2},{1... | collective-permute-start | bytes 196616 | tf_op jit(solution)/shard_map/ppermute | solution.py:433
  23.0 1.5 %collective-permute-start.5 = (f32[136,128]{1,0:T(8,128)S(1)}, f32[136,128]{1,0:T(8,128)S(1)}, u32[]{:S(2)}, u32[]{:S(2)}) collective-permute-start(f32[136,128]{1,0:T(8,128)S(1)} %get-tuple-element.32), channel_id=1, source_target_pairs={{0,2},{1,3},{2,0},{3,1},{4,6},{5,7},{6,4},{7,5},{8,10},{9,11},{10,... | collective-permute-start | bytes 208904 | tf_op jit(solution)/shard_map/ppermute | solution.py:473
  24.5 2.0 %collective-permute-done.8.refs_0_ = f32[128,128]{1,0:T(8,128)S(1)} collective-permute-done((f32[128,128]{1,0:T(8,128)S(1)}, f32[128,128]{1,0:T(8,128)S(1)}, u32[]{:S(2)}, u32[]{:S(2)}) %collective-permute-start.8) | collective-permute-done | bytes 65568 | tf_op jit(solution)/shard_map/ppermute | solution.py:433
  26.6 1.0 %collective-permute-done.10.refs_2_ = f32[128,128]{1,0:T(8,128)S(1)} collective-permute-done((f32[128,128]{1,0:T(8,128)S(1)}, f32[128,128]{1,0:T(8,128)S(1)}, u32[]{:S(2)}, u32[]{:S(2)}) %collective-permute-start.10) | collective-permute-done | bytes 65568 | tf_op jit(solution)/shard_map/ppermute | solution.py:433
  27.6 0.3 place.3
  27.9 1.6 %collective-permute-start.11 = (f32[128,128]{1,0:T(8,128)S(1)}, f32[128,128]{1,0:T(8,128)S(1)}, u32[]{:S(2)}, u32[]{:S(2)}) collective-permute-start(f32[128,128]{1,0:T(8,128)S(1)} %get-tuple-element.43), channel_id=1, source_target_pairs={{0,2},{1,3},{2,0},{3,1},{4,6},{5,7},{6,4},{7,5},{8,10},{9,11},{10,... | collective-permute-start | bytes 196616 | tf_op jit(solution)/shard_map/ppermute | solution.py:473
  29.4 0.4 %collective-permute-start.12 = (f32[128,128]{1,0:T(8,128)S(1)}, f32[128,128]{1,0:T(8,128)S(1)}, u32[]{:S(2)}, u32[]{:S(2)}) collective-permute-start(f32[128,128]{1,0:T(8,128)S(1)} %get-tuple-element.44), channel_id=1, source_target_pairs={{0,3},{1,2},{2,1},{3,0},{4,7},{5,6},{6,5},{7,4},{8,11},{9,10},{10,... | collective-permute-start | bytes 196616 | tf_op jit(solution)/shard_map/ppermute | solution.py:473
  29.9 0.2 collective-permute-start.13
  30.1 0.9 %collective-permute-done.6.refs_1_ = f32[136,128]{1,0:T(8,128)S(1)} collective-permute-done((f32[136,128]{1,0:T(8,128)S(1)}, f32[136,128]{1,0:T(8,128)S(1)}, u32[]{:S(2)}, u32[]{:S(2)}) %collective-permute-start.6) | collective-permute-done | bytes 69664 | tf_op jit(solution)/shard_map/ppermute | solution.py:473
  31.0 1.7 %collective-permute-done.11.refs_4_ = f32[128,128]{1,0:T(8,128)S(1)} collective-permute-done((f32[128,128]{1,0:T(8,128)S(1)}, f32[128,128]{1,0:T(8,128)S(1)}, u32[]{:S(2)}, u32[]{:S(2)}) %collective-permute-start.11) | collective-permute-done | bytes 65568 | tf_op jit(solution)/shard_map/ppermute | solution.py:473
  32.6 1.2 %collective-permute-done.12.refs_5_ = f32[128,128]{1,0:T(8,128)S(1)} collective-permute-done((f32[128,128]{1,0:T(8,128)S(1)}, f32[128,128]{1,0:T(8,128)S(1)}, u32[]{:S(2)}, u32[]{:S(2)}) %collective-permute-start.12) | collective-permute-done | bytes 65568 | tf_op jit(solution)/shard_map/ppermute | solution.py:473
  33.8 0.7 %total.1 = f32[16,2,16,128]{3,2,1,0:T(8,128)} custom-call(f32[136,128]{1,0:T(8,128)S(1)} %collective-permute-done.5.refs_0_, f32[136,128]{1,0:T(8,128)S(1)} %collective-permute-done.6.refs_1_, f32[128,128]{1,0:T(8,128)S(1)} %get-tuple-element.34.refs_2_, f32[128,128]{1,0:T(8,128)S(1)} %collective-permute-done.7.refs_5_.refs_3_, ...), custom_call_target="tpu_custom_call" | custom-call | tf_op jit(solution)/shard_map/total/pallas_call | solution.py:483
  (14 shorter events, 0.1 us)
Async XLA Ops:
  5.9 1.5 %collective-permute-start = (f32[272,128]{1,0:T(8,128)S(1)}, f32[272,128]{1,0:T(8,128)S(1)}, u32[]{:S(2)}, u32[]{:S(2)}) collective-permute-start(f32[272,128]{1,0:T(8,128)S(1)} %get-tuple-element.27), channel_id=1, source_target_pairs={{0,1},{1,0},{2,3},{3,2},{4,5},{5,4},{6,7},{7,6},{8,9},{9,8},{10,11... | collective-permute-start | bytes 417800 | tf_op jit(solution)/shard_map/ppermute | solution.py:428
  7.4 5.2 %collective-permute-start.3 = (f32[784,128]{1,0:T(8,128)S(1)}, f32[784,128]{1,0:T(8,128)S(1)}, u32[]{:S(2)}, u32[]{:S(2)}) collective-permute-start(f32[784,128]{1,0:T(8,128)S(1)} %keep.1), channel_id=1, source_target_pairs={{0,1},{1,0},{2,3},{3,2},{4,5},{5,4},{6,7},{7,6},{8,9},{9,8},{10,11... | collective-permute-start | bytes 1204232 | tf_op jit(solution)/shard_map/ppermute | solution.py:429
  7.8 12.3 %collective-permute-start.2 = (f32[136,128]{1,0:T(8,128)S(1)}, f32[136,128]{1,0:T(8,128)S(1)}, u32[]{:S(2)}, u32[]{:S(2)}) collective-permute-start(f32[136,128]{1,0:T(8,128)S(1)} %get-tuple-element.49), channel_id=1, source_target_pairs={{0,12},{4,8},{8,4},{12,0},{1,13},{5,9},{9,5},{13,1},{2,14},{6,10},... | collective-permute-start | bytes 208904 | tf_op jit(solution)/shard_map/ppermute | solution.py:433
  12.6 6.3 %collective-permute-start.1 = (f32[136,128]{1,0:T(8,128)S(1)}, f32[136,128]{1,0:T(8,128)S(1)}, u32[]{:S(2)}, u32[]{:S(2)}) collective-permute-start(f32[136,128]{1,0:T(8,128)S(1)} %get-tuple-element.50), channel_id=1, source_target_pairs={{0,8},{4,12},{8,0},{12,4},{1,9},{5,13},{9,1},{13,5},{2,10},{6,14},... | collective-permute-start | bytes 208904 | tf_op jit(solution)/shard_map/ppermute | solution.py:433
  12.6 8.9 %collective-permute-start.4 = (f32[136,128]{1,0:T(8,128)S(1)}, f32[136,128]{1,0:T(8,128)S(1)}, u32[]{:S(2)}, u32[]{:S(2)}) collective-permute-start(f32[136,128]{1,0:T(8,128)S(1)} %get-tuple-element.48), channel_id=1, source_target_pairs={{0,4},{4,0},{8,12},{12,8},{1,5},{5,1},{9,13},{13,9},{2,6},{6,2},{1... | collective-permute-start | bytes 208904 | tf_op jit(solution)/shard_map/ppermute | solution.py:433
  18.9 7.6 %collective-permute-start.8 = (f32[128,128]{1,0:T(8,128)S(1)}, f32[128,128]{1,0:T(8,128)S(1)}, u32[]{:S(2)}, u32[]{:S(2)}) collective-permute-start(f32[128,128]{1,0:T(8,128)S(1)} %join.3), channel_id=1, source_target_pairs={{0,8},{4,12},{8,0},{12,4},{1,9},{5,13},{9,1},{13,5},{2,10},{6,14},... | collective-permute-start | bytes 196616 | tf_op jit(solution)/shard_map/ppermute | solution.py:433
  20.1 6.4 %collective-permute-start.9 = (f32[128,128]{1,0:T(8,128)S(1)}, f32[128,128]{1,0:T(8,128)S(1)}, u32[]{:S(2)}, u32[]{:S(2)}) collective-permute-start(f32[128,128]{1,0:T(8,128)S(1)} %join.4), channel_id=1, source_target_pairs={{0,12},{4,8},{8,4},{12,0},{1,13},{5,9},{9,5},{13,1},{2,14},{6,10},... | collective-permute-start | bytes 196616 | tf_op jit(solution)/shard_map/ppermute | solution.py:433
  21.9 4.7 %collective-permute-start.7 = (f32[128,128]{1,0:T(8,128)S(1)}, f32[128,128]{1,0:T(8,128)S(1)}, u32[]{:S(2)}, u32[]{:S(2)}) collective-permute-start(f32[128,128]{1,0:T(8,128)S(1)} %get-tuple-element.35), channel_id=1, source_target_pairs={{0,1},{1,0},{2,3},{3,2},{4,5},{5,4},{6,7},{7,6},{8,9},{9,8},{10,11... | collective-permute-start | bytes 196616 | tf_op jit(solution)/shard_map/ppermute | solution.py:473
  22.0 5.6 %collective-permute-start.10 = (f32[128,128]{1,0:T(8,128)S(1)}, f32[128,128]{1,0:T(8,128)S(1)}, u32[]{:S(2)}, u32[]{:S(2)}) collective-permute-start(f32[128,128]{1,0:T(8,128)S(1)} %get-tuple-element.41), channel_id=1, source_target_pairs={{0,4},{4,0},{8,12},{12,8},{1,5},{5,1},{9,13},{13,9},{2,6},{6,2},{1... | collective-permute-start | bytes 196616 | tf_op jit(solution)/shard_map/ppermute | solution.py:433
  23.0 7.1 %collective-permute-start.5 = (f32[136,128]{1,0:T(8,128)S(1)}, f32[136,128]{1,0:T(8,128)S(1)}, u32[]{:S(2)}, u32[]{:S(2)}) collective-permute-start(f32[136,128]{1,0:T(8,128)S(1)} %get-tuple-element.32), channel_id=1, source_target_pairs={{0,2},{1,3},{2,0},{3,1},{4,6},{5,7},{6,4},{7,5},{8,10},{9,11},{10,... | collective-permute-start | bytes 208904 | tf_op jit(solution)/shard_map/ppermute | solution.py:473
  26.5 4.4 %collective-permute-start.6 = (f32[136,128]{1,0:T(8,128)S(1)}, f32[136,128]{1,0:T(8,128)S(1)}, u32[]{:S(2)}, u32[]{:S(2)}) collective-permute-start(f32[136,128]{1,0:T(8,128)S(1)} %get-tuple-element.33), channel_id=1, source_target_pairs={{0,3},{1,2},{2,1},{3,0},{4,7},{5,6},{6,5},{7,4},{8,11},{9,10},{10,... | collective-permute-start | bytes 208904 | tf_op jit(solution)/shard_map/ppermute | solution.py:473
  27.9 4.8 %collective-permute-start.11 = (f32[128,128]{1,0:T(8,128)S(1)}, f32[128,128]{1,0:T(8,128)S(1)}, u32[]{:S(2)}, u32[]{:S(2)}) collective-permute-start(f32[128,128]{1,0:T(8,128)S(1)} %get-tuple-element.43), channel_id=1, source_target_pairs={{0,2},{1,3},{2,0},{3,1},{4,6},{5,7},{6,4},{7,5},{8,10},{9,11},{10,... | collective-permute-start | bytes 196616 | tf_op jit(solution)/shard_map/ppermute | solution.py:473
  29.4 4.4 %collective-permute-start.12 = (f32[128,128]{1,0:T(8,128)S(1)}, f32[128,128]{1,0:T(8,128)S(1)}, u32[]{:S(2)}, u32[]{:S(2)}) collective-permute-start(f32[128,128]{1,0:T(8,128)S(1)} %get-tuple-element.44), channel_id=1, source_target_pairs={{0,3},{1,2},{2,1},{3,0},{4,7},{5,6},{6,5},{7,4},{8,11},{9,10},{10,... | collective-permute-start | bytes 196616 | tf_op jit(solution)/shard_map/ppermute | solution.py:473
  29.9 3.9 %collective-permute-start.13 = (f32[128,128]{1,0:T(8,128)S(1)}, f32[128,128]{1,0:T(8,128)S(1)}, u32[]{:S(2)}, u32[]{:S(2)}) collective-permute-start(f32[128,128]{1,0:T(8,128)S(1)} %get-tuple-element.46), channel_id=1, source_target_pairs={{0,1},{1,0},{2,3},{3,2},{4,5},{5,4},{6,7},{7,6},{8,9},{9,8},{10,11... | collective-permute-start | bytes 196616 | tf_op jit(solution)/shard_map/ppermute | solution.py:473

commit v14 on v12

--- a/solution.py
+++ b/solution.py
@@ -25,7 +25,7 @@
 
 def slab_steps(peers):
     if peers <= REACH + 1:
-        return tuple(sorted(range(peers), key=lambda k: (k == 0, k < peers // 2, k)))
+        return tuple(sorted(range(peers), key=lambda k: (k == 0, -k)))
     ring = [s for k in range(REACH, 0, -1) for s in (peers - k, k)]
     return (*ring, 0)
 

time: 31.8 us -> 34.6 us (1.088)
  waiting for transfers between devices: 9.08 us -> 11.1 us
  starting transfers between devices: 15.2 us -> 16 us
    ppermute x6, waiting for transfers between devices: 4.55 us -> 6.58 us  [send(): return lax.ppermute(block, 'slab', ring)]
    ppermute x6, starting transfers between devices: 10.2 us -> 11 us  [send(): return lax.ppermute(block, 'slab', ring)]
  transfers between devices with their start and end apart: 14 -> 14, of which waited for: 6 -> 5; matrix products, arithmetic and copies ran while one was open for 0% -> 0% of each run, Pallas kernels for 2% -> 2%
where the time goes in v14:
time: 34.6 us; the launch traced here: 34.5 us
  starting transfers between devices  16 us (46%)
  waiting for transfers between devices  11.1 us (32%)
  Pallas kernels  7.23 us (21%)
    ppermute x6, starting transfers between devices, send(): return lax.ppermute(block, 'slab', ring)  11 us
    ppermute x6, waiting for transfers between devices, send(): return lax.ppermute(block, 'slab', ring)  6.58 us
    pallas_call x1, Pallas kernels, on_device(): pl.pallas_call(functools.partial(frame_kernel, shifts), out_shape=shapes,...  5.84 us
    ppermute x6, starting transfers between devices, share_out(): return lax.ppermute(part, ('tilt', 'rep'), route)  4.14 us
    ppermute x6, waiting for transfers between devices, share_out(): return lax.ppermute(part, ('tilt', 'rep'), route)  3.53 us
    ppermute x1, waiting for transfers between devices, on_device(): got = [lax.ppermute(other[0], 'rep', swap)]  1 us
    pallas_call x1, Pallas kernels, on_device(): pl.pallas_call(functools.partial(sum_kernel, owners), out_shape=jax.Shape...  0.75 us
  transfers between devices with their start and end apart: 14, of which 5 were waited for; matrix products, arithmetic and copies ran while one was open for 0% of the time, Pallas kernels for 2%

profile of v14, /device:TPU:0, one launch (start us, length us, event | category | flops | bytes accessed | tf_op | source)
XLA Modules:
  0.0 34.5 jit_solution(3133884209313894302)
XLA Ops:
  0.0 5.8 %frame.1 = (f32[136,128]{1,0:T(8,128)S(1)}, f32[136,128]{1,0:T(8,128)S(1)}, f32[136,128]{1,0:T(8,128)S(1)}, f32[136,128]{1,0:T(8,128)S(1)}, f32[128,128]{1,0:T(8...) custom-call(s32[1,4]{1,0:T(1,128)} %pos_hbm.1, ...), custom_call_target="tpu_custom_call" | custom-call | tf_op jit(solution)/shard_map/frame/pallas_call | solution.py:401
  5.8 0.5 %collective-permute-start = (f32[272,128]{1,0:T(8,128)S(1)}, f32[272,128]{1,0:T(8,128)S(1)}, u32[]{:S(2)}, u32[]{:S(2)}) collective-permute-start(f32[272,128]{1,0:T(8,128)S(1)} %get-tuple-element.28), channel_id=1, source_target_pairs={{0,1},{1,0},{2,3},{3,2},{4,5},{5,4},{6,7},{7,6},{8,9},{9,8},{10,11... | collective-permute-start | bytes 417800 | tf_op jit(solution)/shard_map/ppermute | solution.py:428
  6.4 1.0 %collective-permute-done.after_ref = f32[272,128]{1,0:T(8,128)S(1)} collective-permute-done((f32[272,128]{1,0:T(8,128)S(1)}, f32[272,128]{1,0:T(8,128)S(1)}, u32[]{:S(2)}, u32[]{:S(2)}) %collective-permute-start) | collective-permute-done | bytes 139296 | tf_op jit(solution)/shard_map/ppermute | solution.py:428
  7.4 0.4 %collective-permute-start.3 = (f32[784,128]{1,0:T(8,128)S(1)}, f32[784,128]{1,0:T(8,128)S(1)}, u32[]{:S(2)}, u32[]{:S(2)}) collective-permute-start(f32[784,128]{1,0:T(8,128)S(1)} %keep.1), channel_id=1, source_target_pairs={{0,1},{1,0},{2,3},{3,2},{4,5},{5,4},{6,7},{7,6},{8,9},{9,8},{10,11... | collective-permute-start | bytes 1204232 | tf_op jit(solution)/shard_map/ppermute | solution.py:429
  7.7 3.8 %collective-permute-start.2 = (f32[136,128]{1,0:T(8,128)S(1)}, f32[136,128]{1,0:T(8,128)S(1)}, u32[]{:S(2)}, u32[]{:S(2)}) collective-permute-start(f32[136,128]{1,0:T(8,128)S(1)} %get-tuple-element.51), channel_id=1, source_target_pairs={{0,8},{4,12},{8,0},{12,4},{1,9},{5,13},{9,1},{13,5},{2,10},{6,14},... | collective-permute-start | bytes 208904 | tf_op jit(solution)/shard_map/ppermute | solution.py:433
  11.6 1.3 %collective-permute-start.1 = (f32[136,128]{1,0:T(8,128)S(1)}, f32[136,128]{1,0:T(8,128)S(1)}, u32[]{:S(2)}, u32[]{:S(2)}) collective-permute-start(f32[136,128]{1,0:T(8,128)S(1)} %get-tuple-element.52), channel_id=1, source_target_pairs={{0,12},{4,8},{8,4},{12,0},{1,13},{5,9},{9,5},{13,1},{2,14},{6,10},... | collective-permute-start | bytes 208904 | tf_op jit(solution)/shard_map/ppermute | solution.py:433
  12.9 0.3 collective-permute-start.4
  13.2 2.8 %collective-permute-done.2.refs_1_.first_ref = f32[136,128]{1,0:T(8,128)S(1)} collective-permute-done((f32[136,128]{1,0:T(8,128)S(1)}, f32[136,128]{1,0:T(8,128)S(1)}, u32[]{:S(2)}, u32[]{:S(2)}) %collective-permute-start.2) | collective-permute-done | bytes 69664 | tf_op jit(solution)/shard_map/ppermute | solution.py:433
  16.1 1.4 %collective-permute-start.9 = (f32[128,128]{1,0:T(8,128)S(1)}, f32[128,128]{1,0:T(8,128)S(1)}, u32[]{:S(2)}, u32[]{:S(2)}) collective-permute-start(f32[128,128]{1,0:T(8,128)S(1)} %get-tuple-element.41), channel_id=1, source_target_pairs={{0,8},{4,12},{8,0},{12,4},{1,9},{5,13},{9,1},{13,5},{2,10},{6,14},... | collective-permute-start | bytes 196616 | tf_op jit(solution)/shard_map/ppermute | solution.py:433
  17.5 4.1 %collective-permute-start.10 = (f32[128,128]{1,0:T(8,128)S(1)}, f32[128,128]{1,0:T(8,128)S(1)}, u32[]{:S(2)}, u32[]{:S(2)}) collective-permute-start(f32[128,128]{1,0:T(8,128)S(1)} %get-tuple-element.42), channel_id=1, source_target_pairs={{0,4},{4,0},{8,12},{12,8},{1,5},{5,1},{9,13},{13,9},{2,6},{6,2},{1... | collective-permute-start | bytes 196616 | tf_op jit(solution)/shard_map/ppermute | solution.py:433
  21.6 0.0 collective-permute-done.1.refs_0_.first_ref
  21.6 0.1 collective-permute-start.8
  21.6 0.0 collective-permute-done.4.refs_2_
  21.7 0.3 place.2
  22.0 0.1 collective-permute-start.7
  22.0 1.6 %collective-permute-start.5 = (f32[136,128]{1,0:T(8,128)S(1)}, f32[136,128]{1,0:T(8,128)S(1)}, u32[]{:S(2)}, u32[]{:S(2)}) collective-permute-start(f32[136,128]{1,0:T(8,128)S(1)} %get-tuple-element.33), channel_id=1, source_target_pairs={{0,2},{1,3},{2,0},{3,1},{4,6},{5,7},{6,4},{7,5},{8,10},{9,11},{10,... | collective-permute-start | bytes 208904 | tf_op jit(solution)/shard_map/ppermute | solution.py:473
  23.6 0.3 collective-permute-start.6
  23.9 3.8 %collective-permute-done.8.refs_0_ = f32[128,128]{1,0:T(8,128)S(1)} collective-permute-done((f32[128,128]{1,0:T(8,128)S(1)}, f32[128,128]{1,0:T(8,128)S(1)}, u32[]{:S(2)}, u32[]{:S(2)}) %collective-permute-start.8) | collective-permute-done | bytes 65568 | tf_op jit(solution)/shard_map/ppermute | solution.py:433
  27.7 0.3 place.3
  28.0 1.6 %collective-permute-start.11 = (f32[128,128]{1,0:T(8,128)S(1)}, f32[128,128]{1,0:T(8,128)S(1)}, u32[]{:S(2)}, u32[]{:S(2)}) collective-permute-start(f32[128,128]{1,0:T(8,128)S(1)} %get-tuple-element.45), channel_id=1, source_target_pairs={{0,2},{1,3},{2,0},{3,1},{4,6},{5,7},{6,4},{7,5},{8,10},{9,11},{10,... | collective-permute-start | bytes 196616 | tf_op jit(solution)/shard_map/ppermute | solution.py:473
  29.6 0.6 %collective-permute-start.13 = (f32[128,128]{1,0:T(8,128)S(1)}, f32[128,128]{1,0:T(8,128)S(1)}, u32[]{:S(2)}, u32[]{:S(2)}) collective-permute-start(f32[128,128]{1,0:T(8,128)S(1)} %get-tuple-element.48), channel_id=1, source_target_pairs={{0,1},{1,0},{2,3},{3,2},{4,5},{5,4},{6,7},{7,6},{8,9},{9,8},{10,11... | collective-permute-start | bytes 196616 | tf_op jit(solution)/shard_map/ppermute | solution.py:473
  30.2 2.1 %collective-permute-done.11.refs_4_ = f32[128,128]{1,0:T(8,128)S(1)} collective-permute-done((f32[128,128]{1,0:T(8,128)S(1)}, f32[128,128]{1,0:T(8,128)S(1)}, u32[]{:S(2)}, u32[]{:S(2)}) %collective-permute-start.11) | collective-permute-done | bytes 65568 | tf_op jit(solution)/shard_map/ppermute | solution.py:473
  32.3 1.4 %collective-permute-done.12.refs_5_ = f32[128,128]{1,0:T(8,128)S(1)} collective-permute-done((f32[128,128]{1,0:T(8,128)S(1)}, f32[128,128]{1,0:T(8,128)S(1)}, u32[]{:S(2)}, u32[]{:S(2)}) %collective-permute-start.12) | collective-permute-done | bytes 65568 | tf_op jit(solution)/shard_map/ppermute | solution.py:473
  33.7 0.7 %total.1 = f32[16,2,16,128]{3,2,1,0:T(8,128)} custom-call(f32[136,128]{1,0:T(8,128)S(1)} %collective-permute-done.5.refs_0_, f32[136,128]{1,0:T(8,128)S(1)} %collective-permute-done.6.refs_1_, f32[128,128]{1,0:T(8,128)S(1)} %get-tuple-element.35.refs_2_, f32[128,128]{1,0:T(8,128)S(1)} %collective-permute-done.7.refs_5_.refs_3_, ...), custom_call_target="tpu_custom_call" | custom-call | tf_op jit(solution)/shard_map/total/pallas_call | solution.py:484
  (13 shorter events, 0.1 us)
Async XLA Ops:
  5.8 1.5 %collective-permute-start = (f32[272,128]{1,0:T(8,128)S(1)}, f32[272,128]{1,0:T(8,128)S(1)}, u32[]{:S(2)}, u32[]{:S(2)}) collective-permute-start(f32[272,128]{1,0:T(8,128)S(1)} %get-tuple-element.28), channel_id=1, source_target_pairs={{0,1},{1,0},{2,3},{3,2},{4,5},{5,4},{6,7},{7,6},{8,9},{9,8},{10,11... | collective-permute-start | bytes 417800 | tf_op jit(solution)/shard_map/ppermute | solution.py:428
  7.4 5.5 %collective-permute-start.3 = (f32[784,128]{1,0:T(8,128)S(1)}, f32[784,128]{1,0:T(8,128)S(1)}, u32[]{:S(2)}, u32[]{:S(2)}) collective-permute-start(f32[784,128]{1,0:T(8,128)S(1)} %keep.1), channel_id=1, source_target_pairs={{0,1},{1,0},{2,3},{3,2},{4,5},{5,4},{6,7},{7,6},{8,9},{9,8},{10,11... | collective-permute-start | bytes 1204232 | tf_op jit(solution)/shard_map/ppermute | solution.py:429
  7.7 8.3 %collective-permute-start.2 = (f32[136,128]{1,0:T(8,128)S(1)}, f32[136,128]{1,0:T(8,128)S(1)}, u32[]{:S(2)}, u32[]{:S(2)}) collective-permute-start(f32[136,128]{1,0:T(8,128)S(1)} %get-tuple-element.51), channel_id=1, source_target_pairs={{0,8},{4,12},{8,0},{12,4},{1,9},{5,13},{9,1},{13,5},{2,10},{6,14},... | collective-permute-start | bytes 208904 | tf_op jit(solution)/shard_map/ppermute | solution.py:433
  11.6 10.0 %collective-permute-start.1 = (f32[136,128]{1,0:T(8,128)S(1)}, f32[136,128]{1,0:T(8,128)S(1)}, u32[]{:S(2)}, u32[]{:S(2)}) collective-permute-start(f32[136,128]{1,0:T(8,128)S(1)} %get-tuple-element.52), channel_id=1, source_target_pairs={{0,12},{4,8},{8,4},{12,0},{1,13},{5,9},{9,5},{13,1},{2,14},{6,10},... | collective-permute-start | bytes 208904 | tf_op jit(solution)/shard_map/ppermute | solution.py:433
  12.9 8.7 %collective-permute-start.4 = (f32[136,128]{1,0:T(8,128)S(1)}, f32[136,128]{1,0:T(8,128)S(1)}, u32[]{:S(2)}, u32[]{:S(2)}) collective-permute-start(f32[136,128]{1,0:T(8,128)S(1)} %get-tuple-element.50), channel_id=1, source_target_pairs={{0,4},{4,0},{8,12},{12,8},{1,5},{5,1},{9,13},{13,9},{2,6},{6,2},{1... | collective-permute-start | bytes 208904 | tf_op jit(solution)/shard_map/ppermute | solution.py:433
  16.1 7.6 %collective-permute-start.9 = (f32[128,128]{1,0:T(8,128)S(1)}, f32[128,128]{1,0:T(8,128)S(1)}, u32[]{:S(2)}, u32[]{:S(2)}) collective-permute-start(f32[128,128]{1,0:T(8,128)S(1)} %get-tuple-element.41), channel_id=1, source_target_pairs={{0,8},{4,12},{8,0},{12,4},{1,9},{5,13},{9,1},{13,5},{2,10},{6,14},... | collective-permute-start | bytes 196616 | tf_op jit(solution)/shard_map/ppermute | solution.py:433
  17.5 6.4 %collective-permute-start.10 = (f32[128,128]{1,0:T(8,128)S(1)}, f32[128,128]{1,0:T(8,128)S(1)}, u32[]{:S(2)}, u32[]{:S(2)}) collective-permute-start(f32[128,128]{1,0:T(8,128)S(1)} %get-tuple-element.42), channel_id=1, source_target_pairs={{0,4},{4,0},{8,12},{12,8},{1,5},{5,1},{9,13},{13,9},{2,6},{6,2},{1... | collective-permute-start | bytes 196616 | tf_op jit(solution)/shard_map/ppermute | solution.py:433
  21.6 6.1 %collective-permute-start.8 = (f32[128,128]{1,0:T(8,128)S(1)}, f32[128,128]{1,0:T(8,128)S(1)}, u32[]{:S(2)}, u32[]{:S(2)}) collective-permute-start(f32[128,128]{1,0:T(8,128)S(1)} %join.2), channel_id=1, source_target_pairs={{0,12},{4,8},{8,4},{12,0},{1,13},{5,9},{9,5},{13,1},{2,14},{6,10},... | collective-permute-start | bytes 196616 | tf_op jit(solution)/shard_map/ppermute | solution.py:433
  22.0 5.7 %collective-permute-start.7 = (f32[128,128]{1,0:T(8,128)S(1)}, f32[128,128]{1,0:T(8,128)S(1)}, u32[]{:S(2)}, u32[]{:S(2)}) collective-permute-start(f32[128,128]{1,0:T(8,128)S(1)} %get-tuple-element.36), channel_id=1, source_target_pairs={{0,1},{1,0},{2,3},{3,2},{4,5},{5,4},{6,7},{7,6},{8,9},{9,8},{10,11... | collective-permute-start | bytes 196616 | tf_op jit(solution)/shard_map/ppermute | solution.py:473
  22.0 8.2 %collective-permute-start.5 = (f32[136,128]{1,0:T(8,128)S(1)}, f32[136,128]{1,0:T(8,128)S(1)}, u32[]{:S(2)}, u32[]{:S(2)}) collective-permute-start(f32[136,128]{1,0:T(8,128)S(1)} %get-tuple-element.33), channel_id=1, source_target_pairs={{0,2},{1,3},{2,0},{3,1},{4,6},{5,7},{6,4},{7,5},{8,10},{9,11},{10,... | collective-permute-start | bytes 208904 | tf_op jit(solution)/shard_map/ppermute | solution.py:473
  23.6 6.6 %collective-permute-start.6 = (f32[136,128]{1,0:T(8,128)S(1)}, f32[136,128]{1,0:T(8,128)S(1)}, u32[]{:S(2)}, u32[]{:S(2)}) collective-permute-start(f32[136,128]{1,0:T(8,128)S(1)} %get-tuple-element.34), channel_id=1, source_target_pairs={{0,3},{1,2},{2,1},{3,0},{4,7},{5,6},{6,5},{7,4},{8,11},{9,10},{10,... | collective-permute-start | bytes 208904 | tf_op jit(solution)/shard_map/ppermute | solution.py:473
  28.0 4.3 %collective-permute-start.11 = (f32[128,128]{1,0:T(8,128)S(1)}, f32[128,128]{1,0:T(8,128)S(1)}, u32[]{:S(2)}, u32[]{:S(2)}) collective-permute-start(f32[128,128]{1,0:T(8,128)S(1)} %get-tuple-element.45), channel_id=1, source_target_pairs={{0,2},{1,3},{2,0},{3,1},{4,6},{5,7},{6,4},{7,5},{8,10},{9,11},{10,... | collective-permute-start | bytes 196616 | tf_op jit(solution)/shard_map/ppermute | solution.py:473
  29.6 4.2 %collective-permute-start.12 = (f32[128,128]{1,0:T(8,128)S(1)}, f32[128,128]{1,0:T(8,128)S(1)}, u32[]{:S(2)}, u32[]{:S(2)}) collective-permute-start(f32[128,128]{1,0:T(8,128)S(1)} %get-tuple-element.46), channel_id=1, source_target_pairs={{0,3},{1,2},{2,1},{3,0},{4,7},{5,6},{6,5},{7,4},{8,11},{9,10},{10,... | collective-permute-start | bytes 196616 | tf_op jit(solution)/shard_map/ppermute | solution.py:473
  29.6 4.2 %collective-permute-start.13 = (f32[128,128]{1,0:T(8,128)S(1)}, f32[128,128]{1,0:T(8,128)S(1)}, u32[]{:S(2)}, u32[]{:S(2)}) collective-permute-start(f32[128,128]{1,0:T(8,128)S(1)} %get-tuple-element.48), channel_id=1, source_target_pairs={{0,1},{1,0},{2,3},{3,2},{4,5},{5,4},{6,7},{7,6},{8,9},{9,8},{10,11... | collective-permute-start | bytes 196616 | tf_op jit(solution)/shard_map/ppermute | solution.py:473

commit v15 on v12

--- a/solution.py
+++ b/solution.py
@@ -13,6 +13,7 @@
 REACH = 3
 CHUNKS = 2
 CHUNK_ROWS = 8
+BATCH = 8
 HIGH = lax.Precision.HIGHEST
 SMEM = pltpu.SMEM
 VMEM = pltpu.VMEM
@@ -63,6 +64,74 @@
         [jnp.concatenate([krt, kit], 1), jnp.concatenate([-kit, krt], 1)], 0
     ).astype(jnp.bfloat16)
     return whole, turned
+
+
+def mix_blocks(shifts, which, index_ref, count_ref, band, col_bf, row_scr, put):
+    me, core = lax.axis_index("slab"), lax.axis_index("rep")
+    peers = lax.axis_size("slab")
+    f32, bf16 = jnp.float32, jnp.bfloat16
+    capacity = index_ref.shape[-1]
+    block_rows, block_cols = band.shape[-2:]
+    wide = BATCH * block_rows
+    strip = lax.div(lax.broadcasted_iota(jnp.int32, (block_rows, wide), 1), block_rows)
+    half = block_rows // CHUNKS
+    mark_down = lax.broadcasted_iota(jnp.int32, (half, capacity * half), 0)
+    mark_along = lax.broadcasted_iota(jnp.int32, (half, capacity * half), 1)
+    mark_slot = jnp.where(lax.rem(mark_along, half) == mark_down, lax.div(mark_along, half), -1)
+    for k in which:
+        dest = partner(me, shifts[k], peers)
+        live = count_ref[0, 0, dest]
+        marks = jnp.full(mark_slot.shape, VB_DEV, jnp.int32)
+        for first in range(0, capacity, BATCH):
+            inner, picks = [], []
+            for slot in range(first, first + BATCH, 2):
+                pairs, factors = [], []
+                for one in (slot, slot + 1):
+                    block = index_ref[0, 0, 0, dest, one]
+                    target = index_ref[1, 0, 0, dest, one]
+                    t = index_ref[2, 0, 0, dest, one]
+                    target = jnp.where(one < live, target, VB_DEV)
+                    marks = jnp.where(mark_slot == one, target, marks)
+                    pairs += [band[core, block], band[1 - core, block]]
+                    factors.append(col_bf[t])
+                    picked = jnp.where(strip == one - first, row_scr[t], 0.0)
+                    picks.append(picked.astype(bf16))
+                mixed = dot(jnp.concatenate(pairs, 0), jnp.concatenate(factors, 1)).astype(bf16)
+                for n in (0, 1):
+                    lanes = slice(n * block_cols, (n + 1) * block_cols)
+                    top = 2 * n * block_rows
+                    inner.append(
+                        jnp.concatenate(
+                            [
+                                mixed[top : top + block_rows, lanes],
+                                mixed[top + block_rows : top + 2 * block_rows, lanes],
+                            ],
+                            1,
+                        )
+                    )
+            result = dot(jnp.concatenate(picks, 0), jnp.concatenate(inner, 0))
+            for h in range(CHUNKS):
+                for slot in range(first, first + BATCH):
+                    top = (slot - first) * block_rows + h * half
+                    put(k, h, slot * half, result[top : top + half])
+        marks = marks.astype(f32)
+        put(k, 0, capacity * half, jnp.concatenate([marks, jnp.zeros_like(marks)], 1))
+
+
+def near_kernel(shifts, index_ref, count_ref, band, col_bf, row_scr, spare, *refs):
+    mine, other = refs[:-1], refs[-1]
+    far, near = len(shifts) - 2, 2
+    half, cols = CHUNK_ROWS, band.shape[-1]
+    lines = index_ref.shape[-1] * half
+    late = near * (lines + half)
+    other[late : late + far * lines] = spare[...]
+
+    def put(k, h, row, value):
+        base = late + k * lines if h else (k - far) * (lines + half)
+        mine[h * near + k - far][row : row + half] = value[:, :cols]
+        other[base + row : base + row + half] = value[:, cols:]
+
+    mix_blocks(shifts, range(far, far + near), index_ref, count_ref, band, col_bf, row_scr, put)
 
 
 def frame_kernel(
@@ -79,11 +148,13 @@
     col_hbm,
     *rest,
 ):
-    far, steps = len(shifts) - 2, len(shifts)
-    mine, other, scratch = rest[: 2 * steps], rest[2 * steps : 2 * steps + 2], rest[2 * steps + 2 :]
+    far = len(shifts) - 2
+    mine, swaps = rest[: 2 * far], rest[2 * far : 2 * far + 2]
+    band, col_bf, row_scr = rest[2 * far + 2 : 2 * far + 5]
+    scratch = rest[2 * far + 5 :]
     pos_ref, index_ref, count_ref = scratch[0:3]
     phase_ref, table_ref, obj_ref, probe_ref, cot_ref, row_ref, col_ref = scratch[3:10]
-    sems, band, window, col_bf, row_scr = scratch[10:]
+    sems, window = scratch[10:]
     slices = obj_ref.shape[2]
     copies = [
         pltpu.make_async_copy(src, dst, sems.at[i])
@@ -112,9 +183,6 @@
     for copy in (got_index, got_count, got_row, got_col):
         copy.start()
 
-    me, core = lax.axis_index("slab"), lax.axis_index("rep")
-    peers = lax.axis_size("slab")
-    capacity = index_ref.shape[-1]
     size = probe_ref.shape[-1]
     rows, cols = obj_ref.shape[3:]
     count = cot_ref.shape[1]
@@ -224,71 +292,21 @@
                         ]
 
     tiles = row_ref.shape[0]
-    batch = 8
-    wide = batch * block_rows
+    wide = BATCH * block_rows
     col_bf[...] = col_ref[...].astype(bf16)
     down = lax.broadcasted_iota(jnp.int32, (block_rows, wide), 0)
     along = lax.broadcasted_iota(jnp.int32, (block_rows, wide), 1)
     repeat = (lax.rem(along, block_rows) == down).astype(bf16)
     row_wide = dot(row_ref[...].reshape(tiles * block_rows, block_rows).astype(bf16), repeat)
     row_scr[...] = row_wide.reshape(tiles, block_rows, wide)
-    strip = lax.div(along, block_rows)
     half = block_rows // CHUNKS
-    mark_down = lax.broadcasted_iota(jnp.int32, (half, capacity * half), 0)
-    mark_along = lax.broadcasted_iota(jnp.int32, (half, capacity * half), 1)
-    mark_slot = jnp.where(lax.rem(mark_along, half) == mark_down, lax.div(mark_along, half), -1)
-    lines = capacity * half
-    late = (steps - far) * (lines + half)
-
-    def put(k, h, slot, value):
-        at = slot * half
-        if h:
-            swap, base = other[1], late + k * lines
-        elif k < far:
-            swap, base = other[0], k * (lines + half)
-        else:
-            swap, base = other[1], (k - far) * (lines + half)
-        mine[h * steps + k][at : at + half] = value[:, :block_cols]
-        swap[base + at : base + at + half] = value[:, block_cols:]
-
-    for k, shift in enumerate(shifts):
-        dest = partner(me, shift, peers)
-        live = count_ref[0, 0, dest]
-        marks = jnp.full(mark_slot.shape, VB_DEV, jnp.int32)
-        for first in range(0, capacity, batch):
-            inner, picks = [], []
-            for slot in range(first, first + batch, 2):
-                pairs, factors = [], []
-                for one in (slot, slot + 1):
-                    block = index_ref[0, 0, 0, dest, one]
-                    target = index_ref[1, 0, 0, dest, one]
-                    t = index_ref[2, 0, 0, dest, one]
-                    target = jnp.where(one < live, target, VB_DEV)
-                    marks = jnp.where(mark_slot == one, target, marks)
-                    pairs += [band[core, block], band[1 - core, block]]
-                    factors.append(col_bf[t])
-                    picked = jnp.where(strip == one - first, row_scr[t], 0.0)
-                    picks.append(picked.astype(bf16))
-                mixed = dot(jnp.concatenate(pairs, 0), jnp.concatenate(factors, 1)).astype(bf16)
-                for n in (0, 1):
-                    lanes = slice(n * block_cols, (n + 1) * block_cols)
-                    top = 2 * n * block_rows
-                    inner.append(
-                        jnp.concatenate(
-                            [
-                                mixed[top : top + block_rows, lanes],
-                                mixed[top + block_rows : top + 2 * block_rows, lanes],
-                            ],
-                            1,
-                        )
-                    )
-            result = dot(jnp.concatenate(picks, 0), jnp.concatenate(inner, 0))
-            for slot in range(first, first + batch):
-                for h in range(CHUNKS):
-                    top = (slot - first) * block_rows + h * half
-                    put(k, h, slot, result[top : top + half])
-        marks = marks.astype(f32)
-        put(k, 0, capacity, jnp.concatenate([marks, jnp.zeros_like(marks)], 1))
+
+    def put(k, h, row, value):
+        base = k * mine[h * far].shape[0] + row
+        mine[h * far + k][row : row + half] = value[:, :block_cols]
+        swaps[h][base : base + half] = value[:, block_cols:]
+
+    mix_blocks(shifts, range(far), index_ref, count_ref, band, col_bf, row_scr, put)
 
 
 def keep_until(value, after):
@@ -398,23 +416,38 @@
         (col_interp, VMEM),
     ]
     scalars = [positions, pair_index, pair_counts]
-    held = pl.pallas_call(
+    in_hbm = functools.partial(pltpu.with_memory_space_constraint, memory_space=pltpu.HBM)
+    passed = [
+        jax.ShapeDtypeStruct((2,) + frames, bf16),
+        jax.ShapeDtypeStruct(col_interp.shape, bf16),
+        jax.ShapeDtypeStruct((row_interp.shape[0], block_rows, BATCH * block_rows), f32),
+    ]
+    spare = jax.ShapeDtypeStruct((far * lanes, block_cols), f32)
+    outs = shapes[:far] + shapes[sources : sources + far] + [shapes[-2], spare] + passed
+    *held, other, spare, band, col_bf, row_wide = pl.pallas_call(
         functools.partial(frame_kernel, shifts),
-        out_shape=shapes,
+        out_shape=outs,
         in_specs=[hbm] * 10,
-        out_specs=[vmem] * len(shapes),
+        out_specs=[vmem] * len(outs),
         scratch_shapes=[SMEM(x.shape, x.dtype) for x in scalars]
         + [space(x.shape, x.dtype) for x, space in fetched]
         + [
             pltpu.SemaphoreType.DMA((9 + slices,)),
-            VMEM((2,) + frames, bf16),
             VMEM((slices, 2 * rows, windows * size), bf16),
-            VMEM(col_interp.shape, bf16),
-            VMEM((row_interp.shape[0], block_rows, 8 * block_rows), f32),
         ],
         compiler_params=LIMIT,
         name="frame",
-    )(*[pltpu.with_memory_space_constraint(x, pltpu.HBM) for x in scalars + [x for x, _ in fetched]])
+    )(*[in_hbm(x) for x in scalars + [x for x, _ in fetched]])
+    outs = shapes[far:sources] + shapes[sources + far : 2 * sources] + [shapes[-1]]
+    *near, rest = pl.pallas_call(
+        functools.partial(near_kernel, shifts),
+        out_shape=outs,
+        in_specs=[pl.BlockSpec(memory_space=SMEM)] * 2 + [vmem] * 4,
+        out_specs=[vmem] * len(outs),
+        compiler_params=LIMIT,
+        name="near",
+    )(in_hbm(pair_index), in_hbm(pair_counts), band, col_bf, row_wide, spare)
+    mine = held[:far] + near[:2] + held[far:] + near[2:]
 
     swap = [(r, (r + 1) % cores) for r in range(cores)]
     owners = sorted(
@@ -424,9 +457,8 @@
     share = jax.ShapeDtypeStruct((each * CHUNK_ROWS, block_cols), f32)
     mark = jax.ShapeDtypeStruct((sources, CHUNK_ROWS, block_cols), f32)
     padded = jax.ShapeDtypeStruct(((each + 1) * CHUNK_ROWS, block_cols), f32)
-    mine, other = held[: len(heights)], held[len(heights) :]
-    got = [lax.ppermute(other[0], "rep", swap)]
-    got.append(lax.ppermute(keep_until(other[1], got[0]), "rep", swap))
+    got = [lax.ppermute(other, "rep", swap)]
+    got.append(lax.ppermute(keep_until(rest, got[0]), "rep", swap))
 
     def send(block, step):
         ring = [(p, partner(p, step, peers)) for p in range(peers)]

time: 31.8 us -> 31.9 us (level)
  waiting for transfers between devices: 9.08 us -> 7.95 us
  Pallas kernels: 7.24 us -> 8.13 us
    ppermute x2, waiting for transfers between devices: 1 us -> 0.01 us  [the longest x1 0.01 us: on_device(): got = [lax.ppermute(other, 'rep', swap)]]
    pallas_call x1 -> x2, Pallas kernels: 5.86 us -> 6.76 us  [the longest x1 5.13 us: on_device(): pl.pallas_call(functools.partial(frame_kernel, shifts), out_shape=outs, i...]
    ppermute x6, starting transfers between devices: 10.2 us -> 10.7 us  [send(): return lax.ppermute(block, 'slab', ring)]
  transfers between devices with their start and end apart: 14 -> 14, of which waited for: 6 -> 6; matrix products, arithmetic and copies ran while one was open for 0% -> 0% of each run, Pallas kernels for 2% -> 7%
where the time goes in v15:
time: 31.9 us; the launch traced here: 31.7 us
  starting transfers between devices  15.5 us (49%)
  Pallas kernels  8.13 us (25%)
  waiting for transfers between devices  7.95 us (25%)
    ppermute x6, starting transfers between devices, send(): return lax.ppermute(block, 'slab', ring)  10.7 us
    pallas_call x1, Pallas kernels, on_device(): pl.pallas_call(functools.partial(frame_kernel, shifts), out_shape=outs, i...  5.13 us
    ppermute x6, waiting for transfers between devices, send(): return lax.ppermute(block, 'slab', ring)  4.41 us
    ppermute x6, starting transfers between devices, share_out(): return lax.ppermute(part, ('tilt', 'rep'), route)  4.14 us
    ppermute x6, waiting for transfers between devices, share_out(): return lax.ppermute(part, ('tilt', 'rep'), route)  3.53 us
    pallas_call x1, Pallas kernels, on_device(): pl.pallas_call(functools.partial(near_kernel, shifts), out_shape=outs, in...  1.64 us
    pallas_call x1, Pallas kernels, on_device(): pl.pallas_call(functools.partial(sum_kernel, owners), out_shape=jax.Shape...  0.75 us
  transfers between devices with their start and end apart: 14, of which 6 were waited for; matrix products, arithmetic and copies ran while one was open for 0% of the time, Pallas kernels for 7%

profile of v15, /device:TPU:0, one launch (start us, length us, event | category | flops | bytes accessed | tf_op | source)
XLA Modules:
  0.0 31.7 jit_solution(4817092148769864043)
XLA Ops:
  0.0 5.1 %frame.1 = (f32[136,128]{1,0:T(8,128)S(1)}, f32[136,128]{1,0:T(8,128)S(1)}, f32[128,128]{1,0:T(8,128)S(1)}, f32[128,128]{1,0:T(8,128)S(1)}, f32[272,128]{1,0:T(8...) custom-call(s32[1,4]{1,0:T(1,128)} %pos_hbm.1, ...), custom_call_target="tpu_custom_call" | custom-call | tf_op jit(solution)/shard_map/frame/pallas_call | solution.py:427
  5.1 0.5 %collective-permute-start = (f32[272,128]{1,0:T(8,128)S(1)}, f32[272,128]{1,0:T(8,128)S(1)}, u32[]{:S(2)}, u32[]{:S(2)}) collective-permute-start(f32[272,128]{1,0:T(8,128)S(1)} %get-tuple-element.32), channel_id=1, source_target_pairs={{0,1},{1,0},{2,3},{3,2},{4,5},{5,4},{6,7},{7,6},{8,9},{9,8},{10,11... | collective-permute-start | bytes 417800 | tf_op jit(solution)/shard_map/ppermute | solution.py:460
  5.7 1.6 %near.1 = (f32[136,128]{1,0:T(8,128)S(1)}, f32[136,128]{1,0:T(8,128)S(1)}, f32[128,128]{1,0:T(8,128)S(1)}, f32[128,128]{1,0:T(8,128)S(1)}, f32[784,128]{1,0:T(8,128)S(1)}) custom-call(s32[3,1,1,4,16]{4,3,2,1,0:T(4,128)} %index_ref.1, s32[1,1,4]{2,1,0:T(1,128)} %count_ref.1, bf16[2,128,16,128]{3,2,1,0:T(8,128)(2,1)S(1)} %get-tuple-element.34.band, ...), custom_call_target="tpu_custom_call" | custom-call | tf_op jit(solution)/shard_map/near/pallas_call | solution.py:442
  7.3 0.0 collective-permute-done.after_ref
  7.3 0.1 collective-permute-start.3
  7.5 5.1 %collective-permute-start.2 = (f32[136,128]{1,0:T(8,128)S(1)}, f32[136,128]{1,0:T(8,128)S(1)}, u32[]{:S(2)}, u32[]{:S(2)}) collective-permute-start(f32[136,128]{1,0:T(8,128)S(1)} %get-tuple-element.59), channel_id=1, source_target_pairs={{0,12},{4,8},{8,4},{12,0},{1,13},{5,9},{9,5},{13,1},{2,14},{6,10},... | collective-permute-start | bytes 208904 | tf_op jit(solution)/shard_map/ppermute | solution.py:465
  12.6 0.0 collective-permute-start.1
  12.6 0.7 %collective-permute-start.4 = (f32[136,128]{1,0:T(8,128)S(1)}, f32[136,128]{1,0:T(8,128)S(1)}, u32[]{:S(2)}, u32[]{:S(2)}) collective-permute-start(f32[136,128]{1,0:T(8,128)S(1)} %get-tuple-element.58), channel_id=1, source_target_pairs={{0,4},{4,0},{8,12},{12,8},{1,5},{5,1},{9,13},{13,9},{2,6},{6,2},{1... | collective-permute-start | bytes 208904 | tf_op jit(solution)/shard_map/ppermute | solution.py:465
  13.3 1.9 %collective-permute-done.2.refs_1_.first_ref = f32[136,128]{1,0:T(8,128)S(1)} collective-permute-done((f32[136,128]{1,0:T(8,128)S(1)}, f32[136,128]{1,0:T(8,128)S(1)}, u32[]{:S(2)}, u32[]{:S(2)}) %collective-permute-start.2) | collective-permute-done | bytes 69664 | tf_op jit(solution)/shard_map/ppermute | solution.py:465
  15.2 4.3 %collective-permute-start.9 = (f32[128,128]{1,0:T(8,128)S(1)}, f32[128,128]{1,0:T(8,128)S(1)}, u32[]{:S(2)}, u32[]{:S(2)}) collective-permute-start(f32[128,128]{1,0:T(8,128)S(1)} %get-tuple-element.49), channel_id=1, source_target_pairs={{0,12},{4,8},{8,4},{12,0},{1,13},{5,9},{9,5},{13,1},{2,14},{6,10},... | collective-permute-start | bytes 196616 | tf_op jit(solution)/shard_map/ppermute | solution.py:465
  19.5 0.1 collective-permute-done.1.refs_0_.first_ref
  19.7 0.6 %collective-permute-start.8 = (f32[128,128]{1,0:T(8,128)S(1)}, f32[128,128]{1,0:T(8,128)S(1)}, u32[]{:S(2)}, u32[]{:S(2)}) collective-permute-start(f32[128,128]{1,0:T(8,128)S(1)} %join.2), channel_id=1, source_target_pairs={{0,8},{4,12},{8,0},{12,4},{1,9},{5,13},{9,1},{13,5},{2,10},{6,14},... | collective-permute-start | bytes 196616 | tf_op jit(solution)/shard_map/ppermute | solution.py:465
  20.3 0.3 place.2
  20.6 0.1 collective-permute-start.7
  20.6 1.6 %collective-permute-start.5 = (f32[136,128]{1,0:T(8,128)S(1)}, f32[136,128]{1,0:T(8,128)S(1)}, u32[]{:S(2)}, u32[]{:S(2)}) collective-permute-start(f32[136,128]{1,0:T(8,128)S(1)} %get-tuple-element.41), channel_id=1, source_target_pairs={{0,2},{1,3},{2,0},{3,1},{4,6},{5,7},{6,4},{7,5},{8,10},{9,11},{10,... | collective-permute-start | bytes 208904 | tf_op jit(solution)/shard_map/ppermute | solution.py:505
  22.2 0.3 collective-permute-start.6
  22.5 1.9 %collective-permute-done.10.refs_2_ = f32[128,128]{1,0:T(8,128)S(1)} collective-permute-done((f32[128,128]{1,0:T(8,128)S(1)}, f32[128,128]{1,0:T(8,128)S(1)}, u32[]{:S(2)}, u32[]{:S(2)}) %collective-permute-start.10) | collective-permute-done | bytes 65568 | tf_op jit(solution)/shard_map/ppermute | solution.py:465
  24.4 0.5 %collective-permute-done.8.refs_0_ = f32[128,128]{1,0:T(8,128)S(1)} collective-permute-done((f32[128,128]{1,0:T(8,128)S(1)}, f32[128,128]{1,0:T(8,128)S(1)}, u32[]{:S(2)}, u32[]{:S(2)}) %collective-permute-start.8) | collective-permute-done | bytes 65568 | tf_op jit(solution)/shard_map/ppermute | solution.py:465
  24.9 0.3 place.3
  25.2 1.7 %collective-permute-start.11 = (f32[128,128]{1,0:T(8,128)S(1)}, f32[128,128]{1,0:T(8,128)S(1)}, u32[]{:S(2)}, u32[]{:S(2)}) collective-permute-start(f32[128,128]{1,0:T(8,128)S(1)} %get-tuple-element.53), channel_id=1, source_target_pairs={{0,2},{1,3},{2,0},{3,1},{4,6},{5,7},{6,4},{7,5},{8,10},{9,11},{10,... | collective-permute-start | bytes 196616 | tf_op jit(solution)/shard_map/ppermute | solution.py:505
  26.9 0.5 %collective-permute-start.13 = (f32[128,128]{1,0:T(8,128)S(1)}, f32[128,128]{1,0:T(8,128)S(1)}, u32[]{:S(2)}, u32[]{:S(2)}) collective-permute-start(f32[128,128]{1,0:T(8,128)S(1)} %get-tuple-element.56), channel_id=1, source_target_pairs={{0,1},{1,0},{2,3},{3,2},{4,5},{5,4},{6,7},{7,6},{8,9},{9,8},{10,11... | collective-permute-start | bytes 196616 | tf_op jit(solution)/shard_map/ppermute | solution.py:505
  27.4 2.1 %collective-permute-done.11.refs_4_ = f32[128,128]{1,0:T(8,128)S(1)} collective-permute-done((f32[128,128]{1,0:T(8,128)S(1)}, f32[128,128]{1,0:T(8,128)S(1)}, u32[]{:S(2)}, u32[]{:S(2)}) %collective-permute-start.11) | collective-permute-done | bytes 65568 | tf_op jit(solution)/shard_map/ppermute | solution.py:505
  29.5 1.4 %collective-permute-done.12.refs_5_ = f32[128,128]{1,0:T(8,128)S(1)} collective-permute-done((f32[128,128]{1,0:T(8,128)S(1)}, f32[128,128]{1,0:T(8,128)S(1)}, u32[]{:S(2)}, u32[]{:S(2)}) %collective-permute-start.12) | collective-permute-done | bytes 65568 | tf_op jit(solution)/shard_map/ppermute | solution.py:505
  30.9 0.7 %total.1 = f32[16,2,16,128]{3,2,1,0:T(8,128)} custom-call(f32[136,128]{1,0:T(8,128)S(1)} %collective-permute-done.5.refs_0_, f32[136,128]{1,0:T(8,128)S(1)} %collective-permute-done.6.refs_1_, f32[128,128]{1,0:T(8,128)S(1)} %get-tuple-element.43.refs_2_, f32[128,128]{1,0:T(8,128)S(1)} %collective-permute-done.7.refs_5_.refs_3_, ...), custom_call_target="tpu_custom_call" | custom-call | tf_op jit(solution)/shard_map/total/pallas_call | solution.py:516
  (14 shorter events, 0.1 us)
Async XLA Ops:
  5.1 2.2 %collective-permute-start = (f32[272,128]{1,0:T(8,128)S(1)}, f32[272,128]{1,0:T(8,128)S(1)}, u32[]{:S(2)}, u32[]{:S(2)}) collective-permute-start(f32[272,128]{1,0:T(8,128)S(1)} %get-tuple-element.32), channel_id=1, source_target_pairs={{0,1},{1,0},{2,3},{3,2},{4,5},{5,4},{6,7},{7,6},{8,9},{9,8},{10,11... | collective-permute-start | bytes 417800 | tf_op jit(solution)/shard_map/ppermute | solution.py:460
  7.3 5.3 %collective-permute-start.3 = (f32[784,128]{1,0:T(8,128)S(1)}, f32[784,128]{1,0:T(8,128)S(1)}, u32[]{:S(2)}, u32[]{:S(2)}) collective-permute-start(f32[784,128]{1,0:T(8,128)S(1)} %keep.1), channel_id=1, source_target_pairs={{0,1},{1,0},{2,3},{3,2},{4,5},{5,4},{6,7},{7,6},{8,9},{9,8},{10,11... | collective-permute-start | bytes 1204232 | tf_op jit(solution)/shard_map/ppermute | solution.py:461
  7.5 7.7 %collective-permute-start.2 = (f32[136,128]{1,0:T(8,128)S(1)}, f32[136,128]{1,0:T(8,128)S(1)}, u32[]{:S(2)}, u32[]{:S(2)}) collective-permute-start(f32[136,128]{1,0:T(8,128)S(1)} %get-tuple-element.59), channel_id=1, source_target_pairs={{0,12},{4,8},{8,4},{12,0},{1,13},{5,9},{9,5},{13,1},{2,14},{6,10},... | collective-permute-start | bytes 208904 | tf_op jit(solution)/shard_map/ppermute | solution.py:465
  12.6 7.1 %collective-permute-start.1 = (f32[136,128]{1,0:T(8,128)S(1)}, f32[136,128]{1,0:T(8,128)S(1)}, u32[]{:S(2)}, u32[]{:S(2)}) collective-permute-start(f32[136,128]{1,0:T(8,128)S(1)} %get-tuple-element.60), channel_id=1, source_target_pairs={{0,8},{4,12},{8,0},{12,4},{1,9},{5,13},{9,1},{13,5},{2,10},{6,14},... | collective-permute-start | bytes 208904 | tf_op jit(solution)/shard_map/ppermute | solution.py:465
  12.6 7.7 %collective-permute-start.4 = (f32[136,128]{1,0:T(8,128)S(1)}, f32[136,128]{1,0:T(8,128)S(1)}, u32[]{:S(2)}, u32[]{:S(2)}) collective-permute-start(f32[136,128]{1,0:T(8,128)S(1)} %get-tuple-element.58), channel_id=1, source_target_pairs={{0,4},{4,0},{8,12},{12,8},{1,5},{5,1},{9,13},{13,9},{2,6},{6,2},{1... | collective-permute-start | bytes 208904 | tf_op jit(solution)/shard_map/ppermute | solution.py:465
  15.2 7.0 %collective-permute-start.9 = (f32[128,128]{1,0:T(8,128)S(1)}, f32[128,128]{1,0:T(8,128)S(1)}, u32[]{:S(2)}, u32[]{:S(2)}) collective-permute-start(f32[128,128]{1,0:T(8,128)S(1)} %get-tuple-element.49), channel_id=1, source_target_pairs={{0,12},{4,8},{8,4},{12,0},{1,13},{5,9},{9,5},{13,1},{2,14},{6,10},... | collective-permute-start | bytes 196616 | tf_op jit(solution)/shard_map/ppermute | solution.py:465
  19.5 4.9 %collective-permute-start.10 = (f32[128,128]{1,0:T(8,128)S(1)}, f32[128,128]{1,0:T(8,128)S(1)}, u32[]{:S(2)}, u32[]{:S(2)}) collective-permute-start(f32[128,128]{1,0:T(8,128)S(1)} %get-tuple-element.50), channel_id=1, source_target_pairs={{0,4},{4,0},{8,12},{12,8},{1,5},{5,1},{9,13},{13,9},{2,6},{6,2},{1... | collective-permute-start | bytes 196616 | tf_op jit(solution)/shard_map/ppermute | solution.py:465
  19.7 5.3 %collective-permute-start.8 = (f32[128,128]{1,0:T(8,128)S(1)}, f32[128,128]{1,0:T(8,128)S(1)}, u32[]{:S(2)}, u32[]{:S(2)}) collective-permute-start(f32[128,128]{1,0:T(8,128)S(1)} %join.2), channel_id=1, source_target_pairs={{0,8},{4,12},{8,0},{12,4},{1,9},{5,13},{9,1},{13,5},{2,10},{6,14},... | collective-permute-start | bytes 196616 | tf_op jit(solution)/shard_map/ppermute | solution.py:465
  20.6 4.3 %collective-permute-start.7 = (f32[128,128]{1,0:T(8,128)S(1)}, f32[128,128]{1,0:T(8,128)S(1)}, u32[]{:S(2)}, u32[]{:S(2)}) collective-permute-start(f32[128,128]{1,0:T(8,128)S(1)} %get-tuple-element.44), channel_id=1, source_target_pairs={{0,1},{1,0},{2,3},{3,2},{4,5},{5,4},{6,7},{7,6},{8,9},{9,8},{10,11... | collective-permute-start | bytes 196616 | tf_op jit(solution)/shard_map/ppermute | solution.py:505
  20.6 6.8 %collective-permute-start.5 = (f32[136,128]{1,0:T(8,128)S(1)}, f32[136,128]{1,0:T(8,128)S(1)}, u32[]{:S(2)}, u32[]{:S(2)}) collective-permute-start(f32[136,128]{1,0:T(8,128)S(1)} %get-tuple-element.41), channel_id=1, source_target_pairs={{0,2},{1,3},{2,0},{3,1},{4,6},{5,7},{6,4},{7,5},{8,10},{9,11},{10,... | collective-permute-start | bytes 208904 | tf_op jit(solution)/shard_map/ppermute | solution.py:505
  22.2 5.2 %collective-permute-start.6 = (f32[136,128]{1,0:T(8,128)S(1)}, f32[136,128]{1,0:T(8,128)S(1)}, u32[]{:S(2)}, u32[]{:S(2)}) collective-permute-start(f32[136,128]{1,0:T(8,128)S(1)} %get-tuple-element.42), channel_id=1, source_target_pairs={{0,3},{1,2},{2,1},{3,0},{4,7},{5,6},{6,5},{7,4},{8,11},{9,10},{10,... | collective-permute-start | bytes 208904 | tf_op jit(solution)/shard_map/ppermute | solution.py:505
  25.2 4.3 %collective-permute-start.11 = (f32[128,128]{1,0:T(8,128)S(1)}, f32[128,128]{1,0:T(8,128)S(1)}, u32[]{:S(2)}, u32[]{:S(2)}) collective-permute-start(f32[128,128]{1,0:T(8,128)S(1)} %get-tuple-element.53), channel_id=1, source_target_pairs={{0,2},{1,3},{2,0},{3,1},{4,6},{5,7},{6,4},{7,5},{8,10},{9,11},{10,... | collective-permute-start | bytes 196616 | tf_op jit(solution)/shard_map/ppermute | solution.py:505
  26.9 4.0 %collective-permute-start.12 = (f32[128,128]{1,0:T(8,128)S(1)}, f32[128,128]{1,0:T(8,128)S(1)}, u32[]{:S(2)}, u32[]{:S(2)}) collective-permute-start(f32[128,128]{1,0:T(8,128)S(1)} %get-tuple-element.54), channel_id=1, source_target_pairs={{0,3},{1,2},{2,1},{3,0},{4,7},{5,6},{6,5},{7,4},{8,11},{9,10},{10,... | collective-permute-start | bytes 196616 | tf_op jit(solution)/shard_map/ppermute | solution.py:505
  26.9 4.0 %collective-permute-start.13 = (f32[128,128]{1,0:T(8,128)S(1)}, f32[128,128]{1,0:T(8,128)S(1)}, u32[]{:S(2)}, u32[]{:S(2)}) collective-permute-start(f32[128,128]{1,0:T(8,128)S(1)} %get-tuple-element.56), channel_id=1, source_target_pairs={{0,1},{1,0},{2,3},{3,2},{4,5},{5,4},{6,7},{7,6},{8,9},{9,8},{10,11... | collective-permute-start | bytes 196616 | tf_op jit(solution)/shard_map/ppermute | solution.py:505

commit v16 on v15

--- a/solution.py
+++ b/solution.py
@@ -150,8 +150,8 @@
 ):
     far = len(shifts) - 2
     mine, swaps = rest[: 2 * far], rest[2 * far : 2 * far + 2]
-    band, col_bf, row_scr = rest[2 * far + 2 : 2 * far + 5]
-    scratch = rest[2 * far + 5 :]
+    band, col_bf, row_scr, index_out, count_out = rest[2 * far + 2 : 2 * far + 7]
+    scratch = rest[2 * far + 7 :]
     pos_ref, index_ref, count_ref = scratch[0:3]
     phase_ref, table_ref, obj_ref, probe_ref, cot_ref, row_ref, col_ref = scratch[3:10]
     sems, window = scratch[10:]
@@ -177,10 +177,14 @@
     ]
     got_cot = pltpu.make_async_copy(cot_hbm, cot_ref, sems.at[len(copies) + slices])
     got_col = pltpu.make_async_copy(col_hbm, col_ref, sems.at[len(copies) + slices + 1])
+    got_lists = [
+        pltpu.make_async_copy(index_hbm, index_out, sems.at[len(copies) + slices + 2]),
+        pltpu.make_async_copy(count_hbm, count_out, sems.at[len(copies) + slices + 3]),
+    ]
     order = [s for i in range((slices + 1) // 2) for s in sorted({i, slices - 1 - i})]
     for copy in (got_pos, got_phase, got_table, *[got_obj[s] for s in order], got_probe, got_cot):
         copy.start()
-    for copy in (got_index, got_count, got_row, got_col):
+    for copy in (got_index, got_count, got_row, got_col, *got_lists):
         copy.start()
 
     size = probe_ref.shape[-1]
@@ -207,6 +211,8 @@
     got_col.wait()
     got_index.wait()
     got_count.wait()
+    for copy in got_lists:
+        copy.wait()
     for s in order:
         source = jnp.concatenate([obj_ref[0, 0, s], obj_ref[0, 1, s]], 0)
         window[s] = dot(source, cut).astype(bf16)
@@ -421,10 +427,12 @@
         jax.ShapeDtypeStruct((2,) + frames, bf16),
         jax.ShapeDtypeStruct(col_interp.shape, bf16),
         jax.ShapeDtypeStruct((row_interp.shape[0], block_rows, BATCH * block_rows), f32),
+        jax.ShapeDtypeStruct(pair_index.shape, pair_index.dtype),
+        jax.ShapeDtypeStruct(pair_counts.shape, pair_counts.dtype),
     ]
     spare = jax.ShapeDtypeStruct((far * lanes, block_cols), f32)
     outs = shapes[:far] + shapes[sources : sources + far] + [shapes[-2], spare] + passed
-    *held, other, spare, band, col_bf, row_wide = pl.pallas_call(
+    *held, other, spare, band, col_bf, row_wide, index_near, count_near = pl.pallas_call(
         functools.partial(frame_kernel, shifts),
         out_shape=outs,
         in_specs=[hbm] * 10,
@@ -432,7 +440,7 @@
         scratch_shapes=[SMEM(x.shape, x.dtype) for x in scalars]
         + [space(x.shape, x.dtype) for x, space in fetched]
         + [
-            pltpu.SemaphoreType.DMA((9 + slices,)),
+            pltpu.SemaphoreType.DMA((11 + slices,)),
             VMEM((slices, 2 * rows, windows * size), bf16),
         ],
         compiler_params=LIMIT,
@@ -446,7 +454,7 @@
         out_specs=[vmem] * len(outs),
         compiler_params=LIMIT,
         name="near",
-    )(in_hbm(pair_index), in_hbm(pair_counts), band, col_bf, row_wide, spare)
+    )(index_near, count_near, band, col_bf, row_wide, spare)
     mine = held[:far] + near[:2] + held[far:] + near[2:]
 
     swap = [(r, (r + 1) % cores) for r in range(cores)]

time: 31.9 us -> 31.8 us (level)
  no operation moved by 1% of the time
where the time goes in v16:
time: 31.8 us; the launch traced here: 31.6 us
  starting transfers between devices  15.5 us (49%)
  Pallas kernels  8.02 us (25%)
  waiting for transfers between devices  7.97 us (25%)
    ppermute x6, starting transfers between devices, send(): return lax.ppermute(block, 'slab', ring)  10.7 us
    pallas_call x1, Pallas kernels, on_device(): pl.pallas_call(functools.partial(frame_kernel, shifts), out_shape=outs, i...  5.14 us
    ppermute x6, waiting for transfers between devices, send(): return lax.ppermute(block, 'slab', ring)  4.43 us
    ppermute x6, starting transfers between devices, share_out(): return lax.ppermute(part, ('tilt', 'rep'), route)  4.14 us
    ppermute x6, waiting for transfers between devices, share_out(): return lax.ppermute(part, ('tilt', 'rep'), route)  3.53 us
    pallas_call x1, Pallas kernels, on_device(): pl.pallas_call(functools.partial(near_kernel, shifts), out_shape=outs, in...  1.5 us
    pallas_call x1, Pallas kernels, on_device(): pl.pallas_call(functools.partial(sum_kernel, owners), out_shape=jax.Shape...  0.75 us
  transfers between devices with their start and end apart: 14, of which 6 were waited for; matrix products, arithmetic and copies ran while one was open for 0% of the time, Pallas kernels for 7%

profile of v16, /device:TPU:0, one launch (start us, length us, event | category | flops | bytes accessed | tf_op | source)
XLA Modules:
  0.0 31.6 jit_solution(10228037760768010965)
XLA Ops:
  0.0 5.1 %frame.1 = (f32[136,128]{1,0:T(8,128)S(1)}, f32[136,128]{1,0:T(8,128)S(1)}, f32[128,128]{1,0:T(8,128)S(1)}, f32[128,128]{1,0:T(8,128)S(1)}, f32[272,128]{1,0:T(8...) custom-call(s32[1,4]{1,0:T(1,128)} %pos_hbm.1, ...), custom_call_target="tpu_custom_call" | custom-call | tf_op jit(solution)/shard_map/frame/pallas_call | solution.py:435
  5.2 0.5 %collective-permute-start = (f32[272,128]{1,0:T(8,128)S(1)}, f32[272,128]{1,0:T(8,128)S(1)}, u32[]{:S(2)}, u32[]{:S(2)}) collective-permute-start(f32[272,128]{1,0:T(8,128)S(1)} %get-tuple-element.34), channel_id=1, source_target_pairs={{0,1},{1,0},{2,3},{3,2},{4,5},{5,4},{6,7},{7,6},{8,9},{9,8},{10,11... | collective-permute-start | bytes 417800 | tf_op jit(solution)/shard_map/ppermute | solution.py:468
  5.7 1.5 %near.1 = (f32[136,128]{1,0:T(8,128)S(1)}, f32[136,128]{1,0:T(8,128)S(1)}, f32[128,128]{1,0:T(8,128)S(1)}, f32[128,128]{1,0:T(8,128)S(1)}, f32[784,128]{1,0:T(8,128)S(1)}) custom-call(s32[3,1,1,4,16]{4,3,2,1,0:T(4,128)S(1)} %get-tuple-element.36.index_ref, s32[1,1,4]{2,1,0:T(1,128)S(1)} %get-tuple-element.37.count_ref, ...), custom_call_target="tpu_custom_call" | custom-call | tf_op jit(solution)/shard_map/near/pallas_call | solution.py:450
  7.2 0.0 collective-permute-done.after_ref
  7.2 0.1 collective-permute-start.3
  7.3 5.1 %collective-permute-start.2 = (f32[136,128]{1,0:T(8,128)S(1)}, f32[136,128]{1,0:T(8,128)S(1)}, u32[]{:S(2)}, u32[]{:S(2)}) collective-permute-start(f32[136,128]{1,0:T(8,128)S(1)} %get-tuple-element.63), channel_id=1, source_target_pairs={{0,12},{4,8},{8,4},{12,0},{1,13},{5,9},{9,5},{13,1},{2,14},{6,10},... | collective-permute-start | bytes 208904 | tf_op jit(solution)/shard_map/ppermute | solution.py:473
  12.5 0.0 collective-permute-start.1
  12.5 0.7 %collective-permute-start.4 = (f32[136,128]{1,0:T(8,128)S(1)}, f32[136,128]{1,0:T(8,128)S(1)}, u32[]{:S(2)}, u32[]{:S(2)}) collective-permute-start(f32[136,128]{1,0:T(8,128)S(1)} %get-tuple-element.62), channel_id=1, source_target_pairs={{0,4},{4,0},{8,12},{12,8},{1,5},{5,1},{9,13},{13,9},{2,6},{6,2},{1... | collective-permute-start | bytes 208904 | tf_op jit(solution)/shard_map/ppermute | solution.py:473
  13.2 1.9 %collective-permute-done.2.refs_1_.first_ref = f32[136,128]{1,0:T(8,128)S(1)} collective-permute-done((f32[136,128]{1,0:T(8,128)S(1)}, f32[136,128]{1,0:T(8,128)S(1)}, u32[]{:S(2)}, u32[]{:S(2)}) %collective-permute-start.2) | collective-permute-done | bytes 69664 | tf_op jit(solution)/shard_map/ppermute | solution.py:473
  15.2 4.3 %collective-permute-start.9 = (f32[128,128]{1,0:T(8,128)S(1)}, f32[128,128]{1,0:T(8,128)S(1)}, u32[]{:S(2)}, u32[]{:S(2)}) collective-permute-start(f32[128,128]{1,0:T(8,128)S(1)} %get-tuple-element.53), channel_id=1, source_target_pairs={{0,12},{4,8},{8,4},{12,0},{1,13},{5,9},{9,5},{13,1},{2,14},{6,10},... | collective-permute-start | bytes 196616 | tf_op jit(solution)/shard_map/ppermute | solution.py:473
  19.5 0.1 collective-permute-done.1.refs_0_.first_ref
  19.6 0.6 %collective-permute-start.8 = (f32[128,128]{1,0:T(8,128)S(1)}, f32[128,128]{1,0:T(8,128)S(1)}, u32[]{:S(2)}, u32[]{:S(2)}) collective-permute-start(f32[128,128]{1,0:T(8,128)S(1)} %join.2), channel_id=1, source_target_pairs={{0,8},{4,12},{8,0},{12,4},{1,9},{5,13},{9,1},{13,5},{2,10},{6,14},... | collective-permute-start | bytes 196616 | tf_op jit(solution)/shard_map/ppermute | solution.py:473
  20.2 0.3 place.2
  20.5 0.1 collective-permute-start.7
  20.6 1.5 %collective-permute-start.5 = (f32[136,128]{1,0:T(8,128)S(1)}, f32[136,128]{1,0:T(8,128)S(1)}, u32[]{:S(2)}, u32[]{:S(2)}) collective-permute-start(f32[136,128]{1,0:T(8,128)S(1)} %get-tuple-element.45), channel_id=1, source_target_pairs={{0,2},{1,3},{2,0},{3,1},{4,6},{5,7},{6,4},{7,5},{8,10},{9,11},{10,... | collective-permute-start | bytes 208904 | tf_op jit(solution)/shard_map/ppermute | solution.py:513
  22.1 0.3 collective-permute-start.6
  22.4 1.9 %collective-permute-done.10.refs_2_ = f32[128,128]{1,0:T(8,128)S(1)} collective-permute-done((f32[128,128]{1,0:T(8,128)S(1)}, f32[128,128]{1,0:T(8,128)S(1)}, u32[]{:S(2)}, u32[]{:S(2)}) %collective-permute-start.10) | collective-permute-done | bytes 65568 | tf_op jit(solution)/shard_map/ppermute | solution.py:473
  24.3 0.5 %collective-permute-done.8.refs_0_ = f32[128,128]{1,0:T(8,128)S(1)} collective-permute-done((f32[128,128]{1,0:T(8,128)S(1)}, f32[128,128]{1,0:T(8,128)S(1)}, u32[]{:S(2)}, u32[]{:S(2)}) %collective-permute-start.8) | collective-permute-done | bytes 65568 | tf_op jit(solution)/shard_map/ppermute | solution.py:473
  24.8 0.3 place.3
  25.1 1.7 %collective-permute-start.11 = (f32[128,128]{1,0:T(8,128)S(1)}, f32[128,128]{1,0:T(8,128)S(1)}, u32[]{:S(2)}, u32[]{:S(2)}) collective-permute-start(f32[128,128]{1,0:T(8,128)S(1)} %get-tuple-element.57), channel_id=1, source_target_pairs={{0,2},{1,3},{2,0},{3,1},{4,6},{5,7},{6,4},{7,5},{8,10},{9,11},{10,... | collective-permute-start | bytes 196616 | tf_op jit(solution)/shard_map/ppermute | solution.py:513
  26.8 0.5 %collective-permute-start.13 = (f32[128,128]{1,0:T(8,128)S(1)}, f32[128,128]{1,0:T(8,128)S(1)}, u32[]{:S(2)}, u32[]{:S(2)}) collective-permute-start(f32[128,128]{1,0:T(8,128)S(1)} %get-tuple-element.60), channel_id=1, source_target_pairs={{0,1},{1,0},{2,3},{3,2},{4,5},{5,4},{6,7},{7,6},{8,9},{9,8},{10,11... | collective-permute-start | bytes 196616 | tf_op jit(solution)/shard_map/ppermute | solution.py:513
  27.3 2.1 %collective-permute-done.11.refs_4_ = f32[128,128]{1,0:T(8,128)S(1)} collective-permute-done((f32[128,128]{1,0:T(8,128)S(1)}, f32[128,128]{1,0:T(8,128)S(1)}, u32[]{:S(2)}, u32[]{:S(2)}) %collective-permute-start.11) | collective-permute-done | bytes 65568 | tf_op jit(solution)/shard_map/ppermute | solution.py:513
  29.5 1.4 %collective-permute-done.12.refs_5_ = f32[128,128]{1,0:T(8,128)S(1)} collective-permute-done((f32[128,128]{1,0:T(8,128)S(1)}, f32[128,128]{1,0:T(8,128)S(1)}, u32[]{:S(2)}, u32[]{:S(2)}) %collective-permute-start.12) | collective-permute-done | bytes 65568 | tf_op jit(solution)/shard_map/ppermute | solution.py:513
  30.9 0.7 %total.1 = f32[16,2,16,128]{3,2,1,0:T(8,128)} custom-call(f32[136,128]{1,0:T(8,128)S(1)} %collective-permute-done.5.refs_0_, f32[136,128]{1,0:T(8,128)S(1)} %collective-permute-done.6.refs_1_, f32[128,128]{1,0:T(8,128)S(1)} %get-tuple-element.47.refs_2_, f32[128,128]{1,0:T(8,128)S(1)} %collective-permute-done.7.refs_5_.refs_3_, ...), custom_call_target="tpu_custom_call" | custom-call | tf_op jit(solution)/shard_map/total/pallas_call | solution.py:524
  (14 shorter events, 0.1 us)
Async XLA Ops:
  5.2 2.0 %collective-permute-start = (f32[272,128]{1,0:T(8,128)S(1)}, f32[272,128]{1,0:T(8,128)S(1)}, u32[]{:S(2)}, u32[]{:S(2)}) collective-permute-start(f32[272,128]{1,0:T(8,128)S(1)} %get-tuple-element.34), channel_id=1, source_target_pairs={{0,1},{1,0},{2,3},{3,2},{4,5},{5,4},{6,7},{7,6},{8,9},{9,8},{10,11... | collective-permute-start | bytes 417800 | tf_op jit(solution)/shard_map/ppermute | solution.py:468
  7.2 5.3 %collective-permute-start.3 = (f32[784,128]{1,0:T(8,128)S(1)}, f32[784,128]{1,0:T(8,128)S(1)}, u32[]{:S(2)}, u32[]{:S(2)}) collective-permute-start(f32[784,128]{1,0:T(8,128)S(1)} %keep.1), channel_id=1, source_target_pairs={{0,1},{1,0},{2,3},{3,2},{4,5},{5,4},{6,7},{7,6},{8,9},{9,8},{10,11... | collective-permute-start | bytes 1204232 | tf_op jit(solution)/shard_map/ppermute | solution.py:469
  7.3 7.8 %collective-permute-start.2 = (f32[136,128]{1,0:T(8,128)S(1)}, f32[136,128]{1,0:T(8,128)S(1)}, u32[]{:S(2)}, u32[]{:S(2)}) collective-permute-start(f32[136,128]{1,0:T(8,128)S(1)} %get-tuple-element.63), channel_id=1, source_target_pairs={{0,12},{4,8},{8,4},{12,0},{1,13},{5,9},{9,5},{13,1},{2,14},{6,10},... | collective-permute-start | bytes 208904 | tf_op jit(solution)/shard_map/ppermute | solution.py:473
  12.5 7.1 %collective-permute-start.1 = (f32[136,128]{1,0:T(8,128)S(1)}, f32[136,128]{1,0:T(8,128)S(1)}, u32[]{:S(2)}, u32[]{:S(2)}) collective-permute-start(f32[136,128]{1,0:T(8,128)S(1)} %get-tuple-element.64), channel_id=1, source_target_pairs={{0,8},{4,12},{8,0},{12,4},{1,9},{5,13},{9,1},{13,5},{2,10},{6,14},... | collective-permute-start | bytes 208904 | tf_op jit(solution)/shard_map/ppermute | solution.py:473
  12.5 7.7 %collective-permute-start.4 = (f32[136,128]{1,0:T(8,128)S(1)}, f32[136,128]{1,0:T(8,128)S(1)}, u32[]{:S(2)}, u32[]{:S(2)}) collective-permute-start(f32[136,128]{1,0:T(8,128)S(1)} %get-tuple-element.62), channel_id=1, source_target_pairs={{0,4},{4,0},{8,12},{12,8},{1,5},{5,1},{9,13},{13,9},{2,6},{6,2},{1... | collective-permute-start | bytes 208904 | tf_op jit(solution)/shard_map/ppermute | solution.py:473
  15.2 6.9 %collective-permute-start.9 = (f32[128,128]{1,0:T(8,128)S(1)}, f32[128,128]{1,0:T(8,128)S(1)}, u32[]{:S(2)}, u32[]{:S(2)}) collective-permute-start(f32[128,128]{1,0:T(8,128)S(1)} %get-tuple-element.53), channel_id=1, source_target_pairs={{0,12},{4,8},{8,4},{12,0},{1,13},{5,9},{9,5},{13,1},{2,14},{6,10},... | collective-permute-start | bytes 196616 | tf_op jit(solution)/shard_map/ppermute | solution.py:473
  19.5 4.9 %collective-permute-start.10 = (f32[128,128]{1,0:T(8,128)S(1)}, f32[128,128]{1,0:T(8,128)S(1)}, u32[]{:S(2)}, u32[]{:S(2)}) collective-permute-start(f32[128,128]{1,0:T(8,128)S(1)} %get-tuple-element.54), channel_id=1, source_target_pairs={{0,4},{4,0},{8,12},{12,8},{1,5},{5,1},{9,13},{13,9},{2,6},{6,2},{1... | collective-permute-start | bytes 196616 | tf_op jit(solution)/shard_map/ppermute | solution.py:473
  19.6 5.3 %collective-permute-start.8 = (f32[128,128]{1,0:T(8,128)S(1)}, f32[128,128]{1,0:T(8,128)S(1)}, u32[]{:S(2)}, u32[]{:S(2)}) collective-permute-start(f32[128,128]{1,0:T(8,128)S(1)} %join.2), channel_id=1, source_target_pairs={{0,8},{4,12},{8,0},{12,4},{1,9},{5,13},{9,1},{13,5},{2,10},{6,14},... | collective-permute-start | bytes 196616 | tf_op jit(solution)/shard_map/ppermute | solution.py:473
  20.5 4.3 %collective-permute-start.7 = (f32[128,128]{1,0:T(8,128)S(1)}, f32[128,128]{1,0:T(8,128)S(1)}, u32[]{:S(2)}, u32[]{:S(2)}) collective-permute-start(f32[128,128]{1,0:T(8,128)S(1)} %get-tuple-element.48), channel_id=1, source_target_pairs={{0,1},{1,0},{2,3},{3,2},{4,5},{5,4},{6,7},{7,6},{8,9},{9,8},{10,11... | collective-permute-start | bytes 196616 | tf_op jit(solution)/shard_map/ppermute | solution.py:513
  20.6 6.8 %collective-permute-start.5 = (f32[136,128]{1,0:T(8,128)S(1)}, f32[136,128]{1,0:T(8,128)S(1)}, u32[]{:S(2)}, u32[]{:S(2)}) collective-permute-start(f32[136,128]{1,0:T(8,128)S(1)} %get-tuple-element.45), channel_id=1, source_target_pairs={{0,2},{1,3},{2,0},{3,1},{4,6},{5,7},{6,4},{7,5},{8,10},{9,11},{10,... | collective-permute-start | bytes 208904 | tf_op jit(solution)/shard_map/ppermute | solution.py:513
  22.1 5.2 %collective-permute-start.6 = (f32[136,128]{1,0:T(8,128)S(1)}, f32[136,128]{1,0:T(8,128)S(1)}, u32[]{:S(2)}, u32[]{:S(2)}) collective-permute-start(f32[136,128]{1,0:T(8,128)S(1)} %get-tuple-element.46), channel_id=1, source_target_pairs={{0,3},{1,2},{2,1},{3,0},{4,7},{5,6},{6,5},{7,4},{8,11},{9,10},{10,... | collective-permute-start | bytes 208904 | tf_op jit(solution)/shard_map/ppermute | solution.py:513
  25.1 4.3 %collective-permute-start.11 = (f32[128,128]{1,0:T(8,128)S(1)}, f32[128,128]{1,0:T(8,128)S(1)}, u32[]{:S(2)}, u32[]{:S(2)}) collective-permute-start(f32[128,128]{1,0:T(8,128)S(1)} %get-tuple-element.57), channel_id=1, source_target_pairs={{0,2},{1,3},{2,0},{3,1},{4,6},{5,7},{6,4},{7,5},{8,10},{9,11},{10,... | collective-permute-start | bytes 196616 | tf_op jit(solution)/shard_map/ppermute | solution.py:513
  26.8 4.1 %collective-permute-start.12 = (f32[128,128]{1,0:T(8,128)S(1)}, f32[128,128]{1,0:T(8,128)S(1)}, u32[]{:S(2)}, u32[]{:S(2)}) collective-permute-start(f32[128,128]{1,0:T(8,128)S(1)} %get-tuple-element.58), channel_id=1, source_target_pairs={{0,3},{1,2},{2,1},{3,0},{4,7},{5,6},{6,5},{7,4},{8,11},{9,10},{10,... | collective-permute-start | bytes 196616 | tf_op jit(solution)/shard_map/ppermute | solution.py:513
  26.8 4.1 %collective-permute-start.13 = (f32[128,128]{1,0:T(8,128)S(1)}, f32[128,128]{1,0:T(8,128)S(1)}, u32[]{:S(2)}, u32[]{:S(2)}) collective-permute-start(f32[128,128]{1,0:T(8,128)S(1)} %get-tuple-element.60), channel_id=1, source_target_pairs={{0,1},{1,0},{2,3},{3,2},{4,5},{5,4},{6,7},{7,6},{8,9},{9,8},{10,11... | collective-permute-start | bytes 196616 | tf_op jit(solution)/shard_map/ppermute | solution.py:513

commit v17 on v16

--- a/solution.py
+++ b/solution.py
@@ -118,20 +118,21 @@
         put(k, 0, capacity * half, jnp.concatenate([marks, jnp.zeros_like(marks)], 1))
 
 
-def near_kernel(shifts, index_ref, count_ref, band, col_bf, row_scr, spare, *refs):
-    mine, other = refs[:-1], refs[-1]
-    far, near = len(shifts) - 2, 2
+def own_kernel(shifts, index_ref, count_ref, band, col_bf, row_scr, spare, *refs):
+    mine, other = refs[:CHUNKS], refs[CHUNKS]
+    last = len(shifts) - 1
     half, cols = CHUNK_ROWS, band.shape[-1]
     lines = index_ref.shape[-1] * half
-    late = near * (lines + half)
-    other[late : late + far * lines] = spare[...]
+    tall = lines + half
+    other[:tall] = spare[:tall]
+    other[2 * tall : 2 * tall + last * lines] = spare[tall:]
 
     def put(k, h, row, value):
-        base = late + k * lines if h else (k - far) * (lines + half)
-        mine[h * near + k - far][row : row + half] = value[:, :cols]
-        other[base + row : base + row + half] = value[:, cols:]
-
-    mix_blocks(shifts, range(far, far + near), index_ref, count_ref, band, col_bf, row_scr, put)
+        base = (2 * tall + last * lines if h else tall) + row
+        mine[h][row : row + half] = value[:, :cols]
+        other[base : base + half] = value[:, cols:]
+
+    mix_blocks(shifts, [last], index_ref, count_ref, band, col_bf, row_scr, put)
 
 
 def frame_kernel(
@@ -149,9 +150,10 @@
     *rest,
 ):
     far = len(shifts) - 2
-    mine, swaps = rest[: 2 * far], rest[2 * far : 2 * far + 2]
-    band, col_bf, row_scr, index_out, count_out = rest[2 * far + 2 : 2 * far + 7]
-    scratch = rest[2 * far + 7 :]
+    sent = far + 1
+    mine, (other, spare) = rest[: 2 * sent], rest[2 * sent : 2 * sent + 2]
+    band, col_bf, row_scr, index_out, count_out = rest[2 * sent + 2 : 2 * sent + 7]
+    scratch = rest[2 * sent + 7 :]
     pos_ref, index_ref, count_ref = scratch[0:3]
     phase_ref, table_ref, obj_ref, probe_ref, cot_ref, row_ref, col_ref = scratch[3:10]
     sems, window = scratch[10:]
@@ -308,11 +310,15 @@
     half = block_rows // CHUNKS
 
     def put(k, h, row, value):
-        base = k * mine[h * far].shape[0] + row
-        mine[h * far + k][row : row + half] = value[:, :block_cols]
-        swaps[h][base : base + half] = value[:, block_cols:]
-
-    mix_blocks(shifts, range(far), index_ref, count_ref, band, col_bf, row_scr, put)
+        tall, lines = mine[0].shape[0], mine[sent].shape[0]
+        if h:
+            swap, base = spare, tall + k * lines + row
+        else:
+            swap, base = (other, k * tall + row) if k < far else (spare, row)
+        mine[h * sent + k][row : row + half] = value[:, :block_cols]
+        swap[base : base + half] = value[:, block_cols:]
+
+    mix_blocks(shifts, range(sent), index_ref, count_ref, band, col_bf, row_scr, put)
 
 
 def keep_until(value, after):
@@ -430,8 +436,9 @@
         jax.ShapeDtypeStruct(pair_index.shape, pair_index.dtype),
         jax.ShapeDtypeStruct(pair_counts.shape, pair_counts.dtype),
     ]
-    spare = jax.ShapeDtypeStruct((far * lanes, block_cols), f32)
-    outs = shapes[:far] + shapes[sources : sources + far] + [shapes[-2], spare] + passed
+    sent = far + 1
+    spare = jax.ShapeDtypeStruct((tall + sent * lanes, block_cols), f32)
+    outs = shapes[:sent] + shapes[sources : sources + sent] + [shapes[-2], spare] + passed
     *held, other, spare, band, col_bf, row_wide, index_near, count_near = pl.pallas_call(
         functools.partial(frame_kernel, shifts),
         out_shape=outs,
@@ -446,16 +453,16 @@
         compiler_params=LIMIT,
         name="frame",
     )(*[in_hbm(x) for x in scalars + [x for x, _ in fetched]])
-    outs = shapes[far:sources] + shapes[sources + far : 2 * sources] + [shapes[-1]]
-    *near, rest = pl.pallas_call(
-        functools.partial(near_kernel, shifts),
+    outs = [shapes[sent], shapes[sources + sent], shapes[-1]]
+    *own, rest = pl.pallas_call(
+        functools.partial(own_kernel, shifts),
         out_shape=outs,
         in_specs=[pl.BlockSpec(memory_space=SMEM)] * 2 + [vmem] * 4,
         out_specs=[vmem] * len(outs),
         compiler_params=LIMIT,
-        name="near",
+        name="own",
     )(index_near, count_near, band, col_bf, row_wide, spare)
-    mine = held[:far] + near[:2] + held[far:] + near[2:]
+    mine = held[:sent] + own[:1] + held[sent:] + own[1:]
 
     swap = [(r, (r + 1) % cores) for r in range(cores)]
     owners = sorted(

time: 31.8 us -> 32.2 us (1.013)
  waiting for transfers between devices: 7.97 us -> 8.88 us
  starting transfers between devices: 15.5 us -> 15 us
    ppermute x6, waiting for transfers between devices: 4.43 us -> 5.35 us  [send(): return lax.ppermute(block, 'slab', ring)]
    ppermute x6, starting transfers between devices: 10.7 us -> 10.1 us  [send(): return lax.ppermute(block, 'slab', ring)]
    pallas_call x1, Pallas kernels: 5.14 us -> 5.51 us  [on_device(): pl.pallas_call(functools.partial(frame_kernel, shifts), out_shape=outs, i...]
    pallas_call x1, Pallas kernels: 1.5 us -> 1.16 us  [on_device(): pl.pallas_call(functools.partial(own_kernel, shifts), out_shape=outs, in_...]
  transfers between devices with their start and end apart: 14 -> 14, of which waited for: 6 -> 6; matrix products, arithmetic and copies ran while one was open for 0% -> 0% of each run, Pallas kernels for 7% -> 6%
where the time goes in v17:
time: 32.2 us; the launch traced here: 32 us
  starting transfers between devices  15 us (47%)
  waiting for transfers between devices  8.88 us (28%)
  Pallas kernels  8.04 us (25%)
    ppermute x6, starting transfers between devices, send(): return lax.ppermute(block, 'slab', ring)  10.1 us
    pallas_call x1, Pallas kernels, on_device(): pl.pallas_call(functools.partial(frame_kernel, shifts), out_shape=outs, i...  5.51 us
    ppermute x6, waiting for transfers between devices, send(): return lax.ppermute(block, 'slab', ring)  5.35 us
    ppermute x6, starting transfers between devices, share_out(): return lax.ppermute(part, ('tilt', 'rep'), route)  4.14 us
    ppermute x6, waiting for transfers between devices, share_out(): return lax.ppermute(part, ('tilt', 'rep'), route)  3.53 us
    pallas_call x1, Pallas kernels, on_device(): pl.pallas_call(functools.partial(own_kernel, shifts), out_shape=outs, in_...  1.16 us
    pallas_call x1, Pallas kernels, on_device(): pl.pallas_call(functools.partial(sum_kernel, owners), out_shape=jax.Shape...  0.75 us
  transfers between devices with their start and end apart: 14, of which 6 were waited for; matrix products, arithmetic and copies ran while one was open for 0% of the time, Pallas kernels for 6%

profile of v17, /device:TPU:0, one launch (start us, length us, event | category | flops | bytes accessed | tf_op | source)
XLA Modules:
  0.0 32.0 jit_solution(8069659358155834232)
XLA Ops:
  0.0 5.5 %frame.1 = (f32[136,128]{1,0:T(8,128)S(1)}, f32[136,128]{1,0:T(8,128)S(1)}, f32[136,128]{1,0:T(8,128)S(1)}, f32[128,128]{1,0:T(8,128)S(1)}, f32[128,128]{1,0:T(8...) custom-call(s32[1,4]{1,0:T(1,128)} %pos_hbm.1, ...), custom_call_target="tpu_custom_call" | custom-call | tf_op jit(solution)/shard_map/frame/pallas_call | solution.py:442
  5.5 0.5 %collective-permute-start = (f32[272,128]{1,0:T(8,128)S(1)}, f32[272,128]{1,0:T(8,128)S(1)}, u32[]{:S(2)}, u32[]{:S(2)}) collective-permute-start(f32[272,128]{1,0:T(8,128)S(1)} %get-tuple-element.34), channel_id=1, source_target_pairs={{0,1},{1,0},{2,3},{3,2},{4,5},{5,4},{6,7},{7,6},{8,9},{9,8},{10,11... | collective-permute-start | bytes 417800 | tf_op jit(solution)/shard_map/ppermute | solution.py:475
  6.0 1.2 %own.1 = (f32[136,128]{1,0:T(8,128)S(1)}, f32[128,128]{1,0:T(8,128)S(1)}, f32[784,128]{1,0:T(8,128)S(1)}) custom-call(s32[3,1,1,4,16]{4,3,2,1,0:T(4,128)S(1)} %get-tuple-element.37.index_ref, s32[1,1,4]{2,1,0:T(1,128)S(1)} %get-tuple-element.38.count_ref, bf16[2,128,16,128]{3,2,1,0:T(8,128)(2,1)S(1)} %get-tuple-element.39.band, ...), custom_call_target="tpu_custom_call" | custom-call | tf_op jit(solution)/shard_map/own/pallas_call | solution.py:457
  7.2 0.2 collective-permute-start.3
  7.4 5.1 %collective-permute-start.2 = (f32[136,128]{1,0:T(8,128)S(1)}, f32[136,128]{1,0:T(8,128)S(1)}, u32[]{:S(2)}, u32[]{:S(2)}) collective-permute-start(f32[136,128]{1,0:T(8,128)S(1)} %get-tuple-element.63), channel_id=1, source_target_pairs={{0,12},{4,8},{8,4},{12,0},{1,13},{5,9},{9,5},{13,1},{2,14},{6,10},... | collective-permute-start | bytes 208904 | tf_op jit(solution)/shard_map/ppermute | solution.py:480
  12.5 0.7 %collective-permute-start.4 = (f32[136,128]{1,0:T(8,128)S(1)}, f32[136,128]{1,0:T(8,128)S(1)}, u32[]{:S(2)}, u32[]{:S(2)}) collective-permute-start(f32[136,128]{1,0:T(8,128)S(1)} %get-tuple-element.62), channel_id=1, source_target_pairs={{0,4},{4,0},{8,12},{12,8},{1,5},{5,1},{9,13},{13,9},{2,6},{6,2},{1... | collective-permute-start | bytes 208904 | tf_op jit(solution)/shard_map/ppermute | solution.py:480
  13.2 2.0 %collective-permute-done.2.refs_1_.first_ref = f32[136,128]{1,0:T(8,128)S(1)} collective-permute-done((f32[136,128]{1,0:T(8,128)S(1)}, f32[136,128]{1,0:T(8,128)S(1)}, u32[]{:S(2)}, u32[]{:S(2)}) %collective-permute-start.2) | collective-permute-done | bytes 69664 | tf_op jit(solution)/shard_map/ppermute | solution.py:480
  15.2 4.2 %collective-permute-start.9 = (f32[128,128]{1,0:T(8,128)S(1)}, f32[128,128]{1,0:T(8,128)S(1)}, u32[]{:S(2)}, u32[]{:S(2)}) collective-permute-start(f32[128,128]{1,0:T(8,128)S(1)} %get-tuple-element.53), channel_id=1, source_target_pairs={{0,12},{4,8},{8,4},{12,0},{1,13},{5,9},{9,5},{13,1},{2,14},{6,10},... | collective-permute-start | bytes 196616 | tf_op jit(solution)/shard_map/ppermute | solution.py:480
  19.5 0.5 %collective-permute-done.1.refs_0_.first_ref = f32[136,128]{1,0:T(8,128)S(1)} collective-permute-done((f32[136,128]{1,0:T(8,128)S(1)}, f32[136,128]{1,0:T(8,128)S(1)}, u32[]{:S(2)}, u32[]{:S(2)}) %collective-permute-start.1) | collective-permute-done | bytes 69664 | tf_op jit(solution)/shard_map/ppermute | solution.py:480
  20.0 0.2 collective-permute-start.8
  20.2 0.0 collective-permute-done.4.refs_2_
  20.2 0.3 place.2
  20.5 0.1 collective-permute-start.7
  20.6 1.6 %collective-permute-start.5 = (f32[136,128]{1,0:T(8,128)S(1)}, f32[136,128]{1,0:T(8,128)S(1)}, u32[]{:S(2)}, u32[]{:S(2)}) collective-permute-start(f32[136,128]{1,0:T(8,128)S(1)} %get-tuple-element.45), channel_id=1, source_target_pairs={{0,2},{1,3},{2,0},{3,1},{4,6},{5,7},{6,4},{7,5},{8,10},{9,11},{10,... | collective-permute-start | bytes 208904 | tf_op jit(solution)/shard_map/ppermute | solution.py:520
  22.1 0.3 collective-permute-start.6
  22.4 1.7 %collective-permute-done.10.refs_2_ = f32[128,128]{1,0:T(8,128)S(1)} collective-permute-done((f32[128,128]{1,0:T(8,128)S(1)}, f32[128,128]{1,0:T(8,128)S(1)}, u32[]{:S(2)}, u32[]{:S(2)}) %collective-permute-start.10) | collective-permute-done | bytes 65568 | tf_op jit(solution)/shard_map/ppermute | solution.py:480
  24.1 1.1 %collective-permute-done.8.refs_0_ = f32[128,128]{1,0:T(8,128)S(1)} collective-permute-done((f32[128,128]{1,0:T(8,128)S(1)}, f32[128,128]{1,0:T(8,128)S(1)}, u32[]{:S(2)}, u32[]{:S(2)}) %collective-permute-start.8) | collective-permute-done | bytes 65568 | tf_op jit(solution)/shard_map/ppermute | solution.py:480
  25.2 0.0 collective-permute-done.7.refs_5_.refs_3_
  25.2 0.3 place.3
  25.5 1.4 %collective-permute-start.11 = (f32[128,128]{1,0:T(8,128)S(1)}, f32[128,128]{1,0:T(8,128)S(1)}, u32[]{:S(2)}, u32[]{:S(2)}) collective-permute-start(f32[128,128]{1,0:T(8,128)S(1)} %get-tuple-element.57), channel_id=1, source_target_pairs={{0,2},{1,3},{2,0},{3,1},{4,6},{5,7},{6,4},{7,5},{8,10},{9,11},{10,... | collective-permute-start | bytes 196616 | tf_op jit(solution)/shard_map/ppermute | solution.py:520
  27.0 0.8 %collective-permute-start.13 = (f32[128,128]{1,0:T(8,128)S(1)}, f32[128,128]{1,0:T(8,128)S(1)}, u32[]{:S(2)}, u32[]{:S(2)}) collective-permute-start(f32[128,128]{1,0:T(8,128)S(1)} %get-tuple-element.60), channel_id=1, source_target_pairs={{0,1},{1,0},{2,3},{3,2},{4,5},{5,4},{6,7},{7,6},{8,9},{9,8},{10,11... | collective-permute-start | bytes 196616 | tf_op jit(solution)/shard_map/ppermute | solution.py:520
  27.7 2.1 %collective-permute-done.11.refs_4_ = f32[128,128]{1,0:T(8,128)S(1)} collective-permute-done((f32[128,128]{1,0:T(8,128)S(1)}, f32[128,128]{1,0:T(8,128)S(1)}, u32[]{:S(2)}, u32[]{:S(2)}) %collective-permute-start.11) | collective-permute-done | bytes 65568 | tf_op jit(solution)/shard_map/ppermute | solution.py:520
  29.9 1.4 %collective-permute-done.12.refs_5_ = f32[128,128]{1,0:T(8,128)S(1)} collective-permute-done((f32[128,128]{1,0:T(8,128)S(1)}, f32[128,128]{1,0:T(8,128)S(1)}, u32[]{:S(2)}, u32[]{:S(2)}) %collective-permute-start.12) | collective-permute-done | bytes 65568 | tf_op jit(solution)/shard_map/ppermute | solution.py:520
  31.3 0.7 %total.1 = f32[16,2,16,128]{3,2,1,0:T(8,128)} custom-call(f32[136,128]{1,0:T(8,128)S(1)} %collective-permute-done.5.refs_0_, f32[136,128]{1,0:T(8,128)S(1)} %collective-permute-done.6.refs_1_, f32[128,128]{1,0:T(8,128)S(1)} %get-tuple-element.47.refs_2_, f32[128,128]{1,0:T(8,128)S(1)} %collective-permute-done.7.refs_5_.refs_3_, ...), custom_call_target="tpu_custom_call" | custom-call | tf_op jit(solution)/shard_map/total/pallas_call | solution.py:531
  (14 shorter events, 0.1 us)
Async XLA Ops:
  5.5 1.7 %collective-permute-start = (f32[272,128]{1,0:T(8,128)S(1)}, f32[272,128]{1,0:T(8,128)S(1)}, u32[]{:S(2)}, u32[]{:S(2)}) collective-permute-start(f32[272,128]{1,0:T(8,128)S(1)} %get-tuple-element.34), channel_id=1, source_target_pairs={{0,1},{1,0},{2,3},{3,2},{4,5},{5,4},{6,7},{7,6},{8,9},{9,8},{10,11... | collective-permute-start | bytes 417800 | tf_op jit(solution)/shard_map/ppermute | solution.py:475
  7.2 5.3 %collective-permute-start.3 = (f32[784,128]{1,0:T(8,128)S(1)}, f32[784,128]{1,0:T(8,128)S(1)}, u32[]{:S(2)}, u32[]{:S(2)}) collective-permute-start(f32[784,128]{1,0:T(8,128)S(1)} %keep.1), channel_id=1, source_target_pairs={{0,1},{1,0},{2,3},{3,2},{4,5},{5,4},{6,7},{7,6},{8,9},{9,8},{10,11... | collective-permute-start | bytes 1204232 | tf_op jit(solution)/shard_map/ppermute | solution.py:476
  7.4 7.8 %collective-permute-start.2 = (f32[136,128]{1,0:T(8,128)S(1)}, f32[136,128]{1,0:T(8,128)S(1)}, u32[]{:S(2)}, u32[]{:S(2)}) collective-permute-start(f32[136,128]{1,0:T(8,128)S(1)} %get-tuple-element.63), channel_id=1, source_target_pairs={{0,12},{4,8},{8,4},{12,0},{1,13},{5,9},{9,5},{13,1},{2,14},{6,10},... | collective-permute-start | bytes 208904 | tf_op jit(solution)/shard_map/ppermute | solution.py:480
  12.5 7.5 %collective-permute-start.1 = (f32[136,128]{1,0:T(8,128)S(1)}, f32[136,128]{1,0:T(8,128)S(1)}, u32[]{:S(2)}, u32[]{:S(2)}) collective-permute-start(f32[136,128]{1,0:T(8,128)S(1)} %get-tuple-element.64), channel_id=1, source_target_pairs={{0,8},{4,12},{8,0},{12,4},{1,9},{5,13},{9,1},{13,5},{2,10},{6,14},... | collective-permute-start | bytes 208904 | tf_op jit(solution)/shard_map/ppermute | solution.py:480
  12.5 7.7 %collective-permute-start.4 = (f32[136,128]{1,0:T(8,128)S(1)}, f32[136,128]{1,0:T(8,128)S(1)}, u32[]{:S(2)}, u32[]{:S(2)}) collective-permute-start(f32[136,128]{1,0:T(8,128)S(1)} %get-tuple-element.62), channel_id=1, source_target_pairs={{0,4},{4,0},{8,12},{12,8},{1,5},{5,1},{9,13},{13,9},{2,6},{6,2},{1... | collective-permute-start | bytes 208904 | tf_op jit(solution)/shard_map/ppermute | solution.py:480
  15.2 6.9 %collective-permute-start.9 = (f32[128,128]{1,0:T(8,128)S(1)}, f32[128,128]{1,0:T(8,128)S(1)}, u32[]{:S(2)}, u32[]{:S(2)}) collective-permute-start(f32[128,128]{1,0:T(8,128)S(1)} %get-tuple-element.53), channel_id=1, source_target_pairs={{0,12},{4,8},{8,4},{12,0},{1,13},{5,9},{9,5},{13,1},{2,14},{6,10},... | collective-permute-start | bytes 196616 | tf_op jit(solution)/shard_map/ppermute | solution.py:480
  19.5 4.6 %collective-permute-start.10 = (f32[128,128]{1,0:T(8,128)S(1)}, f32[128,128]{1,0:T(8,128)S(1)}, u32[]{:S(2)}, u32[]{:S(2)}) collective-permute-start(f32[128,128]{1,0:T(8,128)S(1)} %get-tuple-element.54), channel_id=1, source_target_pairs={{0,4},{4,0},{8,12},{12,8},{1,5},{5,1},{9,13},{13,9},{2,6},{6,2},{1... | collective-permute-start | bytes 196616 | tf_op jit(solution)/shard_map/ppermute | solution.py:480
  20.0 5.2 %collective-permute-start.8 = (f32[128,128]{1,0:T(8,128)S(1)}, f32[128,128]{1,0:T(8,128)S(1)}, u32[]{:S(2)}, u32[]{:S(2)}) collective-permute-start(f32[128,128]{1,0:T(8,128)S(1)} %join.2), channel_id=1, source_target_pairs={{0,8},{4,12},{8,0},{12,4},{1,9},{5,13},{9,1},{13,5},{2,10},{6,14},... | collective-permute-start | bytes 196616 | tf_op jit(solution)/shard_map/ppermute | solution.py:480
  20.5 4.8 %collective-permute-start.7 = (f32[128,128]{1,0:T(8,128)S(1)}, f32[128,128]{1,0:T(8,128)S(1)}, u32[]{:S(2)}, u32[]{:S(2)}) collective-permute-start(f32[128,128]{1,0:T(8,128)S(1)} %get-tuple-element.48), channel_id=1, source_target_pairs={{0,1},{1,0},{2,3},{3,2},{4,5},{5,4},{6,7},{7,6},{8,9},{9,8},{10,11... | collective-permute-start | bytes 196616 | tf_op jit(solution)/shard_map/ppermute | solution.py:520
  20.6 7.2 %collective-permute-start.5 = (f32[136,128]{1,0:T(8,128)S(1)}, f32[136,128]{1,0:T(8,128)S(1)}, u32[]{:S(2)}, u32[]{:S(2)}) collective-permute-start(f32[136,128]{1,0:T(8,128)S(1)} %get-tuple-element.45), channel_id=1, source_target_pairs={{0,2},{1,3},{2,0},{3,1},{4,6},{5,7},{6,4},{7,5},{8,10},{9,11},{10,... | collective-permute-start | bytes 208904 | tf_op jit(solution)/shard_map/ppermute | solution.py:520
  22.1 5.6 %collective-permute-start.6 = (f32[136,128]{1,0:T(8,128)S(1)}, f32[136,128]{1,0:T(8,128)S(1)}, u32[]{:S(2)}, u32[]{:S(2)}) collective-permute-start(f32[136,128]{1,0:T(8,128)S(1)} %get-tuple-element.46), channel_id=1, source_target_pairs={{0,3},{1,2},{2,1},{3,0},{4,7},{5,6},{6,5},{7,4},{8,11},{9,10},{10,... | collective-permute-start | bytes 208904 | tf_op jit(solution)/shard_map/ppermute | solution.py:520
  25.5 4.3 %collective-permute-start.11 = (f32[128,128]{1,0:T(8,128)S(1)}, f32[128,128]{1,0:T(8,128)S(1)}, u32[]{:S(2)}, u32[]{:S(2)}) collective-permute-start(f32[128,128]{1,0:T(8,128)S(1)} %get-tuple-element.57), channel_id=1, source_target_pairs={{0,2},{1,3},{2,0},{3,1},{4,6},{5,7},{6,4},{7,5},{8,10},{9,11},{10,... | collective-permute-start | bytes 196616 | tf_op jit(solution)/shard_map/ppermute | solution.py:520
  27.0 4.3 %collective-permute-start.12 = (f32[128,128]{1,0:T(8,128)S(1)}, f32[128,128]{1,0:T(8,128)S(1)}, u32[]{:S(2)}, u32[]{:S(2)}) collective-permute-start(f32[128,128]{1,0:T(8,128)S(1)} %get-tuple-element.58), channel_id=1, source_target_pairs={{0,3},{1,2},{2,1},{3,0},{4,7},{5,6},{6,5},{7,4},{8,11},{9,10},{10,... | collective-permute-start | bytes 196616 | tf_op jit(solution)/shard_map/ppermute | solution.py:520
  27.0 4.3 %collective-permute-start.13 = (f32[128,128]{1,0:T(8,128)S(1)}, f32[128,128]{1,0:T(8,128)S(1)}, u32[]{:S(2)}, u32[]{:S(2)}) collective-permute-start(f32[128,128]{1,0:T(8,128)S(1)} %get-tuple-element.60), channel_id=1, source_target_pairs={{0,1},{1,0},{2,3},{3,2},{4,5},{5,4},{6,7},{7,6},{8,9},{9,8},{10,11... | collective-permute-start | bytes 196616 | tf_op jit(solution)/shard_map/ppermute | solution.py:520

commit v18 on v12

--- a/solution.py
+++ b/solution.py
@@ -474,7 +474,8 @@
 
     joined = []
     for k in range(far):
-        joined += join(first[k], slice(k, k + 1 if k + 1 < far else sources))
+        joined += join(first[k], slice(k, k + 1))
+    joined += join(first[0], slice(far, sources))
     second = [send(block, k) if k else block for block, k in zip(joined, shifts)]
     *parts, marks = place(first, [], 0)
     extra = [share_out(part, owner) for part, owner in zip(parts, owners)]

time: 31.8 us -> 35.3 us (1.11)
  waiting for transfers between devices: 9.08 us -> 12.7 us
    ppermute x6, waiting for transfers between devices: 4.55 us -> 8.17 us  [send(): return lax.ppermute(block, 'slab', ring)]
where the time goes in v18:
time: 35.3 us; the launch traced here: 35.1 us
  starting transfers between devices  15.1 us (43%)
  waiting for transfers between devices  12.7 us (36%)
  Pallas kernels  7.23 us (20%)
    ppermute x6, starting transfers between devices, send(): return lax.ppermute(block, 'slab', ring)  10.1 us
    ppermute x6, waiting for transfers between devices, send(): return lax.ppermute(block, 'slab', ring)  8.17 us
    pallas_call x1, Pallas kernels, on_device(): pl.pallas_call(functools.partial(frame_kernel, shifts), out_shape=shapes,...  5.85 us
    ppermute x6, starting transfers between devices, share_out(): return lax.ppermute(part, ('tilt', 'rep'), route)  4.14 us
    ppermute x6, waiting for transfers between devices, share_out(): return lax.ppermute(part, ('tilt', 'rep'), route)  3.53 us
    ppermute x1, waiting for transfers between devices, on_device(): got = [lax.ppermute(other[0], 'rep', swap)]  1 us
    pallas_call x1, Pallas kernels, on_device(): pl.pallas_call(functools.partial(sum_kernel, owners), out_shape=jax.Shape...  0.75 us
  transfers between devices with their start and end apart: 14, of which 6 were waited for; matrix products, arithmetic and copies ran while one was open for 0% of the time, Pallas kernels for 2%

profile of v18, /device:TPU:0, one launch (start us, length us, event | category | flops | bytes accessed | tf_op | source)
XLA Modules:
  0.0 35.1 jit_solution(2363124010856365536)
XLA Ops:
  0.0 5.8 %frame.1 = (f32[136,128]{1,0:T(8,128)S(1)}, f32[136,128]{1,0:T(8,128)S(1)}, f32[136,128]{1,0:T(8,128)S(1)}, f32[136,128]{1,0:T(8,128)S(1)}, f32[128,128]{1,0:T(8...) custom-call(s32[1,4]{1,0:T(1,128)} %pos_hbm.1, ...), custom_call_target="tpu_custom_call" | custom-call | tf_op jit(solution)/shard_map/frame/pallas_call | solution.py:401
  5.9 0.5 %collective-permute-start = (f32[272,128]{1,0:T(8,128)S(1)}, f32[272,128]{1,0:T(8,128)S(1)}, u32[]{:S(2)}, u32[]{:S(2)}) collective-permute-start(f32[272,128]{1,0:T(8,128)S(1)} %get-tuple-element.27), channel_id=1, source_target_pairs={{0,1},{1,0},{2,3},{3,2},{4,5},{5,4},{6,7},{7,6},{8,9},{9,8},{10,11... | collective-permute-start | bytes 417800 | tf_op jit(solution)/shard_map/ppermute | solution.py:428
  6.4 1.0 %collective-permute-done.after_ref = f32[272,128]{1,0:T(8,128)S(1)} collective-permute-done((f32[272,128]{1,0:T(8,128)S(1)}, f32[272,128]{1,0:T(8,128)S(1)}, u32[]{:S(2)}, u32[]{:S(2)}) %collective-permute-start) | collective-permute-done | bytes 139296 | tf_op jit(solution)/shard_map/ppermute | solution.py:428
  7.4 0.4 %collective-permute-start.3 = (f32[784,128]{1,0:T(8,128)S(1)}, f32[784,128]{1,0:T(8,128)S(1)}, u32[]{:S(2)}, u32[]{:S(2)}) collective-permute-start(f32[784,128]{1,0:T(8,128)S(1)} %keep.1), channel_id=1, source_target_pairs={{0,1},{1,0},{2,3},{3,2},{4,5},{5,4},{6,7},{7,6},{8,9},{9,8},{10,11... | collective-permute-start | bytes 1204232 | tf_op jit(solution)/shard_map/ppermute | solution.py:429
  7.8 4.8 %collective-permute-start.2 = (f32[136,128]{1,0:T(8,128)S(1)}, f32[136,128]{1,0:T(8,128)S(1)}, u32[]{:S(2)}, u32[]{:S(2)}) collective-permute-start(f32[136,128]{1,0:T(8,128)S(1)} %get-tuple-element.49), channel_id=1, source_target_pairs={{0,12},{4,8},{8,4},{12,0},{1,13},{5,9},{9,5},{13,1},{2,14},{6,10},... | collective-permute-start | bytes 208904 | tf_op jit(solution)/shard_map/ppermute | solution.py:433
  12.6 0.7 %collective-permute-start.4 = (f32[136,128]{1,0:T(8,128)S(1)}, f32[136,128]{1,0:T(8,128)S(1)}, u32[]{:S(2)}, u32[]{:S(2)}) collective-permute-start(f32[136,128]{1,0:T(8,128)S(1)} %get-tuple-element.48), channel_id=1, source_target_pairs={{0,4},{4,0},{8,12},{12,8},{1,5},{5,1},{9,13},{13,9},{2,6},{6,2},{1... | collective-permute-start | bytes 208904 | tf_op jit(solution)/shard_map/ppermute | solution.py:433
  13.3 5.6 %collective-permute-done.1.refs_0_.first_ref = f32[136,128]{1,0:T(8,128)S(1)} collective-permute-done((f32[136,128]{1,0:T(8,128)S(1)}, f32[136,128]{1,0:T(8,128)S(1)}, u32[]{:S(2)}, u32[]{:S(2)}) %collective-permute-start.1) | collective-permute-done | bytes 69664 | tf_op jit(solution)/shard_map/ppermute | solution.py:433
  18.9 0.1 collective-permute-start.10
  19.0 3.1 %collective-permute-start.8 = (f32[128,128]{1,0:T(8,128)S(1)}, f32[128,128]{1,0:T(8,128)S(1)}, u32[]{:S(2)}, u32[]{:S(2)}) collective-permute-start(f32[128,128]{1,0:T(8,128)S(1)} %join.3), channel_id=1, source_target_pairs={{0,8},{4,12},{8,0},{12,4},{1,9},{5,13},{9,1},{13,5},{2,10},{6,14},... | collective-permute-start | bytes 196616 | tf_op jit(solution)/shard_map/ppermute | solution.py:433
  22.1 1.4 %collective-permute-start.9 = (f32[128,128]{1,0:T(8,128)S(1)}, f32[128,128]{1,0:T(8,128)S(1)}, u32[]{:S(2)}, u32[]{:S(2)}) collective-permute-start(f32[128,128]{1,0:T(8,128)S(1)} %join.4), channel_id=1, source_target_pairs={{0,12},{4,8},{8,4},{12,0},{1,13},{5,9},{9,5},{13,1},{2,14},{6,10},... | collective-permute-start | bytes 196616 | tf_op jit(solution)/shard_map/ppermute | solution.py:433
  23.5 0.3 place.2
  23.8 0.1 collective-permute-start.7
  23.9 1.6 %collective-permute-start.5 = (f32[136,128]{1,0:T(8,128)S(1)}, f32[136,128]{1,0:T(8,128)S(1)}, u32[]{:S(2)}, u32[]{:S(2)}) collective-permute-start(f32[136,128]{1,0:T(8,128)S(1)} %get-tuple-element.32), channel_id=1, source_target_pairs={{0,2},{1,3},{2,0},{3,1},{4,6},{5,7},{6,4},{7,5},{8,10},{9,11},{10,... | collective-permute-start | bytes 208904 | tf_op jit(solution)/shard_map/ppermute | solution.py:473
  25.5 0.0 collective-permute-done.10.refs_2_
  25.5 0.3 collective-permute-start.6
  25.8 1.2 %collective-permute-done.8.refs_0_ = f32[128,128]{1,0:T(8,128)S(1)} collective-permute-done((f32[128,128]{1,0:T(8,128)S(1)}, f32[128,128]{1,0:T(8,128)S(1)}, u32[]{:S(2)}, u32[]{:S(2)}) %collective-permute-start.8) | collective-permute-done | bytes 65568 | tf_op jit(solution)/shard_map/ppermute | solution.py:433
  27.0 1.4 %collective-permute-done.9.refs_1_ = f32[128,128]{1,0:T(8,128)S(1)} collective-permute-done((f32[128,128]{1,0:T(8,128)S(1)}, f32[128,128]{1,0:T(8,128)S(1)}, u32[]{:S(2)}, u32[]{:S(2)}) %collective-permute-start.9) | collective-permute-done | bytes 65568 | tf_op jit(solution)/shard_map/ppermute | solution.py:433
  28.4 0.0 collective-permute-done.7.refs_5_.refs_3_
  28.4 0.3 place.3
  28.7 1.6 %collective-permute-start.11 = (f32[128,128]{1,0:T(8,128)S(1)}, f32[128,128]{1,0:T(8,128)S(1)}, u32[]{:S(2)}, u32[]{:S(2)}) collective-permute-start(f32[128,128]{1,0:T(8,128)S(1)} %get-tuple-element.43), channel_id=1, source_target_pairs={{0,2},{1,3},{2,0},{3,1},{4,6},{5,7},{6,4},{7,5},{8,10},{9,11},{10,... | collective-permute-start | bytes 196616 | tf_op jit(solution)/shard_map/ppermute | solution.py:473
  30.2 0.6 %collective-permute-start.13 = (f32[128,128]{1,0:T(8,128)S(1)}, f32[128,128]{1,0:T(8,128)S(1)}, u32[]{:S(2)}, u32[]{:S(2)}) collective-permute-start(f32[128,128]{1,0:T(8,128)S(1)} %get-tuple-element.46), channel_id=1, source_target_pairs={{0,1},{1,0},{2,3},{3,2},{4,5},{5,4},{6,7},{7,6},{8,9},{9,8},{10,11... | collective-permute-start | bytes 196616 | tf_op jit(solution)/shard_map/ppermute | solution.py:473
  30.9 2.1 %collective-permute-done.11.refs_4_ = f32[128,128]{1,0:T(8,128)S(1)} collective-permute-done((f32[128,128]{1,0:T(8,128)S(1)}, f32[128,128]{1,0:T(8,128)S(1)}, u32[]{:S(2)}, u32[]{:S(2)}) %collective-permute-start.11) | collective-permute-done | bytes 65568 | tf_op jit(solution)/shard_map/ppermute | solution.py:473
  33.0 1.4 %collective-permute-done.12.refs_5_ = f32[128,128]{1,0:T(8,128)S(1)} collective-permute-done((f32[128,128]{1,0:T(8,128)S(1)}, f32[128,128]{1,0:T(8,128)S(1)}, u32[]{:S(2)}, u32[]{:S(2)}) %collective-permute-start.12) | collective-permute-done | bytes 65568 | tf_op jit(solution)/shard_map/ppermute | solution.py:473
  34.4 0.7 %total.1 = f32[16,2,16,128]{3,2,1,0:T(8,128)} custom-call(f32[136,128]{1,0:T(8,128)S(1)} %collective-permute-done.5.refs_0_, f32[136,128]{1,0:T(8,128)S(1)} %collective-permute-done.6.refs_1_, f32[128,128]{1,0:T(8,128)S(1)} %get-tuple-element.34.refs_2_, f32[128,128]{1,0:T(8,128)S(1)} %collective-permute-done.7.refs_5_.refs_3_, ...), custom_call_target="tpu_custom_call" | custom-call | tf_op jit(solution)/shard_map/total/pallas_call | solution.py:485
  (14 shorter events, 0.1 us)
Async XLA Ops:
  5.9 1.5 %collective-permute-start = (f32[272,128]{1,0:T(8,128)S(1)}, f32[272,128]{1,0:T(8,128)S(1)}, u32[]{:S(2)}, u32[]{:S(2)}) collective-permute-start(f32[272,128]{1,0:T(8,128)S(1)} %get-tuple-element.27), channel_id=1, source_target_pairs={{0,1},{1,0},{2,3},{3,2},{4,5},{5,4},{6,7},{7,6},{8,9},{9,8},{10,11... | collective-permute-start | bytes 417800 | tf_op jit(solution)/shard_map/ppermute | solution.py:428
  7.4 5.2 %collective-permute-start.3 = (f32[784,128]{1,0:T(8,128)S(1)}, f32[784,128]{1,0:T(8,128)S(1)}, u32[]{:S(2)}, u32[]{:S(2)}) collective-permute-start(f32[784,128]{1,0:T(8,128)S(1)} %keep.1), channel_id=1, source_target_pairs={{0,1},{1,0},{2,3},{3,2},{4,5},{5,4},{6,7},{7,6},{8,9},{9,8},{10,11... | collective-permute-start | bytes 1204232 | tf_op jit(solution)/shard_map/ppermute | solution.py:429
  7.8 14.3 %collective-permute-start.2 = (f32[136,128]{1,0:T(8,128)S(1)}, f32[136,128]{1,0:T(8,128)S(1)}, u32[]{:S(2)}, u32[]{:S(2)}) collective-permute-start(f32[136,128]{1,0:T(8,128)S(1)} %get-tuple-element.49), channel_id=1, source_target_pairs={{0,12},{4,8},{8,4},{12,0},{1,13},{5,9},{9,5},{13,1},{2,14},{6,10},... | collective-permute-start | bytes 208904 | tf_op jit(solution)/shard_map/ppermute | solution.py:433
  12.6 6.3 %collective-permute-start.1 = (f32[136,128]{1,0:T(8,128)S(1)}, f32[136,128]{1,0:T(8,128)S(1)}, u32[]{:S(2)}, u32[]{:S(2)}) collective-permute-start(f32[136,128]{1,0:T(8,128)S(1)} %get-tuple-element.50), channel_id=1, source_target_pairs={{0,8},{4,12},{8,0},{12,4},{1,9},{5,13},{9,1},{13,5},{2,10},{6,14},... | collective-permute-start | bytes 208904 | tf_op jit(solution)/shard_map/ppermute | solution.py:433
  12.6 10.9 %collective-permute-start.4 = (f32[136,128]{1,0:T(8,128)S(1)}, f32[136,128]{1,0:T(8,128)S(1)}, u32[]{:S(2)}, u32[]{:S(2)}) collective-permute-start(f32[136,128]{1,0:T(8,128)S(1)} %get-tuple-element.48), channel_id=1, source_target_pairs={{0,4},{4,0},{8,12},{12,8},{1,5},{5,1},{9,13},{13,9},{2,6},{6,2},{1... | collective-permute-start | bytes 208904 | tf_op jit(solution)/shard_map/ppermute | solution.py:433
  18.9 6.6 %collective-permute-start.10 = (f32[128,128]{1,0:T(8,128)S(1)}, f32[128,128]{1,0:T(8,128)S(1)}, u32[]{:S(2)}, u32[]{:S(2)}) collective-permute-start(f32[128,128]{1,0:T(8,128)S(1)} %get-tuple-element.40), channel_id=1, source_target_pairs={{0,4},{4,0},{8,12},{12,8},{1,5},{5,1},{9,13},{13,9},{2,6},{6,2},{1... | collective-permute-start | bytes 196616 | tf_op jit(solution)/shard_map/ppermute | solution.py:433
  19.0 8.0 %collective-permute-start.8 = (f32[128,128]{1,0:T(8,128)S(1)}, f32[128,128]{1,0:T(8,128)S(1)}, u32[]{:S(2)}, u32[]{:S(2)}) collective-permute-start(f32[128,128]{1,0:T(8,128)S(1)} %join.3), channel_id=1, source_target_pairs={{0,8},{4,12},{8,0},{12,4},{1,9},{5,13},{9,1},{13,5},{2,10},{6,14},... | collective-permute-start | bytes 196616 | tf_op jit(solution)/shard_map/ppermute | solution.py:433
  22.1 6.2 %collective-permute-start.9 = (f32[128,128]{1,0:T(8,128)S(1)}, f32[128,128]{1,0:T(8,128)S(1)}, u32[]{:S(2)}, u32[]{:S(2)}) collective-permute-start(f32[128,128]{1,0:T(8,128)S(1)} %join.4), channel_id=1, source_target_pairs={{0,12},{4,8},{8,4},{12,0},{1,13},{5,9},{9,5},{13,1},{2,14},{6,10},... | collective-permute-start | bytes 196616 | tf_op jit(solution)/shard_map/ppermute | solution.py:433
  23.8 4.5 %collective-permute-start.7 = (f32[128,128]{1,0:T(8,128)S(1)}, f32[128,128]{1,0:T(8,128)S(1)}, u32[]{:S(2)}, u32[]{:S(2)}) collective-permute-start(f32[128,128]{1,0:T(8,128)S(1)} %get-tuple-element.35), channel_id=1, source_target_pairs={{0,1},{1,0},{2,3},{3,2},{4,5},{5,4},{6,7},{7,6},{8,9},{9,8},{10,11... | collective-permute-start | bytes 196616 | tf_op jit(solution)/shard_map/ppermute | solution.py:473
  23.9 7.0 %collective-permute-start.5 = (f32[136,128]{1,0:T(8,128)S(1)}, f32[136,128]{1,0:T(8,128)S(1)}, u32[]{:S(2)}, u32[]{:S(2)}) collective-permute-start(f32[136,128]{1,0:T(8,128)S(1)} %get-tuple-element.32), channel_id=1, source_target_pairs={{0,2},{1,3},{2,0},{3,1},{4,6},{5,7},{6,4},{7,5},{8,10},{9,11},{10,... | collective-permute-start | bytes 208904 | tf_op jit(solution)/shard_map/ppermute | solution.py:473
  25.5 5.4 %collective-permute-start.6 = (f32[136,128]{1,0:T(8,128)S(1)}, f32[136,128]{1,0:T(8,128)S(1)}, u32[]{:S(2)}, u32[]{:S(2)}) collective-permute-start(f32[136,128]{1,0:T(8,128)S(1)} %get-tuple-element.33), channel_id=1, source_target_pairs={{0,3},{1,2},{2,1},{3,0},{4,7},{5,6},{6,5},{7,4},{8,11},{9,10},{10,... | collective-permute-start | bytes 208904 | tf_op jit(solution)/shard_map/ppermute | solution.py:473
  28.7 4.3 %collective-permute-start.11 = (f32[128,128]{1,0:T(8,128)S(1)}, f32[128,128]{1,0:T(8,128)S(1)}, u32[]{:S(2)}, u32[]{:S(2)}) collective-permute-start(f32[128,128]{1,0:T(8,128)S(1)} %get-tuple-element.43), channel_id=1, source_target_pairs={{0,2},{1,3},{2,0},{3,1},{4,6},{5,7},{6,4},{7,5},{8,10},{9,11},{10,... | collective-permute-start | bytes 196616 | tf_op jit(solution)/shard_map/ppermute | solution.py:473
  30.2 4.2 %collective-permute-start.12 = (f32[128,128]{1,0:T(8,128)S(1)}, f32[128,128]{1,0:T(8,128)S(1)}, u32[]{:S(2)}, u32[]{:S(2)}) collective-permute-start(f32[128,128]{1,0:T(8,128)S(1)} %get-tuple-element.44), channel_id=1, source_target_pairs={{0,3},{1,2},{2,1},{3,0},{4,7},{5,6},{6,5},{7,4},{8,11},{9,10},{10,... | collective-permute-start | bytes 196616 | tf_op jit(solution)/shard_map/ppermute | solution.py:473
  30.2 4.2 %collective-permute-start.13 = (f32[128,128]{1,0:T(8,128)S(1)}, f32[128,128]{1,0:T(8,128)S(1)}, u32[]{:S(2)}, u32[]{:S(2)}) collective-permute-start(f32[128,128]{1,0:T(8,128)S(1)} %get-tuple-element.46), channel_id=1, source_target_pairs={{0,1},{1,0},{2,3},{3,2},{4,5},{5,4},{6,7},{7,6},{8,9},{9,8},{10,11... | collective-permute-start | bytes 196616 | tf_op jit(solution)/shard_map/ppermute | solution.py:473
